TPU v7x, 32 devices: a whole 2x2x4 slice. The times are simulated.
32 devices in a mesh: parts: 2 (over y), item: 4 (over z), user: 2 (over x), ka: 2 (over core).
Axes of the slice: x: 2, y: 2, z: 4, core: 2. Of those that a mesh axis runs over, the one named last changes fastest.
Arguments:
- counts: int32 [8, 2, 64, 128, 128], P(('parts', 'item'), 'user'), parts along dimension 0, may hold values from 0 to 5, as said below
- tile_user: int32 [8, 2, 64], P(('parts', 'item'), 'user'), parts along dimension 0, may hold values from 0 to 15, as said below
- tile_item: int32 [8, 2, 64], P(('parts', 'item'), 'user'), parts along dimension 0, may hold values from 0 to 7
- tile_live: int32 [8, 2], P(('parts', 'item'), 'user'), parts along dimension 0, may hold values from 1 to 64, as said below
- theta_shape: float32 [4, 2048, 512], P(('parts', 'user'), 'item', 'ka'), parts along dimension 0, may hold values from 0.3 to 3
- theta_rate: float32 [4, 2048, 512], P(('parts', 'user'), 'item', 'ka'), parts along dimension 0, may hold values from 512 to 32768
- user_activity: float32 [4, 2048], P(('parts', 'user'), 'item'), parts along dimension 0, may hold values from 0.3 to 3
- beta_shape: float32 [8, 1024, 512], P(('parts', 'item'), 'user', 'ka'), parts along dimension 0, may hold values from 0.3 to 3
- beta_rate: float32 [8, 1024, 512], P(('parts', 'item'), 'user', 'ka'), parts along dimension 0, may hold values from 512 to 32768
- item_popularity: float32 [8, 1024], P(('parts', 'item'), 'user'), parts along dimension 0, may hold values from 0.3 to 3
Outputs:
- new_theta_shape: float32 [4, 2048, 512], P(('parts', 'user'), 'item', 'ka'), parts along dimension 0
- new_theta_rate: float32 [4, 2048, 512], P(('parts', 'user'), 'item', 'ka'), parts along dimension 0
- new_beta_shape: float32 [8, 1024, 512], P(('parts', 'item'), 'user', 'ka'), parts along dimension 0
- new_beta_rate: float32 [8, 1024, 512], P(('parts', 'item'), 'user', 'ka'), parts along dimension 0
There are 2 independent parts, one for each index of `parts`. A program takes and returns all parts, laid end to end along the dimension named above; each array names one. Nothing has to cross between parts.
Inputs may be any that keep to these rules, and one draw needn't show every extreme that they name: `tile_live`: slots at or beyond a device's live count hold stale tiles; some device has all 64 slots live. `counts`: most cells are 0. The pairs (tile_user, tile_item) of the 64 slots of one device are all different.
All inputs are finite; a program needn't handle non-finite values.
Results may differ from a plain program's by a relative error of at most 0.006.
Values may be sent and summed in bfloat16 or wider, within the bound.
No kernel may reach another device: no remote copies, remote signals or barrier semaphores. Data moves between devices by JAX's collectives and lax.ppermute only.
A program may use at most 64 MiB of HBM per device.

v0:
```python
import jax
import jax.numpy as jnp
from jax import lax
from jax.sharding import PartitionSpec as P


def expected_exp(shape_arg, rate_arg):
    return jnp.exp(lax.digamma(shape_arg) - jnp.log(rate_arg)).astype(jnp.bfloat16)


def body(
    counts,
    tile_user,
    tile_item,
    tile_live,
    theta_shape,
    theta_rate,
    user_activity,
    beta_shape,
    beta_rate,
    item_popularity,
):
    n_slots = counts.shape[2]
    tile = counts.shape[3]
    user_exp = expected_exp(theta_shape, theta_rate)
    item_exp = expected_exp(beta_shape, beta_rate)
    user_block = lax.all_gather(user_exp, "item", axis=1, tiled=True)[0]
    panel = lax.all_gather(item_exp, "user", axis=1, tiled=True)[0]
    half = user_block.shape[1]
    user_tiles_n = user_block.shape[0] // tile
    item_tiles_n = panel.shape[0] // tile
    users = tile_user[0, 0]
    items = tile_item[0, 0]
    live = tile_live[0, 0]
    grid_all = counts[0, 0]
    user_rows = user_block.reshape(user_tiles_n, tile, half)
    item_rows = panel.reshape(item_tiles_n, tile, half)
    slot_index = jnp.arange(n_slots, dtype=jnp.int32)
    left = user_rows[users]
    right = item_rows[items]
    part = jnp.einsum("bik,bjk->bij", left, right, preferred_element_type=jnp.float32).astype(
        jnp.bfloat16
    )
    total = lax.optimization_barrier(part).astype(jnp.float32)
    norms = total
    norms = lax.psum(norms.astype(jnp.bfloat16), "ka").astype(jnp.float32)
    mask = (slot_index < live)[:, None, None]
    ratio = jnp.where(mask, grid_all.astype(jnp.float32) / jnp.where(mask, norms, 1.0), 0.0).astype(
        jnp.bfloat16
    )
    left = user_rows[users]
    right = item_rows[items]
    user_part = jnp.einsum("bij,bjk->bik", ratio, right, preferred_element_type=jnp.float32)
    item_part = jnp.einsum("bij,bik->bjk", ratio, left, preferred_element_type=jnp.float32)
    user_onehot = (users[:, None] == jnp.arange(user_tiles_n, dtype=jnp.int32)[None, :]).astype(
        jnp.float32
    )
    item_onehot = (items[:, None] == jnp.arange(item_tiles_n, dtype=jnp.int32)[None, :]).astype(
        jnp.float32
    )
    user_acc = jnp.einsum("bu,bik->uik", user_onehot, user_part, precision=lax.Precision.HIGHEST)
    item_acc = jnp.einsum("bv,bjk->vjk", item_onehot, item_part, precision=lax.Precision.HIGHEST)
    user_acc, item_acc = (user_acc, item_acc)
    user_sum = lax.psum_scatter(
        user_acc.reshape(user_tiles_n * tile, half).astype(jnp.bfloat16),
        "item",
        scatter_dimension=0,
        tiled=True,
    ).astype(jnp.float32)
    item_sum = lax.psum_scatter(
        item_acc.reshape(item_tiles_n * tile, half).astype(jnp.bfloat16),
        "user",
        scatter_dimension=0,
        tiled=True,
    ).astype(jnp.float32)
    beta_local = jnp.sum(beta_shape / beta_rate, axis=(0, 1))
    theta_local = jnp.sum(theta_shape / theta_rate, axis=(0, 1))
    beta_total, theta_total = lax.psum((beta_local, theta_local), ("item", "user"))
    new_theta_shape = 0.3 + user_exp.astype(jnp.float32) * user_sum[None]
    new_theta_rate = user_activity[..., None] + beta_total
    new_beta_shape = 0.3 + item_exp.astype(jnp.float32) * item_sum[None]
    new_beta_rate = item_popularity[..., None] + theta_total
    return (new_theta_shape, new_theta_rate, new_beta_shape, new_beta_rate)


def solution(mesh):
    in_specs = (
        P(("parts", "item"), "user", None, None, None),
        P(("parts", "item"), "user", None),
        P(("parts", "item"), "user", None),
        P(("parts", "item"), "user"),
        P(("parts", "user"), "item", "ka"),
        P(("parts", "user"), "item", "ka"),
        P(("parts", "user"), "item"),
        P(("parts", "item"), "user", "ka"),
        P(("parts", "item"), "user", "ka"),
        P(("parts", "item"), "user"),
    )
    out_specs = (
        P(("parts", "user"), "item", "ka"),
        P(("parts", "user"), "item", "ka"),
        P(("parts", "item"), "user", "ka"),
        P(("parts", "item"), "user", "ka"),
    )
    return jax.shard_map(body, mesh=mesh, in_specs=in_specs, out_specs=out_specs, check_vma=False)
```

profile of v0, /device:TPU:0, one launch (start us, length us, event | category | flops | bytes accessed | tf_op | source)
XLA Modules:
  0.0 142.0 jit_solution(1251894438747012246)
XLA Ops:
  7.2 0.0 all-gather.2.cloned.1.call-start
  7.2 5.5 %divide_reduce_fusion = (f32[256]{0:T(256)S(1)}, bf16[1,512,256]{2,1,0:T(8,128)(2,1)}) fusion(f32[1,512,256]{2,1,0:T(8,128)} %param.14, f32[1,512,256]{2,1,0:T(8,128)} %param.15), kind=kLoop, calls=%fused_computation.30 | loop fusion | flops 10354432 | bytes 1311744 | tf_op jit(solution)/shard_map/reduce_sum | solution.py:77
  12.7 0.0 all-reduce.3.cloned.1.call-start
  12.7 0.7 fusion.33
  13.4 4.8 %divide_reduce_fusion.1 = (f32[256]{0:T(256)S(1)}, bf16[1,512,256]{2,1,0:T(8,128)(2,1)S(1)}) fusion(f32[1,512,256]{2,1,0:T(8,128)} %param.17, f32[1,512,256]{2,1,0:T(8,128)} %param.18), kind=kLoop, calls=%fused_computation.31 | loop fusion | flops 10354432 | bytes 1311744 | tf_op jit(solution)/shard_map/reduce_sum | solution.py:76
  18.2 9.9 %all_gather.7 = bf16[1,1024,256]{2,1,0:T(8,128)(2,1)S(1)} all-gather(bf16[1,512,256]{2,1,0:T(8,128)(2,1)S(1)} %get-tuple-element.9), channel_id=1, replica_groups=mesh['parts'=2,'item'=4,'user'=2,'ka'=2] {'user'}, dimensions={1}, use_global_device_ids=true | all-gather | bytes 786432 | tf_op jit(solution)/shard_map/all_gather | solution.py:28
  28.1 2.8 %gather_fusion.1 = bf16[64,128,256]{2,1,0:T(8,128)(2,1)} fusion(bf16[8,128,256]{2,1,0:T(8,128)(2,1)S(1)} %bitcast.42, s32[1024]{0:T(1024)S(1)} %pad_clamp_fusion), kind=kCustom, calls=%fused_computation.1 | custom fusion | bytes 8388864 | tf_op jit(solution)/shard_map/gather | solution.py:40
  30.9 12.6 %all-gather.2.cloned.1.call-done = bf16[1,2048,256]{2,1,0:T(8,128)(2,1)} async-done(((bf16[1,512,256]{2,1,0:T(8,128)(2,1)}), bf16[1,2048,256]{2,1,0:T(8,128)(2,1)}) %all-gather.2.cloned.1.call-update) | async-done | bytes 1048592 | tf_op jit(solution)/shard_map/all_gather | solution.py:27
  43.5 4.0 %gather_fusion = bf16[64,128,256]{2,1,0:T(8,128)(2,1)} fusion(bf16[16,128,256]{2,1,0:T(8,128)(2,1)} %bitcast.43, s32[1024]{0:T(1024)S(1)} %pad_clamp_fusion.1), kind=kCustom, calls=%fused_computation | custom fusion | bytes 8388864 | tf_op jit(solution)/shard_map/gather | solution.py:39
  47.5 6.0 %convolution_convert_fusion = bf16[64,128,128]{2,1,0:T(8,128)(2,1)} fusion(bf16[64,128,256]{2,1,0:T(8,128)(2,1)} %gather_fusion, bf16[64,128,256]{2,1,0:T(8,128)(2,1)} %gather_fusion.1), kind=kOutput, calls=%fused_computation.9 | convolution fusion | flops 537919488 | bytes 10485760 | tf_op jit(solution)/shard_map/bik,bjk->bij/dot_general | solution.py:41
  53.5 0.2 reduce-scatter.5.cloned.1.call-start
  54.4 20.0 %all-reduce.3.cloned.1.call-done = bf16[64,128,128]{2,1,0:T(8,128)(2,1)} async-done(((bf16[64,128,128]{2,1,0:T(8,128)(2,1)}), bf16[64,128,128]{2,1,0:T(8,128)(2,1)}) %all-reduce.3.cloned.1.call-update) | async-done | bytes 2097168 | tf_op jit(solution)/shard_map/psum | solution.py:46
  74.4 5.6 %fusion.34 = f32[64,128,256]{2,1,0:T(8,128)S(1)} fusion(bf16[64,128,256]{2,1,0:T(8,128)(2,1)} %gather_fusion, bf16[64,128,128]{2,1,0:T(8,128)(2,1)} %all-reduce.3.cloned.1.call-done, s32[1,1,64,128,128]{4,3,2,1,0:T(8,128)} %param.10, pred[64]{0:T(512)(128)(4,1)S(1)} %iota_compare_fusion.2), kind=kOutput, calls=%fused_computation.49 | convolution fusion | flops 543162368 | bytes 18874432 | tf_op jit(solution)/shard_map/bij,bik->bjk/dot_general | solution.py:54
  80.0 7.5 %fusion.9 = bf16[8,128,256]{2,0,1:T(8,128)(2,1)S(1)} fusion(f32[64,128,256]{2,1,0:T(8,128)S(1)} %fusion.34, s32[64]{0:T(128)S(1)} %bitcast.48), kind=kOutput, calls=%fused_computation.11 | convolution fusion | flops 201589248 | bytes 8913152 | tf_op jit(solution)/shard_map/bv,bjk->vjk/dot_general | solution.py:62
  87.5 0.9 copy.15
  88.4 0.3 reduce-scatter.3.cloned.1.call-start
  88.7 4.8 %fusion.36 = f32[64,128,256]{2,1,0:T(8,128)S(1)} fusion(bf16[64,128,256]{2,1,0:T(8,128)(2,1)} %gather_fusion.1, bf16[64,128,128]{2,1,0:T(8,128)(2,1)S(1)} %copy-done.5, s32[1,1,64,128,128]{4,3,2,1,0:T(8,128)} %param.10, pred[64]{0:T(512)(128)(4,1)S(1)} %iota_compare_fusion.2), kind=kOutput, calls=%fused_computation.50 | convolution fusion | flops 543162368 | bytes 18874432 | tf_op jit(solution)/shard_map/bij,bjk->bik/dot_general | solution.py:53
  93.5 7.5 %fusion.6 = bf16[16,128,256]{2,0,1:T(8,128)(2,1)S(1)} fusion(f32[64,128,256]{2,1,0:T(8,128)S(1)} %fusion.36, s32[64]{0:T(128)S(1)} %bitcast.49), kind=kOutput, calls=%fused_computation.10 | convolution fusion | flops 403178496 | bytes 9437440 | tf_op jit(solution)/shard_map/bu,bik->uik/dot_general | solution.py:61
  101.1 1.3 copy.14
  102.4 22.0 %all-reduce = (f32[256]{0:T(256)S(1)}, f32[256]{0:T(256)S(1)}) all-reduce(f32[256]{0:T(256)S(1)} %get-tuple-element.8, f32[256]{0:T(256)S(1)} %get-tuple-element.6), channel_id=1, replica_groups=mesh['parts'=2,'item'=4,'user'=2,'ka'=2] {'item','user'}, use_global_device_ids=true, to_apply=%region_3.4 | all-reduce | flops 512 | bytes 4096 | tf_op jit(solution)/shard_map/psum | solution.py:78
  124.5 1.2 broadcast_add_fusion
  125.6 1.8 %fusion.22 = f32[1,512,256]{2,1,0:T(8,128)} fusion(bf16[1,512,256]{2,1,0:T(8,128)(2,1)S(1)} %get-tuple-element.9, bf16[512,256]{1,0:T(8,128)(2,1)} %reduce-scatter.5.cloned.1.call-done), kind=kLoop, calls=%fused_computation.27 | loop fusion | flops 524288 | bytes 1048576 | tf_op jit(solution)/shard_map/add | solution.py:81
  127.4 6.2 %reduce-scatter.3.cloned.1.call-done = bf16[512,256]{1,0:T(8,128)(2,1)} async-done(((bf16[2048,256]{1,0:T(8,128)(2,1)}), bf16[512,256]{1,0:T(8,128)(2,1)}) %reduce-scatter.3.cloned.1.call-update) | async-done | bytes 262160 | tf_op jit(solution)/shard_map/reduce_scatter | solution.py:64
  133.7 1.8 %fusion.23 = f32[1,512,256]{2,1,0:T(8,128)} fusion(bf16[1,512,256]{2,1,0:T(8,128)(2,1)S(1)} %copy-done, bf16[512,256]{1,0:T(8,128)(2,1)} %reduce-scatter.3.cloned.1.call-done), kind=kLoop, calls=%fused_computation.29 | loop fusion | flops 524288 | bytes 1048576 | tf_op jit(solution)/shard_map/add | solution.py:79
  (21 shorter events, 0.1 us)
Async XLA Ops:
  7.2 36.3 %all-gather.2.cloned.1.call-start = ((), (), s32[]{:S(2)}) async-start(), calls=%async_computation.2 | async-start | bytes 1310720 | tf_op jit(solution)/shard_map/all_gather | solution.py:27
  12.7 61.7 %all-reduce.3.cloned.1.call-start = ((), (), s32[]{:S(2)}) async-start(), calls=%async_computation.3 | async-start | bytes 4194304 | tf_op jit(solution)/shard_map/psum | solution.py:46
  28.1 2.8 %copy-start.4 = (s32[1,1,64]{2,1,0:T(1,128)S(1)}, s32[1,1,64]{2,1,0:T(1,128)}, u32[]{:S(2)}) copy-start(s32[1,1,64]{2,1,0:T(1,128)} %param.11) | copy-start | bytes 772
  53.5 72.1 %reduce-scatter.5.cloned.1.call-start = ((), (), s32[]{:S(2)}) async-start(), calls=%async_computation.5 | async-start | bytes 786432 | tf_op jit(solution)/shard_map/reduce_scatter | solution.py:70
  54.4 25.6 %copy-start.3 = (s32[1,1,64]{2,1,0:T(1,128)S(1)}, s32[1,1,64]{2,1,0:T(1,128)}, u32[]{:S(2)}) copy-start(s32[1,1,64]{2,1,0:T(1,128)} %param.12) | copy-start | bytes 772
  80.0 8.7 %copy-start.5 = (bf16[64,128,128]{2,1,0:T(8,128)(2,1)S(1)}, bf16[64,128,128]{2,1,0:T(8,128)(2,1)}, u32[]{:S(2)}) copy-start(bf16[64,128,128]{2,1,0:T(8,128)(2,1)} %all-reduce.3.cloned.1.call-done) | copy-start | bytes 6291460
  88.4 45.3 %reduce-scatter.3.cloned.1.call-start = ((), (), s32[]{:S(2)}) async-start(), calls=%async_computation.4 | async-start | bytes 1310720 | tf_op jit(solution)/shard_map/reduce_scatter | solution.py:64
  93.5 31.0 %copy-start.1 = (f32[1,512]{1,0:T(1,128)S(1)}, f32[1,512]{1,0:T(1,128)}, u32[]{:S(2)}) copy-start(f32[1,512]{1,0:T(1,128)} %param.19) | copy-start | bytes 6148
  93.5 30.9 %copy-start.2 = (f32[1,512]{1,0:T(1,128)S(1)}, f32[1,512]{1,0:T(1,128)}, u32[]{:S(2)}) copy-start(f32[1,512]{1,0:T(1,128)} %param.16) | copy-start | bytes 6148
  101.1 32.6 %copy-start = (bf16[1,512,256]{2,1,0:T(8,128)(2,1)S(1)}, bf16[1,512,256]{2,1,0:T(8,128)(2,1)}, u32[]{:S(2)}) copy-start(bf16[1,512,256]{2,1,0:T(8,128)(2,1)} %get-tuple-element.7) | copy-start | bytes 786436
Sparse Core Ops, SparseCore 0:
  12.8 30.6 all-gather.1
  53.7 20.7 all-reduce.2
  88.5 15.7 reduce-scatter.4
  106.5 27.1 reduce-scatter.2
where the time goes:
time: 142 us
  waiting for transfers between devices  38.9 us (27%)
  blocking collectives  31.9 us (22%)
  matrix products  31.4 us (22%)
  other arithmetic  15.7 us (11%)
  between operations  14.5 us (10%)
  local copies, waits for them, and re-layouts  9.01 us (6%)
    psum x1, blocking collectives, body(): lax.psum((beta_local, theta_local), ('item', 'user'))  22 us
    psum x1, waiting for transfers between devices, body(): norms = lax.psum(norms.astype(jnp.bfloat16), 'ka').astype(jnp.float32)  20 us
    all_gather x1, waiting for transfers between devices, body(): user_block = lax.all_gather(user_exp, 'item', axis=1, tiled=True)[0]  12.6 us
    all_gather x1, blocking collectives, body(): panel = lax.all_gather(item_exp, 'user', axis=1, tiled=True)[0]  9.91 us
    dot_general x1, matrix products, body(): jnp.einsum('bu,bik->uik', user_onehot, user_part, precision=lax.Precision...  7.55 us
    dot_general x1, matrix products, body(): jnp.einsum('bv,bjk->vjk', item_onehot, item_part, precision=lax.Precision...  7.47 us
    reduce_scatter x1, waiting for transfers between devices, body(): lax.psum_scatter(user_acc.reshape(user_tiles_n * tile, half).astype(jnp.b...  6.24 us
    dot_general x1, matrix products, body(): jnp.einsum('bik,bjk->bij', left, right, preferred_element_type=jnp.float32)  6.03 us
  transfers between devices with their start and end apart: 4, of which 3 were waited for; matrix products, arithmetic and copies ran while one was open for 18% of the time, Pallas kernels for 0%

commit v1 on v0

v1 whole, which is shorter than its diff:
```python
import functools

import jax
import jax.numpy as jnp
from jax import lax
from jax.experimental import pallas as pl
from jax.experimental.pallas import tpu as pltpu
from jax.sharding import PartitionSpec as P

BF16 = jnp.bfloat16
F32 = jnp.float32
VMEM_LIMIT = 48 * 1024 * 1024


def exp_digamma_over(x, inv_rate):
    w = x * (x + 5.0)
    shift = (2.0 * x + 5.0) * (3.0 * w * w + 20.0 * w + 24.0) / (w * (w + 4.0) * (w + 6.0))
    y = x + 6.0
    iy = 1.0 / y
    iy2 = iy * iy
    series = iy * 0.5 + iy2 * (1.0 / 12.0 - iy2 * (1.0 / 120.0 - iy2 * (1.0 / 252.0)))
    return y * inv_rate * jnp.exp(-(series + shift))


def expected_kernel(shape_ref, rate_ref, exp_ref, total_ref):
    x = shape_ref[...]
    inv_rate = 1.0 / rate_ref[...]
    exp_ref[...] = exp_digamma_over(x, inv_rate).astype(BF16)
    part = jnp.sum(x * inv_rate, axis=0, keepdims=True)

    @pl.when(pl.program_id(0) == 0)
    def _():
        total_ref[...] = part

    @pl.when(pl.program_id(0) != 0)
    def _():
        total_ref[...] += part


def expected(shape_arg, rate_arg, name):
    rows, cols = shape_arg.shape
    block = min(rows, 128)
    spec = pl.BlockSpec((block, cols), lambda g: (g, 0))
    return pl.pallas_call(
        expected_kernel,
        grid=(rows // block,),
        in_specs=[spec, spec],
        out_specs=[spec, pl.BlockSpec((1, cols), lambda g: (0, 0))],
        out_shape=[
            jax.ShapeDtypeStruct((rows, cols), BF16),
            jax.ShapeDtypeStruct((1, cols), F32),
        ],
        cost_estimate=pl.CostEstimate(
            flops=40 * rows * cols, transcendentals=4 * rows * cols, bytes_accessed=10 * rows * cols
        ),
        name=name,
    )(shape_arg, rate_arg)


def dense_kernel(n_user, shard_tiles, chunk, users_ref, items_ref, live_ref, me_ref, counts_ref, out_ref):
    g = pl.program_id(0)
    tile = counts_ref.shape[1]

    @pl.when(g == 0)
    def _():
        out_ref[...] = jnp.zeros_like(out_ref)

    def place(t, carry):
        slot = g * chunk + t
        item = items_ref[slot]
        owner = lax.div(item, shard_tiles)
        position = lax.rem(me_ref[0] - owner + n_user, n_user)
        column = position * shard_tiles + lax.rem(item, shard_tiles)
        row = pl.multiple_of(users_ref[slot] * tile, tile)
        col = pl.multiple_of(column * tile, tile)
        out_ref[pl.ds(row, tile), pl.ds(col, tile)] = counts_ref[t].astype(F32).astype(BF16)
        return carry

    lax.fori_loop(0, jnp.clip(live_ref[0] - g * chunk, 0, chunk), place, 0)


def dense_counts(counts, users, items, live, me, user_rows, item_rows, n_user):
    slots, tile, _ = counts.shape
    chunk = 8
    shard_tiles = item_rows // n_user // tile
    return pl.pallas_call(
        functools.partial(dense_kernel, n_user, shard_tiles, chunk),
        grid_spec=pltpu.PrefetchScalarGridSpec(
            num_scalar_prefetch=4,
            grid=(slots // chunk,),
            in_specs=[pl.BlockSpec((chunk, tile, tile), lambda g, *_: (g, 0, 0))],
            out_specs=pl.BlockSpec((user_rows, item_rows), lambda g, *_: (0, 0)),
        ),
        out_shape=jax.ShapeDtypeStruct((user_rows, item_rows), BF16),
        compiler_params=pltpu.CompilerParams(vmem_limit_bytes=VMEM_LIMIT),
        cost_estimate=pl.CostEstimate(
            flops=slots * tile * tile,
            transcendentals=0,
            bytes_accessed=4 * slots * tile * tile + 2 * user_rows * item_rows,
        ),
        name="dense_counts",
    )(users, items, live, me, counts)


def stat_kernel(pieces, has_sum, has_acc, index_ref, mine_ref, other_ref, *refs):
    refs = list(refs)
    item_mine = [refs.pop(0) for _ in range(pieces)]
    item_other = [refs.pop(0) for _ in range(pieces)]
    counts_ref = refs.pop(0)
    sum_ref = refs.pop(0) if has_sum else None
    acc_in = [refs.pop(0) for _ in range(pieces)] if has_acc else None
    stat_ref = refs.pop(0)
    acc_out = [refs.pop(0) for _ in range(pieces)]
    acc = [refs.pop(0) for _ in range(pieces)]
    g = pl.program_id(0)

    @pl.when(g == 0)
    def _():
        for p in range(pieces):
            if has_acc:
                acc[p][...] = acc_in[p][...]
            else:
                acc[p][...] = jnp.zeros_like(acc[p])

    mine = mine_ref[...]
    other = other_ref[...]
    dims_nt = (((1,), (1,)), ((), ()))
    dims_tn = (((0,), (0,)), ((), ()))
    total = sum_ref[...].astype(F32) if has_sum else None
    width = 256
    for p in range(pieces):
        rows = item_mine[p].shape[0]
        for c in range(rows // width):
            part = slice(c * width, (c + 1) * width)
            left = item_mine[p][part, :]
            norm = lax.dot_general(mine, left, dims_nt, preferred_element_type=F32)
            norm += lax.dot_general(other, item_other[p][part, :], dims_nt, preferred_element_type=F32)
            grid = counts_ref[:, p * rows + c * width : p * rows + (c + 1) * width].astype(F32)
            ratio = (grid / norm).astype(BF16)
            stat = jnp.dot(ratio, left, preferred_element_type=F32)
            total = stat if total is None else total + stat
            acc[p][:, part] += lax.dot_general(mine, ratio, dims_tn, preferred_element_type=F32)
    stat_ref[...] = total.astype(stat_ref.dtype)

    @pl.when(g == pl.num_programs(0) - 1)
    def _():
        for p in range(pieces):
            acc_out[p][...] = acc[p][...].astype(acc_out[p].dtype)


def statistics(index, mine, other, item_mine, item_other, dense, running, acc, stat_dtype, acc_dtypes, name):
    rows, half = mine.shape
    pieces = len(item_mine)
    item_rows = dense.shape[1]
    block = min(rows, 256)
    steps = rows // block
    row_spec = pl.BlockSpec((block, half), lambda g, i: (g, 0))
    piece_spec = pl.BlockSpec((item_rows // pieces, half), lambda g, i: (0, 0))
    acc_spec = pl.BlockSpec((half, item_rows // pieces), lambda g, i: (0, 0))
    args = [mine, other, *item_mine, *item_other, dense]
    in_specs = [row_spec, row_spec] + [piece_spec] * (2 * pieces)
    in_specs.append(pl.BlockSpec((block, item_rows), lambda g, i: (i[0] * steps + g, 0)))
    if running is not None:
        args.append(running)
        in_specs.append(row_spec)
    if acc is not None:
        args += acc
        in_specs += [acc_spec] * pieces
    out = pl.pallas_call(
        functools.partial(stat_kernel, pieces, running is not None, acc is not None),
        grid_spec=pltpu.PrefetchScalarGridSpec(
            num_scalar_prefetch=1,
            grid=(steps,),
            in_specs=in_specs,
            out_specs=[row_spec] + [acc_spec] * pieces,
            scratch_shapes=[pltpu.VMEM((half, item_rows // pieces), F32)] * pieces,
        ),
        out_shape=[jax.ShapeDtypeStruct((rows, half), stat_dtype)]
        + [jax.ShapeDtypeStruct((half, item_rows // pieces), d) for d in acc_dtypes],
        compiler_params=pltpu.CompilerParams(vmem_limit_bytes=VMEM_LIMIT),
        cost_estimate=pl.CostEstimate(
            flops=8 * rows * item_rows * half,
            transcendentals=rows * item_rows,
            bytes_accessed=4 * rows * half + 4 * item_rows * half + 2 * rows * item_rows + 8 * item_rows * half,
        ),
        name=name,
    )(index, *args)
    return out[0], list(out[1:])


def finish_users_kernel(exp_ref, own_ref, came_ref, out_ref):
    total = own_ref[...] + came_ref[...].astype(F32)
    out_ref[...] = 0.3 + exp_ref[...].astype(F32) * total


def finish_items_kernel(pieces, exp_ref, own_ref, *refs):
    total = own_ref[...]
    for p in range(pieces):
        total += refs[p][...].astype(F32)
    refs[pieces][...] = 0.3 + exp_ref[...].astype(F32) * total.T


def ring(x, axis, n, shift):
    return lax.ppermute(x, axis, [(i, (i + shift) % n) for i in range(n)])


def body(
    n_item,
    n_user,
    n_ka,
    counts,
    tile_user,
    tile_item,
    tile_live,
    theta_shape,
    theta_rate,
    user_activity,
    beta_shape,
    beta_rate,
    item_popularity,
):
    def sibling(x):
        return ring(x, "ka", n_ka, 1)

    user_exp, theta_local = expected(theta_shape[0], theta_rate[0], "expected_users")
    item_exp, beta_local = expected(beta_shape[0], beta_rate[0], "expected_items")
    rows = user_exp.shape[0]
    user_rows = rows * n_item
    item_rows = item_exp.shape[0] * n_user

    item_mine = [item_exp]
    for t in range(1, n_user):
        item_mine.append(ring(item_mine[-1], "user", n_user, 1))
    item_other = [sibling(x) for x in item_mine]

    b_index = lax.axis_index("user").astype(jnp.int32)
    s_index = lax.axis_index("item").astype(jnp.int32)
    dense = dense_counts(
        counts[0, 0],
        tile_user[0, 0],
        tile_item[0, 0],
        tile_live[0],
        b_index[None],
        user_rows,
        item_rows,
        n_user,
    )

    own_stat = None
    running = None
    acc = None
    mine = user_exp
    for t in range(n_item):
        last = t == n_item - 1
        following = None if last else ring(mine, "item", n_item, 1)
        other = sibling(mine)
        index = lax.rem(s_index - t + n_item, n_item)[None]
        acc_dtypes = [F32] + [BF16 if last else F32] * (n_user - 1)
        stat, acc = statistics(
            index,
            mine,
            other,
            item_mine,
            item_other,
            dense,
            running,
            acc,
            F32 if t == 0 else BF16,
            acc_dtypes,
            "statistics_%d" % t,
        )
        if t == 0:
            own_stat = stat
        else:
            running = ring(stat, "item", n_item, 1)
        mine = following

    came = [ring(acc[t], "user", n_user, -t) for t in range(1, n_user)]

    totals = jnp.concatenate([theta_local, beta_local], axis=0)
    moving = totals
    for t in range(1, n_user):
        moving = ring(moving, "user", n_user, 1)
        totals = totals + moving
    moving = totals
    for t in range(1, n_item):
        moving = ring(moving, "item", n_item, 1)
        totals = totals + moving
    theta_total = totals[0]
    beta_total = totals[1]

    half = user_exp.shape[1]
    user_block = min(rows, 256)
    user_spec = pl.BlockSpec((user_block, half), lambda g: (g, 0))
    new_theta_shape = pl.pallas_call(
        finish_users_kernel,
        grid=(rows // user_block,),
        in_specs=[user_spec] * 3,
        out_specs=user_spec,
        out_shape=jax.ShapeDtypeStruct((rows, half), F32),
        cost_estimate=pl.CostEstimate(flops=3 * rows * half, transcendentals=0, bytes_accessed=12 * rows * half),
        name="finish_users",
    )(user_exp, own_stat, running)
    own_items = item_exp.shape[0]
    item_block = min(own_items, 256)
    item_spec = pl.BlockSpec((item_block, half), lambda g: (g, 0))
    acc_spec = pl.BlockSpec((half, item_block), lambda g: (0, g))
    new_beta_shape = pl.pallas_call(
        functools.partial(finish_items_kernel, n_user - 1),
        grid=(own_items // item_block,),
        in_specs=[item_spec] + [acc_spec] * n_user,
        out_specs=item_spec,
        out_shape=jax.ShapeDtypeStruct((own_items, half), F32),
        cost_estimate=pl.CostEstimate(
            flops=3 * own_items * half, transcendentals=0, bytes_accessed=12 * own_items * half
        ),
        name="finish_items",
    )(item_exp, acc[0], *came)
    new_theta_rate = user_activity[..., None] + beta_total
    new_beta_rate = item_popularity[..., None] + theta_total
    return (new_theta_shape[None], new_theta_rate, new_beta_shape[None], new_beta_rate)


def solution(mesh):
    in_specs = (
        P(("parts", "item"), "user", None, None, None),
        P(("parts", "item"), "user", None),
        P(("parts", "item"), "user", None),
        P(("parts", "item"), "user"),
        P(("parts", "user"), "item", "ka"),
        P(("parts", "user"), "item", "ka"),
        P(("parts", "user"), "item"),
        P(("parts", "item"), "user", "ka"),
        P(("parts", "item"), "user", "ka"),
        P(("parts", "item"), "user"),
    )
    out_specs = (
        P(("parts", "user"), "item", "ka"),
        P(("parts", "user"), "item", "ka"),
        P(("parts", "item"), "user", "ka"),
        P(("parts", "item"), "user", "ka"),
    )
    run = functools.partial(body, mesh.shape["item"], mesh.shape["user"], mesh.shape["ka"])
    return jax.shard_map(run, mesh=mesh, in_specs=in_specs, out_specs=out_specs, check_vma=False)
```

time: 142 us -> 95.7 us (0.67)
  Pallas kernels: 0 us -> 33.4 us
  blocking collectives: 31.9 us -> 0 us
  matrix products: 31.4 us -> 0 us
  other arithmetic: 15.7 us -> 1.2 us
  between operations: 14.5 us -> 1.45 us
  starting transfers between devices: 0.57 us -> 9.31 us
    ppermute x0 -> x18, waiting for transfers between devices: none -> 40.2 us  [ring(): return lax.ppermute(x, axis, [(i, (i + shift) % n) for i in range(n)])]
    pallas_call x0 -> x9, Pallas kernels: none -> 33.4 us  [the longest x4 16.6 us: statistics(): pl.pallas_call(functools.partial(stat_kernel, pieces, running is not None...]
    dot_general x5 -> x0, matrix products: 31.4 us -> none  [the longest x1 7.55 us: body(): jnp.einsum('bu,bik->uik', user_onehot, user_part, precision=lax.Precision...]
    psum x1 -> x0, blocking collectives: 22 us -> none  [body(): lax.psum((beta_local, theta_local), ('item', 'user'))]
    psum x1 -> x0, waiting for transfers between devices: 20 us -> none  [body(): norms = lax.psum(norms.astype(jnp.bfloat16), 'ka').astype(jnp.float32)]
    all_gather x1 -> x0, waiting for transfers between devices: 12.6 us -> none  [body(): user_block = lax.all_gather(user_exp, 'item', axis=1, tiled=True)[0]]
    reduce_sum x2 -> x0, other arithmetic: 10.3 us -> none  [the longest x1 5.46 us: body(): theta_local = jnp.sum(theta_shape / theta_rate, axis=(0, 1))]
    all_gather x1 -> x0, blocking collectives: 9.91 us -> none  [body(): panel = lax.all_gather(item_exp, 'user', axis=1, tiled=True)[0]]
  transfers between devices with their start and end apart: 4 -> 18, of which waited for: 3 -> 7; matrix products, arithmetic and copies ran while one was open for 18% -> 1% of each run, Pallas kernels for 0% -> 25%
where the time goes in v1:
time: 95.7 us; the launch traced here: 95.1 us
  waiting for transfers between devices  40.2 us (42%)
  Pallas kernels  33.4 us (35%)
  local copies, waits for them, and re-layouts  9.58 us (10%)
  starting transfers between devices  9.31 us (10%)
  between operations  1.45 us (2%)
  other arithmetic  1.2 us (1%)
    ppermute x18, waiting for transfers between devices, ring(): return lax.ppermute(x, axis, [(i, (i + shift) % n) for i in range(n)])  40.2 us
    pallas_call x4, Pallas kernels, statistics(): pl.pallas_call(functools.partial(stat_kernel, pieces, running is not None...  16.6 us
    unnamed x34, local copies, waits for them, and re-layouts  9.58 us
    ppermute x18, starting transfers between devices, ring(): return lax.ppermute(x, axis, [(i, (i + shift) % n) for i in range(n)])  9.31 us
    pallas_call x2, Pallas kernels, expected(): pl.pallas_call(expected_kernel, grid=(rows // block,), in_specs=[spec, sp...  7.14 us
    pallas_call x1, Pallas kernels, dense_counts(): pl.pallas_call(functools.partial(dense_kernel, n_user, shard_tiles, chunk...  5.57 us
    pallas_call x1, Pallas kernels, body(): pl.pallas_call(functools.partial(finish_items_kernel, n_user - 1), grid=(...  2.07 us
    pallas_call x1, Pallas kernels, body(): pl.pallas_call(finish_users_kernel, grid=(rows // user_block,), in_specs=...  1.98 us
  transfers between devices with their start and end apart: 18, of which 7 were waited for; matrix products, arithmetic and copies ran while one was open for 1% of the time, Pallas kernels for 25%

profile of v1, /device:TPU:0, one launch (start us, length us, event | category | flops | bytes accessed | tf_op | source)
XLA Modules:
  0.0 95.1 jit_solution(4060554040622912855)
XLA Ops:
  0.6 3.6 %expected_items.1 = (bf16[512,256]{1,0:T(8,128)(2,1)}, f32[1,256]{1,0:T(1,128)}) custom-call(f32[512,256]{1,0:T(8,128)} %bitcast.25, f32[512,256]{1,0:T(8,128)} %bitcast.26), custom_call_target="tpu_custom_call" | custom-call | flops 5242880 | bytes 1310720 | tf_op jit(solution)/shard_map/expected_items/pallas_call | solution.py:44
  4.2 2.9 %collective-permute-start.1 = (bf16[512,256]{1,0:T(8,128)(2,1)}, bf16[512,256]{1,0:T(8,128)(2,1)S(1)}, u32[]{:S(2)}, u32[]{:S(2)}) collective-permute-start(bf16[512,256]{1,0:T(8,128)(2,1)} %get-tuple-element.21.refs_0_.exp_ref), channel_id=1, source_target_pairs={{0,2},{2,0},{1,3},{3,1},{4,6},{6,4},{5,7},{7,5},{8,10},{10,8},{9,1... | collective-permute-start | bytes 786440 | tf_op jit(solution)/shard_map/ppermute | solution.py:204
  7.1 3.6 %expected_users.1 = (bf16[512,256]{1,0:T(8,128)(2,1)}, f32[1,256]{1,0:T(1,128)}) custom-call(f32[512,256]{1,0:T(8,128)} %bitcast.27, f32[512,256]{1,0:T(8,128)} %bitcast.28), custom_call_target="tpu_custom_call" | custom-call | flops 5242880 | bytes 1310720 | tf_op jit(solution)/shard_map/expected_users/pallas_call | solution.py:44
  10.7 1.6 %collective-permute-start.4 = (bf16[512,256]{1,0:T(8,128)(2,1)}, bf16[512,256]{1,0:T(8,128)(2,1)S(1)}, u32[]{:S(2)}, u32[]{:S(2)}) collective-permute-start(bf16[512,256]{1,0:T(8,128)(2,1)} %get-tuple-element.20.mine_ref.exp_ref), channel_id=1, source_target_pairs={{0,4},{4,8},{8,12},{12,0},{1,5},{5,9},{9,13},{13,1},{2,6},{6,10},{... | collective-permute-start | bytes 786440 | tf_op jit(solution)/shard_map/ppermute | solution.py:204
  12.8 0.9 collective-permute-done.1.refs_1_
  13.7 6.9 %collective-permute-done.4.mine_ref = bf16[512,256]{1,0:T(8,128)(2,1)S(1)} collective-permute-done((bf16[512,256]{1,0:T(8,128)(2,1)}, bf16[512,256]{1,0:T(8,128)(2,1)S(1)}, u32[]{:S(2)}, u32[]{:S(2)}) %collective-permute-start.4) | collective-permute-done | bytes 262176 | tf_op jit(solution)/shard_map/ppermute | solution.py:204
  22.5 5.6 %dense_counts.1.refs_4_ = bf16[2048,1024]{1,0:T(8,128)(2,1)S(1)} custom-call(s32[64]{0:T(128)S(1)} %bitcast.20, s32[64]{0:T(128)S(1)} %bitcast.21, s32[1]{0:T(128)} %bitcast.19.live_ref, s32[1]{0:T(128)} %bitcast.8.me_ref, s32[64,128,128]{2,1,0:T(8,128)} %bitcast.22), custom_call_target="tpu_custom_call" | custom-call | flops 1048576 | bytes 8388608 | tf_op jit(solution)/shard_map/dense_counts/pallas_call | solution.py:86
  28.1 2.0 %copy-done = bf16[2048,1024]{1,0:T(8,128)(2,1)} copy-done((bf16[2048,1024]{1,0:T(8,128)(2,1)}, bf16[2048,1024]{1,0:T(8,128)(2,1)S(1)}, u32[]{:S(2)}) %copy-start) | copy-done | bytes 4194328
  30.1 3.8 %statistics_0.1 = (f32[512,256]{1,0:T(8,128)S(1)}, f32[256,512]{1,0:T(8,128)S(1)}, f32[256,512]{1,0:T(8,128)S(1)}) custom-call(s32[1]{0:T(128)} %bitcast.2.index_ref, bf16[512,256]{1,0:T(8,128)(2,1)S(1)} %copy-done.2, bf16[512,256]{1,0:T(8,128)(2,1)S(1)} %collective-permute-done.other_ref, bf16[512,256]{1,0:T(8,128)(2,1)S(1)} %copy-done.1, ...), custom_call_target="tpu_custom_call" | custom-call | flops 1073741824 | bytes 4718592 | tf_op jit(solution)/shard_map/statistics_0/pallas_call | solution.py:169
  34.8 3.9 %statistics_1.1 = (bf16[512,256]{1,0:T(8,128)(2,1)S(1)}, f32[256,512]{1,0:T(8,128)S(1)}, f32[256,512]{1,0:T(8,128)S(1)}) custom-call(s32[1]{0:T(128)} %bitcast.12.index_ref, bf16[512,256]{1,0:T(8,128)(2,1)S(1)} %collective-permute-done.4.mine_ref, bf16[512,256]{1,0:T(8,128)(2,1)S(1)} %collective-permute-done.9.other_ref, bf16[512,256]{1,0:T(8,128)(2,1)S(1)} %copy-done.1, ...), custom_call_target="tpu_custom_call" | custom-call | flops 1073741824 | bytes 4718592 | tf_op jit(solution)/shard_map/statistics_1/pallas_call | solution.py:169
  38.6 1.2 %collective-permute-start.10 = (bf16[512,256]{1,0:T(8,128)(2,1)S(1)}, bf16[512,256]{1,0:T(8,128)(2,1)S(1)}, u32[]{:S(2)}, u32[]{:S(2)}) collective-permute-start(bf16[512,256]{1,0:T(8,128)(2,1)S(1)} %get-tuple-element.25), channel_id=1, source_target_pairs={{0,4},{4,8},{8,12},{12,0},{1,5},{5,9},{9,13},{13,1},{2,6},{6,10},{... | collective-permute-start | bytes 786440 | tf_op jit(solution)/shard_map/ppermute | solution.py:204
  39.8 1.6 %collective-permute-start.6 = (bf16[512,256]{1,0:T(8,128)(2,1)S(1)}, bf16[512,256]{1,0:T(8,128)(2,1)}, u32[]{:S(2)}, u32[]{:S(2)}) collective-permute-start(bf16[512,256]{1,0:T(8,128)(2,1)S(1)} %collective-permute-done.5.mine_ref), channel_id=1, source_target_pairs={{0,4},{4,8},{8,12},{12,0},{1,5},{5,9},{9,13},{13,1},{2,6},{6,10},{... | collective-permute-start | bytes 786440 | tf_op jit(solution)/shard_map/ppermute | solution.py:204
  41.9 8.0 %collective-permute-done.10.refs_5_ = bf16[512,256]{1,0:T(8,128)(2,1)S(1)} collective-permute-done((bf16[512,256]{1,0:T(8,128)(2,1)S(1)}, bf16[512,256]{1,0:T(8,128)(2,1)S(1)}, u32[]{:S(2)}, u32[]{:S(2)}) %collective-permute-start.10) | collective-permute-done | bytes 262176 | tf_op jit(solution)/shard_map/ppermute | solution.py:204
  51.3 0.9 copy-done.6
  52.3 0.9 copy-done.8
  53.2 4.7 %statistics_2.1 = (bf16[512,256]{1,0:T(8,128)(2,1)}, f32[256,512]{1,0:T(8,128)S(1)}, f32[256,512]{1,0:T(8,128)S(1)}) custom-call(s32[1]{0:T(128)} %bitcast.11.index_ref, bf16[512,256]{1,0:T(8,128)(2,1)S(1)} %collective-permute-done.5.mine_ref, bf16[512,256]{1,0:T(8,128)(2,1)S(1)} %copy-done.8, bf16[512,256]{1,0:T(8,128)(2,1)S(1)} %copy-done.1, ...), custom_call_target="tpu_custom_call" | custom-call | flops 1073741824 | bytes 4718592 | tf_op jit(solution)/shard_map/statistics_2/pallas_call | solution.py:169
  58.7 8.8 %collective-permute-done.14 = f32[2,256]{1,0:T(2,128)S(1)} collective-permute-done((f32[2,256]{1,0:T(2,128)S(1)}, f32[2,256]{1,0:T(2,128)S(1)}, u32[]{:S(2)}, u32[]{:S(2)}) %collective-permute-start.14) | collective-permute-done | bytes 2080 | tf_op jit(solution)/shard_map/ppermute | solution.py:204
  67.6 5.4 %collective-permute-done.15 = f32[2,256]{1,0:T(2,128)S(1)} collective-permute-done((f32[2,256]{1,0:T(2,128)S(1)}, f32[2,256]{1,0:T(2,128)S(1)}, u32[]{:S(2)}, u32[]{:S(2)}) %collective-permute-start.15) | collective-permute-done | bytes 2080 | tf_op jit(solution)/shard_map/ppermute | solution.py:204
  72.9 5.4 %collective-permute-done.16 = f32[2,256]{1,0:T(2,128)S(1)} collective-permute-done((f32[2,256]{1,0:T(2,128)S(1)}, f32[2,256]{1,0:T(2,128)S(1)}, u32[]{:S(2)}, u32[]{:S(2)}) %collective-permute-start.16) | collective-permute-done | bytes 2080 | tf_op jit(solution)/shard_map/ppermute | solution.py:204
  78.4 4.2 %statistics_3.1 = (bf16[512,256]{1,0:T(8,128)(2,1)S(1)}, f32[256,512]{1,0:T(8,128)S(1)}, bf16[256,512]{1,0:T(8,128)(2,1)S(1)}) custom-call(s32[1]{0:T(128)} %bitcast.10.index_ref, bf16[512,256]{1,0:T(8,128)(2,1)} %collective-permute-done.6.mine_ref, bf16[512,256]{1,0:T(8,128)(2,1)S(1)} %collective-permute-done.7.other_ref, bf16[512,256]{1,0:T(8,128)(2,1)S(1)} %copy-done.1, ...), custom_call_target="tpu_custom_call" | custom-call | flops 1073741824 | bytes 4718592 | tf_op jit(solution)/shard_map/statistics_3/pallas_call | solution.py:169
  83.6 1.2 %broadcast_add_fusion = (f32[1,512,256]{2,1,0:T(8,128)}, f32[1,512,256]{2,1,0:T(8,128)}) fusion(f32[256]{0:T(256)S(1)} %bitcast.29, f32[512]{0:T(512)S(1)} %bitcast.31, f32[256]{0:T(256)S(1)} %bitcast.30, f32[512]{0:T(512)S(1)} %bitcast.32), kind=kLoop, calls=%fused_computation | loop fusion | flops 262144 | bytes 1054720 | tf_op jit(solution)/shard_map/add | solution.py:320
  84.8 4.9 %collective-permute-done.17.refs_0_ = bf16[256,512]{1,0:T(8,128)(2,1)S(1)} collective-permute-done((bf16[256,512]{1,0:T(8,128)(2,1)S(1)}, bf16[256,512]{1,0:T(8,128)(2,1)S(1)}, u32[]{:S(2)}, u32[]{:S(2)}) %collective-permute-start.17) | collective-permute-done | bytes 262176 | tf_op jit(solution)/shard_map/ppermute | solution.py:204
  90.4 2.1 %finish_items.1 = f32[512,256]{1,0:T(8,128)} custom-call(bf16[512,256]{1,0:T(8,128)(2,1)} %get-tuple-element.21.refs_0_.exp_ref, f32[256,512]{1,0:T(8,128)} %copy-done.4, bf16[256,512]{1,0:T(8,128)(2,1)} %copy-done.12), custom_call_target="tpu_custom_call" | custom-call | flops 393216 | bytes 1572864 | tf_op jit(solution)/shard_map/finish_items/pallas_call | solution.py:308
  93.2 2.0 %finish_users.1 = f32[512,256]{1,0:T(8,128)} custom-call(bf16[512,256]{1,0:T(8,128)(2,1)} %get-tuple-element.20.mine_ref.exp_ref, f32[512,256]{1,0:T(8,128)} %copy-done.3, bf16[512,256]{1,0:T(8,128)(2,1)} %copy-done.11), custom_call_target="tpu_custom_call" | custom-call | flops 393216 | bytes 1572864 | tf_op jit(solution)/shard_map/finish_users/pallas_call | solution.py:295
  (60 shorter events, 7.8 us)
Async XLA Ops:
  4.2 9.5 %collective-permute-start.1 = (bf16[512,256]{1,0:T(8,128)(2,1)}, bf16[512,256]{1,0:T(8,128)(2,1)S(1)}, u32[]{:S(2)}, u32[]{:S(2)}) collective-permute-start(bf16[512,256]{1,0:T(8,128)(2,1)} %get-tuple-element.21.refs_0_.exp_ref), channel_id=1, source_target_pairs={{0,2},{2,0},{1,3},{3,1},{4,6},{6,4},{5,7},{7,5},{8,10},{10,8},{9,1... | collective-permute-start | bytes 786440 | tf_op jit(solution)/shard_map/ppermute | solution.py:204
  10.7 9.8 %collective-permute-start.4 = (bf16[512,256]{1,0:T(8,128)(2,1)}, bf16[512,256]{1,0:T(8,128)(2,1)S(1)}, u32[]{:S(2)}, u32[]{:S(2)}) collective-permute-start(bf16[512,256]{1,0:T(8,128)(2,1)} %get-tuple-element.20.mine_ref.exp_ref), channel_id=1, source_target_pairs={{0,4},{4,8},{8,12},{12,0},{1,5},{5,9},{9,13},{13,1},{2,6},{6,10},{... | collective-permute-start | bytes 786440 | tf_op jit(solution)/shard_map/ppermute | solution.py:204
  12.3 17.8 %collective-permute-start.2 = (bf16[512,256]{1,0:T(8,128)(2,1)}, bf16[512,256]{1,0:T(8,128)(2,1)S(1)}, u32[]{:S(2)}, u32[]{:S(2)}) collective-permute-start(bf16[512,256]{1,0:T(8,128)(2,1)} %get-tuple-element.21.refs_0_.exp_ref), channel_id=1, source_target_pairs={{0,1},{1,0},{2,3},{3,2},{4,5},{5,4},{6,7},{7,6},{8,9},{9,8},{10,11... | collective-permute-start | bytes 786440 | tf_op jit(solution)/shard_map/ppermute | solution.py:204
  12.3 17.8 %collective-permute-start = (bf16[512,256]{1,0:T(8,128)(2,1)}, bf16[512,256]{1,0:T(8,128)(2,1)S(1)}, u32[]{:S(2)}, u32[]{:S(2)}) collective-permute-start(bf16[512,256]{1,0:T(8,128)(2,1)} %get-tuple-element.20.mine_ref.exp_ref), channel_id=1, source_target_pairs={{0,1},{1,0},{2,3},{3,2},{4,5},{5,4},{6,7},{7,6},{8,9},{9,8},{10,11... | collective-permute-start | bytes 786440 | tf_op jit(solution)/shard_map/ppermute | solution.py:204
  13.7 16.4 %collective-permute-start.3 = (bf16[512,256]{1,0:T(8,128)(2,1)S(1)}, bf16[512,256]{1,0:T(8,128)(2,1)S(1)}, u32[]{:S(2)}, u32[]{:S(2)}) collective-permute-start(bf16[512,256]{1,0:T(8,128)(2,1)S(1)} %collective-permute-done.1.refs_1_), channel_id=1, source_target_pairs={{0,1},{1,0},{2,3},{3,2},{4,5},{5,4},{6,7},{7,6},{8,9},{9,8},{10,11... | collective-permute-start | bytes 786440 | tf_op jit(solution)/shard_map/ppermute | solution.py:204
  20.5 14.2 %collective-permute-start.9 = (bf16[512,256]{1,0:T(8,128)(2,1)S(1)}, bf16[512,256]{1,0:T(8,128)(2,1)S(1)}, u32[]{:S(2)}, u32[]{:S(2)}) collective-permute-start(bf16[512,256]{1,0:T(8,128)(2,1)S(1)} %collective-permute-done.4.mine_ref), channel_id=1, source_target_pairs={{0,1},{1,0},{2,3},{3,2},{4,5},{5,4},{6,7},{7,6},{8,9},{9,8},{10,11... | collective-permute-start | bytes 786440 | tf_op jit(solution)/shard_map/ppermute | solution.py:204
  20.5 19.2 %collective-permute-start.5 = (bf16[512,256]{1,0:T(8,128)(2,1)S(1)}, bf16[512,256]{1,0:T(8,128)(2,1)S(1)}, u32[]{:S(2)}, u32[]{:S(2)}) collective-permute-start(bf16[512,256]{1,0:T(8,128)(2,1)S(1)} %collective-permute-done.4.mine_ref), channel_id=1, source_target_pairs={{0,4},{4,8},{8,12},{12,0},{1,5},{5,9},{9,13},{13,1},{2,6},{6,10},{... | collective-permute-start | bytes 786440 | tf_op jit(solution)/shard_map/ppermute | solution.py:204
  22.5 7.6 %copy-start.1 = (bf16[512,256]{1,0:T(8,128)(2,1)S(1)}, bf16[512,256]{1,0:T(8,128)(2,1)}, u32[]{:S(2)}) copy-start(bf16[512,256]{1,0:T(8,128)(2,1)} %get-tuple-element.21.refs_0_.exp_ref) | copy-start | bytes 786436
  22.5 7.6 %copy-start.2 = (bf16[512,256]{1,0:T(8,128)(2,1)S(1)}, bf16[512,256]{1,0:T(8,128)(2,1)}, u32[]{:S(2)}) copy-start(bf16[512,256]{1,0:T(8,128)(2,1)} %get-tuple-element.20.mine_ref.exp_ref) | copy-start | bytes 786436
  34.8 6.6 %copy-start.13 = (f32[1,256]{1,0:T(1,128)S(1)}, f32[1,256]{1,0:T(1,128)}, u32[]{:S(2)}) copy-start(f32[1,256]{1,0:T(1,128)} %get-tuple-element.33) | copy-start | bytes 3076
  34.8 6.6 %copy-start.14 = (f32[1,256]{1,0:T(1,128)S(1)}, f32[1,256]{1,0:T(1,128)}, u32[]{:S(2)}) copy-start(f32[1,256]{1,0:T(1,128)} %get-tuple-element.32) | copy-start | bytes 3076
  38.6 11.3 %collective-permute-start.10 = (bf16[512,256]{1,0:T(8,128)(2,1)S(1)}, bf16[512,256]{1,0:T(8,128)(2,1)S(1)}, u32[]{:S(2)}, u32[]{:S(2)}) collective-permute-start(bf16[512,256]{1,0:T(8,128)(2,1)S(1)} %get-tuple-element.25), channel_id=1, source_target_pairs={{0,4},{4,8},{8,12},{12,0},{1,5},{5,9},{9,13},{13,1},{2,6},{6,10},{... | collective-permute-start | bytes 786440 | tf_op jit(solution)/shard_map/ppermute | solution.py:204
  39.8 10.8 %collective-permute-start.8 = (bf16[512,256]{1,0:T(8,128)(2,1)S(1)}, bf16[512,256]{1,0:T(8,128)(2,1)S(1)}, u32[]{:S(2)}, u32[]{:S(2)}) collective-permute-start(bf16[512,256]{1,0:T(8,128)(2,1)S(1)} %collective-permute-done.5.mine_ref), channel_id=1, source_target_pairs={{0,1},{1,0},{2,3},{3,2},{4,5},{5,4},{6,7},{7,6},{8,9},{9,8},{10,11... | collective-permute-start | bytes 786440 | tf_op jit(solution)/shard_map/ppermute | solution.py:204
  39.8 18.2 %collective-permute-start.6 = (bf16[512,256]{1,0:T(8,128)(2,1)S(1)}, bf16[512,256]{1,0:T(8,128)(2,1)}, u32[]{:S(2)}, u32[]{:S(2)}) collective-permute-start(bf16[512,256]{1,0:T(8,128)(2,1)S(1)} %collective-permute-done.5.mine_ref), channel_id=1, source_target_pairs={{0,4},{4,8},{8,12},{12,0},{1,5},{5,9},{9,13},{13,1},{2,6},{6,10},{... | collective-permute-start | bytes 786440 | tf_op jit(solution)/shard_map/ppermute | solution.py:204
  41.4 16.7 %collective-permute-start.13 = (f32[2,256]{1,0:T(2,128)S(1)}, f32[2,256]{1,0:T(2,128)S(1)}, u32[]{:S(2)}, u32[]{:S(2)}) collective-permute-start(f32[2,256]{1,0:T(2,128)S(1)} %pad_maximum_fusion), channel_id=1, source_target_pairs={{0,2},{2,0},{1,3},{3,1},{4,6},{6,4},{5,7},{7,5},{8,10},{10,8},{9,1... | collective-permute-start | bytes 6152 | tf_op jit(solution)/shard_map/ppermute | solution.py:204
  57.9 25.7 %copy-start.15 = (f32[1,512]{1,0:T(1,128)S(1)}, f32[1,512]{1,0:T(1,128)}, u32[]{:S(2)}) copy-start(f32[1,512]{1,0:T(1,128)} %param.19) | copy-start | bytes 6148
  57.9 25.7 %copy-start.16 = (f32[1,512]{1,0:T(1,128)S(1)}, f32[1,512]{1,0:T(1,128)}, u32[]{:S(2)}) copy-start(f32[1,512]{1,0:T(1,128)} %param.16) | copy-start | bytes 6148
  57.9 20.4 %collective-permute-start.11 = (bf16[512,256]{1,0:T(8,128)(2,1)}, bf16[512,256]{1,0:T(8,128)(2,1)S(1)}, u32[]{:S(2)}, u32[]{:S(2)}) collective-permute-start(bf16[512,256]{1,0:T(8,128)(2,1)} %get-tuple-element.28), channel_id=1, source_target_pairs={{0,4},{4,8},{8,12},{12,0},{1,5},{5,9},{9,13},{13,1},{2,6},{6,10},{... | collective-permute-start | bytes 786440 | tf_op jit(solution)/shard_map/ppermute | solution.py:204
  58.0 20.4 %collective-permute-start.7 = (bf16[512,256]{1,0:T(8,128)(2,1)}, bf16[512,256]{1,0:T(8,128)(2,1)S(1)}, u32[]{:S(2)}, u32[]{:S(2)}) collective-permute-start(bf16[512,256]{1,0:T(8,128)(2,1)} %collective-permute-done.6.mine_ref), channel_id=1, source_target_pairs={{0,1},{1,0},{2,3},{3,2},{4,5},{5,4},{6,7},{7,6},{8,9},{9,8},{10,11... | collective-permute-start | bytes 786440 | tf_op jit(solution)/shard_map/ppermute | solution.py:204
  58.1 9.5 %collective-permute-start.14 = (f32[2,256]{1,0:T(2,128)S(1)}, f32[2,256]{1,0:T(2,128)S(1)}, u32[]{:S(2)}, u32[]{:S(2)}) collective-permute-start(f32[2,256]{1,0:T(2,128)S(1)} %fusion), channel_id=1, source_target_pairs={{0,4},{4,8},{8,12},{12,0},{1,5},{5,9},{9,13},{13,1},{2,6},{6,10},{... | collective-permute-start | bytes 6152 | tf_op jit(solution)/shard_map/ppermute | solution.py:204
  67.6 5.4 %collective-permute-start.15 = (f32[2,256]{1,0:T(2,128)S(1)}, f32[2,256]{1,0:T(2,128)S(1)}, u32[]{:S(2)}, u32[]{:S(2)}) collective-permute-start(f32[2,256]{1,0:T(2,128)S(1)} %collective-permute-done.14), channel_id=1, source_target_pairs={{0,4},{4,8},{8,12},{12,0},{1,5},{5,9},{9,13},{13,1},{2,6},{6,10},{... | collective-permute-start | bytes 6152 | tf_op jit(solution)/shard_map/ppermute | solution.py:204
  72.9 5.4 %collective-permute-start.16 = (f32[2,256]{1,0:T(2,128)S(1)}, f32[2,256]{1,0:T(2,128)S(1)}, u32[]{:S(2)}, u32[]{:S(2)}) collective-permute-start(f32[2,256]{1,0:T(2,128)S(1)} %collective-permute-done.15), channel_id=1, source_target_pairs={{0,4},{4,8},{8,12},{12,0},{1,5},{5,9},{9,13},{13,1},{2,6},{6,10},{... | collective-permute-start | bytes 6152 | tf_op jit(solution)/shard_map/ppermute | solution.py:204
  83.3 6.4 %collective-permute-start.17 = (bf16[256,512]{1,0:T(8,128)(2,1)S(1)}, bf16[256,512]{1,0:T(8,128)(2,1)S(1)}, u32[]{:S(2)}, u32[]{:S(2)}) collective-permute-start(bf16[256,512]{1,0:T(8,128)(2,1)S(1)} %get-tuple-element.35), channel_id=1, source_target_pairs={{0,2},{2,0},{1,3},{3,1},{4,6},{6,4},{5,7},{7,5},{8,10},{10,8},{9,1... | collective-permute-start | bytes 786440 | tf_op jit(solution)/shard_map/ppermute | solution.py:204
  83.6 8.9 %collective-permute-start.12 = (bf16[512,256]{1,0:T(8,128)(2,1)S(1)}, bf16[512,256]{1,0:T(8,128)(2,1)S(1)}, u32[]{:S(2)}, u32[]{:S(2)}) collective-permute-start(bf16[512,256]{1,0:T(8,128)(2,1)S(1)} %get-tuple-element.31), channel_id=1, source_target_pairs={{0,4},{4,8},{8,12},{12,0},{1,5},{5,9},{9,13},{13,1},{2,6},{6,10},{... | collective-permute-start | bytes 786440 | tf_op jit(solution)/shard_map/ppermute | solution.py:204
  (11 other events, 9.6 us)

commit v2 on v0

v2 whole, which is shorter than its diff:
```python
import functools

import jax
import jax.numpy as jnp
from jax import lax
from jax.experimental import pallas as pl
from jax.experimental.pallas import tpu as pltpu
from jax.sharding import PartitionSpec as P

BF16 = jnp.bfloat16
F32 = jnp.float32
VMEM = pltpu.MemorySpace.VMEM
SMEM = pltpu.MemorySpace.SMEM
DIMS_NT = (((1,), (1,)), ((), ()))
DIMS_TN = (((0,), (0,)), ((), ()))


def exp_digamma(x, inv_rate):
    w = x * (x + 3.0)
    p = w * (w + 2.0)
    y = x + 4.0
    inv = 1.0 / (y * p)
    iy = inv * p
    iy2 = iy * iy
    shift = (2.0 * x + 3.0) * (2.0 * w + 2.0) * (inv * y)
    series = iy * 0.5 + iy2 * (1.0 / 12.0 - iy2 * (1.0 / 120.0 - iy2 * (1.0 / 252.0)))
    return y * inv_rate * jnp.exp(-(series + shift))


def users_kernel(steps, core_ref, shape_ref, rate_ref, keep_ref, give_ref, total_ref):
    g = pl.program_id(0)
    x = shape_ref[...]
    inv_rate = 1.0 / rate_ref[...]
    value = exp_digamma(x, inv_rate).astype(BF16)
    part = jnp.sum(x * inv_rate, axis=0, keepdims=True)

    @pl.when(g < steps)
    def _():
        give_ref[...] = value

    @pl.when(g >= steps)
    def _():
        keep_ref[...] = value

    @pl.when(g == 0)
    def _():
        total_ref[...] = part

    @pl.when(g != 0)
    def _():
        total_ref[...] += part


def expected_users(core, shape_arg, rate_arg):
    rows, cols = shape_arg.shape
    half = rows // 2
    block = min(half, 128)
    steps = half // block
    in_spec = pl.BlockSpec(
        (block, cols), lambda g, c: (lax.rem(c[0] + 1 + lax.div(g, steps), 2) * steps + lax.rem(g, steps), 0)
    )
    return pl.pallas_call(
        functools.partial(users_kernel, steps),
        grid_spec=pltpu.PrefetchScalarGridSpec(
            num_scalar_prefetch=1,
            grid=(2 * steps,),
            in_specs=[in_spec, in_spec],
            out_specs=[
                pl.BlockSpec((block, cols), lambda g, c: (jnp.maximum(g - steps, 0), 0)),
                pl.BlockSpec((block, cols), lambda g, c: (jnp.minimum(g, steps - 1), 0)),
                pl.BlockSpec((1, cols), lambda g, c: (0, 0)),
            ],
        ),
        out_shape=[
            jax.ShapeDtypeStruct((half, cols), BF16),
            jax.ShapeDtypeStruct((half, cols), BF16),
            jax.ShapeDtypeStruct((1, cols), F32),
        ],
        cost_estimate=pl.CostEstimate(
            flops=40 * rows * cols, transcendentals=3 * rows * cols, bytes_accessed=10 * rows * cols
        ),
        name="expected_users",
    )(core, shape_arg, rate_arg)


def items_kernel(shape_ref, rate_ref, exp_ref, total_ref):
    x = shape_ref[...]
    inv_rate = 1.0 / rate_ref[...]
    exp_ref[...] = exp_digamma(x, inv_rate).astype(BF16)
    part = jnp.sum(x * inv_rate, axis=0, keepdims=True)

    @pl.when(pl.program_id(0) == 0)
    def _():
        total_ref[...] = part

    @pl.when(pl.program_id(0) != 0)
    def _():
        total_ref[...] += part


def expected_items(shape_arg, rate_arg):
    rows, cols = shape_arg.shape
    block = min(rows, 128)
    spec = pl.BlockSpec((block, cols), lambda g: (g, 0))
    return pl.pallas_call(
        items_kernel,
        grid=(rows // block,),
        in_specs=[spec, spec],
        out_specs=[spec, pl.BlockSpec((1, cols), lambda g: (0, 0))],
        out_shape=[
            jax.ShapeDtypeStruct((rows, cols), BF16),
            jax.ShapeDtypeStruct((1, cols), F32),
        ],
        cost_estimate=pl.CostEstimate(
            flops=40 * rows * cols, transcendentals=3 * rows * cols, bytes_accessed=10 * rows * cols
        ),
        name="expected_items",
    )(shape_arg, rate_arg)


def dense_kernel(n_user, shard_tiles, chunk, rows, users_ref, items_ref, live_ref, me_ref, counts_ref, out_ref):
    g = pl.program_id(0)
    tile = counts_ref.shape[1]
    half = rows // 2
    piece = min(half, tile)

    @pl.when(g == 0)
    def _():
        out_ref[...] = jnp.zeros_like(out_ref)

    def place(t, carry):
        slot = g * chunk + t
        item = items_ref[slot]
        owner = lax.div(item, shard_tiles)
        column = (owner ^ me_ref[1]) * shard_tiles + lax.rem(item, shard_tiles)
        col = pl.multiple_of(column * tile, tile)
        for j in range(tile // piece):
            row = users_ref[slot] * tile + j * piece
            shard = lax.div(row, rows)
            within = lax.rem(row, rows)

            @pl.when(lax.div(within, half) == me_ref[2])
            def _():
                start = (shard ^ me_ref[0]) * half + lax.rem(within, half)
                start = pl.multiple_of(start, piece)
                value = counts_ref[t, j * piece : (j + 1) * piece, :].astype(F32).astype(BF16)
                out_ref[pl.ds(start, piece), pl.ds(col, tile)] = value

        return carry

    lax.fori_loop(0, jnp.clip(live_ref[0] - g * chunk, 0, chunk), place, 0)


def dense_counts(counts, users, items, live, me, rows, n_item, item_rows, n_user):
    slots, tile, _ = counts.shape
    chunk = 8
    shard_tiles = item_rows // n_user // tile
    out_rows = n_item * rows // 2
    return pl.pallas_call(
        functools.partial(dense_kernel, n_user, shard_tiles, chunk, rows),
        grid_spec=pltpu.PrefetchScalarGridSpec(
            num_scalar_prefetch=4,
            grid=(slots // chunk,),
            in_specs=[pl.BlockSpec((chunk, tile, tile), lambda g, *_: (g, 0, 0))],
            out_specs=pl.BlockSpec((out_rows, item_rows), lambda g, *_: (0, 0)),
        ),
        out_shape=jax.ShapeDtypeStruct((out_rows, item_rows), BF16),
        compiler_params=pltpu.CompilerParams(vmem_limit_bytes=12 * 1024 * 1024),
        cost_estimate=pl.CostEstimate(
            flops=slots * tile * tile,
            transcendentals=0,
            bytes_accessed=4 * slots * tile * tile + 2 * out_rows * item_rows,
        ),
        name="dense_counts",
    )(users, items, live, me, counts)


def stat_kernel(pieces, joined_in, joined_out, has_acc, at, *refs):
    refs = list(refs)
    take = lambda n: [refs.pop(0) for _ in range(n)]
    if joined_in:
        (both_ref,) = take(1)
        half = both_ref.shape[0] // 2
        mine = both_ref[:half, :]
        other = both_ref[half:, :]
    else:
        mine_ref, other_ref = take(2)
        half = mine_ref.shape[0]
        mine = mine_ref[...]
        other = other_ref[...]
    item_mine = take(pieces)
    item_other = take(pieces)
    (counts_ref,) = take(1)
    acc_mine_in = take(pieces) if has_acc else None
    acc_other_in = take(pieces) if has_acc else None
    stat_refs = take(1 if joined_out else 2)
    acc_mine = take(pieces)
    acc_other = take(pieces)
    total_mine = None
    total_other = None
    width = 256
    for p in range(pieces):
        rows = item_mine[p].shape[0]
        for c in range(rows // width):
            part = slice(c * width, (c + 1) * width)
            left = item_mine[p][part, :]
            right = item_other[p][part, :]
            norm = lax.dot_general(mine, left, DIMS_NT, preferred_element_type=F32)
            norm += lax.dot_general(other, right, DIMS_NT, preferred_element_type=F32)
            columns = slice(p * rows + c * width, p * rows + (c + 1) * width)
            grid = counts_ref[at * half : (at + 1) * half, columns].astype(F32)
            ratio = (grid / norm).astype(BF16)
            stat = jnp.dot(ratio, left, preferred_element_type=F32)
            total_mine = stat if total_mine is None else total_mine + stat
            stat = jnp.dot(ratio, right, preferred_element_type=F32)
            total_other = stat if total_other is None else total_other + stat
            update = lax.dot_general(mine, ratio, DIMS_TN, preferred_element_type=F32)
            if has_acc:
                update += acc_mine_in[p][:, part]
            acc_mine[p][:, part] = update.astype(acc_mine[p].dtype)
            update = lax.dot_general(other, ratio, DIMS_TN, preferred_element_type=F32)
            if has_acc:
                update += acc_other_in[p][:, part]
            acc_other[p][:, part] = update.astype(acc_other[p].dtype)
    if joined_out:
        stat_refs[0][:half, :] = total_mine.astype(stat_refs[0].dtype)
        stat_refs[0][half:, :] = total_other.astype(stat_refs[0].dtype)
    else:
        stat_refs[0][...] = total_mine.astype(stat_refs[0].dtype)
        stat_refs[1][...] = total_other.astype(stat_refs[1].dtype)


def statistics(at, users, item_mine, item_other, dense, acc, last, name):
    half_rows = users[0].shape[0] * len(users) // 2
    half = users[0].shape[1]
    pieces = len(item_mine)
    item_rows = dense.shape[1]
    piece_rows = item_rows // pieces
    args = [*users, *item_mine, *item_other, dense]
    if acc is not None:
        args += acc
    joined_out = at != 0 and not last
    if joined_out:
        out_shape = [jax.ShapeDtypeStruct((2 * half_rows, half), BF16)]
    else:
        out_shape = [jax.ShapeDtypeStruct((half_rows, half), BF16 if at else F32)] * 2
    n_stats = len(out_shape)
    for group in range(2):
        for p in range(pieces):
            kept = not last or (group == 0 and p == 0)
            out_shape.append(jax.ShapeDtypeStruct((half, piece_rows), F32 if kept else BF16))
    spec = pl.BlockSpec(memory_space=VMEM)
    out = pl.pallas_call(
        functools.partial(stat_kernel, pieces, len(users) == 1, joined_out, acc is not None, at),
        in_specs=[spec] * len(args),
        out_specs=[spec] * len(out_shape),
        out_shape=out_shape,
        compiler_params=pltpu.CompilerParams(vmem_limit_bytes=24 * 1024 * 1024),
        cost_estimate=pl.CostEstimate(
            flops=12 * half_rows * item_rows * half,
            transcendentals=half_rows * item_rows,
            bytes_accessed=8 * half_rows * half + 4 * item_rows * half + 2 * half_rows * item_rows,
        ),
        name=name,
    )(*args)
    return list(out[:n_stats]), list(out[n_stats:])


def finish_users_kernel(joined, core_ref, keep_ref, give_ref, own_ref, sum_ref, *refs):
    out_ref = refs[-1]
    g = pl.program_id(0)
    half = keep_ref.shape[0]

    @pl.when(g == 0)
    def _():
        total = own_ref[...]
        for k in range(joined):
            total += refs[k][:half, :].astype(F32)
        total += refs[joined][...].astype(F32)
        out_ref[...] = 0.3 + keep_ref[...].astype(F32) * total

    @pl.when(g == 1)
    def _():
        total = sum_ref[...].astype(F32) + refs[joined + 1][...].astype(F32)
        out_ref[...] = 0.3 + give_ref[...].astype(F32) * total


def finish_users(core, keep, give, own, other_sum, joined, same, cross):
    half_rows, half = keep.shape
    spec = pl.BlockSpec((half_rows, half), lambda g, c: (0, 0))
    joined_spec = pl.BlockSpec((2 * half_rows, half), lambda g, c: (0, 0))
    return pl.pallas_call(
        functools.partial(finish_users_kernel, len(joined)),
        grid_spec=pltpu.PrefetchScalarGridSpec(
            num_scalar_prefetch=1,
            grid=(2,),
            in_specs=[spec] * 4 + [joined_spec] * len(joined) + [spec] * 2,
            out_specs=pl.BlockSpec((half_rows, half), lambda g, c: (lax.rem(c[0] + g, 2), 0)),
        ),
        out_shape=jax.ShapeDtypeStruct((2 * half_rows, half), F32),
        cost_estimate=pl.CostEstimate(
            flops=8 * half_rows * half, transcendentals=0, bytes_accessed=24 * half_rows * half
        ),
        name="finish_users",
    )(core, keep, give, own, other_sum, *joined, same, cross)


def finish_items_kernel(n, exp_ref, own_ref, *refs):
    total = own_ref[...]
    for p in range(n):
        total += refs[p][...].astype(F32)
    refs[n][...] = 0.3 + exp_ref[...].astype(F32) * total.T


def finish_items(item_exp, own, came):
    rows, half = item_exp.shape
    block = min(rows, 256)
    spec = pl.BlockSpec((block, half), lambda g: (g, 0))
    acc_spec = pl.BlockSpec((half, block), lambda g: (0, g))
    return pl.pallas_call(
        functools.partial(finish_items_kernel, len(came)),
        grid=(rows // block,),
        in_specs=[spec] + [acc_spec] * (1 + len(came)),
        out_specs=spec,
        out_shape=jax.ShapeDtypeStruct((rows, half), F32),
        cost_estimate=pl.CostEstimate(flops=6 * rows * half, transcendentals=0, bytes_accessed=16 * rows * half),
        name="finish_items",
    )(item_exp, own, *came)


def move(x, axis, n, n_ka, distance, cross):
    if not cross:
        return lax.ppermute(x, axis, [(i, i ^ distance) for i in range(n)])
    pairs = [
        (i * n_ka + h, (i ^ distance) * n_ka + (n_ka - 1 - h)) for i in range(n) for h in range(n_ka)
    ]
    return lax.ppermute(x, (axis, "ka"), pairs)


def body(
    n_item,
    n_user,
    n_ka,
    counts,
    tile_user,
    tile_item,
    tile_live,
    theta_shape,
    theta_rate,
    user_activity,
    beta_shape,
    beta_rate,
    item_popularity,
):
    def sibling(x):
        return lax.ppermute(x, "ka", [(h, n_ka - 1 - h) for h in range(n_ka)])

    core = lax.axis_index("ka").astype(jnp.int32)[None]
    keep, give, theta_local = expected_users(core, theta_shape[0], theta_rate[0])
    beta_shape, beta_rate, keep, give = lax.optimization_barrier((beta_shape, beta_rate, keep, give))
    item_exp, beta_local = expected_items(beta_shape[0], beta_rate[0])
    half_rows = keep.shape[0]
    item_rows = item_exp.shape[0] * n_user

    came_give = sibling(give)
    users = {0: [keep, came_give]}
    for k in range(1, n_item):
        low = k & -k
        if k == 1:
            users[k] = [move(jnp.concatenate([keep, came_give]), "item", n_item, n_ka, k, False)]
        else:
            users[k] = [move(x, "item", n_item, n_ka, low, False) for x in users[k ^ low]]

    item_mine = [item_exp]
    for p in range(1, n_user):
        low = p & -p
        item_mine.append(move(item_mine[p ^ low], "user", n_user, n_ka, low, False))
    item_other = [sibling(x) for x in item_mine]

    me = jnp.stack([lax.axis_index(a) for a in ("item", "user", "ka")]).astype(jnp.int32)
    dense = dense_counts(
        counts[0, 0],
        tile_user[0, 0],
        tile_item[0, 0],
        tile_live[0],
        me,
        2 * half_rows,
        n_item,
        item_rows,
        n_user,
    )

    totals = jnp.concatenate([theta_local, beta_local], axis=0)
    hops = []
    for axis, n in (("user", n_user), ("item", n_item)):
        distance = 1
        while distance < n:
            hops.append((axis, n, distance))
            distance *= 2

    acc = None
    joined = []
    for k in range(n_item):
        last = k == n_item - 1
        stats, acc = statistics(k, users[k], item_mine, item_other, dense, acc, last, "statistics_%d" % k)
        if k < len(hops):
            totals, stats[-1] = lax.optimization_barrier((totals, stats[-1]))
            axis, n, distance = hops[k]
            totals = totals + move(totals, axis, n, n_ka, distance, False)
        if k == 0:
            own, other_sum = stats
        elif not last:
            joined.append(move(stats[0], "item", n_item, n_ka, k, False))
            other_sum = other_sum + joined[-1][half_rows:].astype(F32)
        else:
            same = move(stats[0], "item", n_item, n_ka, k, False)
            cross = move(stats[1], "item", n_item, n_ka, k, True)
    other_sum = sibling(other_sum.astype(BF16))

    came = [sibling(acc[n_user])]
    for p in range(1, n_user):
        came.append(move(acc[p], "user", n_user, n_ka, p, False))
        came.append(move(acc[n_user + p], "user", n_user, n_ka, p, True))
    theta_total = totals[0]
    beta_total = totals[1]

    new_theta_shape = finish_users(core, keep, give, own, other_sum, joined, same, cross)
    new_beta_shape = finish_items(item_exp, acc[0], came)
    new_theta_rate = user_activity[..., None] + beta_total
    new_beta_rate = item_popularity[..., None] + theta_total
    return (new_theta_shape[None], new_theta_rate, new_beta_shape[None], new_beta_rate)


def solution(mesh):
    in_specs = (
        P(("parts", "item"), "user", None, None, None),
        P(("parts", "item"), "user", None),
        P(("parts", "item"), "user", None),
        P(("parts", "item"), "user"),
        P(("parts", "user"), "item", "ka"),
        P(("parts", "user"), "item", "ka"),
        P(("parts", "user"), "item"),
        P(("parts", "item"), "user", "ka"),
        P(("parts", "item"), "user", "ka"),
        P(("parts", "item"), "user"),
    )
    out_specs = (
        P(("parts", "user"), "item", "ka"),
        P(("parts", "user"), "item", "ka"),
        P(("parts", "item"), "user", "ka"),
        P(("parts", "item"), "user", "ka"),
    )
    run = functools.partial(body, mesh.shape["item"], mesh.shape["user"], mesh.shape["ka"])
    return jax.shard_map(run, mesh=mesh, in_specs=in_specs, out_specs=out_specs, check_vma=False)
```

time: 142 us -> 83.4 us (0.59)
  blocking collectives: 31.9 us -> 0 us
  matrix products: 31.4 us -> 0 us
  starting transfers between devices: 0.57 us -> 24.6 us
  Pallas kernels: 0 us -> 19.7 us
  other arithmetic: 15.7 us -> 2.24 us
  between operations: 14.5 us -> 1.54 us
  waiting for transfers between devices: 38.9 us -> 29.2 us
  local copies, waits for them, and re-layouts: 9.01 us -> 5.73 us
    dot_general x5 -> x0, matrix products: 31.4 us -> none  [the longest x1 7.55 us: body(): jnp.einsum('bu,bik->uik', user_onehot, user_part, precision=lax.Precision...]
    ppermute x0 -> x20, waiting for transfers between devices: none -> 29.2 us  [the longest x13 24.3 us: move(): return lax.ppermute(x, axis, [(i, i ^ distance) for i in range(n)])]
    ppermute x0 -> x20, starting transfers between devices: none -> 24.6 us  [the longest x13 23.2 us: move(): return lax.ppermute(x, axis, [(i, i ^ distance) for i in range(n)])]
    psum x1 -> x0, blocking collectives: 22 us -> none  [body(): lax.psum((beta_local, theta_local), ('item', 'user'))]
    psum x1 -> x0, waiting for transfers between devices: 20 us -> none  [body(): norms = lax.psum(norms.astype(jnp.bfloat16), 'ka').astype(jnp.float32)]
    pallas_call x0 -> x9, Pallas kernels: none -> 19.7 us  [the longest x4 6.52 us: statistics(): pl.pallas_call(functools.partial(stat_kernel, pieces, len(users) == 1, jo...]
    all_gather x1 -> x0, waiting for transfers between devices: 12.6 us -> none  [body(): user_block = lax.all_gather(user_exp, 'item', axis=1, tiled=True)[0]]
    reduce_sum x2 -> x0, other arithmetic: 10.3 us -> none  [the longest x1 5.46 us: body(): theta_local = jnp.sum(theta_shape / theta_rate, axis=(0, 1))]
  transfers between devices with their start and end apart: 4 -> 20, of which waited for: 3 -> 6; matrix products, arithmetic and copies ran while one was open for 18% -> 3% of each run, Pallas kernels for 0% -> 12%
where the time goes in v2:
time: 83.4 us; the launch traced here: 82.9 us
  waiting for transfers between devices  29.2 us (35%)
  starting transfers between devices  24.6 us (29%)
  Pallas kernels  19.7 us (24%)
  local copies, waits for them, and re-layouts  5.73 us (7%)
  other arithmetic  2.24 us (3%)
  between operations  1.54 us (2%)
    ppermute x13, waiting for transfers between devices, move(): return lax.ppermute(x, axis, [(i, i ^ distance) for i in range(n)])  24.3 us
    ppermute x13, starting transfers between devices, move(): return lax.ppermute(x, axis, [(i, i ^ distance) for i in range(n)])  23.2 us
    pallas_call x4, Pallas kernels, statistics(): pl.pallas_call(functools.partial(stat_kernel, pieces, len(users) == 1, jo...  6.52 us
    unnamed x38, local copies, waits for them, and re-layouts  5.72 us
    ppermute x2, waiting for transfers between devices, move(): return lax.ppermute(x, (axis, 'ka'), pairs)  4.83 us
    pallas_call x1, Pallas kernels, expected_users(): pl.pallas_call(functools.partial(users_kernel, steps), grid_spec=pltpu.Pr...  3.72 us
    pallas_call x1, Pallas kernels, expected_items(): pl.pallas_call(items_kernel, grid=(rows // block,), in_specs=[spec, spec]...  3.58 us
    pallas_call x1, Pallas kernels, finish_users(): pl.pallas_call(functools.partial(finish_users_kernel, len(joined)), grid_...  2.27 us
  transfers between devices with their start and end apart: 20, of which 6 were waited for; matrix products, arithmetic and copies ran while one was open for 3% of the time, Pallas kernels for 12%

profile of v2, /device:TPU:0, one launch (start us, length us, event | category | flops | bytes accessed | tf_op | source)
XLA Modules:
  0.0 82.9 jit_solution(7019147056519754709)
XLA Ops:
  0.6 3.7 %expected_users.1 = (bf16[256,256]{1,0:T(8,128)(2,1)}, bf16[256,256]{1,0:T(8,128)(2,1)}, f32[1,256]{1,0:T(1,128)}) custom-call(s32[1]{0:T(128)} %bitcast.core_ref, f32[512,256]{1,0:T(8,128)} %bitcast.24, f32[512,256]{1,0:T(8,128)} %bitcast.25), custom_call_target="tpu_custom_call" | custom-call | flops 5242880 | bytes 1310720 | tf_op jit(solution)/shard_map/expected_users/pallas_call | solution.py:62
  4.4 3.6 %expected_items.1 = (bf16[512,256]{1,0:T(8,128)(2,1)}, f32[1,256]{1,0:T(1,128)}) custom-call(f32[512,256]{1,0:T(8,128)} %bitcast.22, f32[512,256]{1,0:T(8,128)} %bitcast.23), custom_call_target="tpu_custom_call" | custom-call | flops 5242880 | bytes 1310720 | tf_op jit(solution)/shard_map/expected_items/pallas_call | solution.py:105
  7.9 3.0 %collective-permute-start.1 = (bf16[512,256]{1,0:T(8,128)(2,1)}, bf16[512,256]{1,0:T(8,128)(2,1)S(1)}, u32[]{:S(2)}, u32[]{:S(2)}) collective-permute-start(bf16[512,256]{1,0:T(8,128)(2,1)} %get-tuple-element.47.refs_2_.refs_1_.exp_ref), channel_id=1, source_target_pairs={{0,2},{2,0},{1,3},{3,1},{4,6},{6,4},{5,7},{7,5},{8,10},{10,8},{9,1... | collective-permute-start | bytes 786440 | tf_op jit(solution)/shard_map/ppermute | solution.py:333
  11.4 2.6 %collective-permute-start.8 = (bf16[256,256]{1,0:T(8,128)(2,1)}, bf16[256,256]{1,0:T(8,128)(2,1)S(1)}, u32[]{:S(2)}, u32[]{:S(2)}) collective-permute-start(bf16[256,256]{1,0:T(8,128)(2,1)} %get-tuple-element.43.refs_0_.keep_ref), channel_id=1, source_target_pairs={{0,8},{4,12},{8,0},{12,4},{1,9},{5,13},{9,1},{13,5},{2,10},{6,14},... | collective-permute-start | bytes 393224 | tf_op jit(solution)/shard_map/ppermute | solution.py:333
  14.0 3.4 %collective-permute-done.1.refs_3_.refs_2_ = bf16[512,256]{1,0:T(8,128)(2,1)S(1)} collective-permute-done((bf16[512,256]{1,0:T(8,128)(2,1)}, bf16[512,256]{1,0:T(8,128)(2,1)S(1)}, u32[]{:S(2)}, u32[]{:S(2)}) %collective-permute-start.1) | collective-permute-done | bytes 262176 | tf_op jit(solution)/shard_map/ppermute | solution.py:333
  18.4 1.9 %collective-permute-start.5 = (bf16[512,256]{1,0:T(8,128)(2,1)S(1)}, bf16[512,256]{1,0:T(8,128)(2,1)S(1)}, u32[]{:S(2)}, u32[]{:S(2)}) collective-permute-start(bf16[512,256]{1,0:T(8,128)(2,1)S(1)} %pad_maximum_fusion), channel_id=1, source_target_pairs={{0,4},{4,0},{8,12},{12,8},{1,5},{5,1},{9,13},{13,9},{2,6},{6,2},{1... | collective-permute-start | bytes 786440 | tf_op jit(solution)/shard_map/ppermute | solution.py:333
  20.3 2.6 %collective-permute-start.9 = (bf16[256,256]{1,0:T(8,128)(2,1)S(1)}, bf16[256,256]{1,0:T(8,128)(2,1)S(1)}, u32[]{:S(2)}, u32[]{:S(2)}) collective-permute-start(bf16[256,256]{1,0:T(8,128)(2,1)S(1)} %collective-permute-done.refs_1_), channel_id=1, source_target_pairs={{0,8},{4,12},{8,0},{12,4},{1,9},{5,13},{9,1},{13,5},{2,10},{6,14},... | collective-permute-start | bytes 393224 | tf_op jit(solution)/shard_map/ppermute | solution.py:333
  23.6 2.2 %copy-done.1 = s32[1,1,64,128,128]{4,3,2,1,0:T(8,128)S(1)} copy-done((s32[1,1,64,128,128]{4,3,2,1,0:T(8,128)S(1)}, s32[1,1,64,128,128]{4,3,2,1,0:T(8,128)}, u32[]{:S(2)}) %copy-start.1) | copy-done | bytes 4194328
  27.1 1.3 %dense_counts.1.refs_6_.refs_5_ = bf16[1024,1024]{1,0:T(8,128)(2,1)S(1)} custom-call(s32[64]{0:T(128)S(1)} %bitcast.19, s32[64]{0:T(128)S(1)} %bitcast.20, s32[1]{0:T(128)} %bitcast.17.live_ref, s32[3]{0:T(128)S(1)} %pad_add_fusion.me_ref, s32[64,128,128]{2,1,0:T(8,128)S(1)} %bitcast.18), custom_call_target="tpu_custom_call" | custom-call | flops 1048576 | bytes 6291456 | tf_op jit(solution)/shard_map/dense_counts/pallas_call | solution.py:159
  29.7 3.5 %collective-permute-start.13 = (bf16[256,256]{1,0:T(8,128)(2,1)S(1)}, bf16[256,256]{1,0:T(8,128)(2,1)S(1)}, u32[]{:S(2)}, u32[]{:S(2)}) collective-permute-start(bf16[256,256]{1,0:T(8,128)(2,1)S(1)} %collective-permute-done.9.refs_1_), channel_id=1, source_target_pairs={{0,4},{4,0},{8,12},{12,8},{1,5},{5,1},{9,13},{13,9},{2,6},{6,2},{1... | collective-permute-start | bytes 393224 | tf_op jit(solution)/shard_map/ppermute | solution.py:333
  33.2 1.6 %statistics_0.1 = (f32[256,256]{1,0:T(8,128)S(1)}, f32[256,256]{1,0:T(8,128)S(1)}, f32[256,512]{1,0:T(8,128)S(1)}, f32[256,512]{1,0:T(8,128)S(1)}, f32[256,512]{1,0:T(8,128)S(1)}, /*index=5*/f32[256,512]{1,0:T(8,128)S(1)}) custom-call(bf16[256,256]{1,0:T(8,128)(2,1)S(1)} %copy-done.2, bf16[256,256]{1,0:T(8,128)(2,1)S(1)} %collective-permute-done.refs_1_, ...), custom_call_target="tpu_custom_call" | custom-call | flops 805306368 | bytes 2097152 | tf_op jit(solution)/shard_map/statistics_0/pallas_call | solution.py:253
  34.9 1.6 %collective-permute-start.4 = (f32[2,256]{1,0:T(2,128)S(1)}, f32[2,256]{1,0:T(2,128)S(1)}, u32[]{:S(2)}, u32[]{:S(2)}) collective-permute-start(f32[2,256]{1,0:T(2,128)S(1)} %pad_maximum_fusion.1), channel_id=1, source_target_pairs={{0,2},{2,0},{1,3},{3,1},{4,6},{6,4},{5,7},{7,5},{8,10},{10,8},{9,1... | collective-permute-start | bytes 6152 | tf_op jit(solution)/shard_map/ppermute | solution.py:333
  36.4 1.6 %statistics_1.1 = (bf16[512,256]{1,0:T(8,128)(2,1)S(1)}, f32[256,512]{1,0:T(8,128)S(1)}, f32[256,512]{1,0:T(8,128)S(1)}, f32[256,512]{1,0:T(8,128)S(1)}, f32[256,512]{1,0:T(8,128)S(1)}) custom-call(bf16[512,256]{1,0:T(8,128)(2,1)S(1)} %collective-permute-done.5.refs_0_, bf16[512,256]{1,0:T(8,128)(2,1)S(1)} %copy-done, ...), custom_call_target="tpu_custom_call" | custom-call | flops 805306368 | bytes 2097152 | tf_op jit(solution)/shard_map/statistics_1/pallas_call | solution.py:253
  38.5 1.6 %statistics_2.1 = (bf16[512,256]{1,0:T(8,128)(2,1)S(1)}, f32[256,512]{1,0:T(8,128)S(1)}, f32[256,512]{1,0:T(8,128)S(1)}, f32[256,512]{1,0:T(8,128)S(1)}, f32[256,512]{1,0:T(8,128)S(1)}) custom-call(bf16[256,256]{1,0:T(8,128)(2,1)S(1)} %collective-permute-done.8.refs_0_, bf16[256,256]{1,0:T(8,128)(2,1)S(1)} %collective-permute-done.9.refs_1_, ...), custom_call_target="tpu_custom_call" | custom-call | flops 805306368 | bytes 2097152 | tf_op jit(solution)/shard_map/statistics_2/pallas_call | solution.py:253
  40.2 2.1 %collective-permute-start.6 = (bf16[512,256]{1,0:T(8,128)(2,1)S(1)}, bf16[512,256]{1,0:T(8,128)(2,1)S(1)}, u32[]{:S(2)}, u32[]{:S(2)}) collective-permute-start(bf16[512,256]{1,0:T(8,128)(2,1)S(1)} %get-tuple-element.59), channel_id=1, source_target_pairs={{0,4},{4,0},{8,12},{12,8},{1,5},{5,1},{9,13},{13,9},{2,6},{6,2},{1... | collective-permute-start | bytes 786440 | tf_op jit(solution)/shard_map/ppermute | solution.py:333
  42.3 2.9 %collective-permute-start.16 = (f32[2,256]{1,0:T(2,128)S(1)}, f32[2,256]{1,0:T(2,128)S(1)}, u32[]{:S(2)}, u32[]{:S(2)}) collective-permute-start(f32[2,256]{1,0:T(2,128)S(1)} %add.63), channel_id=1, source_target_pairs={{0,8},{4,12},{8,0},{12,4},{1,9},{5,13},{9,1},{13,5},{2,10},{6,14},... | collective-permute-start | bytes 6152 | tf_op jit(solution)/shard_map/ppermute | solution.py:333
  45.2 1.6 %statistics_3.1 = (bf16[256,256]{1,0:T(8,128)(2,1)S(1)}, bf16[256,256]{1,0:T(8,128)(2,1)S(1)}, f32[256,512]{1,0:T(8,128)S(1)}, bf16[256,512]{1,0:T(8,128)(2,1)S(...) custom-call(bf16[256,256]{1,0:T(8,128)(2,1)S(1)} %collective-permute-done.12.refs_0_, ...), custom_call_target="tpu_custom_call" | custom-call | flops 805306368 | bytes 2097152 | tf_op jit(solution)/shard_map/statistics_3/pallas_call | solution.py:253
  47.7 1.3 %collective-permute-start.14 = (bf16[256,256]{1,0:T(8,128)(2,1)S(1)}, bf16[256,256]{1,0:T(8,128)(2,1)S(1)}, u32[]{:S(2)}, u32[]{:S(2)}) collective-permute-start(bf16[256,256]{1,0:T(8,128)(2,1)S(1)} %get-tuple-element.71), channel_id=1, source_target_pairs={{0,12},{4,8},{8,4},{12,0},{1,13},{5,9},{9,5},{13,1},{2,14},{6,10},... | collective-permute-start | bytes 393224 | tf_op jit(solution)/shard_map/ppermute | solution.py:333
  49.0 13.9 %collective-permute-done.16 = f32[2,256]{1,0:T(2,128)S(1)} collective-permute-done((f32[2,256]{1,0:T(2,128)S(1)}, f32[2,256]{1,0:T(2,128)S(1)}, u32[]{:S(2)}, u32[]{:S(2)}) %collective-permute-start.16) | collective-permute-done | bytes 2080 | tf_op jit(solution)/shard_map/ppermute | solution.py:333
  62.9 1.4 %collective-permute-start.18 = (bf16[256,512]{1,0:T(8,128)(2,1)S(1)}, bf16[256,512]{1,0:T(8,128)(2,1)S(1)}, u32[]{:S(2)}, u32[]{:S(2)}) collective-permute-start(bf16[256,512]{1,0:T(8,128)(2,1)S(1)} %get-tuple-element.76), channel_id=1, source_target_pairs={{0,2},{2,0},{1,3},{3,1},{4,6},{6,4},{5,7},{7,5},{8,10},{10,8},{9,1... | collective-permute-start | bytes 786440 | tf_op jit(solution)/shard_map/ppermute | solution.py:333
  66.5 5.6 %collective-permute-done.18.refs_1_ = bf16[256,512]{1,0:T(8,128)(2,1)S(1)} collective-permute-done((bf16[256,512]{1,0:T(8,128)(2,1)S(1)}, bf16[256,512]{1,0:T(8,128)(2,1)S(1)}, u32[]{:S(2)}, u32[]{:S(2)}) %collective-permute-start.18) | collective-permute-done | bytes 262176 | tf_op jit(solution)/shard_map/ppermute | solution.py:333
  72.1 4.8 %collective-permute-done.19.refs_2_ = bf16[256,512]{1,0:T(8,128)(2,1)S(1)} collective-permute-done((bf16[256,512]{1,0:T(8,128)(2,1)S(1)}, bf16[256,512]{1,0:T(8,128)(2,1)S(1)}, u32[]{:S(2)}, u32[]{:S(2)}) %collective-permute-start.19) | collective-permute-done | bytes 262176 | tf_op jit(solution)/shard_map/ppermute | solution.py:337
  77.6 2.2 %finish_items.1 = f32[512,256]{1,0:T(8,128)} custom-call(bf16[512,256]{1,0:T(8,128)(2,1)} %get-tuple-element.47.refs_2_.refs_1_.exp_ref, f32[256,512]{1,0:T(8,128)} %copy-done.3, bf16[256,512]{1,0:T(8,128)(2,1)} %copy-done.9, bf16[256,512]{1,0:T(8,128)(2,1)} %copy-done.10, bf16[256,512]{1,0:T(8,128)(2,1)} %copy-done.11), custom_call_target="tpu_custom_call" | custom-call | flops 786432 | bytes 2097152 | tf_op jit(solution)/shard_map/finish_items/pallas_call | solution.py:320
  80.6 2.3 %finish_users.1 = f32[512,256]{1,0:T(8,128)} custom-call(s32[1]{0:T(128)} %bitcast.core_ref, bf16[256,256]{1,0:T(8,128)(2,1)} %get-tuple-element.43.refs_0_.keep_ref, bf16[256,256]{1,0:T(8,128)(2,1)} %get-tuple-element.44.give_ref, f32[256,256]{1,0:T(8,128)} %copy-done.4, bf16[256,256]{1,0:T(8,128)(2,1)} %copy-done.14, bf16[512,256]{1,0:T(8,128)(2,1)} %copy-done.7, ...), custom_call_target="tpu_custom_call" | custom-call | flops 524288 | bytes 1572864 | tf_op jit(solution)/shard_map/finish_users/pallas_call | solution.py:292
  (72 shorter events, 8.9 us)
Async XLA Ops:
  4.4 28.8 %copy-start.2 = (bf16[256,256]{1,0:T(8,128)(2,1)S(1)}, bf16[256,256]{1,0:T(8,128)(2,1)}, u32[]{:S(2)}) copy-start(bf16[256,256]{1,0:T(8,128)(2,1)} %get-tuple-element.43.refs_0_.keep_ref) | copy-start | bytes 393220
  7.9 25.3 %copy-start = (bf16[512,256]{1,0:T(8,128)(2,1)S(1)}, bf16[512,256]{1,0:T(8,128)(2,1)}, u32[]{:S(2)}) copy-start(bf16[512,256]{1,0:T(8,128)(2,1)} %get-tuple-element.47.refs_2_.refs_1_.exp_ref) | copy-start | bytes 786436
  7.9 9.5 %collective-permute-start.1 = (bf16[512,256]{1,0:T(8,128)(2,1)}, bf16[512,256]{1,0:T(8,128)(2,1)S(1)}, u32[]{:S(2)}, u32[]{:S(2)}) collective-permute-start(bf16[512,256]{1,0:T(8,128)(2,1)} %get-tuple-element.47.refs_2_.refs_1_.exp_ref), channel_id=1, source_target_pairs={{0,2},{2,0},{1,3},{3,1},{4,6},{6,4},{5,7},{7,5},{8,10},{10,8},{9,1... | collective-permute-start | bytes 786440 | tf_op jit(solution)/shard_map/ppermute | solution.py:333
  10.9 6.5 %collective-permute-start = (bf16[256,256]{1,0:T(8,128)(2,1)}, bf16[256,256]{1,0:T(8,128)(2,1)S(1)}, u32[]{:S(2)}, u32[]{:S(2)}) collective-permute-start(bf16[256,256]{1,0:T(8,128)(2,1)} %get-tuple-element.44.give_ref), channel_id=1, source_target_pairs={{0,1},{1,0},{2,3},{3,2},{4,5},{5,4},{6,7},{7,6},{8,9},{9,8},{10,11... | collective-permute-start | bytes 393224 | tf_op jit(solution)/shard_map/ppermute | solution.py:356
  10.9 22.3 %collective-permute-start.2 = (bf16[512,256]{1,0:T(8,128)(2,1)}, bf16[512,256]{1,0:T(8,128)(2,1)S(1)}, u32[]{:S(2)}, u32[]{:S(2)}) collective-permute-start(bf16[512,256]{1,0:T(8,128)(2,1)} %get-tuple-element.47.refs_2_.refs_1_.exp_ref), channel_id=1, source_target_pairs={{0,1},{1,0},{2,3},{3,2},{4,5},{5,4},{6,7},{7,6},{8,9},{9,8},{10,11... | collective-permute-start | bytes 786440 | tf_op jit(solution)/shard_map/ppermute | solution.py:356
  11.4 17.0 %collective-permute-start.8 = (bf16[256,256]{1,0:T(8,128)(2,1)}, bf16[256,256]{1,0:T(8,128)(2,1)S(1)}, u32[]{:S(2)}, u32[]{:S(2)}) collective-permute-start(bf16[256,256]{1,0:T(8,128)(2,1)} %get-tuple-element.43.refs_0_.keep_ref), channel_id=1, source_target_pairs={{0,8},{4,12},{8,0},{12,4},{1,9},{5,13},{9,1},{13,5},{2,10},{6,14},... | collective-permute-start | bytes 393224 | tf_op jit(solution)/shard_map/ppermute | solution.py:333
  17.5 15.7 %collective-permute-start.3 = (bf16[512,256]{1,0:T(8,128)(2,1)S(1)}, bf16[512,256]{1,0:T(8,128)(2,1)S(1)}, u32[]{:S(2)}, u32[]{:S(2)}) collective-permute-start(bf16[512,256]{1,0:T(8,128)(2,1)S(1)} %collective-permute-done.1.refs_3_.refs_2_), channel_id=1, source_target_pairs={{0,1},{1,0},{2,3},{3,2},{4,5},{5,4},{6,7},{7,6},{8,9},{9,8},{10,11... | collective-permute-start | bytes 786440 | tf_op jit(solution)/shard_map/ppermute | solution.py:356
  18.4 18.0 %collective-permute-start.5 = (bf16[512,256]{1,0:T(8,128)(2,1)S(1)}, bf16[512,256]{1,0:T(8,128)(2,1)S(1)}, u32[]{:S(2)}, u32[]{:S(2)}) collective-permute-start(bf16[512,256]{1,0:T(8,128)(2,1)S(1)} %pad_maximum_fusion), channel_id=1, source_target_pairs={{0,4},{4,0},{8,12},{12,8},{1,5},{5,1},{9,13},{13,9},{2,6},{6,2},{1... | collective-permute-start | bytes 786440 | tf_op jit(solution)/shard_map/ppermute | solution.py:333
  20.3 9.4 %collective-permute-start.9 = (bf16[256,256]{1,0:T(8,128)(2,1)S(1)}, bf16[256,256]{1,0:T(8,128)(2,1)S(1)}, u32[]{:S(2)}, u32[]{:S(2)}) collective-permute-start(bf16[256,256]{1,0:T(8,128)(2,1)S(1)} %collective-permute-done.refs_1_), channel_id=1, source_target_pairs={{0,8},{4,12},{8,0},{12,4},{1,9},{5,13},{9,1},{13,5},{2,10},{6,14},... | collective-permute-start | bytes 393224 | tf_op jit(solution)/shard_map/ppermute | solution.py:333
  28.5 16.7 %collective-permute-start.12 = (bf16[256,256]{1,0:T(8,128)(2,1)S(1)}, bf16[256,256]{1,0:T(8,128)(2,1)S(1)}, u32[]{:S(2)}, u32[]{:S(2)}) collective-permute-start(bf16[256,256]{1,0:T(8,128)(2,1)S(1)} %collective-permute-done.8.refs_0_), channel_id=1, source_target_pairs={{0,4},{4,0},{8,12},{12,8},{1,5},{5,1},{9,13},{13,9},{2,6},{6,2},{1... | collective-permute-start | bytes 393224 | tf_op jit(solution)/shard_map/ppermute | solution.py:333
  29.7 15.5 %collective-permute-start.13 = (bf16[256,256]{1,0:T(8,128)(2,1)S(1)}, bf16[256,256]{1,0:T(8,128)(2,1)S(1)}, u32[]{:S(2)}, u32[]{:S(2)}) collective-permute-start(bf16[256,256]{1,0:T(8,128)(2,1)S(1)} %collective-permute-done.9.refs_1_), channel_id=1, source_target_pairs={{0,4},{4,0},{8,12},{12,8},{1,5},{5,1},{9,13},{13,9},{2,6},{6,2},{1... | collective-permute-start | bytes 393224 | tf_op jit(solution)/shard_map/ppermute | solution.py:333
  34.9 3.7 %collective-permute-start.4 = (f32[2,256]{1,0:T(2,128)S(1)}, f32[2,256]{1,0:T(2,128)S(1)}, u32[]{:S(2)}, u32[]{:S(2)}) collective-permute-start(f32[2,256]{1,0:T(2,128)S(1)} %pad_maximum_fusion.1), channel_id=1, source_target_pairs={{0,2},{2,0},{1,3},{3,1},{4,6},{6,4},{5,7},{7,5},{8,10},{10,8},{9,1... | collective-permute-start | bytes 6152 | tf_op jit(solution)/shard_map/ppermute | solution.py:333
  38.5 3.8 %collective-permute-start.7 = (f32[2,256]{1,0:T(2,128)S(1)}, f32[2,256]{1,0:T(2,128)S(1)}, u32[]{:S(2)}, u32[]{:S(2)}) collective-permute-start(f32[2,256]{1,0:T(2,128)S(1)} %add.61), channel_id=1, source_target_pairs={{0,4},{4,0},{8,12},{12,8},{1,5},{5,1},{9,13},{13,9},{2,6},{6,2},{1... | collective-permute-start | bytes 6152 | tf_op jit(solution)/shard_map/ppermute | solution.py:333
  40.2 25.1 %copy-start.15 = (f32[1,512]{1,0:T(1,128)S(1)}, f32[1,512]{1,0:T(1,128)}, u32[]{:S(2)}) copy-start(f32[1,512]{1,0:T(1,128)} %param.19) | copy-start | bytes 6148
  40.2 25.1 %copy-start.16 = (f32[1,512]{1,0:T(1,128)S(1)}, f32[1,512]{1,0:T(1,128)}, u32[]{:S(2)}) copy-start(f32[1,512]{1,0:T(1,128)} %param.16) | copy-start | bytes 6148
  40.2 22.7 %collective-permute-start.6 = (bf16[512,256]{1,0:T(8,128)(2,1)S(1)}, bf16[512,256]{1,0:T(8,128)(2,1)S(1)}, u32[]{:S(2)}, u32[]{:S(2)}) collective-permute-start(bf16[512,256]{1,0:T(8,128)(2,1)S(1)} %get-tuple-element.59), channel_id=1, source_target_pairs={{0,4},{4,0},{8,12},{12,8},{1,5},{5,1},{9,13},{13,9},{2,6},{6,2},{1... | collective-permute-start | bytes 786440 | tf_op jit(solution)/shard_map/ppermute | solution.py:333
  42.3 22.1 %collective-permute-start.10 = (bf16[512,256]{1,0:T(8,128)(2,1)S(1)}, bf16[512,256]{1,0:T(8,128)(2,1)S(1)}, u32[]{:S(2)}, u32[]{:S(2)}) collective-permute-start(bf16[512,256]{1,0:T(8,128)(2,1)S(1)} %get-tuple-element.66), channel_id=1, source_target_pairs={{0,8},{4,12},{8,0},{12,4},{1,9},{5,13},{9,1},{13,5},{2,10},{6,14},... | collective-permute-start | bytes 786440 | tf_op jit(solution)/shard_map/ppermute | solution.py:333
  42.3 20.6 %collective-permute-start.16 = (f32[2,256]{1,0:T(2,128)S(1)}, f32[2,256]{1,0:T(2,128)S(1)}, u32[]{:S(2)}, u32[]{:S(2)}) collective-permute-start(f32[2,256]{1,0:T(2,128)S(1)} %add.63), channel_id=1, source_target_pairs={{0,8},{4,12},{8,0},{12,4},{1,9},{5,13},{9,1},{13,5},{2,10},{6,14},... | collective-permute-start | bytes 6152 | tf_op jit(solution)/shard_map/ppermute | solution.py:333
  47.7 32.2 %collective-permute-start.14 = (bf16[256,256]{1,0:T(8,128)(2,1)S(1)}, bf16[256,256]{1,0:T(8,128)(2,1)S(1)}, u32[]{:S(2)}, u32[]{:S(2)}) collective-permute-start(bf16[256,256]{1,0:T(8,128)(2,1)S(1)} %get-tuple-element.71), channel_id=1, source_target_pairs={{0,12},{4,8},{8,4},{12,0},{1,13},{5,9},{9,5},{13,1},{2,14},{6,10},... | collective-permute-start | bytes 393224 | tf_op jit(solution)/shard_map/ppermute | solution.py:333
  49.0 30.9 %collective-permute-start.15 = (bf16[256,256]{1,0:T(8,128)(2,1)S(1)}, bf16[256,256]{1,0:T(8,128)(2,1)S(1)}, u32[]{:S(2)}, u32[]{:S(2)}) collective-permute-start(bf16[256,256]{1,0:T(8,128)(2,1)S(1)} %get-tuple-element.72), channel_id=1, source_target_pairs={{0,13},{1,12},{4,9},{5,8},{8,5},{9,4},{12,1},{13,0},{2,15},{3,14},... | collective-permute-start | bytes 393224 | tf_op jit(solution)/shard_map/ppermute | solution.py:337
  62.9 2.0 %collective-permute-start.17 = (bf16[256,512]{1,0:T(8,128)(2,1)S(1)}, bf16[256,512]{1,0:T(8,128)(2,1)S(1)}, u32[]{:S(2)}, u32[]{:S(2)}) collective-permute-start(bf16[256,512]{1,0:T(8,128)(2,1)S(1)} %get-tuple-element.75), channel_id=1, source_target_pairs={{0,1},{1,0},{2,3},{3,2},{4,5},{5,4},{6,7},{7,6},{8,9},{9,8},{10,11... | collective-permute-start | bytes 786440 | tf_op jit(solution)/shard_map/ppermute | solution.py:356
  62.9 9.2 %collective-permute-start.18 = (bf16[256,512]{1,0:T(8,128)(2,1)S(1)}, bf16[256,512]{1,0:T(8,128)(2,1)S(1)}, u32[]{:S(2)}, u32[]{:S(2)}) collective-permute-start(bf16[256,512]{1,0:T(8,128)(2,1)S(1)} %get-tuple-element.76), channel_id=1, source_target_pairs={{0,2},{2,0},{1,3},{3,1},{4,6},{6,4},{5,7},{7,5},{8,10},{10,8},{9,1... | collective-permute-start | bytes 786440 | tf_op jit(solution)/shard_map/ppermute | solution.py:333
  64.4 12.6 %collective-permute-start.19 = (bf16[256,512]{1,0:T(8,128)(2,1)S(1)}, bf16[256,512]{1,0:T(8,128)(2,1)S(1)}, u32[]{:S(2)}, u32[]{:S(2)}) collective-permute-start(bf16[256,512]{1,0:T(8,128)(2,1)S(1)} %get-tuple-element.77), channel_id=1, source_target_pairs={{0,3},{1,2},{2,1},{3,0},{4,7},{5,6},{6,5},{7,4},{8,11},{9,10},{10,... | collective-permute-start | bytes 786440 | tf_op jit(solution)/shard_map/ppermute | solution.py:337
  64.9 15.0 %collective-permute-start.11 = (bf16[256,256]{1,0:T(8,128)(2,1)S(1)}, bf16[256,256]{1,0:T(8,128)(2,1)S(1)}, u32[]{:S(2)}, u32[]{:S(2)}) collective-permute-start(bf16[256,256]{1,0:T(8,128)(2,1)S(1)} %add_convert_fusion), channel_id=1, source_target_pairs={{0,1},{1,0},{2,3},{3,2},{4,5},{5,4},{6,7},{7,6},{8,9},{9,8},{10,11... | collective-permute-start | bytes 393224 | tf_op jit(solution)/shard_map/ppermute | solution.py:356
  (15 other events, 106.4 us)

commit v3 on v0

v3 whole, which is shorter than its diff:
```python
import functools

import jax
import jax.numpy as jnp
from jax import lax
from jax.experimental import pallas as pl
from jax.experimental.pallas import tpu as pltpu
from jax.sharding import PartitionSpec as P

BF16 = jnp.bfloat16
F32 = jnp.float32
VMEM = pltpu.MemorySpace.VMEM
SMEM = pltpu.MemorySpace.SMEM
HBM = pltpu.MemorySpace.HBM
EXTRA = 16
MIB = 1024 * 1024
CHEAP = pl.CostEstimate(flops=1024, transcendentals=0, bytes_accessed=1024)
DIMS_NT = (((1,), (1,)), ((), ()))
DIMS_TN = (((0,), (0,)), ((), ()))


def pinned(x):
    return pltpu.with_memory_space_constraint(x, HBM)


def reciprocal(x):
    r = pl.reciprocal(x, approx=True)
    return r * (2.0 - x * r)


def exp_digamma(x, inv_rate):
    w = x * (x + 3.0)
    p = w * (w + 2.0)
    y = x + 4.0
    inv = reciprocal(y * p)
    iy = inv * p
    iy2 = iy * iy
    shift = (2.0 * x + 3.0) * (2.0 * w + 2.0) * (inv * y)
    series = iy * 0.5 + iy2 * (1.0 / 12.0 - iy2 * (1.0 / 120.0 - iy2 * (1.0 / 252.0)))
    return y * inv_rate * jnp.exp(-(series + shift))


def encode(values):
    row = lax.broadcasted_iota(jnp.int32, (EXTRA, values[0].shape[1]), 0)
    out = jnp.zeros(row.shape, F32)
    for i, rest in enumerate(values):
        for j in range(3):
            piece = rest.astype(BF16).astype(F32)
            rest = rest - piece
            out = jnp.where(row == 3 * i + j, piece, out)
    return out.astype(BF16)


def decode(block):
    block = block.astype(F32)
    return [block[3 * i : 3 * i + 1] + block[3 * i + 1 : 3 * i + 2] + block[3 * i + 2 : 3 * i + 3] for i in range(2)]


def chunk_copies(starts, chunk, refs, buffers, sems):
    copies = []
    for j, start in enumerate(starts):
        here = pl.ds(start, chunk)
        copies.append(
            [pltpu.make_async_copy(r.at[here], b.at[here], sems.at[i, j]) for i, (r, b) in enumerate(zip(refs, buffers))]
        )
    for group in copies:
        for copy in group:
            copy.start()
    return copies


def expected_kernel(chunk_u, chunk_i, theta_ref, trate_ref, beta_ref, brate_ref, *refs):
    both_ref, item_ref, pack_ref, theta_buf, trate_buf, beta_buf, brate_buf, user_sems, item_sems = refs
    core = lax.axis_index("ka")
    half = both_ref.shape[0] // 2
    rows = beta_ref.shape[0]
    steps = half // chunk_u
    starts = []
    for side in (1 - core, core):
        starts += [pl.multiple_of(side * half + j * chunk_u, chunk_u) for j in range(steps)]
    item_starts = list(range(0, rows, chunk_i))
    user_copies = chunk_copies(starts, chunk_u, (theta_ref, trate_ref), (theta_buf, trate_buf), user_sems)
    item_copies = chunk_copies(item_starts, chunk_i, (beta_ref, brate_ref), (beta_buf, brate_buf), item_sems)
    theta_total = jnp.zeros((1, both_ref.shape[1]), F32)
    for j, start in enumerate(starts):
        for copy in user_copies[j]:
            copy.wait()
        x = theta_buf[pl.ds(start, chunk_u), :]
        inv_rate = reciprocal(trate_buf[pl.ds(start, chunk_u), :])
        value = exp_digamma(x, inv_rate).astype(BF16)
        at = (j % steps) * chunk_u
        if j < steps:
            both_ref[half + at : half + at + chunk_u, :] = value
            pack_ref[at : at + chunk_u, :] = value
        else:
            both_ref[at : at + chunk_u, :] = value
        theta_total += jnp.sum(x * inv_rate, axis=0, keepdims=True)
    beta_total = jnp.zeros((1, both_ref.shape[1]), F32)
    for j, start in enumerate(item_starts):
        for copy in item_copies[j]:
            copy.wait()
        x = beta_buf[start : start + chunk_i, :]
        inv_rate = reciprocal(brate_buf[start : start + chunk_i, :])
        value = exp_digamma(x, inv_rate).astype(BF16)
        item_ref[start : start + chunk_i, :] = value
        pack_ref[half + start : half + start + chunk_i, :] = value
        beta_total += jnp.sum(x * inv_rate, axis=0, keepdims=True)
    extra = encode([theta_total, beta_total])
    item_ref[rows:, :] = extra
    pack_ref[half + rows :, :] = extra


def expected(theta, trate, beta, brate):
    rows, cols = theta.shape
    item_rows = beta.shape[0]
    half = rows // 2
    chunk_u = min(half, 128)
    chunk_i = min(item_rows, 128)
    shapes = [rows, item_rows + EXTRA, half + item_rows + EXTRA]
    return pl.pallas_call(
        functools.partial(expected_kernel, chunk_u, chunk_i),
        in_specs=[pl.BlockSpec(memory_space=HBM)] * 4,
        out_specs=[pl.BlockSpec(memory_space=VMEM)] * 3,
        out_shape=[jax.ShapeDtypeStruct((r, cols), BF16) for r in shapes],
        scratch_shapes=[
            pltpu.VMEM((rows, cols), F32),
            pltpu.VMEM((rows, cols), F32),
            pltpu.VMEM((item_rows, cols), F32),
            pltpu.VMEM((item_rows, cols), F32),
            pltpu.SemaphoreType.DMA((2, rows // chunk_u)),
            pltpu.SemaphoreType.DMA((2, item_rows // chunk_i)),
        ],
        compiler_params=pltpu.CompilerParams(vmem_limit_bytes=6 * MIB),
        cost_estimate=CHEAP,
        name="expected",
    )(pinned(theta), pinned(trate), pinned(beta), pinned(brate))


def dense_kernel(shard_tiles, chunk, rows, users_in, items_in, live_ref, counts_ref, out_ref, *scratch):
    users_ref, items_ref, buf, sems, index_sems = scratch
    tile = counts_ref.shape[1]
    half = rows // 2
    piece = min(half, tile)
    n_chunks = counts_ref.shape[0] // chunk
    copies = [
        pltpu.make_async_copy(
            counts_ref.at[pl.ds(c * chunk, chunk)], buf.at[pl.ds(c * chunk, chunk)], sems.at[c]
        )
        for c in range(n_chunks)
    ]
    index_copies = [
        pltpu.make_async_copy(users_in, users_ref, index_sems.at[0]),
        pltpu.make_async_copy(items_in, items_ref, index_sems.at[1]),
    ]
    for copy in index_copies + copies:
        copy.start()
    out_ref[...] = jnp.zeros_like(out_ref)
    for copy in index_copies:
        copy.wait()
    z = lax.axis_index("item")
    x = lax.axis_index("user")
    core = lax.axis_index("ka")
    live = live_ref[0]

    def place(slot, carry):
        item = items_ref[slot]
        owner = lax.div(item, shard_tiles)
        column = (owner ^ x) * shard_tiles + lax.rem(item, shard_tiles)
        col = pl.multiple_of(column * tile, tile)
        for j in range(tile // piece):
            row = users_ref[slot] * tile + j * piece
            shard = lax.div(row, rows)
            within = lax.rem(row, rows)

            @pl.when(lax.div(within, half) == core)
            def _():
                start = pl.multiple_of((shard ^ z) * half + lax.rem(within, half), piece)
                value = buf[slot, j * piece : (j + 1) * piece, :].astype(F32).astype(BF16)
                out_ref[pl.ds(start, piece), pl.ds(col, tile)] = value

        return carry

    for c in range(n_chunks):
        copies[c].wait()
        lax.fori_loop(c * chunk, jnp.clip(live, c * chunk, (c + 1) * chunk), place, 0)


def dense_counts(counts, users, items, live, rows, n_item, item_rows, n_user):
    slots, tile, _ = counts.shape
    chunk = 8
    out_rows = n_item * rows // 2
    return pl.pallas_call(
        functools.partial(dense_kernel, item_rows // n_user // tile, chunk, rows),
        in_specs=[pl.BlockSpec(memory_space=m) for m in (HBM, HBM, SMEM, HBM)],
        out_specs=pl.BlockSpec(memory_space=VMEM),
        out_shape=jax.ShapeDtypeStruct((out_rows, item_rows), BF16),
        scratch_shapes=[
            pltpu.SMEM(users.shape, jnp.int32),
            pltpu.SMEM(items.shape, jnp.int32),
            pltpu.VMEM((slots, tile, tile), jnp.int32),
            pltpu.SemaphoreType.DMA((slots // chunk,)),
            pltpu.SemaphoreType.DMA((2,)),
        ],
        compiler_params=pltpu.CompilerParams(vmem_limit_bytes=8 * MIB),
        cost_estimate=CHEAP,
        name="dense_counts",
    )(pinned(users), pinned(items), live, pinned(counts))


def stat_kernel(pieces, half, last, has_acc, at, *refs):
    refs = list(refs)
    take = lambda n: [refs.pop(0) for _ in range(n)]
    mine_ref, other_ref = take(2)
    mine = mine_ref[:half, :]
    other = other_ref[half : 2 * half, :] if at else other_ref[:half, :]
    item_mine = take(pieces)
    item_other = take(pieces)
    (counts_ref,) = take(1)
    (acc_in,) = take(1) if has_acc else (None,)
    joined_out = at != 0 and not last
    stat_refs = take(1 if joined_out else 2)
    acc_refs = take(2 * pieces if last else 1)
    cols = mine.shape[1]
    total_mine = None
    total_other = None
    width = 256
    for p in range(pieces):
        rows = item_mine[p].shape[0] - EXTRA
        skip = item_other[p].shape[0] - EXTRA - rows
        for c in range(rows // width):
            left = item_mine[p][c * width : (c + 1) * width, :]
            right = item_other[p][skip + c * width : skip + (c + 1) * width, :]
            norm = lax.dot_general(mine, left, DIMS_NT, preferred_element_type=F32)
            norm += lax.dot_general(other, right, DIMS_NT, preferred_element_type=F32)
            columns = slice(p * rows + c * width, p * rows + (c + 1) * width)
            grid = counts_ref[at * half : (at + 1) * half, columns].astype(F32)
            ratio = (grid * reciprocal(norm)).astype(BF16)
            stat = jnp.dot(ratio, left, preferred_element_type=F32)
            total_mine = stat if total_mine is None else total_mine + stat
            stat = jnp.dot(ratio, right, preferred_element_type=F32)
            total_other = stat if total_other is None else total_other + stat
            for i, factors in enumerate((mine, other)):
                update = lax.dot_general(factors, ratio, DIMS_TN, preferred_element_type=F32)
                if has_acc:
                    update += acc_in[i * cols : (i + 1) * cols, columns]
                if last:
                    target = acc_refs[i * pieces + p]
                    target[:, c * width : (c + 1) * width] = update.astype(target.dtype)
                else:
                    acc_refs[0][i * cols : (i + 1) * cols, columns] = update
    if joined_out:
        stat_refs[0][:half, :] = total_mine.astype(stat_refs[0].dtype)
        stat_refs[0][half : 2 * half, :] = total_other.astype(stat_refs[0].dtype)
    else:
        stat_refs[0][:half, :] = total_mine.astype(stat_refs[0].dtype)
        stat_refs[1][...] = total_other.astype(stat_refs[1].dtype)
    if at != 0:
        stat_refs[0][-EXTRA:, :] = encode(row_totals(item_mine))


def row_totals(item_refs):
    sums = None
    for ref in item_refs:
        came = decode(ref[-EXTRA:, :])
        sums = came if sums is None else [a + b for a, b in zip(sums, came)]
    return sums


def statistics(at, users, item_mine, item_other, dense, acc, last, half_rows):
    half = users[0].shape[1]
    item_rows = dense.shape[1]
    args = [*users, *item_mine, *item_other, dense]
    if acc is not None:
        args.append(acc)
    if at and not last:
        out_shape = [jax.ShapeDtypeStruct((2 * half_rows + EXTRA, half), BF16)]
    elif at:
        out_shape = [jax.ShapeDtypeStruct((half_rows + e, half), BF16) for e in (EXTRA, 0)]
    else:
        out_shape = [jax.ShapeDtypeStruct((half_rows, half), F32)] * 2
    n_stats = len(out_shape)
    if last:
        pieces = len(item_mine)
        out_shape += [
            jax.ShapeDtypeStruct((half, item_rows // pieces), BF16 if i else F32) for i in range(2 * pieces)
        ]
    else:
        out_shape.append(jax.ShapeDtypeStruct((2 * half, item_rows), F32))
    spec = pl.BlockSpec(memory_space=VMEM)
    out = pl.pallas_call(
        functools.partial(stat_kernel, len(item_mine), half_rows, last, acc is not None, at),
        in_specs=[spec] * len(args),
        out_specs=[spec] * len(out_shape),
        out_shape=out_shape,
        compiler_params=pltpu.CompilerParams(vmem_limit_bytes=16 * MIB),
        cost_estimate=CHEAP,
        name="statistics_%d" % at,
    )(*args)
    return list(out[:n_stats]), list(out[n_stats:])


def finish_users_kernel(n_joined, pieces, *refs):
    refs = list(refs)
    take = lambda n: [refs.pop(0) for _ in range(n)]
    both_ref, own_ref, sum_ref = take(3)
    joined = take(n_joined)
    same_ref, cross_ref = take(2)
    item_refs = take(pieces)
    activity_ref, popularity_ref = take(2)
    outs = take(3)
    bufs = take(3)
    (sems,) = take(1)
    core = lax.axis_index("ka")
    half = own_ref.shape[0]
    copies = []

    total = own_ref[...]
    for ref in joined:
        total += ref[:half, :].astype(F32)
    total += same_ref[:half, :].astype(F32)
    start = pl.multiple_of(core * half, half)
    bufs[0][pl.ds(start, half), :] = 0.3 + both_ref[:half, :].astype(F32) * total
    copies.append(pltpu.make_async_copy(bufs[0].at[pl.ds(start, half)], outs[0].at[pl.ds(start, half)], sems.at[0]))
    copies[-1].start()

    total = sum_ref[...].astype(F32) + cross_ref[...].astype(F32)
    start = pl.multiple_of((1 - core) * half, half)
    bufs[0][pl.ds(start, half), :] = 0.3 + both_ref[half:, :].astype(F32) * total
    copies.append(pltpu.make_async_copy(bufs[0].at[pl.ds(start, half)], outs[0].at[pl.ds(start, half)], sems.at[1]))
    copies[-1].start()

    theta_total, beta_total = row_totals(item_refs)
    for ref in joined + [same_ref]:
        came = decode(ref[-EXTRA:, :])
        theta_total += came[0]
        beta_total += came[1]
    for i, (column_ref, total) in enumerate(((activity_ref, beta_total), (popularity_ref, theta_total))):
        rows = column_ref.shape[1]
        column = jnp.broadcast_to(column_ref[...], (total.shape[1], rows)).T
        bufs[1 + i][...] = column + total
        copies.append(pltpu.make_async_copy(bufs[1 + i], outs[1 + i], sems.at[2 + i]))
        copies[-1].start()
    for copy in copies:
        copy.wait()


def finish_users(both, own, other_sum, joined, same, cross, items, activity, popularity):
    rows, half = both.shape
    args = [both, own, other_sum, *joined, same, cross, *items, activity, popularity]
    out_shape = [
        jax.ShapeDtypeStruct((rows, half), F32),
        jax.ShapeDtypeStruct((activity.shape[1], half), F32),
        jax.ShapeDtypeStruct((popularity.shape[1], half), F32),
    ]
    return pl.pallas_call(
        functools.partial(finish_users_kernel, len(joined), len(items)),
        in_specs=[pl.BlockSpec(memory_space=VMEM)] * len(args),
        out_specs=[pl.BlockSpec(memory_space=HBM)] * 3,
        out_shape=out_shape,
        scratch_shapes=[pltpu.VMEM(o.shape, F32) for o in out_shape] + [pltpu.SemaphoreType.DMA((4,))],
        compiler_params=pltpu.CompilerParams(vmem_limit_bytes=8 * MIB),
        cost_estimate=CHEAP,
        name="finish_users",
    )(*args)


def finish_items_kernel(n, exp_ref, own_ref, *refs):
    out_ref, buf, sems = refs[n:]
    rows = out_ref.shape[0]
    chunk = min(rows, 256)
    copies = []
    for j in range(rows // chunk):
        part = slice(j * chunk, (j + 1) * chunk)
        total = own_ref[:, part]
        for p in range(n):
            total += refs[p][:, part].astype(F32)
        buf[part, :] = 0.3 + exp_ref[part, :].astype(F32) * total.T
        here = pl.ds(j * chunk, chunk)
        copies.append(pltpu.make_async_copy(buf.at[here], out_ref.at[here], sems.at[j]))
        copies[-1].start()
    for copy in copies:
        copy.wait()


def finish_items(item_exp, own, came):
    half, rows = own.shape
    return pl.pallas_call(
        functools.partial(finish_items_kernel, len(came)),
        in_specs=[pl.BlockSpec(memory_space=VMEM)] * (2 + len(came)),
        out_specs=pl.BlockSpec(memory_space=HBM),
        out_shape=jax.ShapeDtypeStruct((rows, half), F32),
        scratch_shapes=[pltpu.VMEM((rows, half), F32), pltpu.SemaphoreType.DMA((rows // min(rows, 256),))],
        compiler_params=pltpu.CompilerParams(vmem_limit_bytes=6 * MIB),
        cost_estimate=CHEAP,
        name="finish_items",
    )(item_exp, own, *came)


def move(x, axis, n, n_ka, distance, cross):
    if not cross:
        return lax.ppermute(x, axis, [(i, i ^ distance) for i in range(n)])
    pairs = [
        (i * n_ka + h, (i ^ distance) * n_ka + (n_ka - 1 - h)) for i in range(n) for h in range(n_ka)
    ]
    return lax.ppermute(x, (axis, "ka"), pairs)


def body(
    n_item,
    n_user,
    n_ka,
    counts,
    tile_user,
    tile_item,
    tile_live,
    theta_shape,
    theta_rate,
    user_activity,
    beta_shape,
    beta_rate,
    item_popularity,
):
    def sibling(x):
        return lax.ppermute(x, "ka", [(h, n_ka - 1 - h) for h in range(n_ka)])

    def along_item(x, distance, cross):
        return move(x, "item", n_item, n_ka, distance, cross)

    both, item_exp, pack = expected(theta_shape[0], theta_rate[0], beta_shape[0], beta_rate[0])
    came_pack = sibling(pack)
    rows = both.shape[0]
    half_rows = rows // 2
    item_rows = beta_shape.shape[1] * n_user

    shards = [both]
    for k in range(1, n_item):
        low = k & -k
        shards.append(along_item(shards[k ^ low], low, False))
    users = [[both, came_pack]] + [[x, sibling(x)] for x in shards[1:]]

    item_mine = [item_exp]
    item_other = [came_pack]
    for p in range(1, n_user):
        item_mine.append(move(item_exp, "user", n_user, n_ka, p, False))
        item_other.append(move(item_exp, "user", n_user, n_ka, p, True))

    dense = dense_counts(
        counts[0, 0],
        tile_user[0, 0],
        tile_item[0, 0],
        tile_live[0],
        rows,
        n_item,
        item_rows,
        n_user,
    )

    order = sorted(range(1, n_item - 1), key=lambda k: (k & (k - 1) != 0, -k if k & (k - 1) == 0 else k))
    acc = None
    joined = []
    for k in order + [0, n_item - 1]:
        last = k == n_item - 1
        stats, accs = statistics(k, users[k], item_mine, item_other, dense, acc, last, half_rows)
        acc = accs[0]
        if k == 0:
            own, own_other = stats
        elif not last:
            joined.append(along_item(stats[0], k, False))
        else:
            same = along_item(stats[0], k, False)
            cross = along_item(stats[1], k, True)
    came = [sibling(accs[n_user])]
    for p in range(1, n_user):
        came.append(move(accs[p], "user", n_user, n_ka, p, False))
        came.append(move(accs[n_user + p], "user", n_user, n_ka, p, True))
    other_sum = own_other
    for x in joined:
        other_sum = other_sum + x[half_rows : 2 * half_rows].astype(F32)
    other_sum = sibling(other_sum.astype(BF16))

    new_beta_shape = finish_items(item_exp, accs[0], came)
    new_theta_shape, new_theta_rate, new_beta_rate = finish_users(
        both, own, other_sum, joined, same, cross, item_mine, user_activity, item_popularity
    )
    return (new_theta_shape[None], new_theta_rate[None], new_beta_shape[None], new_beta_rate[None])


def solution(mesh):
    in_specs = (
        P(("parts", "item"), "user", None, None, None),
        P(("parts", "item"), "user", None),
        P(("parts", "item"), "user", None),
        P(("parts", "item"), "user"),
        P(("parts", "user"), "item", "ka"),
        P(("parts", "user"), "item", "ka"),
        P(("parts", "user"), "item"),
        P(("parts", "item"), "user", "ka"),
        P(("parts", "item"), "user", "ka"),
        P(("parts", "item"), "user"),
    )
    out_specs = (
        P(("parts", "user"), "item", "ka"),
        P(("parts", "user"), "item", "ka"),
        P(("parts", "item"), "user", "ka"),
        P(("parts", "item"), "user", "ka"),
    )
    run = functools.partial(body, mesh.shape["item"], mesh.shape["user"], mesh.shape["ka"])
    return jax.shard_map(run, mesh=mesh, in_specs=in_specs, out_specs=out_specs, check_vma=False)
```

time: 142 us -> 60 us (0.42)
  blocking collectives: 31.9 us -> 0 us
  matrix products: 31.4 us -> 0 us
  starting transfers between devices: 0.57 us -> 22.1 us
  waiting for transfers between devices: 38.9 us -> 22.2 us
  other arithmetic: 15.7 us -> 0.05 us
  Pallas kernels: 0 us -> 14 us
  between operations: 14.5 us -> 1.42 us
  local copies, waits for them, and re-layouts: 9.01 us -> 0.01 us
    dot_general x5 -> x0, matrix products: 31.4 us -> none  [the longest x1 7.55 us: body(): jnp.einsum('bu,bik->uik', user_onehot, user_part, precision=lax.Precision...]
    ppermute x0 -> x17, waiting for transfers between devices: none -> 22.2 us  [the longest x8 15.9 us: move(): return lax.ppermute(x, axis, [(i, i ^ distance) for i in range(n)])]
    ppermute x0 -> x17, starting transfers between devices: none -> 22.1 us  [the longest x8 11.9 us: move(): return lax.ppermute(x, axis, [(i, i ^ distance) for i in range(n)])]
    psum x1 -> x0, blocking collectives: 22 us -> none  [body(): lax.psum((beta_local, theta_local), ('item', 'user'))]
    psum x1 -> x0, waiting for transfers between devices: 20 us -> none  [body(): norms = lax.psum(norms.astype(jnp.bfloat16), 'ka').astype(jnp.float32)]
    pallas_call x0 -> x8, Pallas kernels: none -> 14 us  [the longest x4 6.64 us: statistics(): pl.pallas_call(functools.partial(stat_kernel, len(item_mine), half_rows,...]
    all_gather x1 -> x0, waiting for transfers between devices: 12.6 us -> none  [body(): user_block = lax.all_gather(user_exp, 'item', axis=1, tiled=True)[0]]
    reduce_sum x2 -> x0, other arithmetic: 10.3 us -> none  [the longest x1 5.46 us: body(): theta_local = jnp.sum(theta_shape / theta_rate, axis=(0, 1))]
  transfers between devices with their start and end apart: 4 -> 17, of which waited for: 3 -> 5; matrix products, arithmetic and copies ran while one was open for 18% -> 0% of each run, Pallas kernels for 0% -> 17%
where the time goes in v3:
time: 60 us; the launch traced here: 59.8 us
  waiting for transfers between devices  22.2 us (37%)
  starting transfers between devices  22.1 us (37%)
  Pallas kernels  14 us (23%)
  between operations  1.42 us (2%)
    ppermute x8, waiting for transfers between devices, move(): return lax.ppermute(x, axis, [(i, i ^ distance) for i in range(n)])  15.9 us
    ppermute x8, starting transfers between devices, move(): return lax.ppermute(x, axis, [(i, i ^ distance) for i in range(n)])  11.9 us
    pallas_call x4, Pallas kernels, statistics(): pl.pallas_call(functools.partial(stat_kernel, len(item_mine), half_rows,...  6.64 us
    ppermute x6, starting transfers between devices, sibling(): return lax.ppermute(x, 'ka', [(h, n_ka - 1 - h) for h in range(n_ka)])  6.04 us
    ppermute x3, waiting for transfers between devices, move(): return lax.ppermute(x, (axis, 'ka'), pairs)  5.28 us
    ppermute x3, starting transfers between devices, move(): return lax.ppermute(x, (axis, 'ka'), pairs)  4.21 us
    pallas_call x1, Pallas kernels, expected(): pl.pallas_call(functools.partial(expected_kernel, chunk_u, chunk_i), in_s...  2.76 us
    pallas_call x1, Pallas kernels, dense_counts(): pl.pallas_call(functools.partial(dense_kernel, item_rows // n_user // til...  2.24 us
  transfers between devices with their start and end apart: 17, of which 5 were waited for; matrix products, arithmetic and copies ran while one was open for 0% of the time, Pallas kernels for 17%

profile of v3, /device:TPU:0, one launch (start us, length us, event | category | flops | bytes accessed | tf_op | source)
XLA Modules:
  0.0 59.8 jit_solution(9804110771256453733)
XLA Ops:
  0.6 2.8 %expected.1 = (bf16[512,256]{1,0:T(8,128)(2,1)S(1)}, bf16[528,256]{1,0:T(8,128)(2,1)S(1)}, bf16[784,256]{1,0:T(8,128)(2,1)S(1)}) custom-call(f32[512,256]{1,0:T(8,128)} %bitcast.14, f32[512,256]{1,0:T(8,128)} %bitcast.15, f32[512,256]{1,0:T(8,128)} %bitcast.16, f32[512,256]{1,0:T(8,128)} %bitcast.17), custom_call_target="tpu_custom_call" | custom-call | flops 1024 | bytes 1024 | tf_op jit(solution)/shard_map/expected/pallas_call | solution.py:120
  3.4 3.0 %collective-permute-start.1 = (bf16[528,256]{1,0:T(8,128)(2,1)S(1)}, bf16[528,256]{1,0:T(8,128)(2,1)S(1)}, u32[]{:S(2)}, u32[]{:S(2)}) collective-permute-start(bf16[528,256]{1,0:T(8,128)(2,1)S(1)} %get-tuple-element.25.refs_2_.refs_7_.exp_ref), channel_id=1, source_target_pairs={{0,2},{2,0},{1,3},{3,1},{4,6},{6,4},{5,7},{7,5},{8,10},{10,8},{9,1... | collective-permute-start | bytes 811016 | tf_op jit(solution)/shard_map/ppermute | solution.py:401
  6.4 2.6 %collective-permute-start.5 = (bf16[512,256]{1,0:T(8,128)(2,1)S(1)}, bf16[512,256]{1,0:T(8,128)(2,1)S(1)}, u32[]{:S(2)}, u32[]{:S(2)}) collective-permute-start(bf16[512,256]{1,0:T(8,128)(2,1)S(1)} %get-tuple-element.23.refs_0_), channel_id=1, source_target_pairs={{0,8},{4,12},{8,0},{12,4},{1,9},{5,13},{9,1},{13,5},{2,10},{6,14},... | collective-permute-start | bytes 786440 | tf_op jit(solution)/shard_map/ppermute | solution.py:401
  9.0 1.6 %collective-permute-start.3 = (bf16[512,256]{1,0:T(8,128)(2,1)S(1)}, bf16[512,256]{1,0:T(8,128)(2,1)S(1)}, u32[]{:S(2)}, u32[]{:S(2)}) collective-permute-start(bf16[512,256]{1,0:T(8,128)(2,1)S(1)} %get-tuple-element.23.refs_0_), channel_id=1, source_target_pairs={{0,4},{4,0},{8,12},{12,8},{1,5},{5,1},{9,13},{13,9},{2,6},{6,2},{1... | collective-permute-start | bytes 786440 | tf_op jit(solution)/shard_map/ppermute | solution.py:401
  10.6 0.6 %collective-permute-start.2 = (bf16[528,256]{1,0:T(8,128)(2,1)S(1)}, bf16[528,256]{1,0:T(8,128)(2,1)S(1)}, u32[]{:S(2)}, u32[]{:S(2)}) collective-permute-start(bf16[528,256]{1,0:T(8,128)(2,1)S(1)} %get-tuple-element.25.refs_2_.refs_7_.exp_ref), channel_id=1, source_target_pairs={{0,3},{1,2},{2,1},{3,0},{4,7},{5,6},{6,5},{7,4},{8,11},{9,10},{10,... | collective-permute-start | bytes 811016 | tf_op jit(solution)/shard_map/ppermute | solution.py:405
  11.2 9.6 %collective-permute-done.5.refs_0_ = bf16[512,256]{1,0:T(8,128)(2,1)S(1)} collective-permute-done((bf16[512,256]{1,0:T(8,128)(2,1)S(1)}, bf16[512,256]{1,0:T(8,128)(2,1)S(1)}, u32[]{:S(2)}, u32[]{:S(2)}) %collective-permute-start.5) | collective-permute-done | bytes 262176 | tf_op jit(solution)/shard_map/ppermute | solution.py:401
  21.3 1.1 %collective-permute-start.10 = (bf16[512,256]{1,0:T(8,128)(2,1)S(1)}, bf16[512,256]{1,0:T(8,128)(2,1)S(1)}, u32[]{:S(2)}, u32[]{:S(2)}) collective-permute-start(bf16[512,256]{1,0:T(8,128)(2,1)S(1)} %collective-permute-done.5.refs_0_), channel_id=1, source_target_pairs={{0,4},{4,0},{8,12},{12,8},{1,5},{5,1},{9,13},{13,9},{2,6},{6,2},{1... | collective-permute-start | bytes 786440 | tf_op jit(solution)/shard_map/ppermute | solution.py:401
  23.1 2.2 %dense_counts.1.refs_6_ = bf16[1024,1024]{1,0:T(8,128)(2,1)S(1)} custom-call(s32[64]{0:T(128)} %bitcast.19, s32[64]{0:T(128)} %bitcast.20, s32[1]{0:T(128)} %bitcast.12.live_ref, s32[64,128,128]{2,1,0:T(8,128)} %bitcast.13), custom_call_target="tpu_custom_call" | custom-call | flops 1024 | bytes 1024 | tf_op jit(solution)/shard_map/dense_counts/pallas_call | solution.py:192
  25.4 1.7 %statistics_2.1 = (bf16[528,256]{1,0:T(8,128)(2,1)S(1)}, f32[512,1024]{1,0:T(8,128)S(1)}) custom-call(bf16[512,256]{1,0:T(8,128)(2,1)S(1)} %collective-permute-done.5.refs_0_, bf16[512,256]{1,0:T(8,128)(2,1)S(1)} %collective-permute-done.6.refs_1_, bf16[528,256]{1,0:T(8,128)(2,1)S(1)} %get-tuple-element.25.refs_2_.refs_7_.exp_ref, ...), custom_call_target="tpu_custom_call" | custom-call | flops 1024 | bytes 1024 | tf_op jit(solution)/shard_map/statistics_2/pallas_call | solution.py:290
  27.0 1.7 %statistics_1.1 = (bf16[528,256]{1,0:T(8,128)(2,1)S(1)}, f32[512,1024]{1,0:T(8,128)S(1)}) custom-call(bf16[512,256]{1,0:T(8,128)(2,1)S(1)} %collective-permute-done.3.refs_0_, bf16[512,256]{1,0:T(8,128)(2,1)S(1)} %collective-permute-done.4.refs_1_, bf16[528,256]{1,0:T(8,128)(2,1)S(1)} %get-tuple-element.25.refs_2_.refs_7_.exp_ref, ...), custom_call_target="tpu_custom_call" | custom-call | flops 1024 | bytes 1024 | tf_op jit(solution)/shard_map/statistics_1/pallas_call | solution.py:290
  28.7 1.0 %collective-permute-start.8 = (bf16[528,256]{1,0:T(8,128)(2,1)S(1)}, bf16[528,256]{1,0:T(8,128)(2,1)S(1)}, u32[]{:S(2)}, u32[]{:S(2)}) collective-permute-start(bf16[528,256]{1,0:T(8,128)(2,1)S(1)} %get-tuple-element.31), channel_id=1, source_target_pairs={{0,4},{4,0},{8,12},{12,8},{1,5},{5,1},{9,13},{13,9},{2,6},{6,2},{1... | collective-permute-start | bytes 811016 | tf_op jit(solution)/shard_map/ppermute | solution.py:401
  29.7 2.0 %collective-permute-start.7 = (bf16[528,256]{1,0:T(8,128)(2,1)S(1)}, bf16[528,256]{1,0:T(8,128)(2,1)S(1)}, u32[]{:S(2)}, u32[]{:S(2)}) collective-permute-start(bf16[528,256]{1,0:T(8,128)(2,1)S(1)} %get-tuple-element.30), channel_id=1, source_target_pairs={{0,8},{4,12},{8,0},{12,4},{1,9},{5,13},{9,1},{13,5},{2,10},{6,14},... | collective-permute-start | bytes 811016 | tf_op jit(solution)/shard_map/ppermute | solution.py:401
  31.7 1.7 %statistics_0.1 = (f32[256,256]{1,0:T(8,128)S(1)}, f32[256,256]{1,0:T(8,128)S(1)}, f32[512,1024]{1,0:T(8,128)S(1)}) custom-call(bf16[512,256]{1,0:T(8,128)(2,1)S(1)} %get-tuple-element.23.refs_0_, bf16[784,256]{1,0:T(8,128)(2,1)S(1)} %collective-permute-done.refs_4_.refs_1_, bf16[528,256]{1,0:T(8,128)(2,1)S(1)} %get-tuple-element.25.refs_2_.refs_7_.exp_ref, ...), custom_call_target="tpu_custom_call" | custom-call | flops 1024 | bytes 1024 | tf_op jit(solution)/shard_map/statistics_0/pallas_call | solution.py:290
  33.4 1.7 %statistics_3.1 = (bf16[272,256]{1,0:T(8,128)(2,1)S(1)}, bf16[256,256]{1,0:T(8,128)(2,1)S(1)}, f32[256,512]{1,0:T(8,128)S(1)}, bf16[256,512]{1,0:T(8,128)(2,1)S(...) custom-call(bf16[512,256]{1,0:T(8,128)(2,1)S(1)} %collective-permute-done.10.refs_0_, ...), custom_call_target="tpu_custom_call" | custom-call | flops 1024 | bytes 1024 | tf_op jit(solution)/shard_map/statistics_3/pallas_call | solution.py:290
  35.0 0.6 collective-permute-start.14
  35.6 0.5 collective-permute-start.15
  36.1 0.9 %collective-permute-start.16 = (bf16[256,512]{1,0:T(8,128)(2,1)S(1)}, bf16[256,512]{1,0:T(8,128)(2,1)S(1)}, u32[]{:S(2)}, u32[]{:S(2)}) collective-permute-start(bf16[256,512]{1,0:T(8,128)(2,1)S(1)} %get-tuple-element.40), channel_id=1, source_target_pairs={{0,3},{1,2},{2,1},{3,0},{4,7},{5,6},{6,5},{7,4},{8,11},{9,10},{10,... | collective-permute-start | bytes 786440 | tf_op jit(solution)/shard_map/ppermute | solution.py:405
  37.0 6.1 %collective-permute-done.8.refs_4_ = bf16[528,256]{1,0:T(8,128)(2,1)S(1)} collective-permute-done((bf16[528,256]{1,0:T(8,128)(2,1)S(1)}, bf16[528,256]{1,0:T(8,128)(2,1)S(1)}, u32[]{:S(2)}, u32[]{:S(2)}) %collective-permute-start.8) | collective-permute-done | bytes 270368 | tf_op jit(solution)/shard_map/ppermute | solution.py:401
  43.3 2.7 %collective-permute-start.13 = (bf16[256,256]{1,0:T(8,128)(2,1)S(1)}, bf16[256,256]{1,0:T(8,128)(2,1)S(1)}, u32[]{:S(2)}, u32[]{:S(2)}) collective-permute-start(bf16[256,256]{1,0:T(8,128)(2,1)S(1)} %get-tuple-element.34), channel_id=1, source_target_pairs={{0,13},{1,12},{4,9},{5,8},{8,5},{9,4},{12,1},{13,0},{2,15},{3,14},... | collective-permute-start | bytes 393224 | tf_op jit(solution)/shard_map/ppermute | solution.py:405
  46.0 5.3 %collective-permute-done.13.refs_6_ = bf16[256,256]{1,0:T(8,128)(2,1)S(1)} collective-permute-done((bf16[256,256]{1,0:T(8,128)(2,1)S(1)}, bf16[256,256]{1,0:T(8,128)(2,1)S(1)}, u32[]{:S(2)}, u32[]{:S(2)}) %collective-permute-start.13) | collective-permute-done | bytes 131104 | tf_op jit(solution)/shard_map/ppermute | solution.py:405
  51.3 5.1 %collective-permute-start.9 = (bf16[256,256]{1,0:T(8,128)(2,1)S(1)}, bf16[256,256]{1,0:T(8,128)(2,1)S(1)}, u32[]{:S(2)}, u32[]{:S(2)}) collective-permute-start(bf16[256,256]{1,0:T(8,128)(2,1)S(1)} %add_convert_fusion), channel_id=1, source_target_pairs={{0,1},{1,0},{2,3},{3,2},{4,5},{5,4},{6,7},{7,6},{8,9},{9,8},{10,11... | collective-permute-start | bytes 393224 | tf_op jit(solution)/shard_map/ppermute | solution.py:424
  56.4 1.0 %collective-permute-done.9.refs_2_ = bf16[256,256]{1,0:T(8,128)(2,1)S(1)} collective-permute-done((bf16[256,256]{1,0:T(8,128)(2,1)S(1)}, bf16[256,256]{1,0:T(8,128)(2,1)S(1)}, u32[]{:S(2)}, u32[]{:S(2)}) %collective-permute-start.9) | collective-permute-done | bytes 131104 | tf_op jit(solution)/shard_map/ppermute | solution.py:424
  57.4 1.4 %finish_users.1 = (f32[512,256]{1,0:T(8,128)}, f32[512,256]{1,0:T(8,128)}, f32[512,256]{1,0:T(8,128)}) custom-call(bf16[512,256]{1,0:T(8,128)(2,1)S(1)} %get-tuple-element.23.refs_0_, f32[256,256]{1,0:T(8,128)S(1)} %get-tuple-element.28.refs_1_, bf16[256,256]{1,0:T(8,128)(2,1)S(1)} %collective-permute-done.9.refs_2_, ...), custom_call_target="tpu_custom_call" | custom-call | flops 1024 | bytes 1024 | tf_op jit(solution)/shard_map/finish_users/pallas_call | solution.py:355
  58.9 1.0 %finish_items.1 = f32[512,256]{1,0:T(8,128)} custom-call(bf16[528,256]{1,0:T(8,128)(2,1)S(1)} %get-tuple-element.25.refs_2_.refs_7_.exp_ref, f32[256,512]{1,0:T(8,128)S(1)} %get-tuple-element.37.own_ref, bf16[256,512]{1,0:T(8,128)(2,1)S(1)} %collective-permute-done.14.refs_0_, bf16[256,512]{1,0:T(8,128)(2,1)S(1)} %collective-permute-done.15.refs_1_, ...), custom_call_target="tpu_custom_call" | custom-call | flops 1024 | bytes 1024 | tf_op jit(solution)/shard_map/finish_items/pallas_call | solution.py:387
  (23 shorter events, 0.7 us)
Async XLA Ops:
  3.4 17.9 %collective-permute-start.1 = (bf16[528,256]{1,0:T(8,128)(2,1)S(1)}, bf16[528,256]{1,0:T(8,128)(2,1)S(1)}, u32[]{:S(2)}, u32[]{:S(2)}) collective-permute-start(bf16[528,256]{1,0:T(8,128)(2,1)S(1)} %get-tuple-element.25.refs_2_.refs_7_.exp_ref), channel_id=1, source_target_pairs={{0,2},{2,0},{1,3},{3,1},{4,6},{6,4},{5,7},{7,5},{8,10},{10,8},{9,1... | collective-permute-start | bytes 811016 | tf_op jit(solution)/shard_map/ppermute | solution.py:401
  6.4 14.4 %collective-permute-start.5 = (bf16[512,256]{1,0:T(8,128)(2,1)S(1)}, bf16[512,256]{1,0:T(8,128)(2,1)S(1)}, u32[]{:S(2)}, u32[]{:S(2)}) collective-permute-start(bf16[512,256]{1,0:T(8,128)(2,1)S(1)} %get-tuple-element.23.refs_0_), channel_id=1, source_target_pairs={{0,8},{4,12},{8,0},{12,4},{1,9},{5,13},{9,1},{13,5},{2,10},{6,14},... | collective-permute-start | bytes 786440 | tf_op jit(solution)/shard_map/ppermute | solution.py:401
  9.0 12.0 %collective-permute-start.3 = (bf16[512,256]{1,0:T(8,128)(2,1)S(1)}, bf16[512,256]{1,0:T(8,128)(2,1)S(1)}, u32[]{:S(2)}, u32[]{:S(2)}) collective-permute-start(bf16[512,256]{1,0:T(8,128)(2,1)S(1)} %get-tuple-element.23.refs_0_), channel_id=1, source_target_pairs={{0,4},{4,0},{8,12},{12,8},{1,5},{5,1},{9,13},{13,9},{2,6},{6,2},{1... | collective-permute-start | bytes 786440 | tf_op jit(solution)/shard_map/ppermute | solution.py:401
  10.6 14.8 %collective-permute-start = (bf16[784,256]{1,0:T(8,128)(2,1)S(1)}, bf16[784,256]{1,0:T(8,128)(2,1)S(1)}, u32[]{:S(2)}, u32[]{:S(2)}) collective-permute-start(bf16[784,256]{1,0:T(8,128)(2,1)S(1)} %get-tuple-element.24), channel_id=1, source_target_pairs={{0,1},{1,0},{2,3},{3,2},{4,5},{5,4},{6,7},{7,6},{8,9},{9,8},{10,11... | collective-permute-start | bytes 1204232 | tf_op jit(solution)/shard_map/ppermute | solution.py:424
  10.6 14.8 %collective-permute-start.2 = (bf16[528,256]{1,0:T(8,128)(2,1)S(1)}, bf16[528,256]{1,0:T(8,128)(2,1)S(1)}, u32[]{:S(2)}, u32[]{:S(2)}) collective-permute-start(bf16[528,256]{1,0:T(8,128)(2,1)S(1)} %get-tuple-element.25.refs_2_.refs_7_.exp_ref), channel_id=1, source_target_pairs={{0,3},{1,2},{2,1},{3,0},{4,7},{5,6},{6,5},{7,4},{8,11},{9,10},{10,... | collective-permute-start | bytes 811016 | tf_op jit(solution)/shard_map/ppermute | solution.py:405
  20.8 4.6 %collective-permute-start.6 = (bf16[512,256]{1,0:T(8,128)(2,1)S(1)}, bf16[512,256]{1,0:T(8,128)(2,1)S(1)}, u32[]{:S(2)}, u32[]{:S(2)}) collective-permute-start(bf16[512,256]{1,0:T(8,128)(2,1)S(1)} %collective-permute-done.5.refs_0_), channel_id=1, source_target_pairs={{0,1},{1,0},{2,3},{3,2},{4,5},{5,4},{6,7},{7,6},{8,9},{9,8},{10,11... | collective-permute-start | bytes 786440 | tf_op jit(solution)/shard_map/ppermute | solution.py:424
  21.0 6.0 %collective-permute-start.4 = (bf16[512,256]{1,0:T(8,128)(2,1)S(1)}, bf16[512,256]{1,0:T(8,128)(2,1)S(1)}, u32[]{:S(2)}, u32[]{:S(2)}) collective-permute-start(bf16[512,256]{1,0:T(8,128)(2,1)S(1)} %collective-permute-done.3.refs_0_), channel_id=1, source_target_pairs={{0,1},{1,0},{2,3},{3,2},{4,5},{5,4},{6,7},{7,6},{8,9},{9,8},{10,11... | collective-permute-start | bytes 786440 | tf_op jit(solution)/shard_map/ppermute | solution.py:424
  21.3 10.4 %collective-permute-start.10 = (bf16[512,256]{1,0:T(8,128)(2,1)S(1)}, bf16[512,256]{1,0:T(8,128)(2,1)S(1)}, u32[]{:S(2)}, u32[]{:S(2)}) collective-permute-start(bf16[512,256]{1,0:T(8,128)(2,1)S(1)} %collective-permute-done.5.refs_0_), channel_id=1, source_target_pairs={{0,4},{4,0},{8,12},{12,8},{1,5},{5,1},{9,13},{13,9},{2,6},{6,2},{1... | collective-permute-start | bytes 786440 | tf_op jit(solution)/shard_map/ppermute | solution.py:401
  28.7 14.5 %collective-permute-start.8 = (bf16[528,256]{1,0:T(8,128)(2,1)S(1)}, bf16[528,256]{1,0:T(8,128)(2,1)S(1)}, u32[]{:S(2)}, u32[]{:S(2)}) collective-permute-start(bf16[528,256]{1,0:T(8,128)(2,1)S(1)} %get-tuple-element.31), channel_id=1, source_target_pairs={{0,4},{4,0},{8,12},{12,8},{1,5},{5,1},{9,13},{13,9},{2,6},{6,2},{1... | collective-permute-start | bytes 811016 | tf_op jit(solution)/shard_map/ppermute | solution.py:401
  29.7 13.6 %collective-permute-start.7 = (bf16[528,256]{1,0:T(8,128)(2,1)S(1)}, bf16[528,256]{1,0:T(8,128)(2,1)S(1)}, u32[]{:S(2)}, u32[]{:S(2)}) collective-permute-start(bf16[528,256]{1,0:T(8,128)(2,1)S(1)} %get-tuple-element.30), channel_id=1, source_target_pairs={{0,8},{4,12},{8,0},{12,4},{1,9},{5,13},{9,1},{13,5},{2,10},{6,14},... | collective-permute-start | bytes 811016 | tf_op jit(solution)/shard_map/ppermute | solution.py:401
  31.7 1.7 %collective-permute-start.11 = (bf16[512,256]{1,0:T(8,128)(2,1)S(1)}, bf16[512,256]{1,0:T(8,128)(2,1)S(1)}, u32[]{:S(2)}, u32[]{:S(2)}) collective-permute-start(bf16[512,256]{1,0:T(8,128)(2,1)S(1)} %collective-permute-done.10.refs_0_), channel_id=1, source_target_pairs={{0,1},{1,0},{2,3},{3,2},{4,5},{5,4},{6,7},{7,6},{8,9},{9,8},{10,11... | collective-permute-start | bytes 786440 | tf_op jit(solution)/shard_map/ppermute | solution.py:424
  33.3 24.1 %copy-start = (f32[1,512]{1,0:T(1,128)S(1)}, f32[1,512]{1,0:T(1,128)}, u32[]{:S(2)}) copy-start(f32[1,512]{1,0:T(1,128)} %refs_9_.1) | copy-start | bytes 6148
  33.4 24.0 %copy-start.1 = (f32[1,512]{1,0:T(1,128)S(1)}, f32[1,512]{1,0:T(1,128)}, u32[]{:S(2)}) copy-start(f32[1,512]{1,0:T(1,128)} %refs_10_.1) | copy-start | bytes 6148
  35.0 23.8 %collective-permute-start.14 = (bf16[256,512]{1,0:T(8,128)(2,1)S(1)}, bf16[256,512]{1,0:T(8,128)(2,1)S(1)}, u32[]{:S(2)}, u32[]{:S(2)}) collective-permute-start(bf16[256,512]{1,0:T(8,128)(2,1)S(1)} %get-tuple-element.38), channel_id=1, source_target_pairs={{0,1},{1,0},{2,3},{3,2},{4,5},{5,4},{6,7},{7,6},{8,9},{9,8},{10,11... | collective-permute-start | bytes 786440 | tf_op jit(solution)/shard_map/ppermute | solution.py:424
  35.6 23.3 %collective-permute-start.15 = (bf16[256,512]{1,0:T(8,128)(2,1)S(1)}, bf16[256,512]{1,0:T(8,128)(2,1)S(1)}, u32[]{:S(2)}, u32[]{:S(2)}) collective-permute-start(bf16[256,512]{1,0:T(8,128)(2,1)S(1)} %get-tuple-element.39), channel_id=1, source_target_pairs={{0,2},{2,0},{1,3},{3,1},{4,6},{6,4},{5,7},{7,5},{8,10},{10,8},{9,1... | collective-permute-start | bytes 786440 | tf_op jit(solution)/shard_map/ppermute | solution.py:401
  36.1 22.7 %collective-permute-start.16 = (bf16[256,512]{1,0:T(8,128)(2,1)S(1)}, bf16[256,512]{1,0:T(8,128)(2,1)S(1)}, u32[]{:S(2)}, u32[]{:S(2)}) collective-permute-start(bf16[256,512]{1,0:T(8,128)(2,1)S(1)} %get-tuple-element.40), channel_id=1, source_target_pairs={{0,3},{1,2},{2,1},{3,0},{4,7},{5,6},{6,5},{7,4},{8,11},{9,10},{10,... | collective-permute-start | bytes 786440 | tf_op jit(solution)/shard_map/ppermute | solution.py:405
  43.2 13.2 %collective-permute-start.12 = (bf16[272,256]{1,0:T(8,128)(2,1)S(1)}, bf16[272,256]{1,0:T(8,128)(2,1)S(1)}, u32[]{:S(2)}, u32[]{:S(2)}) collective-permute-start(bf16[272,256]{1,0:T(8,128)(2,1)S(1)} %get-tuple-element.33), channel_id=1, source_target_pairs={{0,12},{4,8},{8,4},{12,0},{1,13},{5,9},{9,5},{13,1},{2,14},{6,10},... | collective-permute-start | bytes 417800 | tf_op jit(solution)/shard_map/ppermute | solution.py:401
  43.3 8.0 %collective-permute-start.13 = (bf16[256,256]{1,0:T(8,128)(2,1)S(1)}, bf16[256,256]{1,0:T(8,128)(2,1)S(1)}, u32[]{:S(2)}, u32[]{:S(2)}) collective-permute-start(bf16[256,256]{1,0:T(8,128)(2,1)S(1)} %get-tuple-element.34), channel_id=1, source_target_pairs={{0,13},{1,12},{4,9},{5,8},{8,5},{9,4},{12,1},{13,0},{2,15},{3,14},... | collective-permute-start | bytes 393224 | tf_op jit(solution)/shard_map/ppermute | solution.py:405
  51.3 6.1 %collective-permute-start.9 = (bf16[256,256]{1,0:T(8,128)(2,1)S(1)}, bf16[256,256]{1,0:T(8,128)(2,1)S(1)}, u32[]{:S(2)}, u32[]{:S(2)}) collective-permute-start(bf16[256,256]{1,0:T(8,128)(2,1)S(1)} %add_convert_fusion), channel_id=1, source_target_pairs={{0,1},{1,0},{2,3},{3,2},{4,5},{5,4},{6,7},{7,6},{8,9},{9,8},{10,11... | collective-permute-start | bytes 393224 | tf_op jit(solution)/shard_map/ppermute | solution.py:424

commit v4 on v3

--- a/solution.py
+++ b/solution.py
@@ -217,9 +217,8 @@
     item_other = take(pieces)
     (counts_ref,) = take(1)
     (acc_in,) = take(1) if has_acc else (None,)
-    joined_out = at != 0 and not last
-    stat_refs = take(1 if joined_out else 2)
-    acc_refs = take(2 * pieces if last else 1)
+    stat_refs = take(1 if at else 2)
+    acc_refs = take(1 + pieces if last else 1)
     cols = mine.shape[1]
     total_mine = None
     total_other = None
@@ -243,19 +242,19 @@
                 update = lax.dot_general(factors, ratio, DIMS_TN, preferred_element_type=F32)
                 if has_acc:
                     update += acc_in[i * cols : (i + 1) * cols, columns]
-                if last:
-                    target = acc_refs[i * pieces + p]
-                    target[:, c * width : (c + 1) * width] = update.astype(target.dtype)
+                if last and i == 0:
+                    acc_refs[0][:, columns] = update
+                elif last:
+                    acc_refs[1 + p][:, c * width : (c + 1) * width] = update.astype(BF16)
                 else:
                     acc_refs[0][i * cols : (i + 1) * cols, columns] = update
-    if joined_out:
-        stat_refs[0][:half, :] = total_mine.astype(stat_refs[0].dtype)
-        stat_refs[0][half : 2 * half, :] = total_other.astype(stat_refs[0].dtype)
+    if at:
+        stat_refs[0][:half, :] = total_mine.astype(BF16)
+        stat_refs[0][half : 2 * half, :] = total_other.astype(BF16)
+        stat_refs[0][2 * half :, :] = encode(row_totals(item_mine))
     else:
-        stat_refs[0][:half, :] = total_mine.astype(stat_refs[0].dtype)
-        stat_refs[1][...] = total_other.astype(stat_refs[1].dtype)
-    if at != 0:
-        stat_refs[0][-EXTRA:, :] = encode(row_totals(item_mine))
+        stat_refs[0][...] = total_mine
+        stat_refs[1][...] = total_other
 
 
 def row_totals(item_refs):
@@ -272,18 +271,14 @@
     args = [*users, *item_mine, *item_other, dense]
     if acc is not None:
         args.append(acc)
-    if at and not last:
+    if at:
         out_shape = [jax.ShapeDtypeStruct((2 * half_rows + EXTRA, half), BF16)]
-    elif at:
-        out_shape = [jax.ShapeDtypeStruct((half_rows + e, half), BF16) for e in (EXTRA, 0)]
     else:
         out_shape = [jax.ShapeDtypeStruct((half_rows, half), F32)] * 2
     n_stats = len(out_shape)
     if last:
-        pieces = len(item_mine)
-        out_shape += [
-            jax.ShapeDtypeStruct((half, item_rows // pieces), BF16 if i else F32) for i in range(2 * pieces)
-        ]
+        out_shape.append(jax.ShapeDtypeStruct((half, item_rows), F32))
+        out_shape += [jax.ShapeDtypeStruct((half, item_rows // len(item_mine)), BF16) for _ in item_mine]
     else:
         out_shape.append(jax.ShapeDtypeStruct((2 * half, item_rows), F32))
     spec = pl.BlockSpec(memory_space=VMEM)
@@ -299,12 +294,29 @@
     return list(out[:n_stats]), list(out[n_stats:])
 
 
+def merge_items_kernel(p, mine_ref, came_ref, out_ref):
+    width = out_ref.shape[1]
+    out_ref[...] = (mine_ref[:, p * width : (p + 1) * width] + came_ref[...].astype(F32)).astype(BF16)
+
+
+def merge_items(p, mine, came):
+    return pl.pallas_call(
+        functools.partial(merge_items_kernel, p),
+        in_specs=[pl.BlockSpec(memory_space=VMEM)] * 2,
+        out_specs=pl.BlockSpec(memory_space=VMEM),
+        out_shape=jax.ShapeDtypeStruct(came.shape, BF16),
+        compiler_params=pltpu.CompilerParams(vmem_limit_bytes=2 * MIB),
+        cost_estimate=CHEAP,
+        name="merge_items",
+    )(mine, came)
+
+
 def finish_users_kernel(n_joined, pieces, *refs):
     refs = list(refs)
     take = lambda n: [refs.pop(0) for _ in range(n)]
     both_ref, own_ref, sum_ref = take(3)
     joined = take(n_joined)
-    same_ref, cross_ref = take(2)
+    (last_ref,) = take(1)
     item_refs = take(pieces)
     activity_ref, popularity_ref = take(2)
     outs = take(3)
@@ -317,20 +329,19 @@
     total = own_ref[...]
     for ref in joined:
         total += ref[:half, :].astype(F32)
-    total += same_ref[:half, :].astype(F32)
     start = pl.multiple_of(core * half, half)
     bufs[0][pl.ds(start, half), :] = 0.3 + both_ref[:half, :].astype(F32) * total
     copies.append(pltpu.make_async_copy(bufs[0].at[pl.ds(start, half)], outs[0].at[pl.ds(start, half)], sems.at[0]))
     copies[-1].start()
 
-    total = sum_ref[...].astype(F32) + cross_ref[...].astype(F32)
+    total = sum_ref[...].astype(F32) + last_ref[...].astype(F32)
     start = pl.multiple_of((1 - core) * half, half)
     bufs[0][pl.ds(start, half), :] = 0.3 + both_ref[half:, :].astype(F32) * total
     copies.append(pltpu.make_async_copy(bufs[0].at[pl.ds(start, half)], outs[0].at[pl.ds(start, half)], sems.at[1]))
     copies[-1].start()
 
     theta_total, beta_total = row_totals(item_refs)
-    for ref in joined + [same_ref]:
+    for ref in joined:
         came = decode(ref[-EXTRA:, :])
         theta_total += came[0]
         beta_total += came[1]
@@ -344,9 +355,9 @@
         copy.wait()
 
 
-def finish_users(both, own, other_sum, joined, same, cross, items, activity, popularity):
+def finish_users(both, own, other_sum, joined, other_last, items, activity, popularity):
     rows, half = both.shape
-    args = [both, own, other_sum, *joined, same, cross, *items, activity, popularity]
+    args = [both, own, other_sum, *joined, other_last, *items, activity, popularity]
     out_shape = [
         jax.ShapeDtypeStruct((rows, half), F32),
         jax.ShapeDtypeStruct((activity.shape[1], half), F32),
@@ -383,7 +394,7 @@
 
 
 def finish_items(item_exp, own, came):
-    half, rows = own.shape
+    half, rows = came[0].shape
     return pl.pallas_call(
         functools.partial(finish_items_kernel, len(came)),
         in_specs=[pl.BlockSpec(memory_space=VMEM)] * (2 + len(came)),
@@ -394,6 +405,10 @@
         cost_estimate=CHEAP,
         name="finish_items",
     )(item_exp, own, *came)
+
+
+def after(x, y):
+    return lax.optimization_barrier((x, y))[0]
 
 
 def move(x, axis, n, n_ka, distance, cross):
@@ -427,23 +442,9 @@
         return move(x, "item", n_item, n_ka, distance, cross)
 
     both, item_exp, pack = expected(theta_shape[0], theta_rate[0], beta_shape[0], beta_rate[0])
-    came_pack = sibling(pack)
     rows = both.shape[0]
     half_rows = rows // 2
     item_rows = beta_shape.shape[1] * n_user
-
-    shards = [both]
-    for k in range(1, n_item):
-        low = k & -k
-        shards.append(along_item(shards[k ^ low], low, False))
-    users = [[both, came_pack]] + [[x, sibling(x)] for x in shards[1:]]
-
-    item_mine = [item_exp]
-    item_other = [came_pack]
-    for p in range(1, n_user):
-        item_mine.append(move(item_exp, "user", n_user, n_ka, p, False))
-        item_other.append(move(item_exp, "user", n_user, n_ka, p, True))
-
     dense = dense_counts(
         counts[0, 0],
         tile_user[0, 0],
@@ -454,33 +455,50 @@
         item_rows,
         n_user,
     )
+    pack, dense = lax.optimization_barrier((pack, dense))
+    came_pack = sibling(pack)
+
+    shards = [both]
+    for k in range(1, n_item):
+        low = k & -k
+        shards.append(along_item(shards[k ^ low], low, False))
+    users = [[both, came_pack]] + [[x, sibling(x)] for x in shards[1:-1]]
+
+    item_mine = [item_exp]
+    for p in range(1, n_user):
+        low = p & -p
+        item_mine.append(move(item_mine[p ^ low], "user", n_user, n_ka, low, False))
+    item_other = [came_pack] + [sibling(x) for x in item_mine[1:]]
 
     order = sorted(range(1, n_item - 1), key=lambda k: (k & (k - 1) != 0, -k if k & (k - 1) == 0 else k))
     acc = None
     joined = []
     for k in order + [0, n_item - 1]:
         last = k == n_item - 1
+        if last:
+            users.append([shards[-1], sibling(after(shards[-1], latest))])
         stats, accs = statistics(k, users[k], item_mine, item_other, dense, acc, last, half_rows)
         acc = accs[0]
         if k == 0:
             own, own_other = stats
-        elif not last:
+        else:
             joined.append(along_item(stats[0], k, False))
-        else:
-            same = along_item(stats[0], k, False)
-            cross = along_item(stats[1], k, True)
-    came = [sibling(accs[n_user])]
+            if k == order[0]:
+                latest = stats[0]
+
+    came = [sibling(accs[1])]
     for p in range(1, n_user):
-        came.append(move(accs[p], "user", n_user, n_ka, p, False))
-        came.append(move(accs[n_user + p], "user", n_user, n_ka, p, True))
+        came.append(move(merge_items(p, acc, sibling(accs[1 + p])), "user", n_user, n_ka, p, False))
+    new_beta_shape = finish_items(item_exp, acc, came)
+
     other_sum = own_other
-    for x in joined:
-        other_sum = other_sum + x[half_rows : 2 * half_rows].astype(F32)
+    for x in joined[:-1]:
+        other_sum = lax.optimization_barrier(other_sum + x[half_rows:rows].astype(F32))
     other_sum = sibling(other_sum.astype(BF16))
-
-    new_beta_shape = finish_items(item_exp, accs[0], came)
+    other_last = sibling(after(joined[-1], other_sum)[half_rows:rows])
+    other_last = after(other_last, new_beta_shape)
     new_theta_shape, new_theta_rate, new_beta_rate = finish_users(
-        both, own, other_sum, joined, same, cross, item_mine, user_activity, item_popularity
+        both, own, other_sum, joined, other_last, item_mine, user_activity, item_popularity
     )
     return (new_theta_shape[None], new_theta_rate[None], new_beta_shape[None], new_beta_rate[None])
 

time: 60 us -> 64.5 us (1.075)
  waiting for transfers between devices: 22.2 us -> 35.9 us
  starting transfers between devices: 22.1 us -> 12.7 us
    ppermute x8, waiting for transfers between devices: 15.9 us -> 35.2 us  [move(): return lax.ppermute(x, axis, [(i, i ^ distance) for i in range(n)])]
    ppermute x3 -> x0, waiting for transfers between devices: 5.28 us -> none  [move(): return lax.ppermute(x, (axis, 'ka'), pairs)]
    ppermute x6 -> x9, starting transfers between devices: 6.04 us -> 1.04 us  [sibling(): return lax.ppermute(x, 'ka', [(h, n_ka - 1 - h) for h in range(n_ka)])]
    ppermute x3 -> x0, starting transfers between devices: 4.21 us -> none  [move(): return lax.ppermute(x, (axis, 'ka'), pairs)]
  transfers between devices with their start and end apart: 17 -> 17, of which waited for: 5 -> 7; matrix products, arithmetic and copies ran while one was open for 0% -> 0% of each run, Pallas kernels for 17% -> 15%
where the time goes in v4:
time: 64.5 us; the launch traced here: 64.2 us
  waiting for transfers between devices  35.9 us (56%)
  Pallas kernels  14.1 us (22%)
  starting transfers between devices  12.7 us (20%)
  between operations  1.45 us (2%)
    ppermute x8, waiting for transfers between devices, move(): return lax.ppermute(x, axis, [(i, i ^ distance) for i in range(n)])  35.2 us
    ppermute x8, starting transfers between devices, move(): return lax.ppermute(x, axis, [(i, i ^ distance) for i in range(n)])  11.6 us
    pallas_call x4, Pallas kernels, statistics(): pl.pallas_call(functools.partial(stat_kernel, len(item_mine), half_rows,...  6.64 us
    pallas_call x1, Pallas kernels, expected(): pl.pallas_call(functools.partial(expected_kernel, chunk_u, chunk_i), in_s...  2.76 us
    pallas_call x1, Pallas kernels, dense_counts(): pl.pallas_call(functools.partial(dense_kernel, item_rows // n_user // til...  2.24 us
    pallas_call x1, Pallas kernels, finish_users(): pl.pallas_call(functools.partial(finish_users_kernel, len(joined), len(it...  1.44 us
  transfers between devices with their start and end apart: 17, of which 7 were waited for; matrix products, arithmetic and copies ran while one was open for 0% of the time, Pallas kernels for 15%

profile of v4, /device:TPU:0, one launch (start us, length us, event | category | flops | bytes accessed | tf_op | source)
XLA Modules:
  0.0 64.2 jit_solution(10976033505997675967)
XLA Ops:
  0.6 2.8 %expected.1 = (bf16[512,256]{1,0:T(8,128)(2,1)S(1)}, bf16[528,256]{1,0:T(8,128)(2,1)S(1)}, bf16[784,256]{1,0:T(8,128)(2,1)S(1)}) custom-call(f32[512,256]{1,0:T(8,128)} %bitcast.14, f32[512,256]{1,0:T(8,128)} %bitcast.15, f32[512,256]{1,0:T(8,128)} %bitcast.16, f32[512,256]{1,0:T(8,128)} %bitcast.17), custom_call_target="tpu_custom_call" | custom-call | flops 1024 | bytes 1024 | tf_op jit(solution)/shard_map/expected/pallas_call | solution.py:120
  3.4 3.0 %collective-permute-start.1 = (bf16[528,256]{1,0:T(8,128)(2,1)S(1)}, bf16[528,256]{1,0:T(8,128)(2,1)S(1)}, u32[]{:S(2)}, u32[]{:S(2)}) collective-permute-start(bf16[528,256]{1,0:T(8,128)(2,1)S(1)} %get-tuple-element.29.refs_2_.exp_ref.refs_7_), channel_id=1, source_target_pairs={{0,2},{2,0},{1,3},{3,1},{4,6},{6,4},{5,7},{7,5},{8,10},{10,8},{9,1... | collective-permute-start | bytes 811016 | tf_op jit(solution)/shard_map/ppermute | solution.py:416
  6.4 2.6 %collective-permute-start.5 = (bf16[512,256]{1,0:T(8,128)(2,1)S(1)}, bf16[512,256]{1,0:T(8,128)(2,1)S(1)}, u32[]{:S(2)}, u32[]{:S(2)}) collective-permute-start(bf16[512,256]{1,0:T(8,128)(2,1)S(1)} %get-tuple-element.26.refs_0_), channel_id=1, source_target_pairs={{0,8},{4,12},{8,0},{12,4},{1,9},{5,13},{9,1},{13,5},{2,10},{6,14},... | collective-permute-start | bytes 786440 | tf_op jit(solution)/shard_map/ppermute | solution.py:416
  9.6 2.2 %dense_counts.1.refs_6_ = bf16[1024,1024]{1,0:T(8,128)(2,1)S(1)} custom-call(s32[64]{0:T(128)} %bitcast.19, s32[64]{0:T(128)} %bitcast.20, s32[1]{0:T(128)} %bitcast.12.live_ref, s32[64,128,128]{2,1,0:T(8,128)} %bitcast.13), custom_call_target="tpu_custom_call" | custom-call | flops 1024 | bytes 1024 | tf_op jit(solution)/shard_map/dense_counts/pallas_call | solution.py:192
  12.0 1.6 %collective-permute-start.3 = (bf16[512,256]{1,0:T(8,128)(2,1)S(1)}, bf16[512,256]{1,0:T(8,128)(2,1)S(1)}, u32[]{:S(2)}, u32[]{:S(2)}) collective-permute-start(bf16[512,256]{1,0:T(8,128)(2,1)S(1)} %get-tuple-element.26.refs_0_), channel_id=1, source_target_pairs={{0,4},{4,0},{8,12},{12,8},{1,5},{5,1},{9,13},{13,9},{2,6},{6,2},{1... | collective-permute-start | bytes 786440 | tf_op jit(solution)/shard_map/ppermute | solution.py:416
  13.8 7.0 %collective-permute-done.5.refs_0_ = bf16[512,256]{1,0:T(8,128)(2,1)S(1)} collective-permute-done((bf16[512,256]{1,0:T(8,128)(2,1)S(1)}, bf16[512,256]{1,0:T(8,128)(2,1)S(1)}, u32[]{:S(2)}, u32[]{:S(2)}) %collective-permute-start.5) | collective-permute-done | bytes 262176 | tf_op jit(solution)/shard_map/ppermute | solution.py:416
  20.8 0.6 collective-permute-start.10
  21.4 4.0 %collective-permute-done.3.refs_0_ = bf16[512,256]{1,0:T(8,128)(2,1)S(1)} collective-permute-done((bf16[512,256]{1,0:T(8,128)(2,1)S(1)}, bf16[512,256]{1,0:T(8,128)(2,1)S(1)}, u32[]{:S(2)}, u32[]{:S(2)}) %collective-permute-start.3) | collective-permute-done | bytes 262176 | tf_op jit(solution)/shard_map/ppermute | solution.py:416
  25.4 1.7 %statistics_2.1 = (bf16[528,256]{1,0:T(8,128)(2,1)S(1)}, f32[512,1024]{1,0:T(8,128)S(1)}) custom-call(bf16[512,256]{1,0:T(8,128)(2,1)S(1)} %collective-permute-done.5.refs_0_, bf16[512,256]{1,0:T(8,128)(2,1)S(1)} %collective-permute-done.6.refs_1_, bf16[528,256]{1,0:T(8,128)(2,1)S(1)} %get-tuple-element.29.refs_2_.exp_ref.refs_7_, ...), custom_call_target="tpu_custom_call" | custom-call | flops 1024 | bytes 1024 | tf_op jit(solution)/shard_map/statistics_2/pallas_call | solution.py:285
  27.1 0.4 collective-permute-start.7
  27.5 3.3 %collective-permute-done.10.refs_0_ = bf16[512,256]{1,0:T(8,128)(2,1)S(1)} collective-permute-done((bf16[512,256]{1,0:T(8,128)(2,1)S(1)}, bf16[512,256]{1,0:T(8,128)(2,1)S(1)}, u32[]{:S(2)}, u32[]{:S(2)}) %collective-permute-start.10) | collective-permute-done | bytes 262176 | tf_op jit(solution)/shard_map/ppermute | solution.py:416
  30.8 1.7 %statistics_1.1 = (bf16[528,256]{1,0:T(8,128)(2,1)S(1)}, f32[512,1024]{1,0:T(8,128)S(1)}) custom-call(bf16[512,256]{1,0:T(8,128)(2,1)S(1)} %collective-permute-done.3.refs_0_, bf16[512,256]{1,0:T(8,128)(2,1)S(1)} %collective-permute-done.4.refs_1_, bf16[528,256]{1,0:T(8,128)(2,1)S(1)} %get-tuple-element.29.refs_2_.exp_ref.refs_7_, ...), custom_call_target="tpu_custom_call" | custom-call | flops 1024 | bytes 1024 | tf_op jit(solution)/shard_map/statistics_1/pallas_call | solution.py:285
  32.5 1.7 %statistics_0.1 = (f32[256,256]{1,0:T(8,128)S(1)}, f32[256,256]{1,0:T(8,128)S(1)}, f32[512,1024]{1,0:T(8,128)S(1)}) custom-call(bf16[512,256]{1,0:T(8,128)(2,1)S(1)} %get-tuple-element.26.refs_0_, bf16[784,256]{1,0:T(8,128)(2,1)S(1)} %collective-permute-done.refs_4_.refs_1_, bf16[528,256]{1,0:T(8,128)(2,1)S(1)} %get-tuple-element.29.refs_2_.exp_ref.refs_7_, ...), custom_call_target="tpu_custom_call" | custom-call | flops 1024 | bytes 1024 | tf_op jit(solution)/shard_map/statistics_0/pallas_call | solution.py:285
  34.2 1.7 %statistics_3.1 = (bf16[528,256]{1,0:T(8,128)(2,1)S(1)}, f32[256,1024]{1,0:T(8,128)S(1)}, bf16[256,512]{1,0:T(8,128)(2,1)S(1)}, bf16[256,512]{1,0:T(8,128)(2,1)S(1)}) custom-call(bf16[512,256]{1,0:T(8,128)(2,1)S(1)} %collective-permute-done.10.refs_0_, bf16[512,256]{1,0:T(8,128)(2,1)S(1)} %collective-permute-done.11.refs_1_, ...), custom_call_target="tpu_custom_call" | custom-call | flops 1024 | bytes 1024 | tf_op jit(solution)/shard_map/statistics_3/pallas_call | solution.py:285
  35.9 2.7 %collective-permute-start.12 = (bf16[528,256]{1,0:T(8,128)(2,1)S(1)}, bf16[528,256]{1,0:T(8,128)(2,1)S(1)}, u32[]{:S(2)}, u32[]{:S(2)}) collective-permute-start(bf16[528,256]{1,0:T(8,128)(2,1)S(1)} %get-tuple-element.39), channel_id=1, source_target_pairs={{0,12},{4,8},{8,4},{12,0},{1,13},{5,9},{9,5},{13,1},{2,14},{6,10},... | collective-permute-start | bytes 811016 | tf_op jit(solution)/shard_map/ppermute | solution.py:416
  38.6 0.5 collective-permute-start.15
  39.1 4.1 %collective-permute-done.7.refs_3_ = bf16[528,256]{1,0:T(8,128)(2,1)S(1)} collective-permute-done((bf16[528,256]{1,0:T(8,128)(2,1)S(1)}, bf16[528,256]{1,0:T(8,128)(2,1)S(1)}, u32[]{:S(2)}, u32[]{:S(2)}) %collective-permute-start.7) | collective-permute-done | bytes 270368 | tf_op jit(solution)/shard_map/ppermute | solution.py:416
  43.2 9.6 %collective-permute-done.8.refs_4_ = bf16[528,256]{1,0:T(8,128)(2,1)S(1)} collective-permute-done((bf16[528,256]{1,0:T(8,128)(2,1)S(1)}, bf16[528,256]{1,0:T(8,128)(2,1)S(1)}, u32[]{:S(2)}, u32[]{:S(2)}) %collective-permute-start.8) | collective-permute-done | bytes 270368 | tf_op jit(solution)/shard_map/ppermute | solution.py:416
  53.0 0.6 collective-permute-start.16
  53.5 0.7 %collective-permute-done.9.refs_2_ = bf16[256,256]{1,0:T(8,128)(2,1)S(1)} collective-permute-done((bf16[256,256]{1,0:T(8,128)(2,1)S(1)}, bf16[256,256]{1,0:T(8,128)(2,1)S(1)}, u32[]{:S(2)}, u32[]{:S(2)}) %collective-permute-start.9) | collective-permute-done | bytes 131104 | tf_op jit(solution)/shard_map/ppermute | solution.py:439
  54.2 0.2 collective-permute-start.13
  54.4 7.3 %collective-permute-done.16.refs_1_ = bf16[256,512]{1,0:T(8,128)(2,1)S(1)} collective-permute-done((bf16[256,512]{1,0:T(8,128)(2,1)S(1)}, bf16[256,512]{1,0:T(8,128)(2,1)S(1)}, u32[]{:S(2)}, u32[]{:S(2)}) %collective-permute-start.16) | collective-permute-done | bytes 262176 | tf_op jit(solution)/shard_map/ppermute | solution.py:416
  61.7 1.0 %finish_items.1 = f32[512,256]{1,0:T(8,128)} custom-call(bf16[528,256]{1,0:T(8,128)(2,1)S(1)} %get-tuple-element.29.refs_2_.exp_ref.refs_7_, f32[256,1024]{1,0:T(8,128)S(1)} %get-tuple-element.41.mine_ref.own_ref, bf16[256,512]{1,0:T(8,128)(2,1)S(1)} %collective-permute-done.14.refs_0_, bf16[256,512]{1,0:T(8,128)(2,1)S(1)} %collective-permute-done.16.refs_1_), custom_call_target="tpu_custom_call" | custom-call | flops 1024 | bytes 1024 | tf_op jit(solution)/shard_map/finish_items/pallas_call | solution.py:398
  62.7 1.4 %finish_users.1 = (f32[512,256]{1,0:T(8,128)}, f32[512,256]{1,0:T(8,128)}, f32[512,256]{1,0:T(8,128)}) custom-call(bf16[512,256]{1,0:T(8,128)(2,1)S(1)} %get-tuple-element.26.refs_0_, f32[256,256]{1,0:T(8,128)S(1)} %get-tuple-element.33.refs_1_, bf16[256,256]{1,0:T(8,128)(2,1)S(1)} %collective-permute-done.9.refs_2_, ...), custom_call_target="tpu_custom_call" | custom-call | flops 1024 | bytes 1024 | tf_op jit(solution)/shard_map/finish_users/pallas_call | solution.py:366
  (26 shorter events, 0.6 us)
Async XLA Ops:
  3.4 10.2 %collective-permute-start.1 = (bf16[528,256]{1,0:T(8,128)(2,1)S(1)}, bf16[528,256]{1,0:T(8,128)(2,1)S(1)}, u32[]{:S(2)}, u32[]{:S(2)}) collective-permute-start(bf16[528,256]{1,0:T(8,128)(2,1)S(1)} %get-tuple-element.29.refs_2_.exp_ref.refs_7_), channel_id=1, source_target_pairs={{0,2},{2,0},{1,3},{3,1},{4,6},{6,4},{5,7},{7,5},{8,10},{10,8},{9,1... | collective-permute-start | bytes 811016 | tf_op jit(solution)/shard_map/ppermute | solution.py:416
  6.4 14.4 %collective-permute-start.5 = (bf16[512,256]{1,0:T(8,128)(2,1)S(1)}, bf16[512,256]{1,0:T(8,128)(2,1)S(1)}, u32[]{:S(2)}, u32[]{:S(2)}) collective-permute-start(bf16[512,256]{1,0:T(8,128)(2,1)S(1)} %get-tuple-element.26.refs_0_), channel_id=1, source_target_pairs={{0,8},{4,12},{8,0},{12,4},{1,9},{5,13},{9,1},{13,5},{2,10},{6,14},... | collective-permute-start | bytes 786440 | tf_op jit(solution)/shard_map/ppermute | solution.py:416
  11.9 13.5 %collective-permute-start = (bf16[784,256]{1,0:T(8,128)(2,1)S(1)}, bf16[784,256]{1,0:T(8,128)(2,1)S(1)}, u32[]{:S(2)}, u32[]{:S(2)}) collective-permute-start(bf16[784,256]{1,0:T(8,128)(2,1)S(1)} %get-tuple-element.28), channel_id=1, source_target_pairs={{0,1},{1,0},{2,3},{3,2},{4,5},{5,4},{6,7},{7,6},{8,9},{9,8},{10,11... | collective-permute-start | bytes 1204232 | tf_op jit(solution)/shard_map/ppermute | solution.py:439
  12.0 13.5 %collective-permute-start.3 = (bf16[512,256]{1,0:T(8,128)(2,1)S(1)}, bf16[512,256]{1,0:T(8,128)(2,1)S(1)}, u32[]{:S(2)}, u32[]{:S(2)}) collective-permute-start(bf16[512,256]{1,0:T(8,128)(2,1)S(1)} %get-tuple-element.26.refs_0_), channel_id=1, source_target_pairs={{0,4},{4,0},{8,12},{12,8},{1,5},{5,1},{9,13},{13,9},{2,6},{6,2},{1... | collective-permute-start | bytes 786440 | tf_op jit(solution)/shard_map/ppermute | solution.py:416
  13.6 11.8 %collective-permute-start.2 = (bf16[528,256]{1,0:T(8,128)(2,1)S(1)}, bf16[528,256]{1,0:T(8,128)(2,1)S(1)}, u32[]{:S(2)}, u32[]{:S(2)}) collective-permute-start(bf16[528,256]{1,0:T(8,128)(2,1)S(1)} %collective-permute-done.1.refs_3_.refs_8_), channel_id=1, source_target_pairs={{0,1},{1,0},{2,3},{3,2},{4,5},{5,4},{6,7},{7,6},{8,9},{9,8},{10,11... | collective-permute-start | bytes 811016 | tf_op jit(solution)/shard_map/ppermute | solution.py:439
  20.8 4.6 %collective-permute-start.6 = (bf16[512,256]{1,0:T(8,128)(2,1)S(1)}, bf16[512,256]{1,0:T(8,128)(2,1)S(1)}, u32[]{:S(2)}, u32[]{:S(2)}) collective-permute-start(bf16[512,256]{1,0:T(8,128)(2,1)S(1)} %collective-permute-done.5.refs_0_), channel_id=1, source_target_pairs={{0,1},{1,0},{2,3},{3,2},{4,5},{5,4},{6,7},{7,6},{8,9},{9,8},{10,11... | collective-permute-start | bytes 786440 | tf_op jit(solution)/shard_map/ppermute | solution.py:439
  20.8 10.0 %collective-permute-start.10 = (bf16[512,256]{1,0:T(8,128)(2,1)S(1)}, bf16[512,256]{1,0:T(8,128)(2,1)S(1)}, u32[]{:S(2)}, u32[]{:S(2)}) collective-permute-start(bf16[512,256]{1,0:T(8,128)(2,1)S(1)} %collective-permute-done.5.refs_0_), channel_id=1, source_target_pairs={{0,4},{4,0},{8,12},{12,8},{1,5},{5,1},{9,13},{13,9},{2,6},{6,2},{1... | collective-permute-start | bytes 786440 | tf_op jit(solution)/shard_map/ppermute | solution.py:416
  25.4 5.4 %collective-permute-start.4 = (bf16[512,256]{1,0:T(8,128)(2,1)S(1)}, bf16[512,256]{1,0:T(8,128)(2,1)S(1)}, u32[]{:S(2)}, u32[]{:S(2)}) collective-permute-start(bf16[512,256]{1,0:T(8,128)(2,1)S(1)} %collective-permute-done.3.refs_0_), channel_id=1, source_target_pairs={{0,1},{1,0},{2,3},{3,2},{4,5},{5,4},{6,7},{7,6},{8,9},{9,8},{10,11... | collective-permute-start | bytes 786440 | tf_op jit(solution)/shard_map/ppermute | solution.py:439
  27.1 16.1 %collective-permute-start.7 = (bf16[528,256]{1,0:T(8,128)(2,1)S(1)}, bf16[528,256]{1,0:T(8,128)(2,1)S(1)}, u32[]{:S(2)}, u32[]{:S(2)}) collective-permute-start(bf16[528,256]{1,0:T(8,128)(2,1)S(1)} %get-tuple-element.35), channel_id=1, source_target_pairs={{0,8},{4,12},{8,0},{12,4},{1,9},{5,13},{9,1},{13,5},{2,10},{6,14},... | collective-permute-start | bytes 811016 | tf_op jit(solution)/shard_map/ppermute | solution.py:416
  30.8 3.4 %collective-permute-start.11 = (bf16[512,256]{1,0:T(8,128)(2,1)S(1)}, bf16[512,256]{1,0:T(8,128)(2,1)S(1)}, u32[]{:S(2)}, u32[]{:S(2)}) collective-permute-start(bf16[512,256]{1,0:T(8,128)(2,1)S(1)} %collective-permute-done.10.refs_0_), channel_id=1, source_target_pairs={{0,1},{1,0},{2,3},{3,2},{4,5},{5,4},{6,7},{7,6},{8,9},{9,8},{10,11... | collective-permute-start | bytes 786440 | tf_op jit(solution)/shard_map/ppermute | solution.py:439
  32.5 20.3 %collective-permute-start.8 = (bf16[528,256]{1,0:T(8,128)(2,1)S(1)}, bf16[528,256]{1,0:T(8,128)(2,1)S(1)}, u32[]{:S(2)}, u32[]{:S(2)}) collective-permute-start(bf16[528,256]{1,0:T(8,128)(2,1)S(1)} %get-tuple-element.36), channel_id=1, source_target_pairs={{0,4},{4,0},{8,12},{12,8},{1,5},{5,1},{9,13},{13,9},{2,6},{6,2},{1... | collective-permute-start | bytes 811016 | tf_op jit(solution)/shard_map/ppermute | solution.py:416
  35.9 18.3 %collective-permute-start.12 = (bf16[528,256]{1,0:T(8,128)(2,1)S(1)}, bf16[528,256]{1,0:T(8,128)(2,1)S(1)}, u32[]{:S(2)}, u32[]{:S(2)}) collective-permute-start(bf16[528,256]{1,0:T(8,128)(2,1)S(1)} %get-tuple-element.39), channel_id=1, source_target_pairs={{0,12},{4,8},{8,4},{12,0},{1,13},{5,9},{9,5},{13,1},{2,14},{6,10},... | collective-permute-start | bytes 811016 | tf_op jit(solution)/shard_map/ppermute | solution.py:416
  38.6 15.8 %collective-permute-start.14 = (bf16[256,512]{1,0:T(8,128)(2,1)S(1)}, bf16[256,512]{1,0:T(8,128)(2,1)S(1)}, u32[]{:S(2)}, u32[]{:S(2)}) collective-permute-start(bf16[256,512]{1,0:T(8,128)(2,1)S(1)} %get-tuple-element.42), channel_id=1, source_target_pairs={{0,1},{1,0},{2,3},{3,2},{4,5},{5,4},{6,7},{7,6},{8,9},{9,8},{10,11... | collective-permute-start | bytes 786440 | tf_op jit(solution)/shard_map/ppermute | solution.py:439
  38.6 14.3 %collective-permute-start.15 = (bf16[256,512]{1,0:T(8,128)(2,1)S(1)}, bf16[256,512]{1,0:T(8,128)(2,1)S(1)}, u32[]{:S(2)}, u32[]{:S(2)}) collective-permute-start(bf16[256,512]{1,0:T(8,128)(2,1)S(1)} %get-tuple-element.43), channel_id=1, source_target_pairs={{0,1},{1,0},{2,3},{3,2},{4,5},{5,4},{6,7},{7,6},{8,9},{9,8},{10,11... | collective-permute-start | bytes 786440 | tf_op jit(solution)/shard_map/ppermute | solution.py:439
  52.8 1.4 %collective-permute-start.9 = (bf16[256,256]{1,0:T(8,128)(2,1)S(1)}, bf16[256,256]{1,0:T(8,128)(2,1)S(1)}, u32[]{:S(2)}, u32[]{:S(2)}) collective-permute-start(bf16[256,256]{1,0:T(8,128)(2,1)S(1)} %convert_add_fusion), channel_id=1, source_target_pairs={{0,1},{1,0},{2,3},{3,2},{4,5},{5,4},{6,7},{7,6},{8,9},{9,8},{10,11... | collective-permute-start | bytes 393224 | tf_op jit(solution)/shard_map/ppermute | solution.py:439
  52.9 9.8 %copy-start = (f32[1,512]{1,0:T(1,128)S(1)}, f32[1,512]{1,0:T(1,128)}, u32[]{:S(2)}) copy-start(f32[1,512]{1,0:T(1,128)} %refs_9_.1) | copy-start | bytes 6148
  52.9 9.8 %copy-start.1 = (f32[1,512]{1,0:T(1,128)S(1)}, f32[1,512]{1,0:T(1,128)}, u32[]{:S(2)}) copy-start(f32[1,512]{1,0:T(1,128)} %refs_10_.1) | copy-start | bytes 6148
  53.0 8.7 %collective-permute-start.16 = (bf16[256,512]{1,0:T(8,128)(2,1)S(1)}, bf16[256,512]{1,0:T(8,128)(2,1)S(1)}, u32[]{:S(2)}, u32[]{:S(2)}) collective-permute-start(bf16[256,512]{1,0:T(8,128)(2,1)S(1)} %merge_items.1), channel_id=1, source_target_pairs={{0,2},{2,0},{1,3},{3,1},{4,6},{6,4},{5,7},{7,5},{8,10},{10,8},{9,1... | collective-permute-start | bytes 786440 | tf_op jit(solution)/shard_map/ppermute | solution.py:416
  54.2 8.5 %collective-permute-start.13 = (bf16[256,256]{1,0:T(8,128)(2,1)S(1)}, bf16[256,256]{1,0:T(8,128)(2,1)S(1)}, u32[]{:S(2)}, u32[]{:S(2)}) collective-permute-start(bf16[256,256]{1,0:T(8,128)(2,1)S(1)} %slice.11), channel_id=1, source_target_pairs={{0,1},{1,0},{2,3},{3,2},{4,5},{5,4},{6,7},{7,6},{8,9},{9,8},{10,11... | collective-permute-start | bytes 393224 | tf_op jit(solution)/shard_map/ppermute | solution.py:439

commit v5 on v4

--- a/solution.py
+++ b/solution.py
@@ -136,7 +136,7 @@
     )(pinned(theta), pinned(trate), pinned(beta), pinned(brate))
 
 
-def dense_kernel(shard_tiles, chunk, rows, users_in, items_in, live_ref, counts_ref, out_ref, *scratch):
+def dense_kernel(n_item, shard_tiles, chunk, rows, users_in, items_in, live_ref, counts_ref, out_ref, *scratch):
     users_ref, items_ref, buf, sems, index_sems = scratch
     tile = counts_ref.shape[1]
     half = rows // 2
@@ -174,7 +174,9 @@
 
             @pl.when(lax.div(within, half) == core)
             def _():
-                start = pl.multiple_of((shard ^ z) * half + lax.rem(within, half), piece)
+                distance = shard ^ z
+                step = jnp.where(core == 0, distance, mirrored(distance, n_item))
+                start = pl.multiple_of(step * half + lax.rem(within, half), piece)
                 value = buf[slot, j * piece : (j + 1) * piece, :].astype(F32).astype(BF16)
                 out_ref[pl.ds(start, piece), pl.ds(col, tile)] = value
 
@@ -190,7 +192,7 @@
     chunk = 8
     out_rows = n_item * rows // 2
     return pl.pallas_call(
-        functools.partial(dense_kernel, item_rows // n_user // tile, chunk, rows),
+        functools.partial(dense_kernel, n_item, item_rows // n_user // tile, chunk, rows),
         in_specs=[pl.BlockSpec(memory_space=m) for m in (HBM, HBM, SMEM, HBM)],
         out_specs=pl.BlockSpec(memory_space=VMEM),
         out_shape=jax.ShapeDtypeStruct((out_rows, item_rows), BF16),
@@ -407,17 +409,30 @@
     )(item_exp, own, *came)
 
 
+def mirrored(k, n):
+    out = k * 0
+    bit = 1
+    while bit < n:
+        out = out * 2 + (k & 1)
+        k = k >> 1
+        bit *= 2
+    return out
+
+
+def along_item(x, k, n, n_ka):
+    pairs = []
+    for i in range(n):
+        for h in range(n_ka):
+            pairs.append((i * n_ka + h, (i ^ (mirrored(k, n) if h else k)) * n_ka + h))
+    return lax.ppermute(x, ("item", "ka"), pairs)
+
+
 def after(x, y):
     return lax.optimization_barrier((x, y))[0]
 
 
-def move(x, axis, n, n_ka, distance, cross):
-    if not cross:
-        return lax.ppermute(x, axis, [(i, i ^ distance) for i in range(n)])
-    pairs = [
-        (i * n_ka + h, (i ^ distance) * n_ka + (n_ka - 1 - h)) for i in range(n) for h in range(n_ka)
-    ]
-    return lax.ppermute(x, (axis, "ka"), pairs)
+def along_user(x, distance, n):
+    return lax.ppermute(x, "user", [(i, i ^ distance) for i in range(n)])
 
 
 def body(
@@ -438,9 +453,6 @@
     def sibling(x):
         return lax.ppermute(x, "ka", [(h, n_ka - 1 - h) for h in range(n_ka)])
 
-    def along_item(x, distance, cross):
-        return move(x, "item", n_item, n_ka, distance, cross)
-
     both, item_exp, pack = expected(theta_shape[0], theta_rate[0], beta_shape[0], beta_rate[0])
     rows = both.shape[0]
     half_rows = rows // 2
@@ -461,40 +473,44 @@
     shards = [both]
     for k in range(1, n_item):
         low = k & -k
-        shards.append(along_item(shards[k ^ low], low, False))
-    users = [[both, came_pack]] + [[x, sibling(x)] for x in shards[1:-1]]
+        shards.append(along_item(shards[k ^ low], low, n_item, n_ka))
 
     item_mine = [item_exp]
     for p in range(1, n_user):
         low = p & -p
-        item_mine.append(move(item_mine[p ^ low], "user", n_user, n_ka, low, False))
+        item_mine.append(along_user(item_mine[p ^ low], low, n_user))
     item_other = [came_pack] + [sibling(x) for x in item_mine[1:]]
 
-    order = sorted(range(1, n_item - 1), key=lambda k: (k & (k - 1) != 0, -k if k & (k - 1) == 0 else k))
+    order = sorted(range(1, n_item - 1), key=lambda k: (k & (k - 1) != 0, k)) + [0, n_item - 1]
     acc = None
     joined = []
-    for k in order + [0, n_item - 1]:
+    latest = None
+    for k in order:
         last = k == n_item - 1
-        if last:
-            users.append([shards[-1], sibling(after(shards[-1], latest))])
-        stats, accs = statistics(k, users[k], item_mine, item_other, dense, acc, last, half_rows)
+        if k == 0:
+            other = came_pack
+        else:
+            passed = shards[mirrored(k, n_item)]
+            other = sibling(after(passed, latest) if last else passed)
+        stats, accs = statistics(k, [shards[k], other], item_mine, item_other, dense, acc, last, half_rows)
         acc = accs[0]
         if k == 0:
             own, own_other = stats
         else:
-            joined.append(along_item(stats[0], k, False))
-            if k == order[0]:
-                latest = stats[0]
+            joined.append(along_item(stats[0], k, n_item, n_ka))
+            latest = stats[0] if latest is None else latest
 
     came = [sibling(accs[1])]
     for p in range(1, n_user):
-        came.append(move(merge_items(p, acc, sibling(accs[1 + p])), "user", n_user, n_ka, p, False))
+        sent = merge_items(p, acc, sibling(accs[1 + p]))
+        came.append(along_user(sent, p, n_user))
     new_beta_shape = finish_items(item_exp, acc, came)
 
     other_sum = own_other
     for x in joined[:-1]:
         other_sum = lax.optimization_barrier(other_sum + x[half_rows:rows].astype(F32))
-    other_sum = sibling(other_sum.astype(BF16))
+    other_sum = other_sum.astype(BF16)
+    other_sum = sibling(other_sum)
     other_last = sibling(after(joined[-1], other_sum)[half_rows:rows])
     other_last = after(other_last, new_beta_shape)
     new_theta_shape, new_theta_rate, new_beta_rate = finish_users(

time: 64.5 us -> 63.7 us (0.988)
  the two profiles are of different devices: /device:TPU:0 before, /device:TPU:24 now
where the time goes in v5:
time: 63.7 us; the launch traced here: 63.5 us
  waiting for transfers between devices  40.6 us (64%)
  Pallas kernels  14.1 us (22%)
  starting transfers between devices  7.3 us (11%)
  between operations  1.44 us (2%)
    ppermute x6, waiting for transfers between devices, along_item(): return lax.ppermute(x, ('item', 'ka'), pairs)  29.2 us
    ppermute x2, waiting for transfers between devices, along_user(): return lax.ppermute(x, 'user', [(i, i ^ distance) for i in range(n)])  9.74 us
    pallas_call x4, Pallas kernels, statistics(): pl.pallas_call(functools.partial(stat_kernel, len(item_mine), half_rows,...  6.64 us
    ppermute x6, starting transfers between devices, along_item(): return lax.ppermute(x, ('item', 'ka'), pairs)  3.77 us
    pallas_call x1, Pallas kernels, expected(): pl.pallas_call(functools.partial(expected_kernel, chunk_u, chunk_i), in_s...  2.76 us
    pallas_call x1, Pallas kernels, dense_counts(): pl.pallas_call(functools.partial(dense_kernel, n_item, item_rows // n_use...  2.24 us
    ppermute x2, starting transfers between devices, along_user(): return lax.ppermute(x, 'user', [(i, i ^ distance) for i in range(n)])  2.16 us
    ppermute x9, waiting for transfers between devices, sibling(): return lax.ppermute(x, 'ka', [(h, n_ka - 1 - h) for h in range(n_ka)])  1.66 us
  transfers between devices with their start and end apart: 17, of which 7 were waited for; matrix products, arithmetic and copies ran while one was open for 0% of the time, Pallas kernels for 16%

profile of v5, /device:TPU:24, one launch (start us, length us, event | category | flops | bytes accessed | tf_op | source)
XLA Modules:
  0.0 63.5 jit_solution(14849715693629517087)
XLA Ops:
  0.6 2.8 %expected.1 = (bf16[512,256]{1,0:T(8,128)(2,1)S(1)}, bf16[528,256]{1,0:T(8,128)(2,1)S(1)}, bf16[784,256]{1,0:T(8,128)(2,1)S(1)}) custom-call(f32[512,256]{1,0:T(8,128)} %bitcast.14, f32[512,256]{1,0:T(8,128)} %bitcast.15, f32[512,256]{1,0:T(8,128)} %bitcast.16, f32[512,256]{1,0:T(8,128)} %bitcast.17), custom_call_target="tpu_custom_call" | custom-call | flops 1024 | bytes 1024 | tf_op jit(solution)/shard_map/expected/pallas_call | solution.py:120
  3.4 1.6 %collective-permute-start.1 = (bf16[528,256]{1,0:T(8,128)(2,1)S(1)}, bf16[528,256]{1,0:T(8,128)(2,1)S(1)}, u32[]{:S(2)}, u32[]{:S(2)}) collective-permute-start(bf16[528,256]{1,0:T(8,128)(2,1)S(1)} %get-tuple-element.29.refs_2_.exp_ref.refs_7_), channel_id=1, source_target_pairs={{0,2},{2,0},{1,3},{3,1},{4,6},{6,4},{5,7},{7,5},{8,10},{10,8},{9,1... | collective-permute-start | bytes 811016 | tf_op jit(solution)/shard_map/ppermute | solution.py:435
  5.0 0.3 collective-permute-start.3
  5.9 2.2 %dense_counts.1.refs_6_ = bf16[1024,1024]{1,0:T(8,128)(2,1)S(1)} custom-call(s32[64]{0:T(128)} %bitcast.19, s32[64]{0:T(128)} %bitcast.20, s32[1]{0:T(128)} %bitcast.12.live_ref, s32[64,128,128]{2,1,0:T(8,128)} %bitcast.13), custom_call_target="tpu_custom_call" | custom-call | flops 1024 | bytes 1024 | tf_op jit(solution)/shard_map/dense_counts/pallas_call | solution.py:194
  8.3 1.0 %collective-permute-start.4 = (bf16[512,256]{1,0:T(8,128)(2,1)S(1)}, bf16[512,256]{1,0:T(8,128)(2,1)S(1)}, u32[]{:S(2)}, u32[]{:S(2)}) collective-permute-start(bf16[512,256]{1,0:T(8,128)(2,1)S(1)} %get-tuple-element.26.refs_0_), channel_id=1, source_target_pairs={{0,4},{1,9},{4,0},{5,13},{8,12},{9,1},{12,8},{13,5},{2,6},{3,11},{... | collective-permute-start | bytes 786440 | tf_op jit(solution)/shard_map/ppermute | solution.py:427
  9.2 2.5 %collective-permute-done.1.refs_3_.refs_8_ = bf16[528,256]{1,0:T(8,128)(2,1)S(1)} collective-permute-done((bf16[528,256]{1,0:T(8,128)(2,1)S(1)}, bf16[528,256]{1,0:T(8,128)(2,1)S(1)}, u32[]{:S(2)}, u32[]{:S(2)}) %collective-permute-start.1) | collective-permute-done | bytes 270368 | tf_op jit(solution)/shard_map/ppermute | solution.py:435
  11.7 11.3 %collective-permute-done.3.refs_0_ = bf16[512,256]{1,0:T(8,128)(2,1)S(1)} collective-permute-done((bf16[512,256]{1,0:T(8,128)(2,1)S(1)}, bf16[512,256]{1,0:T(8,128)(2,1)S(1)}, u32[]{:S(2)}, u32[]{:S(2)}) %collective-permute-start.3) | collective-permute-done | bytes 262176 | tf_op jit(solution)/shard_map/ppermute | solution.py:427
  23.0 0.5 collective-permute-start.5
  23.5 1.0 %collective-permute-done.6.refs_1_ = bf16[512,256]{1,0:T(8,128)(2,1)S(1)} collective-permute-done((bf16[512,256]{1,0:T(8,128)(2,1)S(1)}, bf16[512,256]{1,0:T(8,128)(2,1)S(1)}, u32[]{:S(2)}, u32[]{:S(2)}) %collective-permute-start.6) | collective-permute-done | bytes 262176 | tf_op jit(solution)/shard_map/ppermute | solution.py:454
  24.5 1.7 %statistics_1.1 = (bf16[528,256]{1,0:T(8,128)(2,1)S(1)}, f32[512,1024]{1,0:T(8,128)S(1)}) custom-call(bf16[512,256]{1,0:T(8,128)(2,1)S(1)} %collective-permute-done.4.refs_0_, bf16[512,256]{1,0:T(8,128)(2,1)S(1)} %collective-permute-done.6.refs_1_, bf16[528,256]{1,0:T(8,128)(2,1)S(1)} %get-tuple-element.29.refs_2_.exp_ref.refs_7_, ...), custom_call_target="tpu_custom_call" | custom-call | flops 1024 | bytes 1024 | tf_op jit(solution)/shard_map/statistics_1/pallas_call | solution.py:287
  26.2 0.6 collective-permute-start.7
  26.8 7.4 %collective-permute-done.10.refs_0_ = bf16[512,256]{1,0:T(8,128)(2,1)S(1)} collective-permute-done((bf16[512,256]{1,0:T(8,128)(2,1)S(1)}, bf16[512,256]{1,0:T(8,128)(2,1)S(1)}, u32[]{:S(2)}, u32[]{:S(2)}) %collective-permute-start.10) | collective-permute-done | bytes 262176 | tf_op jit(solution)/shard_map/ppermute | solution.py:427
  34.1 1.7 %statistics_2.1 = (bf16[528,256]{1,0:T(8,128)(2,1)S(1)}, f32[512,1024]{1,0:T(8,128)S(1)}) custom-call(bf16[512,256]{1,0:T(8,128)(2,1)S(1)} %collective-permute-done.3.refs_0_, bf16[512,256]{1,0:T(8,128)(2,1)S(1)} %collective-permute-done.5.refs_1_, bf16[528,256]{1,0:T(8,128)(2,1)S(1)} %get-tuple-element.29.refs_2_.exp_ref.refs_7_, ...), custom_call_target="tpu_custom_call" | custom-call | flops 1024 | bytes 1024 | tf_op jit(solution)/shard_map/statistics_2/pallas_call | solution.py:287
  35.9 1.7 %statistics_0.1 = (f32[256,256]{1,0:T(8,128)S(1)}, f32[256,256]{1,0:T(8,128)S(1)}, f32[512,1024]{1,0:T(8,128)S(1)}) custom-call(bf16[512,256]{1,0:T(8,128)(2,1)S(1)} %get-tuple-element.26.refs_0_, bf16[784,256]{1,0:T(8,128)(2,1)S(1)} %collective-permute-done.refs_4_.refs_1_, bf16[528,256]{1,0:T(8,128)(2,1)S(1)} %get-tuple-element.29.refs_2_.exp_ref.refs_7_, ...), custom_call_target="tpu_custom_call" | custom-call | flops 1024 | bytes 1024 | tf_op jit(solution)/shard_map/statistics_0/pallas_call | solution.py:287
  37.6 1.7 %statistics_3.1 = (bf16[528,256]{1,0:T(8,128)(2,1)S(1)}, f32[256,1024]{1,0:T(8,128)S(1)}, bf16[256,512]{1,0:T(8,128)(2,1)S(1)}, bf16[256,512]{1,0:T(8,128)(2,1)S(1)}) custom-call(bf16[512,256]{1,0:T(8,128)(2,1)S(1)} %collective-permute-done.10.refs_0_, bf16[512,256]{1,0:T(8,128)(2,1)S(1)} %collective-permute-done.11.refs_1_, ...), custom_call_target="tpu_custom_call" | custom-call | flops 1024 | bytes 1024 | tf_op jit(solution)/shard_map/statistics_3/pallas_call | solution.py:287
  39.2 1.8 %collective-permute-start.12 = (bf16[528,256]{1,0:T(8,128)(2,1)S(1)}, bf16[528,256]{1,0:T(8,128)(2,1)S(1)}, u32[]{:S(2)}, u32[]{:S(2)}) collective-permute-start(bf16[528,256]{1,0:T(8,128)(2,1)S(1)} %get-tuple-element.39), channel_id=1, source_target_pairs={{0,12},{1,13},{4,8},{5,9},{8,4},{9,5},{12,0},{13,1},{2,14},{3,15},... | collective-permute-start | bytes 811016 | tf_op jit(solution)/shard_map/ppermute | solution.py:427
  41.0 0.5 collective-permute-start.15
  41.6 10.6 %collective-permute-done.8.refs_4_ = bf16[528,256]{1,0:T(8,128)(2,1)S(1)} collective-permute-done((bf16[528,256]{1,0:T(8,128)(2,1)S(1)}, bf16[528,256]{1,0:T(8,128)(2,1)S(1)}, u32[]{:S(2)}, u32[]{:S(2)}) %collective-permute-start.8) | collective-permute-done | bytes 270368 | tf_op jit(solution)/shard_map/ppermute | solution.py:427
  52.4 0.6 collective-permute-start.16
  53.0 0.6 collective-permute-done.9.refs_2_
  53.6 0.2 collective-permute-start.13
  53.8 7.3 %collective-permute-done.16.refs_1_ = bf16[256,512]{1,0:T(8,128)(2,1)S(1)} collective-permute-done((bf16[256,512]{1,0:T(8,128)(2,1)S(1)}, bf16[256,512]{1,0:T(8,128)(2,1)S(1)}, u32[]{:S(2)}, u32[]{:S(2)}) %collective-permute-start.16) | collective-permute-done | bytes 262176 | tf_op jit(solution)/shard_map/ppermute | solution.py:435
  61.1 1.0 %finish_items.1 = f32[512,256]{1,0:T(8,128)} custom-call(bf16[528,256]{1,0:T(8,128)(2,1)S(1)} %get-tuple-element.29.refs_2_.exp_ref.refs_7_, f32[256,1024]{1,0:T(8,128)S(1)} %get-tuple-element.41.mine_ref.own_ref, bf16[256,512]{1,0:T(8,128)(2,1)S(1)} %collective-permute-done.14.refs_0_, bf16[256,512]{1,0:T(8,128)(2,1)S(1)} %collective-permute-done.16.refs_1_), custom_call_target="tpu_custom_call" | custom-call | flops 1024 | bytes 1024 | tf_op jit(solution)/shard_map/finish_items/pallas_call | solution.py:400
  62.1 1.4 %finish_users.1 = (f32[512,256]{1,0:T(8,128)}, f32[512,256]{1,0:T(8,128)}, f32[512,256]{1,0:T(8,128)}) custom-call(bf16[512,256]{1,0:T(8,128)(2,1)S(1)} %get-tuple-element.26.refs_0_, f32[256,256]{1,0:T(8,128)S(1)} %get-tuple-element.33.refs_1_, bf16[256,256]{1,0:T(8,128)(2,1)S(1)} %collective-permute-done.9.refs_2_, ...), custom_call_target="tpu_custom_call" | custom-call | flops 1024 | bytes 1024 | tf_op jit(solution)/shard_map/finish_users/pallas_call | solution.py:368
  (26 shorter events, 0.4 us)
Async XLA Ops:
  3.4 8.3 %collective-permute-start.1 = (bf16[528,256]{1,0:T(8,128)(2,1)S(1)}, bf16[528,256]{1,0:T(8,128)(2,1)S(1)}, u32[]{:S(2)}, u32[]{:S(2)}) collective-permute-start(bf16[528,256]{1,0:T(8,128)(2,1)S(1)} %get-tuple-element.29.refs_2_.exp_ref.refs_7_), channel_id=1, source_target_pairs={{0,2},{2,0},{1,3},{3,1},{4,6},{6,4},{5,7},{7,5},{8,10},{10,8},{9,1... | collective-permute-start | bytes 811016 | tf_op jit(solution)/shard_map/ppermute | solution.py:435
  5.0 18.0 %collective-permute-start.3 = (bf16[512,256]{1,0:T(8,128)(2,1)S(1)}, bf16[512,256]{1,0:T(8,128)(2,1)S(1)}, u32[]{:S(2)}, u32[]{:S(2)}) collective-permute-start(bf16[512,256]{1,0:T(8,128)(2,1)S(1)} %get-tuple-element.26.refs_0_), channel_id=1, source_target_pairs={{0,8},{1,5},{4,12},{5,1},{8,0},{9,13},{12,4},{13,9},{2,10},{3,7},{... | collective-permute-start | bytes 786440 | tf_op jit(solution)/shard_map/ppermute | solution.py:427
  8.2 15.3 %collective-permute-start = (bf16[784,256]{1,0:T(8,128)(2,1)S(1)}, bf16[784,256]{1,0:T(8,128)(2,1)S(1)}, u32[]{:S(2)}, u32[]{:S(2)}) collective-permute-start(bf16[784,256]{1,0:T(8,128)(2,1)S(1)} %get-tuple-element.28), channel_id=1, source_target_pairs={{0,1},{1,0},{2,3},{3,2},{4,5},{5,4},{6,7},{7,6},{8,9},{9,8},{10,11... | collective-permute-start | bytes 1204232 | tf_op jit(solution)/shard_map/ppermute | solution.py:454
  8.3 14.7 %collective-permute-start.4 = (bf16[512,256]{1,0:T(8,128)(2,1)S(1)}, bf16[512,256]{1,0:T(8,128)(2,1)S(1)}, u32[]{:S(2)}, u32[]{:S(2)}) collective-permute-start(bf16[512,256]{1,0:T(8,128)(2,1)S(1)} %get-tuple-element.26.refs_0_), channel_id=1, source_target_pairs={{0,4},{1,9},{4,0},{5,13},{8,12},{9,1},{12,8},{13,5},{2,6},{3,11},{... | collective-permute-start | bytes 786440 | tf_op jit(solution)/shard_map/ppermute | solution.py:427
  11.7 12.8 %collective-permute-start.2 = (bf16[528,256]{1,0:T(8,128)(2,1)S(1)}, bf16[528,256]{1,0:T(8,128)(2,1)S(1)}, u32[]{:S(2)}, u32[]{:S(2)}) collective-permute-start(bf16[528,256]{1,0:T(8,128)(2,1)S(1)} %collective-permute-done.1.refs_3_.refs_8_), channel_id=1, source_target_pairs={{0,1},{1,0},{2,3},{3,2},{4,5},{5,4},{6,7},{7,6},{8,9},{9,8},{10,11... | collective-permute-start | bytes 811016 | tf_op jit(solution)/shard_map/ppermute | solution.py:454
  23.0 1.5 %collective-permute-start.6 = (bf16[512,256]{1,0:T(8,128)(2,1)S(1)}, bf16[512,256]{1,0:T(8,128)(2,1)S(1)}, u32[]{:S(2)}, u32[]{:S(2)}) collective-permute-start(bf16[512,256]{1,0:T(8,128)(2,1)S(1)} %collective-permute-done.3.refs_0_), channel_id=1, source_target_pairs={{0,1},{1,0},{2,3},{3,2},{4,5},{5,4},{6,7},{7,6},{8,9},{9,8},{10,11... | collective-permute-start | bytes 786440 | tf_op jit(solution)/shard_map/ppermute | solution.py:454
  23.0 11.2 %collective-permute-start.10 = (bf16[512,256]{1,0:T(8,128)(2,1)S(1)}, bf16[512,256]{1,0:T(8,128)(2,1)S(1)}, u32[]{:S(2)}, u32[]{:S(2)}) collective-permute-start(bf16[512,256]{1,0:T(8,128)(2,1)S(1)} %collective-permute-done.3.refs_0_), channel_id=1, source_target_pairs={{0,4},{1,9},{4,0},{5,13},{8,12},{9,1},{12,8},{13,5},{2,6},{3,11},{... | collective-permute-start | bytes 786440 | tf_op jit(solution)/shard_map/ppermute | solution.py:427
  23.0 11.1 %collective-permute-start.5 = (bf16[512,256]{1,0:T(8,128)(2,1)S(1)}, bf16[512,256]{1,0:T(8,128)(2,1)S(1)}, u32[]{:S(2)}, u32[]{:S(2)}) collective-permute-start(bf16[512,256]{1,0:T(8,128)(2,1)S(1)} %collective-permute-done.4.refs_0_), channel_id=1, source_target_pairs={{0,1},{1,0},{2,3},{3,2},{4,5},{5,4},{6,7},{7,6},{8,9},{9,8},{10,11... | collective-permute-start | bytes 786440 | tf_op jit(solution)/shard_map/ppermute | solution.py:454
  26.2 15.4 %collective-permute-start.7 = (bf16[528,256]{1,0:T(8,128)(2,1)S(1)}, bf16[528,256]{1,0:T(8,128)(2,1)S(1)}, u32[]{:S(2)}, u32[]{:S(2)}) collective-permute-start(bf16[528,256]{1,0:T(8,128)(2,1)S(1)} %get-tuple-element.35), channel_id=1, source_target_pairs={{0,4},{1,9},{4,0},{5,13},{8,12},{9,1},{12,8},{13,5},{2,6},{3,11},{... | collective-permute-start | bytes 811016 | tf_op jit(solution)/shard_map/ppermute | solution.py:427
  34.1 3.4 %collective-permute-start.11 = (bf16[512,256]{1,0:T(8,128)(2,1)S(1)}, bf16[512,256]{1,0:T(8,128)(2,1)S(1)}, u32[]{:S(2)}, u32[]{:S(2)}) collective-permute-start(bf16[512,256]{1,0:T(8,128)(2,1)S(1)} %collective-permute-done.10.refs_0_), channel_id=1, source_target_pairs={{0,1},{1,0},{2,3},{3,2},{4,5},{5,4},{6,7},{7,6},{8,9},{9,8},{10,11... | collective-permute-start | bytes 786440 | tf_op jit(solution)/shard_map/ppermute | solution.py:454
  35.8 16.3 %collective-permute-start.8 = (bf16[528,256]{1,0:T(8,128)(2,1)S(1)}, bf16[528,256]{1,0:T(8,128)(2,1)S(1)}, u32[]{:S(2)}, u32[]{:S(2)}) collective-permute-start(bf16[528,256]{1,0:T(8,128)(2,1)S(1)} %get-tuple-element.36), channel_id=1, source_target_pairs={{0,8},{1,5},{4,12},{5,1},{8,0},{9,13},{12,4},{13,9},{2,10},{3,7},{... | collective-permute-start | bytes 811016 | tf_op jit(solution)/shard_map/ppermute | solution.py:427
  39.2 14.4 %collective-permute-start.12 = (bf16[528,256]{1,0:T(8,128)(2,1)S(1)}, bf16[528,256]{1,0:T(8,128)(2,1)S(1)}, u32[]{:S(2)}, u32[]{:S(2)}) collective-permute-start(bf16[528,256]{1,0:T(8,128)(2,1)S(1)} %get-tuple-element.39), channel_id=1, source_target_pairs={{0,12},{1,13},{4,8},{5,9},{8,4},{9,5},{12,0},{13,1},{2,14},{3,15},... | collective-permute-start | bytes 811016 | tf_op jit(solution)/shard_map/ppermute | solution.py:427
  41.0 12.8 %collective-permute-start.14 = (bf16[256,512]{1,0:T(8,128)(2,1)S(1)}, bf16[256,512]{1,0:T(8,128)(2,1)S(1)}, u32[]{:S(2)}, u32[]{:S(2)}) collective-permute-start(bf16[256,512]{1,0:T(8,128)(2,1)S(1)} %get-tuple-element.42), channel_id=1, source_target_pairs={{0,1},{1,0},{2,3},{3,2},{4,5},{5,4},{6,7},{7,6},{8,9},{9,8},{10,11... | collective-permute-start | bytes 786440 | tf_op jit(solution)/shard_map/ppermute | solution.py:454
  41.0 11.2 %collective-permute-start.15 = (bf16[256,512]{1,0:T(8,128)(2,1)S(1)}, bf16[256,512]{1,0:T(8,128)(2,1)S(1)}, u32[]{:S(2)}, u32[]{:S(2)}) collective-permute-start(bf16[256,512]{1,0:T(8,128)(2,1)S(1)} %get-tuple-element.43), channel_id=1, source_target_pairs={{0,1},{1,0},{2,3},{3,2},{4,5},{5,4},{6,7},{7,6},{8,9},{9,8},{10,11... | collective-permute-start | bytes 786440 | tf_op jit(solution)/shard_map/ppermute | solution.py:454
  52.2 1.4 %collective-permute-start.9 = (bf16[256,256]{1,0:T(8,128)(2,1)S(1)}, bf16[256,256]{1,0:T(8,128)(2,1)S(1)}, u32[]{:S(2)}, u32[]{:S(2)}) collective-permute-start(bf16[256,256]{1,0:T(8,128)(2,1)S(1)} %convert_add_fusion), channel_id=1, source_target_pairs={{0,1},{1,0},{2,3},{3,2},{4,5},{5,4},{6,7},{7,6},{8,9},{9,8},{10,11... | collective-permute-start | bytes 393224 | tf_op jit(solution)/shard_map/ppermute | solution.py:454
  52.3 9.8 %copy-start = (f32[1,512]{1,0:T(1,128)S(1)}, f32[1,512]{1,0:T(1,128)}, u32[]{:S(2)}) copy-start(f32[1,512]{1,0:T(1,128)} %refs_9_.1) | copy-start | bytes 6148
  52.3 9.8 %copy-start.1 = (f32[1,512]{1,0:T(1,128)S(1)}, f32[1,512]{1,0:T(1,128)}, u32[]{:S(2)}) copy-start(f32[1,512]{1,0:T(1,128)} %refs_10_.1) | copy-start | bytes 6148
  52.4 8.7 %collective-permute-start.16 = (bf16[256,512]{1,0:T(8,128)(2,1)S(1)}, bf16[256,512]{1,0:T(8,128)(2,1)S(1)}, u32[]{:S(2)}, u32[]{:S(2)}) collective-permute-start(bf16[256,512]{1,0:T(8,128)(2,1)S(1)} %merge_items.1), channel_id=1, source_target_pairs={{0,2},{2,0},{1,3},{3,1},{4,6},{6,4},{5,7},{7,5},{8,10},{10,8},{9,1... | collective-permute-start | bytes 786440 | tf_op jit(solution)/shard_map/ppermute | solution.py:435
  53.6 8.5 %collective-permute-start.13 = (bf16[256,256]{1,0:T(8,128)(2,1)S(1)}, bf16[256,256]{1,0:T(8,128)(2,1)S(1)}, u32[]{:S(2)}, u32[]{:S(2)}) collective-permute-start(bf16[256,256]{1,0:T(8,128)(2,1)S(1)} %slice.11), channel_id=1, source_target_pairs={{0,1},{1,0},{2,3},{3,2},{4,5},{5,4},{6,7},{7,6},{8,9},{9,8},{10,11... | collective-permute-start | bytes 393224 | tf_op jit(solution)/shard_map/ppermute | solution.py:454

commit v6 on v5

--- a/solution.py
+++ b/solution.py
@@ -174,8 +174,7 @@
 
             @pl.when(lax.div(within, half) == core)
             def _():
-                distance = shard ^ z
-                step = jnp.where(core == 0, distance, mirrored(distance, n_item))
+                step = lax.rem(z - shard + n_item, n_item)
                 start = pl.multiple_of(step * half + lax.rem(within, half), piece)
                 value = buf[slot, j * piece : (j + 1) * piece, :].astype(F32).astype(BF16)
                 out_ref[pl.ds(start, piece), pl.ds(col, tile)] = value
@@ -209,7 +208,7 @@
     )(pinned(users), pinned(items), live, pinned(counts))
 
 
-def stat_kernel(pieces, half, last, has_acc, at, *refs):
+def stat_kernel(pieces, half, last, has_sum, has_acc, at, *refs):
     refs = list(refs)
     take = lambda n: [refs.pop(0) for _ in range(n)]
     mine_ref, other_ref = take(2)
@@ -218,6 +217,7 @@
     item_mine = take(pieces)
     item_other = take(pieces)
     (counts_ref,) = take(1)
+    (sum_ref,) = take(1) if has_sum else (None,)
     (acc_in,) = take(1) if has_acc else (None,)
     stat_refs = take(1 if at else 2)
     acc_refs = take(1 + pieces if last else 1)
@@ -250,13 +250,18 @@
                     acc_refs[1 + p][:, c * width : (c + 1) * width] = update.astype(BF16)
                 else:
                     acc_refs[0][i * cols : (i + 1) * cols, columns] = update
-    if at:
-        stat_refs[0][:half, :] = total_mine.astype(BF16)
-        stat_refs[0][half : 2 * half, :] = total_other.astype(BF16)
-        stat_refs[0][2 * half :, :] = encode(row_totals(item_mine))
-    else:
+    if not at:
         stat_refs[0][...] = total_mine
         stat_refs[1][...] = total_other
+        return
+    totals = row_totals(item_mine)
+    if has_sum:
+        total_mine += sum_ref[:half, :].astype(F32)
+        total_other += sum_ref[half : 2 * half, :].astype(F32)
+        totals = [a + b for a, b in zip(totals, decode(sum_ref[2 * half :, :]))]
+    stat_refs[0][:half, :] = total_mine.astype(BF16)
+    stat_refs[0][half : 2 * half, :] = total_other.astype(BF16)
+    stat_refs[0][2 * half :, :] = encode(totals)
 
 
 def row_totals(item_refs):
@@ -267,10 +272,12 @@
     return sums
 
 
-def statistics(at, users, item_mine, item_other, dense, acc, last, half_rows):
+def statistics(at, users, item_mine, item_other, dense, running, acc, last, half_rows):
     half = users[0].shape[1]
     item_rows = dense.shape[1]
     args = [*users, *item_mine, *item_other, dense]
+    if running is not None:
+        args.append(running)
     if acc is not None:
         args.append(acc)
     if at:
@@ -285,7 +292,7 @@
         out_shape.append(jax.ShapeDtypeStruct((2 * half, item_rows), F32))
     spec = pl.BlockSpec(memory_space=VMEM)
     out = pl.pallas_call(
-        functools.partial(stat_kernel, len(item_mine), half_rows, last, acc is not None, at),
+        functools.partial(stat_kernel, len(item_mine), half_rows, last, running is not None, acc is not None, at),
         in_specs=[spec] * len(args),
         out_specs=[spec] * len(out_shape),
         out_shape=out_shape,
@@ -313,12 +320,10 @@
     )(mine, came)
 
 
-def finish_users_kernel(n_joined, pieces, *refs):
+def finish_users_kernel(pieces, *refs):
     refs = list(refs)
     take = lambda n: [refs.pop(0) for _ in range(n)]
-    both_ref, own_ref, sum_ref = take(3)
-    joined = take(n_joined)
-    (last_ref,) = take(1)
+    both_ref, own_ref, came_ref, last_ref = take(4)
     item_refs = take(pieces)
     activity_ref, popularity_ref = take(2)
     outs = take(3)
@@ -328,25 +333,22 @@
     half = own_ref.shape[0]
     copies = []
 
-    total = own_ref[...]
-    for ref in joined:
-        total += ref[:half, :].astype(F32)
+    total = own_ref[...] + came_ref[:half, :].astype(F32)
     start = pl.multiple_of(core * half, half)
     bufs[0][pl.ds(start, half), :] = 0.3 + both_ref[:half, :].astype(F32) * total
     copies.append(pltpu.make_async_copy(bufs[0].at[pl.ds(start, half)], outs[0].at[pl.ds(start, half)], sems.at[0]))
     copies[-1].start()
 
-    total = sum_ref[...].astype(F32) + last_ref[...].astype(F32)
+    total = last_ref[...].astype(F32)
     start = pl.multiple_of((1 - core) * half, half)
     bufs[0][pl.ds(start, half), :] = 0.3 + both_ref[half:, :].astype(F32) * total
     copies.append(pltpu.make_async_copy(bufs[0].at[pl.ds(start, half)], outs[0].at[pl.ds(start, half)], sems.at[1]))
     copies[-1].start()
 
     theta_total, beta_total = row_totals(item_refs)
-    for ref in joined:
-        came = decode(ref[-EXTRA:, :])
-        theta_total += came[0]
-        beta_total += came[1]
+    came = decode(came_ref[2 * half :, :])
+    theta_total += came[0]
+    beta_total += came[1]
     for i, (column_ref, total) in enumerate(((activity_ref, beta_total), (popularity_ref, theta_total))):
         rows = column_ref.shape[1]
         column = jnp.broadcast_to(column_ref[...], (total.shape[1], rows)).T
@@ -357,16 +359,16 @@
         copy.wait()
 
 
-def finish_users(both, own, other_sum, joined, other_last, items, activity, popularity):
+def finish_users(both, own, came, came_other, items, activity, popularity):
     rows, half = both.shape
-    args = [both, own, other_sum, *joined, other_last, *items, activity, popularity]
+    args = [both, own, came, came_other, *items, activity, popularity]
     out_shape = [
         jax.ShapeDtypeStruct((rows, half), F32),
         jax.ShapeDtypeStruct((activity.shape[1], half), F32),
         jax.ShapeDtypeStruct((popularity.shape[1], half), F32),
     ]
     return pl.pallas_call(
-        functools.partial(finish_users_kernel, len(joined), len(items)),
+        functools.partial(finish_users_kernel, len(items)),
         in_specs=[pl.BlockSpec(memory_space=VMEM)] * len(args),
         out_specs=[pl.BlockSpec(memory_space=HBM)] * 3,
         out_shape=out_shape,
@@ -409,22 +411,8 @@
     )(item_exp, own, *came)
 
 
-def mirrored(k, n):
-    out = k * 0
-    bit = 1
-    while bit < n:
-        out = out * 2 + (k & 1)
-        k = k >> 1
-        bit *= 2
-    return out
-
-
-def along_item(x, k, n, n_ka):
-    pairs = []
-    for i in range(n):
-        for h in range(n_ka):
-            pairs.append((i * n_ka + h, (i ^ (mirrored(k, n) if h else k)) * n_ka + h))
-    return lax.ppermute(x, ("item", "ka"), pairs)
+def around_item(x, n):
+    return lax.ppermute(x, "item", [(i, (i + 1) % n) for i in range(n)])
 
 
 def after(x, y):
@@ -471,9 +459,8 @@
     came_pack = sibling(pack)
 
     shards = [both]
-    for k in range(1, n_item):
-        low = k & -k
-        shards.append(along_item(shards[k ^ low], low, n_item, n_ka))
+    for t in range(1, n_item):
+        shards.append(around_item(shards[-1], n_item))
 
     item_mine = [item_exp]
     for p in range(1, n_user):
@@ -481,24 +468,20 @@
         item_mine.append(along_user(item_mine[p ^ low], low, n_user))
     item_other = [came_pack] + [sibling(x) for x in item_mine[1:]]
 
-    order = sorted(range(1, n_item - 1), key=lambda k: (k & (k - 1) != 0, k)) + [0, n_item - 1]
+    order = [1, 0] + list(range(2, n_item))
     acc = None
-    joined = []
-    latest = None
-    for k in order:
-        last = k == n_item - 1
-        if k == 0:
-            other = came_pack
+    running = None
+    for t in order:
+        last = t == order[-1]
+        other = sibling(shards[t]) if t else came_pack
+        users = [shards[t], other]
+        came_sum = running if t else None
+        stats, accs = statistics(t, users, item_mine, item_other, dense, came_sum, acc, last, half_rows)
+        acc = accs[0]
+        if t:
+            running = around_item(stats[0], n_item)
         else:
-            passed = shards[mirrored(k, n_item)]
-            other = sibling(after(passed, latest) if last else passed)
-        stats, accs = statistics(k, [shards[k], other], item_mine, item_other, dense, acc, last, half_rows)
-        acc = accs[0]
-        if k == 0:
             own, own_other = stats
-        else:
-            joined.append(along_item(stats[0], k, n_item, n_ka))
-            latest = stats[0] if latest is None else latest
 
     came = [sibling(accs[1])]
     for p in range(1, n_user):
@@ -506,15 +489,10 @@
         came.append(along_user(sent, p, n_user))
     new_beta_shape = finish_items(item_exp, acc, came)
 
-    other_sum = own_other
-    for x in joined[:-1]:
-        other_sum = lax.optimization_barrier(other_sum + x[half_rows:rows].astype(F32))
-    other_sum = other_sum.astype(BF16)
-    other_sum = sibling(other_sum)
-    other_last = sibling(after(joined[-1], other_sum)[half_rows:rows])
-    other_last = after(other_last, new_beta_shape)
+    came_other = sibling((own_other + running[half_rows:rows].astype(F32)).astype(BF16))
+    came_other = after(came_other, new_beta_shape)
     new_theta_shape, new_theta_rate, new_beta_rate = finish_users(
-        both, own, other_sum, joined, other_last, item_mine, user_activity, item_popularity
+        both, own, running, came_other, item_mine, user_activity, item_popularity
     )
     return (new_theta_shape[None], new_theta_rate[None], new_beta_shape[None], new_beta_rate[None])
 

time: 63.7 us -> 58.3 us (0.915)
  the two profiles are of different devices: /device:TPU:24 before, /device:TPU:0 now
where the time goes in v6:
time: 58.3 us; the launch traced here: 58.2 us
  waiting for transfers between devices  36.6 us (63%)
  Pallas kernels  14 us (24%)
  starting transfers between devices  6.08 us (10%)
  between operations  1.44 us (2%)
    ppermute x6, waiting for transfers between devices, around_item(): return lax.ppermute(x, 'item', [(i, (i + 1) % n) for i in range(n)])  29.2 us
    pallas_call x4, Pallas kernels, statistics(): pl.pallas_call(functools.partial(stat_kernel, len(item_mine), half_rows,...  6.64 us
    ppermute x8, waiting for transfers between devices, sibling(): return lax.ppermute(x, 'ka', [(h, n_ka - 1 - h) for h in range(n_ka)])  4.09 us
    ppermute x2, starting transfers between devices, along_user(): return lax.ppermute(x, 'user', [(i, i ^ distance) for i in range(n)])  3.61 us
    ppermute x2, waiting for transfers between devices, along_user(): return lax.ppermute(x, 'user', [(i, i ^ distance) for i in range(n)])  3.29 us
    pallas_call x1, Pallas kernels, expected(): pl.pallas_call(functools.partial(expected_kernel, chunk_u, chunk_i), in_s...  2.76 us
    pallas_call x1, Pallas kernels, dense_counts(): pl.pallas_call(functools.partial(dense_kernel, n_item, item_rows // n_use...  2.24 us
    ppermute x6, starting transfers between devices, around_item(): return lax.ppermute(x, 'item', [(i, (i + 1) % n) for i in range(n)])  1.76 us
  transfers between devices with their start and end apart: 16, of which 11 were waited for; matrix products, arithmetic and copies ran while one was open for 0% of the time, Pallas kernels for 14%

profile of v6, /device:TPU:0, one launch (start us, length us, event | category | flops | bytes accessed | tf_op | source)
XLA Modules:
  0.0 58.2 jit_solution(16013239873873361729)
XLA Ops:
  0.6 2.8 %expected.1 = (bf16[512,256]{1,0:T(8,128)(2,1)S(1)}, bf16[528,256]{1,0:T(8,128)(2,1)S(1)}, bf16[784,256]{1,0:T(8,128)(2,1)S(1)}) custom-call(f32[512,256]{1,0:T(8,128)} %bitcast.14, f32[512,256]{1,0:T(8,128)} %bitcast.15, f32[512,256]{1,0:T(8,128)} %bitcast.16, f32[512,256]{1,0:T(8,128)} %bitcast.17), custom_call_target="tpu_custom_call" | custom-call | flops 1024 | bytes 1024 | tf_op jit(solution)/shard_map/expected/pallas_call | solution.py:120
  3.4 3.0 %collective-permute-start.1 = (bf16[528,256]{1,0:T(8,128)(2,1)S(1)}, bf16[528,256]{1,0:T(8,128)(2,1)S(1)}, u32[]{:S(2)}, u32[]{:S(2)}) collective-permute-start(bf16[528,256]{1,0:T(8,128)(2,1)S(1)} %get-tuple-element.27.refs_2_.exp_ref.refs_4_), channel_id=1, source_target_pairs={{0,2},{2,0},{1,3},{3,1},{4,6},{6,4},{5,7},{7,5},{8,10},{10,8},{9,1... | collective-permute-start | bytes 811016 | tf_op jit(solution)/shard_map/ppermute | solution.py:423
  6.4 1.6 %collective-permute-start.3 = (bf16[512,256]{1,0:T(8,128)(2,1)S(1)}, bf16[512,256]{1,0:T(8,128)(2,1)S(1)}, u32[]{:S(2)}, u32[]{:S(2)}) collective-permute-start(bf16[512,256]{1,0:T(8,128)(2,1)S(1)} %get-tuple-element.24.refs_0_), channel_id=1, source_target_pairs={{0,4},{4,8},{8,12},{12,0},{1,5},{5,9},{9,13},{13,1},{2,6},{6,10},{... | collective-permute-start | bytes 786440 | tf_op jit(solution)/shard_map/ppermute | solution.py:415
  8.6 2.2 %dense_counts.1.refs_6_ = bf16[1024,1024]{1,0:T(8,128)(2,1)S(1)} custom-call(s32[64]{0:T(128)} %bitcast.19, s32[64]{0:T(128)} %bitcast.20, s32[1]{0:T(128)} %bitcast.12.live_ref, s32[64,128,128]{2,1,0:T(8,128)} %bitcast.13), custom_call_target="tpu_custom_call" | custom-call | flops 1024 | bytes 1024 | tf_op jit(solution)/shard_map/dense_counts/pallas_call | solution.py:193
  10.9 0.1 collective-permute-start
  11.0 1.9 %collective-permute-done.1.refs_3_.refs_5_ = bf16[528,256]{1,0:T(8,128)(2,1)S(1)} collective-permute-done((bf16[528,256]{1,0:T(8,128)(2,1)S(1)}, bf16[528,256]{1,0:T(8,128)(2,1)S(1)}, u32[]{:S(2)}, u32[]{:S(2)}) %collective-permute-start.1) | collective-permute-done | bytes 270368 | tf_op jit(solution)/shard_map/ppermute | solution.py:423
  12.9 3.1 %collective-permute-done.3.refs_0_ = bf16[512,256]{1,0:T(8,128)(2,1)S(1)} collective-permute-done((bf16[512,256]{1,0:T(8,128)(2,1)S(1)}, bf16[512,256]{1,0:T(8,128)(2,1)S(1)}, u32[]{:S(2)}, u32[]{:S(2)}) %collective-permute-start.3) | collective-permute-done | bytes 262176 | tf_op jit(solution)/shard_map/ppermute | solution.py:415
  16.0 1.5 %collective-permute-done.4.refs_1_ = bf16[512,256]{1,0:T(8,128)(2,1)S(1)} collective-permute-done((bf16[512,256]{1,0:T(8,128)(2,1)S(1)}, bf16[512,256]{1,0:T(8,128)(2,1)S(1)}, u32[]{:S(2)}, u32[]{:S(2)}) %collective-permute-start.4) | collective-permute-done | bytes 262176 | tf_op jit(solution)/shard_map/ppermute | solution.py:442
  17.6 1.7 %statistics_1.1 = (bf16[528,256]{1,0:T(8,128)(2,1)S(1)}, f32[512,1024]{1,0:T(8,128)S(1)}) custom-call(bf16[512,256]{1,0:T(8,128)(2,1)S(1)} %collective-permute-done.3.refs_0_, bf16[512,256]{1,0:T(8,128)(2,1)S(1)} %collective-permute-done.4.refs_1_, bf16[528,256]{1,0:T(8,128)(2,1)S(1)} %get-tuple-element.27.refs_2_.exp_ref.refs_4_, ...), custom_call_target="tpu_custom_call" | custom-call | flops 1024 | bytes 1024 | tf_op jit(solution)/shard_map/statistics_1/pallas_call | solution.py:294
  19.3 7.6 %collective-permute-done.5.refs_0_ = bf16[512,256]{1,0:T(8,128)(2,1)S(1)} collective-permute-done((bf16[512,256]{1,0:T(8,128)(2,1)S(1)}, bf16[512,256]{1,0:T(8,128)(2,1)S(1)}, u32[]{:S(2)}, u32[]{:S(2)}) %collective-permute-start.5) | collective-permute-done | bytes 262176 | tf_op jit(solution)/shard_map/ppermute | solution.py:415
  26.9 1.7 %statistics_0.1 = (f32[256,256]{1,0:T(8,128)S(1)}, f32[256,256]{1,0:T(8,128)S(1)}, f32[512,1024]{1,0:T(8,128)S(1)}) custom-call(bf16[512,256]{1,0:T(8,128)(2,1)S(1)} %get-tuple-element.24.refs_0_, bf16[784,256]{1,0:T(8,128)(2,1)S(1)} %collective-permute-done.refs_4_.refs_1_, bf16[528,256]{1,0:T(8,128)(2,1)S(1)} %get-tuple-element.27.refs_2_.exp_ref.refs_4_, ...), custom_call_target="tpu_custom_call" | custom-call | flops 1024 | bytes 1024 | tf_op jit(solution)/shard_map/statistics_0/pallas_call | solution.py:294
  28.6 4.1 %collective-permute-done.9.refs_7_ = bf16[528,256]{1,0:T(8,128)(2,1)S(1)} collective-permute-done((bf16[528,256]{1,0:T(8,128)(2,1)S(1)}, bf16[528,256]{1,0:T(8,128)(2,1)S(1)}, u32[]{:S(2)}, u32[]{:S(2)}) %collective-permute-start.9) | collective-permute-done | bytes 270368 | tf_op jit(solution)/shard_map/ppermute | solution.py:415
  32.7 1.7 %statistics_2.1 = (bf16[528,256]{1,0:T(8,128)(2,1)S(1)}, f32[512,1024]{1,0:T(8,128)S(1)}) custom-call(bf16[512,256]{1,0:T(8,128)(2,1)S(1)} %collective-permute-done.5.refs_0_, bf16[512,256]{1,0:T(8,128)(2,1)S(1)} %collective-permute-done.8.refs_1_, bf16[528,256]{1,0:T(8,128)(2,1)S(1)} %get-tuple-element.27.refs_2_.exp_ref.refs_4_, ...), custom_call_target="tpu_custom_call" | custom-call | flops 1024 | bytes 1024 | tf_op jit(solution)/shard_map/statistics_2/pallas_call | solution.py:294
  34.5 3.5 %collective-permute-done.6.refs_0_ = bf16[512,256]{1,0:T(8,128)(2,1)S(1)} collective-permute-done((bf16[512,256]{1,0:T(8,128)(2,1)S(1)}, bf16[512,256]{1,0:T(8,128)(2,1)S(1)}, u32[]{:S(2)}, u32[]{:S(2)}) %collective-permute-start.6) | collective-permute-done | bytes 262176 | tf_op jit(solution)/shard_map/ppermute | solution.py:415
  38.0 1.5 %collective-permute-done.7.refs_1_ = bf16[512,256]{1,0:T(8,128)(2,1)S(1)} collective-permute-done((bf16[512,256]{1,0:T(8,128)(2,1)S(1)}, bf16[512,256]{1,0:T(8,128)(2,1)S(1)}, u32[]{:S(2)}, u32[]{:S(2)}) %collective-permute-start.7) | collective-permute-done | bytes 262176 | tf_op jit(solution)/shard_map/ppermute | solution.py:442
  39.5 4.5 %collective-permute-done.10.refs_7_ = bf16[528,256]{1,0:T(8,128)(2,1)S(1)} collective-permute-done((bf16[528,256]{1,0:T(8,128)(2,1)S(1)}, bf16[528,256]{1,0:T(8,128)(2,1)S(1)}, u32[]{:S(2)}, u32[]{:S(2)}) %collective-permute-start.10) | collective-permute-done | bytes 270368 | tf_op jit(solution)/shard_map/ppermute | solution.py:415
  44.0 1.7 %statistics_3.1 = (bf16[528,256]{1,0:T(8,128)(2,1)S(1)}, f32[256,1024]{1,0:T(8,128)S(1)}, bf16[256,512]{1,0:T(8,128)(2,1)S(1)}, bf16[256,512]{1,0:T(8,128)(2,1)S(1)}) custom-call(bf16[512,256]{1,0:T(8,128)(2,1)S(1)} %collective-permute-done.6.refs_0_, bf16[512,256]{1,0:T(8,128)(2,1)S(1)} %collective-permute-done.7.refs_1_, ...), custom_call_target="tpu_custom_call" | custom-call | flops 1024 | bytes 1024 | tf_op jit(solution)/shard_map/statistics_3/pallas_call | solution.py:294
  45.8 0.5 collective-permute-start.13
  46.3 1.0 %collective-permute-done.14.came_ref = bf16[256,512]{1,0:T(8,128)(2,1)S(1)} collective-permute-done((bf16[256,512]{1,0:T(8,128)(2,1)S(1)}, bf16[256,512]{1,0:T(8,128)(2,1)S(1)}, u32[]{:S(2)}, u32[]{:S(2)}) %collective-permute-start.14) | collective-permute-done | bytes 262176 | tf_op jit(solution)/shard_map/ppermute | solution.py:442
  47.4 0.6 %collective-permute-start.15 = (bf16[256,512]{1,0:T(8,128)(2,1)S(1)}, bf16[256,512]{1,0:T(8,128)(2,1)S(1)}, u32[]{:S(2)}, u32[]{:S(2)}) collective-permute-start(bf16[256,512]{1,0:T(8,128)(2,1)S(1)} %merge_items.1), channel_id=1, source_target_pairs={{0,2},{2,0},{1,3},{3,1},{4,6},{6,4},{5,7},{7,5},{8,10},{10,8},{9,1... | collective-permute-start | bytes 786440 | tf_op jit(solution)/shard_map/ppermute | solution.py:423
  48.0 6.3 %collective-permute-done.11.refs_2_ = bf16[528,256]{1,0:T(8,128)(2,1)S(1)} collective-permute-done((bf16[528,256]{1,0:T(8,128)(2,1)S(1)}, bf16[528,256]{1,0:T(8,128)(2,1)S(1)}, u32[]{:S(2)}, u32[]{:S(2)}) %collective-permute-start.11) | collective-permute-done | bytes 270368 | tf_op jit(solution)/shard_map/ppermute | solution.py:415
  54.4 1.4 %collective-permute-done.15.refs_1_ = bf16[256,512]{1,0:T(8,128)(2,1)S(1)} collective-permute-done((bf16[256,512]{1,0:T(8,128)(2,1)S(1)}, bf16[256,512]{1,0:T(8,128)(2,1)S(1)}, u32[]{:S(2)}, u32[]{:S(2)}) %collective-permute-start.15) | collective-permute-done | bytes 262176 | tf_op jit(solution)/shard_map/ppermute | solution.py:423
  55.8 1.0 %finish_items.1 = f32[512,256]{1,0:T(8,128)} custom-call(bf16[528,256]{1,0:T(8,128)(2,1)S(1)} %get-tuple-element.27.refs_2_.exp_ref.refs_4_, f32[256,1024]{1,0:T(8,128)S(1)} %get-tuple-element.37.mine_ref.own_ref, bf16[256,512]{1,0:T(8,128)(2,1)S(1)} %collective-permute-done.13.refs_0_, bf16[256,512]{1,0:T(8,128)(2,1)S(1)} %collective-permute-done.15.refs_1_), custom_call_target="tpu_custom_call" | custom-call | flops 1024 | bytes 1024 | tf_op jit(solution)/shard_map/finish_items/pallas_call | solution.py:402
  56.8 1.4 %finish_users.1 = (f32[512,256]{1,0:T(8,128)}, f32[512,256]{1,0:T(8,128)}, f32[512,256]{1,0:T(8,128)}) custom-call(bf16[512,256]{1,0:T(8,128)(2,1)S(1)} %get-tuple-element.24.refs_0_, f32[256,256]{1,0:T(8,128)S(1)} %get-tuple-element.30.refs_1_, bf16[528,256]{1,0:T(8,128)(2,1)S(1)} %collective-permute-done.11.refs_2_, ...), custom_call_target="tpu_custom_call" | custom-call | flops 1024 | bytes 1024 | tf_op jit(solution)/shard_map/finish_users/pallas_call | solution.py:370
  (22 shorter events, 0.4 us)
Async XLA Ops:
  3.4 9.5 %collective-permute-start.1 = (bf16[528,256]{1,0:T(8,128)(2,1)S(1)}, bf16[528,256]{1,0:T(8,128)(2,1)S(1)}, u32[]{:S(2)}, u32[]{:S(2)}) collective-permute-start(bf16[528,256]{1,0:T(8,128)(2,1)S(1)} %get-tuple-element.27.refs_2_.exp_ref.refs_4_), channel_id=1, source_target_pairs={{0,2},{2,0},{1,3},{3,1},{4,6},{6,4},{5,7},{7,5},{8,10},{10,8},{9,1... | collective-permute-start | bytes 811016 | tf_op jit(solution)/shard_map/ppermute | solution.py:423
  6.4 9.6 %collective-permute-start.3 = (bf16[512,256]{1,0:T(8,128)(2,1)S(1)}, bf16[512,256]{1,0:T(8,128)(2,1)S(1)}, u32[]{:S(2)}, u32[]{:S(2)}) collective-permute-start(bf16[512,256]{1,0:T(8,128)(2,1)S(1)} %get-tuple-element.24.refs_0_), channel_id=1, source_target_pairs={{0,4},{4,8},{8,12},{12,0},{1,5},{5,9},{9,13},{13,1},{2,6},{6,10},{... | collective-permute-start | bytes 786440 | tf_op jit(solution)/shard_map/ppermute | solution.py:415
  10.9 5.2 %collective-permute-start = (bf16[784,256]{1,0:T(8,128)(2,1)S(1)}, bf16[784,256]{1,0:T(8,128)(2,1)S(1)}, u32[]{:S(2)}, u32[]{:S(2)}) collective-permute-start(bf16[784,256]{1,0:T(8,128)(2,1)S(1)} %get-tuple-element.26), channel_id=1, source_target_pairs={{0,1},{1,0},{2,3},{3,2},{4,5},{5,4},{6,7},{7,6},{8,9},{9,8},{10,11... | collective-permute-start | bytes 1204232 | tf_op jit(solution)/shard_map/ppermute | solution.py:442
  12.9 4.7 %collective-permute-start.2 = (bf16[528,256]{1,0:T(8,128)(2,1)S(1)}, bf16[528,256]{1,0:T(8,128)(2,1)S(1)}, u32[]{:S(2)}, u32[]{:S(2)}) collective-permute-start(bf16[528,256]{1,0:T(8,128)(2,1)S(1)} %collective-permute-done.1.refs_3_.refs_5_), channel_id=1, source_target_pairs={{0,1},{1,0},{2,3},{3,2},{4,5},{5,4},{6,7},{7,6},{8,9},{9,8},{10,11... | collective-permute-start | bytes 811016 | tf_op jit(solution)/shard_map/ppermute | solution.py:442
  16.0 1.5 %collective-permute-start.4 = (bf16[512,256]{1,0:T(8,128)(2,1)S(1)}, bf16[512,256]{1,0:T(8,128)(2,1)S(1)}, u32[]{:S(2)}, u32[]{:S(2)}) collective-permute-start(bf16[512,256]{1,0:T(8,128)(2,1)S(1)} %collective-permute-done.3.refs_0_), channel_id=1, source_target_pairs={{0,1},{1,0},{2,3},{3,2},{4,5},{5,4},{6,7},{7,6},{8,9},{9,8},{10,11... | collective-permute-start | bytes 786440 | tf_op jit(solution)/shard_map/ppermute | solution.py:442
  16.0 10.9 %collective-permute-start.5 = (bf16[512,256]{1,0:T(8,128)(2,1)S(1)}, bf16[512,256]{1,0:T(8,128)(2,1)S(1)}, u32[]{:S(2)}, u32[]{:S(2)}) collective-permute-start(bf16[512,256]{1,0:T(8,128)(2,1)S(1)} %collective-permute-done.3.refs_0_), channel_id=1, source_target_pairs={{0,4},{4,8},{8,12},{12,0},{1,5},{5,9},{9,13},{13,1},{2,6},{6,10},{... | collective-permute-start | bytes 786440 | tf_op jit(solution)/shard_map/ppermute | solution.py:415
  19.2 13.5 %collective-permute-start.9 = (bf16[528,256]{1,0:T(8,128)(2,1)S(1)}, bf16[528,256]{1,0:T(8,128)(2,1)S(1)}, u32[]{:S(2)}, u32[]{:S(2)}) collective-permute-start(bf16[528,256]{1,0:T(8,128)(2,1)S(1)} %get-tuple-element.31), channel_id=1, source_target_pairs={{0,4},{4,8},{8,12},{12,0},{1,5},{5,9},{9,13},{13,1},{2,6},{6,10},{... | collective-permute-start | bytes 811016 | tf_op jit(solution)/shard_map/ppermute | solution.py:415
  26.9 1.7 %collective-permute-start.8 = (bf16[512,256]{1,0:T(8,128)(2,1)S(1)}, bf16[512,256]{1,0:T(8,128)(2,1)S(1)}, u32[]{:S(2)}, u32[]{:S(2)}) collective-permute-start(bf16[512,256]{1,0:T(8,128)(2,1)S(1)} %collective-permute-done.5.refs_0_), channel_id=1, source_target_pairs={{0,1},{1,0},{2,3},{3,2},{4,5},{5,4},{6,7},{7,6},{8,9},{9,8},{10,11... | collective-permute-start | bytes 786440 | tf_op jit(solution)/shard_map/ppermute | solution.py:442
  26.9 11.0 %collective-permute-start.6 = (bf16[512,256]{1,0:T(8,128)(2,1)S(1)}, bf16[512,256]{1,0:T(8,128)(2,1)S(1)}, u32[]{:S(2)}, u32[]{:S(2)}) collective-permute-start(bf16[512,256]{1,0:T(8,128)(2,1)S(1)} %collective-permute-done.5.refs_0_), channel_id=1, source_target_pairs={{0,4},{4,8},{8,12},{12,0},{1,5},{5,9},{9,13},{13,1},{2,6},{6,10},{... | collective-permute-start | bytes 786440 | tf_op jit(solution)/shard_map/ppermute | solution.py:415
  34.4 9.6 %collective-permute-start.10 = (bf16[528,256]{1,0:T(8,128)(2,1)S(1)}, bf16[528,256]{1,0:T(8,128)(2,1)S(1)}, u32[]{:S(2)}, u32[]{:S(2)}) collective-permute-start(bf16[528,256]{1,0:T(8,128)(2,1)S(1)} %get-tuple-element.33), channel_id=1, source_target_pairs={{0,4},{4,8},{8,12},{12,0},{1,5},{5,9},{9,13},{13,1},{2,6},{6,10},{... | collective-permute-start | bytes 811016 | tf_op jit(solution)/shard_map/ppermute | solution.py:415
  38.0 1.5 %collective-permute-start.7 = (bf16[512,256]{1,0:T(8,128)(2,1)S(1)}, bf16[512,256]{1,0:T(8,128)(2,1)S(1)}, u32[]{:S(2)}, u32[]{:S(2)}) collective-permute-start(bf16[512,256]{1,0:T(8,128)(2,1)S(1)} %collective-permute-done.6.refs_0_), channel_id=1, source_target_pairs={{0,1},{1,0},{2,3},{3,2},{4,5},{5,4},{6,7},{7,6},{8,9},{9,8},{10,11... | collective-permute-start | bytes 786440 | tf_op jit(solution)/shard_map/ppermute | solution.py:442
  45.6 8.6 %collective-permute-start.11 = (bf16[528,256]{1,0:T(8,128)(2,1)S(1)}, bf16[528,256]{1,0:T(8,128)(2,1)S(1)}, u32[]{:S(2)}, u32[]{:S(2)}) collective-permute-start(bf16[528,256]{1,0:T(8,128)(2,1)S(1)} %get-tuple-element.35), channel_id=1, source_target_pairs={{0,4},{4,8},{8,12},{12,0},{1,5},{5,9},{9,13},{13,1},{2,6},{6,10},{... | collective-permute-start | bytes 811016 | tf_op jit(solution)/shard_map/ppermute | solution.py:415
  45.7 1.6 %collective-permute-start.14 = (bf16[256,512]{1,0:T(8,128)(2,1)S(1)}, bf16[256,512]{1,0:T(8,128)(2,1)S(1)}, u32[]{:S(2)}, u32[]{:S(2)}) collective-permute-start(bf16[256,512]{1,0:T(8,128)(2,1)S(1)} %get-tuple-element.39), channel_id=1, source_target_pairs={{0,1},{1,0},{2,3},{3,2},{4,5},{5,4},{6,7},{7,6},{8,9},{9,8},{10,11... | collective-permute-start | bytes 786440 | tf_op jit(solution)/shard_map/ppermute | solution.py:442
  45.8 8.6 %collective-permute-start.13 = (bf16[256,512]{1,0:T(8,128)(2,1)S(1)}, bf16[256,512]{1,0:T(8,128)(2,1)S(1)}, u32[]{:S(2)}, u32[]{:S(2)}) collective-permute-start(bf16[256,512]{1,0:T(8,128)(2,1)S(1)} %get-tuple-element.38), channel_id=1, source_target_pairs={{0,1},{1,0},{2,3},{3,2},{4,5},{5,4},{6,7},{7,6},{8,9},{9,8},{10,11... | collective-permute-start | bytes 786440 | tf_op jit(solution)/shard_map/ppermute | solution.py:442
  47.3 9.4 %copy-start = (f32[1,512]{1,0:T(1,128)S(1)}, f32[1,512]{1,0:T(1,128)}, u32[]{:S(2)}) copy-start(f32[1,512]{1,0:T(1,128)} %refs_6_.1) | copy-start | bytes 6148
  47.3 9.5 %copy-start.1 = (f32[1,512]{1,0:T(1,128)S(1)}, f32[1,512]{1,0:T(1,128)}, u32[]{:S(2)}) copy-start(f32[1,512]{1,0:T(1,128)} %refs_7_.1) | copy-start | bytes 6148
  47.4 8.4 %collective-permute-start.15 = (bf16[256,512]{1,0:T(8,128)(2,1)S(1)}, bf16[256,512]{1,0:T(8,128)(2,1)S(1)}, u32[]{:S(2)}, u32[]{:S(2)}) collective-permute-start(bf16[256,512]{1,0:T(8,128)(2,1)S(1)} %merge_items.1), channel_id=1, source_target_pairs={{0,2},{2,0},{1,3},{3,1},{4,6},{6,4},{5,7},{7,5},{8,10},{10,8},{9,1... | collective-permute-start | bytes 786440 | tf_op jit(solution)/shard_map/ppermute | solution.py:423
  54.3 2.4 %collective-permute-start.12 = (bf16[256,256]{1,0:T(8,128)(2,1)S(1)}, bf16[256,256]{1,0:T(8,128)(2,1)S(1)}, u32[]{:S(2)}, u32[]{:S(2)}) collective-permute-start(bf16[256,256]{1,0:T(8,128)(2,1)S(1)} %add_convert_fusion), channel_id=1, source_target_pairs={{0,1},{1,0},{2,3},{3,2},{4,5},{5,4},{6,7},{7,6},{8,9},{9,8},{10,11... | collective-permute-start | bytes 393224 | tf_op jit(solution)/shard_map/ppermute | solution.py:442

commit v7 on v5

--- a/solution.py
+++ b/solution.py
@@ -174,8 +174,8 @@
 
             @pl.when(lax.div(within, half) == core)
             def _():
-                distance = shard ^ z
-                step = jnp.where(core == 0, distance, mirrored(distance, n_item))
+                back = lax.rem(z - shard + n_item, n_item)
+                step = jnp.where(back == 0, 0, jnp.where(back * 2 <= n_item, 2 * back - 1, 2 * (n_item - back)))
                 start = pl.multiple_of(step * half + lax.rem(within, half), piece)
                 value = buf[slot, j * piece : (j + 1) * piece, :].astype(F32).astype(BF16)
                 out_ref[pl.ds(start, piece), pl.ds(col, tile)] = value
@@ -409,22 +409,8 @@
     )(item_exp, own, *came)
 
 
-def mirrored(k, n):
-    out = k * 0
-    bit = 1
-    while bit < n:
-        out = out * 2 + (k & 1)
-        k = k >> 1
-        bit *= 2
-    return out
-
-
-def along_item(x, k, n, n_ka):
-    pairs = []
-    for i in range(n):
-        for h in range(n_ka):
-            pairs.append((i * n_ka + h, (i ^ (mirrored(k, n) if h else k)) * n_ka + h))
-    return lax.ppermute(x, ("item", "ka"), pairs)
+def along_item(x, shift, n):
+    return lax.ppermute(x, "item", [(i, (i + shift) % n) for i in range(n)])
 
 
 def after(x, y):
@@ -470,10 +456,13 @@
     pack, dense = lax.optimization_barrier((pack, dense))
     came_pack = sibling(pack)
 
+    places = [0]
+    for d in range(1, n_item // 2 + 1):
+        places += [d, -d][: n_item - len(places)]
     shards = [both]
-    for k in range(1, n_item):
-        low = k & -k
-        shards.append(along_item(shards[k ^ low], low, n_item, n_ka))
+    for i in range(1, n_item):
+        step = 1 if places[i] > 0 else -1
+        shards.append(along_item(shards[max(i - 2, 0)], step, n_item))
 
     item_mine = [item_exp]
     for p in range(1, n_user):
@@ -481,24 +470,20 @@
         item_mine.append(along_user(item_mine[p ^ low], low, n_user))
     item_other = [came_pack] + [sibling(x) for x in item_mine[1:]]
 
-    order = sorted(range(1, n_item - 1), key=lambda k: (k & (k - 1) != 0, k)) + [0, n_item - 1]
     acc = None
     joined = []
     latest = None
-    for k in order:
-        last = k == n_item - 1
-        if k == 0:
-            other = came_pack
+    for i in list(range(1, n_item - 1)) + [0, n_item - 1]:
+        last = i == n_item - 1
+        passed = after(shards[i], latest) if last else shards[i]
+        other = sibling(passed) if i else came_pack
+        stats, accs = statistics(i, [shards[i], other], item_mine, item_other, dense, acc, last, half_rows)
+        acc = accs[0]
+        if i:
+            joined.append(along_item(stats[0], -places[i], n_item))
+            latest = stats[0] if latest is None else latest
         else:
-            passed = shards[mirrored(k, n_item)]
-            other = sibling(after(passed, latest) if last else passed)
-        stats, accs = statistics(k, [shards[k], other], item_mine, item_other, dense, acc, last, half_rows)
-        acc = accs[0]
-        if k == 0:
             own, own_other = stats
-        else:
-            joined.append(along_item(stats[0], k, n_item, n_ka))
-            latest = stats[0] if latest is None else latest
 
     came = [sibling(accs[1])]
     for p in range(1, n_user):

time: 63.7 us -> 55.3 us (0.87)
  the two profiles are of different devices: /device:TPU:24 before, /device:TPU:0 now
where the time goes in v7:
time: 55.3 us; the launch traced here: 55.1 us
  waiting for transfers between devices  27.1 us (49%)
  Pallas kernels  14.1 us (25%)
  starting transfers between devices  12.4 us (22%)
  between operations  1.42 us (3%)
    ppermute x6, waiting for transfers between devices, along_item(): return lax.ppermute(x, 'item', [(i, (i + shift) % n) for i in range(n)])  25.6 us
    ppermute x6, starting transfers between devices, along_item(): return lax.ppermute(x, 'item', [(i, (i + shift) % n) for i in range(n)])  8.26 us
    pallas_call x4, Pallas kernels, statistics(): pl.pallas_call(functools.partial(stat_kernel, len(item_mine), half_rows,...  6.63 us
    ppermute x2, starting transfers between devices, along_user(): return lax.ppermute(x, 'user', [(i, i ^ distance) for i in range(n)])  3.07 us
    pallas_call x1, Pallas kernels, expected(): pl.pallas_call(functools.partial(expected_kernel, chunk_u, chunk_i), in_s...  2.76 us
    pallas_call x1, Pallas kernels, dense_counts(): pl.pallas_call(functools.partial(dense_kernel, n_item, item_rows // n_use...  2.24 us
    ppermute x9, waiting for transfers between devices, sibling(): return lax.ppermute(x, 'ka', [(h, n_ka - 1 - h) for h in range(n_ka)])  1.48 us
    pallas_call x1, Pallas kernels, finish_users(): pl.pallas_call(functools.partial(finish_users_kernel, len(joined), len(it...  1.44 us
  transfers between devices with their start and end apart: 17, of which 7 were waited for; matrix products, arithmetic and copies ran while one was open for 0% of the time, Pallas kernels for 18%

profile of v7, /device:TPU:0, one launch (start us, length us, event | category | flops | bytes accessed | tf_op | source)
XLA Modules:
  0.0 55.1 jit_solution(9724788459875905792)
XLA Ops:
  0.6 2.8 %expected.1 = (bf16[512,256]{1,0:T(8,128)(2,1)S(1)}, bf16[528,256]{1,0:T(8,128)(2,1)S(1)}, bf16[784,256]{1,0:T(8,128)(2,1)S(1)}) custom-call(f32[512,256]{1,0:T(8,128)} %bitcast.14, f32[512,256]{1,0:T(8,128)} %bitcast.15, f32[512,256]{1,0:T(8,128)} %bitcast.16, f32[512,256]{1,0:T(8,128)} %bitcast.17), custom_call_target="tpu_custom_call" | custom-call | flops 1024 | bytes 1024 | tf_op jit(solution)/shard_map/expected/pallas_call | solution.py:120
  3.4 3.0 %collective-permute-start.1 = (bf16[528,256]{1,0:T(8,128)(2,1)S(1)}, bf16[528,256]{1,0:T(8,128)(2,1)S(1)}, u32[]{:S(2)}, u32[]{:S(2)}) collective-permute-start(bf16[528,256]{1,0:T(8,128)(2,1)S(1)} %get-tuple-element.29.refs_2_.exp_ref.refs_7_), channel_id=1, source_target_pairs={{0,2},{2,0},{1,3},{3,1},{4,6},{6,4},{5,7},{7,5},{8,10},{10,8},{9,1... | collective-permute-start | bytes 811016 | tf_op jit(solution)/shard_map/ppermute | solution.py:421
  6.4 1.6 %collective-permute-start.5 = (bf16[512,256]{1,0:T(8,128)(2,1)S(1)}, bf16[512,256]{1,0:T(8,128)(2,1)S(1)}, u32[]{:S(2)}, u32[]{:S(2)}) collective-permute-start(bf16[512,256]{1,0:T(8,128)(2,1)S(1)} %get-tuple-element.26.refs_0_), channel_id=1, source_target_pairs={{0,4},{4,8},{8,12},{12,0},{1,5},{5,9},{9,13},{13,1},{2,6},{6,10},{... | collective-permute-start | bytes 786440 | tf_op jit(solution)/shard_map/ppermute | solution.py:413
  8.6 2.2 %dense_counts.1.refs_6_ = bf16[1024,1024]{1,0:T(8,128)(2,1)S(1)} custom-call(s32[64]{0:T(128)} %bitcast.19, s32[64]{0:T(128)} %bitcast.20, s32[1]{0:T(128)} %bitcast.12.live_ref, s32[64,128,128]{2,1,0:T(8,128)} %bitcast.13), custom_call_target="tpu_custom_call" | custom-call | flops 1024 | bytes 1024 | tf_op jit(solution)/shard_map/dense_counts/pallas_call | solution.py:194
  10.9 0.1 collective-permute-start
  11.0 2.3 %collective-permute-start.3 = (bf16[512,256]{1,0:T(8,128)(2,1)S(1)}, bf16[512,256]{1,0:T(8,128)(2,1)S(1)}, u32[]{:S(2)}, u32[]{:S(2)}) collective-permute-start(bf16[512,256]{1,0:T(8,128)(2,1)S(1)} %get-tuple-element.26.refs_0_), channel_id=1, source_target_pairs={{0,12},{4,0},{8,4},{12,8},{1,13},{5,1},{9,5},{13,9},{2,14},{6,2},{... | collective-permute-start | bytes 786440 | tf_op jit(solution)/shard_map/ppermute | solution.py:413
  13.3 0.2 collective-permute-start.2
  13.4 2.7 %collective-permute-done.5.refs_0_ = bf16[512,256]{1,0:T(8,128)(2,1)S(1)} collective-permute-done((bf16[512,256]{1,0:T(8,128)(2,1)S(1)}, bf16[512,256]{1,0:T(8,128)(2,1)S(1)}, u32[]{:S(2)}, u32[]{:S(2)}) %collective-permute-start.5) | collective-permute-done | bytes 262176 | tf_op jit(solution)/shard_map/ppermute | solution.py:413
  16.1 5.5 %collective-permute-done.3.refs_0_ = bf16[512,256]{1,0:T(8,128)(2,1)S(1)} collective-permute-done((bf16[512,256]{1,0:T(8,128)(2,1)S(1)}, bf16[512,256]{1,0:T(8,128)(2,1)S(1)}, u32[]{:S(2)}, u32[]{:S(2)}) %collective-permute-start.3) | collective-permute-done | bytes 262176 | tf_op jit(solution)/shard_map/ppermute | solution.py:413
  21.7 1.6 %statistics_1.1 = (bf16[528,256]{1,0:T(8,128)(2,1)S(1)}, f32[512,1024]{1,0:T(8,128)S(1)}) custom-call(bf16[512,256]{1,0:T(8,128)(2,1)S(1)} %collective-permute-done.5.refs_0_, bf16[512,256]{1,0:T(8,128)(2,1)S(1)} %collective-permute-done.6.refs_1_, bf16[528,256]{1,0:T(8,128)(2,1)S(1)} %get-tuple-element.29.refs_2_.exp_ref.refs_7_, ...), custom_call_target="tpu_custom_call" | custom-call | flops 1024 | bytes 1024 | tf_op jit(solution)/shard_map/statistics_1/pallas_call | solution.py:287
  23.4 2.6 %collective-permute-start.7 = (bf16[528,256]{1,0:T(8,128)(2,1)S(1)}, bf16[528,256]{1,0:T(8,128)(2,1)S(1)}, u32[]{:S(2)}, u32[]{:S(2)}) collective-permute-start(bf16[528,256]{1,0:T(8,128)(2,1)S(1)} %get-tuple-element.35), channel_id=1, source_target_pairs={{0,12},{4,0},{8,4},{12,8},{1,13},{5,1},{9,5},{13,9},{2,14},{6,2},{... | collective-permute-start | bytes 811016 | tf_op jit(solution)/shard_map/ppermute | solution.py:413
  25.9 2.3 %collective-permute-done.10.refs_0_ = bf16[512,256]{1,0:T(8,128)(2,1)S(1)} collective-permute-done((bf16[512,256]{1,0:T(8,128)(2,1)S(1)}, bf16[512,256]{1,0:T(8,128)(2,1)S(1)}, u32[]{:S(2)}, u32[]{:S(2)}) %collective-permute-start.10) | collective-permute-done | bytes 262176 | tf_op jit(solution)/shard_map/ppermute | solution.py:413
  28.2 1.7 %statistics_2.1 = (bf16[528,256]{1,0:T(8,128)(2,1)S(1)}, f32[512,1024]{1,0:T(8,128)S(1)}) custom-call(bf16[512,256]{1,0:T(8,128)(2,1)S(1)} %collective-permute-done.3.refs_0_, bf16[512,256]{1,0:T(8,128)(2,1)S(1)} %collective-permute-done.4.refs_1_, bf16[528,256]{1,0:T(8,128)(2,1)S(1)} %get-tuple-element.29.refs_2_.exp_ref.refs_7_, ...), custom_call_target="tpu_custom_call" | custom-call | flops 1024 | bytes 1024 | tf_op jit(solution)/shard_map/statistics_2/pallas_call | solution.py:287
  29.9 1.7 %statistics_0.1 = (f32[256,256]{1,0:T(8,128)S(1)}, f32[256,256]{1,0:T(8,128)S(1)}, f32[512,1024]{1,0:T(8,128)S(1)}) custom-call(bf16[512,256]{1,0:T(8,128)(2,1)S(1)} %get-tuple-element.26.refs_0_, bf16[784,256]{1,0:T(8,128)(2,1)S(1)} %collective-permute-done.refs_4_.refs_1_, bf16[528,256]{1,0:T(8,128)(2,1)S(1)} %get-tuple-element.29.refs_2_.exp_ref.refs_7_, ...), custom_call_target="tpu_custom_call" | custom-call | flops 1024 | bytes 1024 | tf_op jit(solution)/shard_map/statistics_0/pallas_call | solution.py:287
  31.6 1.7 %statistics_3.1 = (bf16[528,256]{1,0:T(8,128)(2,1)S(1)}, f32[256,1024]{1,0:T(8,128)S(1)}, bf16[256,512]{1,0:T(8,128)(2,1)S(1)}, bf16[256,512]{1,0:T(8,128)(2,1)S(1)}) custom-call(bf16[512,256]{1,0:T(8,128)(2,1)S(1)} %collective-permute-done.10.refs_0_, bf16[512,256]{1,0:T(8,128)(2,1)S(1)} %collective-permute-done.11.refs_1_, ...), custom_call_target="tpu_custom_call" | custom-call | flops 1024 | bytes 1024 | tf_op jit(solution)/shard_map/statistics_3/pallas_call | solution.py:287
  33.3 1.8 %collective-permute-start.12 = (bf16[528,256]{1,0:T(8,128)(2,1)S(1)}, bf16[528,256]{1,0:T(8,128)(2,1)S(1)}, u32[]{:S(2)}, u32[]{:S(2)}) collective-permute-start(bf16[528,256]{1,0:T(8,128)(2,1)S(1)} %get-tuple-element.39), channel_id=1, source_target_pairs={{0,8},{4,12},{8,0},{12,4},{1,9},{5,13},{9,1},{13,5},{2,10},{6,14},... | collective-permute-start | bytes 811016 | tf_op jit(solution)/shard_map/ppermute | solution.py:413
  35.0 0.5 collective-permute-start.15
  35.6 5.5 %collective-permute-done.8.refs_4_ = bf16[528,256]{1,0:T(8,128)(2,1)S(1)} collective-permute-done((bf16[528,256]{1,0:T(8,128)(2,1)S(1)}, bf16[528,256]{1,0:T(8,128)(2,1)S(1)}, u32[]{:S(2)}, u32[]{:S(2)}) %collective-permute-start.8) | collective-permute-done | bytes 270368 | tf_op jit(solution)/shard_map/ppermute | solution.py:413
  41.4 1.2 %collective-permute-done.9.refs_2_ = bf16[256,256]{1,0:T(8,128)(2,1)S(1)} collective-permute-done((bf16[256,256]{1,0:T(8,128)(2,1)S(1)}, bf16[256,256]{1,0:T(8,128)(2,1)S(1)}, u32[]{:S(2)}, u32[]{:S(2)}) %collective-permute-start.9) | collective-permute-done | bytes 131104 | tf_op jit(solution)/shard_map/ppermute | solution.py:440
  42.5 9.7 %collective-permute-done.12.refs_5_ = bf16[528,256]{1,0:T(8,128)(2,1)S(1)} collective-permute-done((bf16[528,256]{1,0:T(8,128)(2,1)S(1)}, bf16[528,256]{1,0:T(8,128)(2,1)S(1)}, u32[]{:S(2)}, u32[]{:S(2)}) %collective-permute-start.12) | collective-permute-done | bytes 270368 | tf_op jit(solution)/shard_map/ppermute | solution.py:413
  52.2 0.1 collective-permute-start.13
  52.4 1.0 %finish_items.1 = f32[512,256]{1,0:T(8,128)} custom-call(bf16[528,256]{1,0:T(8,128)(2,1)S(1)} %get-tuple-element.29.refs_2_.exp_ref.refs_7_, f32[256,1024]{1,0:T(8,128)S(1)} %get-tuple-element.41.mine_ref.own_ref, bf16[256,512]{1,0:T(8,128)(2,1)S(1)} %collective-permute-done.14.refs_0_, bf16[256,512]{1,0:T(8,128)(2,1)S(1)} %collective-permute-done.16.refs_1_), custom_call_target="tpu_custom_call" | custom-call | flops 1024 | bytes 1024 | tf_op jit(solution)/shard_map/finish_items/pallas_call | solution.py:400
  53.3 0.3 collective-permute-done.13.refs_6_
  53.6 1.4 %finish_users.1 = (f32[512,256]{1,0:T(8,128)}, f32[512,256]{1,0:T(8,128)}, f32[512,256]{1,0:T(8,128)}) custom-call(bf16[512,256]{1,0:T(8,128)(2,1)S(1)} %get-tuple-element.26.refs_0_, f32[256,256]{1,0:T(8,128)S(1)} %get-tuple-element.33.refs_1_, bf16[256,256]{1,0:T(8,128)(2,1)S(1)} %collective-permute-done.9.refs_2_, ...), custom_call_target="tpu_custom_call" | custom-call | flops 1024 | bytes 1024 | tf_op jit(solution)/shard_map/finish_users/pallas_call | solution.py:368
  (26 shorter events, 0.4 us)
Async XLA Ops:
  3.4 9.9 %collective-permute-start.1 = (bf16[528,256]{1,0:T(8,128)(2,1)S(1)}, bf16[528,256]{1,0:T(8,128)(2,1)S(1)}, u32[]{:S(2)}, u32[]{:S(2)}) collective-permute-start(bf16[528,256]{1,0:T(8,128)(2,1)S(1)} %get-tuple-element.29.refs_2_.exp_ref.refs_7_), channel_id=1, source_target_pairs={{0,2},{2,0},{1,3},{3,1},{4,6},{6,4},{5,7},{7,5},{8,10},{10,8},{9,1... | collective-permute-start | bytes 811016 | tf_op jit(solution)/shard_map/ppermute | solution.py:421
  6.4 9.7 %collective-permute-start.5 = (bf16[512,256]{1,0:T(8,128)(2,1)S(1)}, bf16[512,256]{1,0:T(8,128)(2,1)S(1)}, u32[]{:S(2)}, u32[]{:S(2)}) collective-permute-start(bf16[512,256]{1,0:T(8,128)(2,1)S(1)} %get-tuple-element.26.refs_0_), channel_id=1, source_target_pairs={{0,4},{4,8},{8,12},{12,0},{1,5},{5,9},{9,13},{13,1},{2,6},{6,10},{... | collective-permute-start | bytes 786440 | tf_op jit(solution)/shard_map/ppermute | solution.py:413
  10.9 10.8 %collective-permute-start = (bf16[784,256]{1,0:T(8,128)(2,1)S(1)}, bf16[784,256]{1,0:T(8,128)(2,1)S(1)}, u32[]{:S(2)}, u32[]{:S(2)}) collective-permute-start(bf16[784,256]{1,0:T(8,128)(2,1)S(1)} %get-tuple-element.28), channel_id=1, source_target_pairs={{0,1},{1,0},{2,3},{3,2},{4,5},{5,4},{6,7},{7,6},{8,9},{9,8},{10,11... | collective-permute-start | bytes 1204232 | tf_op jit(solution)/shard_map/ppermute | solution.py:440
  11.0 10.7 %collective-permute-start.3 = (bf16[512,256]{1,0:T(8,128)(2,1)S(1)}, bf16[512,256]{1,0:T(8,128)(2,1)S(1)}, u32[]{:S(2)}, u32[]{:S(2)}) collective-permute-start(bf16[512,256]{1,0:T(8,128)(2,1)S(1)} %get-tuple-element.26.refs_0_), channel_id=1, source_target_pairs={{0,12},{4,0},{8,4},{12,8},{1,13},{5,1},{9,5},{13,9},{2,14},{6,2},{... | collective-permute-start | bytes 786440 | tf_op jit(solution)/shard_map/ppermute | solution.py:413
  13.3 8.5 %collective-permute-start.2 = (bf16[528,256]{1,0:T(8,128)(2,1)S(1)}, bf16[528,256]{1,0:T(8,128)(2,1)S(1)}, u32[]{:S(2)}, u32[]{:S(2)}) collective-permute-start(bf16[528,256]{1,0:T(8,128)(2,1)S(1)} %collective-permute-done.1.refs_3_.refs_8_), channel_id=1, source_target_pairs={{0,1},{1,0},{2,3},{3,2},{4,5},{5,4},{6,7},{7,6},{8,9},{9,8},{10,11... | collective-permute-start | bytes 811016 | tf_op jit(solution)/shard_map/ppermute | solution.py:440
  16.1 5.6 %collective-permute-start.6 = (bf16[512,256]{1,0:T(8,128)(2,1)S(1)}, bf16[512,256]{1,0:T(8,128)(2,1)S(1)}, u32[]{:S(2)}, u32[]{:S(2)}) collective-permute-start(bf16[512,256]{1,0:T(8,128)(2,1)S(1)} %collective-permute-done.5.refs_0_), channel_id=1, source_target_pairs={{0,1},{1,0},{2,3},{3,2},{4,5},{5,4},{6,7},{7,6},{8,9},{9,8},{10,11... | collective-permute-start | bytes 786440 | tf_op jit(solution)/shard_map/ppermute | solution.py:440
  16.1 12.1 %collective-permute-start.10 = (bf16[512,256]{1,0:T(8,128)(2,1)S(1)}, bf16[512,256]{1,0:T(8,128)(2,1)S(1)}, u32[]{:S(2)}, u32[]{:S(2)}) collective-permute-start(bf16[512,256]{1,0:T(8,128)(2,1)S(1)} %collective-permute-done.5.refs_0_), channel_id=1, source_target_pairs={{0,4},{4,8},{8,12},{12,0},{1,5},{5,9},{9,13},{13,1},{2,6},{6,10},{... | collective-permute-start | bytes 786440 | tf_op jit(solution)/shard_map/ppermute | solution.py:413
  21.6 6.6 %collective-permute-start.4 = (bf16[512,256]{1,0:T(8,128)(2,1)S(1)}, bf16[512,256]{1,0:T(8,128)(2,1)S(1)}, u32[]{:S(2)}, u32[]{:S(2)}) collective-permute-start(bf16[512,256]{1,0:T(8,128)(2,1)S(1)} %collective-permute-done.3.refs_0_), channel_id=1, source_target_pairs={{0,1},{1,0},{2,3},{3,2},{4,5},{5,4},{6,7},{7,6},{8,9},{9,8},{10,11... | collective-permute-start | bytes 786440 | tf_op jit(solution)/shard_map/ppermute | solution.py:440
  23.4 12.2 %collective-permute-start.7 = (bf16[528,256]{1,0:T(8,128)(2,1)S(1)}, bf16[528,256]{1,0:T(8,128)(2,1)S(1)}, u32[]{:S(2)}, u32[]{:S(2)}) collective-permute-start(bf16[528,256]{1,0:T(8,128)(2,1)S(1)} %get-tuple-element.35), channel_id=1, source_target_pairs={{0,12},{4,0},{8,4},{12,8},{1,13},{5,1},{9,5},{13,9},{2,14},{6,2},{... | collective-permute-start | bytes 811016 | tf_op jit(solution)/shard_map/ppermute | solution.py:413
  28.2 3.4 %collective-permute-start.11 = (bf16[512,256]{1,0:T(8,128)(2,1)S(1)}, bf16[512,256]{1,0:T(8,128)(2,1)S(1)}, u32[]{:S(2)}, u32[]{:S(2)}) collective-permute-start(bf16[512,256]{1,0:T(8,128)(2,1)S(1)} %collective-permute-done.10.refs_0_), channel_id=1, source_target_pairs={{0,1},{1,0},{2,3},{3,2},{4,5},{5,4},{6,7},{7,6},{8,9},{9,8},{10,11... | collective-permute-start | bytes 786440 | tf_op jit(solution)/shard_map/ppermute | solution.py:440
  29.9 11.2 %collective-permute-start.8 = (bf16[528,256]{1,0:T(8,128)(2,1)S(1)}, bf16[528,256]{1,0:T(8,128)(2,1)S(1)}, u32[]{:S(2)}, u32[]{:S(2)}) collective-permute-start(bf16[528,256]{1,0:T(8,128)(2,1)S(1)} %get-tuple-element.36), channel_id=1, source_target_pairs={{0,4},{4,8},{8,12},{12,0},{1,5},{5,9},{9,13},{13,1},{2,6},{6,10},{... | collective-permute-start | bytes 811016 | tf_op jit(solution)/shard_map/ppermute | solution.py:413
  33.3 18.9 %collective-permute-start.12 = (bf16[528,256]{1,0:T(8,128)(2,1)S(1)}, bf16[528,256]{1,0:T(8,128)(2,1)S(1)}, u32[]{:S(2)}, u32[]{:S(2)}) collective-permute-start(bf16[528,256]{1,0:T(8,128)(2,1)S(1)} %get-tuple-element.39), channel_id=1, source_target_pairs={{0,8},{4,12},{8,0},{12,4},{1,9},{5,13},{9,1},{13,5},{2,10},{6,14},... | collective-permute-start | bytes 811016 | tf_op jit(solution)/shard_map/ppermute | solution.py:413
  35.0 17.3 %collective-permute-start.14 = (bf16[256,512]{1,0:T(8,128)(2,1)S(1)}, bf16[256,512]{1,0:T(8,128)(2,1)S(1)}, u32[]{:S(2)}, u32[]{:S(2)}) collective-permute-start(bf16[256,512]{1,0:T(8,128)(2,1)S(1)} %get-tuple-element.42), channel_id=1, source_target_pairs={{0,1},{1,0},{2,3},{3,2},{4,5},{5,4},{6,7},{7,6},{8,9},{9,8},{10,11... | collective-permute-start | bytes 786440 | tf_op jit(solution)/shard_map/ppermute | solution.py:440
  35.0 6.2 %collective-permute-start.15 = (bf16[256,512]{1,0:T(8,128)(2,1)S(1)}, bf16[256,512]{1,0:T(8,128)(2,1)S(1)}, u32[]{:S(2)}, u32[]{:S(2)}) collective-permute-start(bf16[256,512]{1,0:T(8,128)(2,1)S(1)} %get-tuple-element.43), channel_id=1, source_target_pairs={{0,1},{1,0},{2,3},{3,2},{4,5},{5,4},{6,7},{7,6},{8,9},{9,8},{10,11... | collective-permute-start | bytes 786440 | tf_op jit(solution)/shard_map/ppermute | solution.py:440
  41.1 1.4 %collective-permute-start.9 = (bf16[256,256]{1,0:T(8,128)(2,1)S(1)}, bf16[256,256]{1,0:T(8,128)(2,1)S(1)}, u32[]{:S(2)}, u32[]{:S(2)}) collective-permute-start(bf16[256,256]{1,0:T(8,128)(2,1)S(1)} %convert_add_fusion), channel_id=1, source_target_pairs={{0,1},{1,0},{2,3},{3,2},{4,5},{5,4},{6,7},{7,6},{8,9},{9,8},{10,11... | collective-permute-start | bytes 393224 | tf_op jit(solution)/shard_map/ppermute | solution.py:440
  41.2 12.4 %copy-start = (f32[1,512]{1,0:T(1,128)S(1)}, f32[1,512]{1,0:T(1,128)}, u32[]{:S(2)}) copy-start(f32[1,512]{1,0:T(1,128)} %refs_9_.1) | copy-start | bytes 6148
  41.2 12.4 %copy-start.1 = (f32[1,512]{1,0:T(1,128)S(1)}, f32[1,512]{1,0:T(1,128)}, u32[]{:S(2)}) copy-start(f32[1,512]{1,0:T(1,128)} %refs_10_.1) | copy-start | bytes 6148
  41.3 11.0 %collective-permute-start.16 = (bf16[256,512]{1,0:T(8,128)(2,1)S(1)}, bf16[256,512]{1,0:T(8,128)(2,1)S(1)}, u32[]{:S(2)}, u32[]{:S(2)}) collective-permute-start(bf16[256,512]{1,0:T(8,128)(2,1)S(1)} %merge_items.1), channel_id=1, source_target_pairs={{0,2},{2,0},{1,3},{3,1},{4,6},{6,4},{5,7},{7,5},{8,10},{10,8},{9,1... | collective-permute-start | bytes 786440 | tf_op jit(solution)/shard_map/ppermute | solution.py:421
  52.2 1.4 %collective-permute-start.13 = (bf16[256,256]{1,0:T(8,128)(2,1)S(1)}, bf16[256,256]{1,0:T(8,128)(2,1)S(1)}, u32[]{:S(2)}, u32[]{:S(2)}) collective-permute-start(bf16[256,256]{1,0:T(8,128)(2,1)S(1)} %slice.11), channel_id=1, source_target_pairs={{0,1},{1,0},{2,3},{3,2},{4,5},{5,4},{6,7},{7,6},{8,9},{9,8},{10,11... | collective-permute-start | bytes 393224 | tf_op jit(solution)/shard_map/ppermute | solution.py:440

commit v8 on v7

--- a/solution.py
+++ b/solution.py
@@ -70,7 +70,7 @@
 
 
 def expected_kernel(chunk_u, chunk_i, theta_ref, trate_ref, beta_ref, brate_ref, *refs):
-    both_ref, item_ref, pack_ref, theta_buf, trate_buf, beta_buf, brate_buf, user_sems, item_sems = refs
+    both_ref, wide_ref, item_ref, pack_ref, theta_buf, trate_buf, beta_buf, brate_buf, user_sems, item_sems = refs
     core = lax.axis_index("ka")
     half = both_ref.shape[0] // 2
     rows = beta_ref.shape[0]
@@ -91,9 +91,11 @@
         at = (j % steps) * chunk_u
         if j < steps:
             both_ref[half + at : half + at + chunk_u, :] = value
+            wide_ref[half + at : half + at + chunk_u, :] = value
             pack_ref[at : at + chunk_u, :] = value
         else:
             both_ref[at : at + chunk_u, :] = value
+            wide_ref[at : at + chunk_u, :] = value
         theta_total += jnp.sum(x * inv_rate, axis=0, keepdims=True)
     beta_total = jnp.zeros((1, both_ref.shape[1]), F32)
     for j, start in enumerate(item_starts):
@@ -105,6 +107,7 @@
         item_ref[start : start + chunk_i, :] = value
         pack_ref[half + start : half + start + chunk_i, :] = value
         beta_total += jnp.sum(x * inv_rate, axis=0, keepdims=True)
+    wide_ref[2 * half :, :] = jnp.zeros((2 * EXTRA, wide_ref.shape[1]), BF16)
     extra = encode([theta_total, beta_total])
     item_ref[rows:, :] = extra
     pack_ref[half + rows :, :] = extra
@@ -116,11 +119,11 @@
     half = rows // 2
     chunk_u = min(half, 128)
     chunk_i = min(item_rows, 128)
-    shapes = [rows, item_rows + EXTRA, half + item_rows + EXTRA]
+    shapes = [rows, rows + 2 * EXTRA, item_rows + EXTRA, half + item_rows + EXTRA]
     return pl.pallas_call(
         functools.partial(expected_kernel, chunk_u, chunk_i),
         in_specs=[pl.BlockSpec(memory_space=HBM)] * 4,
-        out_specs=[pl.BlockSpec(memory_space=VMEM)] * 3,
+        out_specs=[pl.BlockSpec(memory_space=VMEM)] * len(shapes),
         out_shape=[jax.ShapeDtypeStruct((r, cols), BF16) for r in shapes],
         scratch_shapes=[
             pltpu.VMEM((rows, cols), F32),
@@ -259,12 +262,16 @@
         stat_refs[1][...] = total_other
 
 
-def row_totals(item_refs):
+def sum_totals(blocks):
     sums = None
-    for ref in item_refs:
-        came = decode(ref[-EXTRA:, :])
+    for block in blocks:
+        came = decode(block)
         sums = came if sums is None else [a + b for a, b in zip(sums, came)]
     return sums
+
+
+def row_totals(item_refs):
+    return sum_totals([ref[-EXTRA:, :] for ref in item_refs])
 
 
 def statistics(at, users, item_mine, item_other, dense, acc, last, half_rows):
@@ -296,6 +303,24 @@
     return list(out[:n_stats]), list(out[n_stats:])
 
 
+def add_kernel(stat_ref, came_ref, out_ref):
+    rows = stat_ref.shape[0] - EXTRA
+    out_ref[:rows, :] = (stat_ref[:rows, :].astype(F32) + came_ref[:rows, :].astype(F32)).astype(BF16)
+    out_ref[rows:, :] = encode(sum_totals([stat_ref[rows:, :], came_ref[rows:, :]]))
+
+
+def add_came(stat, came):
+    return pl.pallas_call(
+        add_kernel,
+        in_specs=[pl.BlockSpec(memory_space=VMEM)] * 2,
+        out_specs=pl.BlockSpec(memory_space=VMEM),
+        out_shape=jax.ShapeDtypeStruct(stat.shape, BF16),
+        compiler_params=pltpu.CompilerParams(vmem_limit_bytes=2 * MIB),
+        cost_estimate=CHEAP,
+        name="add_came",
+    )(stat, came)
+
+
 def merge_items_kernel(p, mine_ref, came_ref, out_ref):
     width = out_ref.shape[1]
     out_ref[...] = (mine_ref[:, p * width : (p + 1) * width] + came_ref[...].astype(F32)).astype(BF16)
@@ -336,7 +361,7 @@
     copies.append(pltpu.make_async_copy(bufs[0].at[pl.ds(start, half)], outs[0].at[pl.ds(start, half)], sems.at[0]))
     copies[-1].start()
 
-    total = sum_ref[...].astype(F32) + last_ref[...].astype(F32)
+    total = sum_ref[...].astype(F32) + last_ref[half : 2 * half, :].astype(F32)
     start = pl.multiple_of((1 - core) * half, half)
     bufs[0][pl.ds(start, half), :] = 0.3 + both_ref[half:, :].astype(F32) * total
     copies.append(pltpu.make_async_copy(bufs[0].at[pl.ds(start, half)], outs[0].at[pl.ds(start, half)], sems.at[1]))
@@ -439,7 +464,7 @@
     def sibling(x):
         return lax.ppermute(x, "ka", [(h, n_ka - 1 - h) for h in range(n_ka)])
 
-    both, item_exp, pack = expected(theta_shape[0], theta_rate[0], beta_shape[0], beta_rate[0])
+    both, wide, item_exp, pack = expected(theta_shape[0], theta_rate[0], beta_shape[0], beta_rate[0])
     rows = both.shape[0]
     half_rows = rows // 2
     item_rows = beta_shape.shape[1] * n_user
@@ -456,13 +481,13 @@
     pack, dense = lax.optimization_barrier((pack, dense))
     came_pack = sibling(pack)
 
-    places = [0]
-    for d in range(1, n_item // 2 + 1):
-        places += [d, -d][: n_item - len(places)]
-    shards = [both]
-    for i in range(1, n_item):
-        step = 1 if places[i] > 0 else -1
-        shards.append(along_item(shards[max(i - 2, 0)], step, n_item))
+    ahead = range(1, n_item // 2)
+    behind = range(1, n_item // 2 + 1)
+    shards = {0: both}
+    for d in behind:
+        shards[2 * d - 1] = along_item(shards[max(2 * d - 3, 0)], 1, n_item)
+    for d in ahead:
+        shards[2 * d] = along_item(after(wide, shards[1]) if d == 1 else shards[2 * d - 2], -1, n_item)
 
     item_mine = [item_exp]
     for p in range(1, n_user):
@@ -470,20 +495,28 @@
         item_mine.append(along_user(item_mine[p ^ low], low, n_user))
     item_other = [came_pack] + [sibling(x) for x in item_mine[1:]]
 
+    order = [2 * d - 1 for d in behind] + [2 * d for d in ahead]
+    order.insert(len(order) - 1, 0)
     acc = None
+    stats = {}
+    latest = None
+    for i in order:
+        other = sibling(shards[i][:rows]) if i else came_pack
+        stats[i], accs = statistics(
+            i, [shards[i], other], item_mine, item_other, dense, acc, i == order[-1], half_rows
+        )
+        acc = accs[0]
+        latest = stats[i][0]
+    own, own_other = stats[0]
+
     joined = []
-    latest = None
-    for i in list(range(1, n_item - 1)) + [0, n_item - 1]:
-        last = i == n_item - 1
-        passed = after(shards[i], latest) if last else shards[i]
-        other = sibling(passed) if i else came_pack
-        stats, accs = statistics(i, [shards[i], other], item_mine, item_other, dense, acc, last, half_rows)
-        acc = accs[0]
-        if i:
-            joined.append(along_item(stats[0], -places[i], n_item))
-            latest = stats[0] if latest is None else latest
-        else:
-            own, own_other = stats
+    for distances, step in ((ahead, 1), (behind, -1)):
+        moving = None
+        for d in reversed(distances):
+            stat = stats[2 * d - (step < 0)][0]
+            moving = along_item(stat if moving is None else add_came(stat, moving), step, n_item)
+        if moving is not None:
+            joined.append(moving)
 
     came = [sibling(accs[1])]
     for p in range(1, n_user):
@@ -496,7 +529,7 @@
         other_sum = lax.optimization_barrier(other_sum + x[half_rows:rows].astype(F32))
     other_sum = other_sum.astype(BF16)
     other_sum = sibling(other_sum)
-    other_last = sibling(after(joined[-1], other_sum)[half_rows:rows])
+    other_last = sibling(joined[-1])
     other_last = after(other_last, new_beta_shape)
     new_theta_shape, new_theta_rate, new_beta_rate = finish_users(
         both, own, other_sum, joined, other_last, item_mine, user_activity, item_popularity

time: 55.3 us -> 54.7 us (0.989)
  waiting for transfers between devices: 27.1 us -> 24.1 us
  starting transfers between devices: 12.4 us -> 14.6 us
    ppermute x6, waiting for transfers between devices: 25.6 us -> 22.7 us  [along_item(): return lax.ppermute(x, 'item', [(i, (i + shift) % n) for i in range(n)])]
    ppermute x6, starting transfers between devices: 8.26 us -> 10.4 us  [along_item(): return lax.ppermute(x, 'item', [(i, (i + shift) % n) for i in range(n)])]
  transfers between devices with their start and end apart: 17 -> 17, of which waited for: 7 -> 8; matrix products, arithmetic and copies ran while one was open for 0% -> 0% of each run, Pallas kernels for 18% -> 18%
where the time goes in v8:
time: 54.7 us; the launch traced here: 54.3 us
  waiting for transfers between devices  24.1 us (44%)
  starting transfers between devices  14.6 us (27%)
  Pallas kernels  14.1 us (26%)
  between operations  1.43 us (3%)
    ppermute x6, waiting for transfers between devices, along_item(): return lax.ppermute(x, 'item', [(i, (i + shift) % n) for i in range(n)])  22.7 us
    ppermute x6, starting transfers between devices, along_item(): return lax.ppermute(x, 'item', [(i, (i + shift) % n) for i in range(n)])  10.4 us
    pallas_call x4, Pallas kernels, statistics(): pl.pallas_call(functools.partial(stat_kernel, len(item_mine), half_rows,...  6.63 us
    ppermute x2, starting transfers between devices, along_user(): return lax.ppermute(x, 'user', [(i, i ^ distance) for i in range(n)])  2.9 us
    pallas_call x1, Pallas kernels, expected(): pl.pallas_call(functools.partial(expected_kernel, chunk_u, chunk_i), in_s...  2.76 us
    pallas_call x1, Pallas kernels, dense_counts(): pl.pallas_call(functools.partial(dense_kernel, n_item, item_rows // n_use...  2.24 us
    pallas_call x1, Pallas kernels, finish_users(): pl.pallas_call(functools.partial(finish_users_kernel, len(joined), len(it...  1.42 us
    ppermute x9, waiting for transfers between devices, sibling(): return lax.ppermute(x, 'ka', [(h, n_ka - 1 - h) for h in range(n_ka)])  1.38 us
  transfers between devices with their start and end apart: 17, of which 8 were waited for; matrix products, arithmetic and copies ran while one was open for 0% of the time, Pallas kernels for 18%

profile of v8, /device:TPU:0, one launch (start us, length us, event | category | flops | bytes accessed | tf_op | source)
XLA Modules:
  0.0 54.3 jit_solution(733124568267898033)
XLA Ops:
  0.6 2.8 %expected.1 = (bf16[512,256]{1,0:T(8,128)(2,1)S(1)}, bf16[544,256]{1,0:T(8,128)(2,1)S(1)}, bf16[528,256]{1,0:T(8,128)(2,1)S(1)}, bf16[784,256]{1,0:T(8,128)(2,1)S(1)}) custom-call(f32[512,256]{1,0:T(8,128)} %bitcast.14, f32[512,256]{1,0:T(8,128)} %bitcast.15, f32[512,256]{1,0:T(8,128)} %bitcast.16, f32[512,256]{1,0:T(8,128)} %bitcast.17), custom_call_target="tpu_custom_call" | custom-call | flops 1024 | bytes 1024 | tf_op jit(solution)/shard_map/expected/pallas_call | solution.py:123
  3.4 3.1 %collective-permute-start.3 = (bf16[512,256]{1,0:T(8,128)(2,1)S(1)}, bf16[512,256]{1,0:T(8,128)(2,1)S(1)}, u32[]{:S(2)}, u32[]{:S(2)}) collective-permute-start(bf16[512,256]{1,0:T(8,128)(2,1)S(1)} %get-tuple-element.26.refs_0_), channel_id=1, source_target_pairs={{0,4},{4,8},{8,12},{12,0},{1,5},{5,9},{9,13},{13,1},{2,6},{6,10},{... | collective-permute-start | bytes 786440 | tf_op jit(solution)/shard_map/ppermute | solution.py:438
  6.5 1.5 %collective-permute-start.1 = (bf16[528,256]{1,0:T(8,128)(2,1)S(1)}, bf16[528,256]{1,0:T(8,128)(2,1)S(1)}, u32[]{:S(2)}, u32[]{:S(2)}) collective-permute-start(bf16[528,256]{1,0:T(8,128)(2,1)S(1)} %get-tuple-element.29.refs_2_.exp_ref.refs_6_), channel_id=1, source_target_pairs={{0,2},{2,0},{1,3},{3,1},{4,6},{6,4},{5,7},{7,5},{8,10},{10,8},{9,1... | collective-permute-start | bytes 811016 | tf_op jit(solution)/shard_map/ppermute | solution.py:446
  8.0 6.8 %collective-permute-done.3.refs_0_ = bf16[512,256]{1,0:T(8,128)(2,1)S(1)} collective-permute-done((bf16[512,256]{1,0:T(8,128)(2,1)S(1)}, bf16[512,256]{1,0:T(8,128)(2,1)S(1)}, u32[]{:S(2)}, u32[]{:S(2)}) %collective-permute-start.3) | collective-permute-done | bytes 262176 | tf_op jit(solution)/shard_map/ppermute | solution.py:438
  15.5 2.2 %dense_counts.1.refs_6_ = bf16[1024,1024]{1,0:T(8,128)(2,1)S(1)} custom-call(s32[64]{0:T(128)} %bitcast.19, s32[64]{0:T(128)} %bitcast.20, s32[1]{0:T(128)} %bitcast.12.live_ref, s32[64,128,128]{2,1,0:T(8,128)} %bitcast.13), custom_call_target="tpu_custom_call" | custom-call | flops 1024 | bytes 1024 | tf_op jit(solution)/shard_map/dense_counts/pallas_call | solution.py:197
  17.8 0.5 collective-permute-start.2
  18.3 4.5 %collective-permute-start.7 = (bf16[544,256]{1,0:T(8,128)(2,1)S(1)}, bf16[544,256]{1,0:T(8,128)(2,1)S(1)}, u32[]{:S(2)}, u32[]{:S(2)}) collective-permute-start(bf16[544,256]{1,0:T(8,128)(2,1)S(1)} %get-tuple-element.36), channel_id=1, source_target_pairs={{0,12},{4,0},{8,4},{12,8},{1,13},{5,1},{9,5},{13,9},{2,14},{6,2},{... | collective-permute-start | bytes 835592 | tf_op jit(solution)/shard_map/ppermute | solution.py:438
  22.8 1.6 %collective-permute-done.4.refs_0_ = bf16[512,256]{1,0:T(8,128)(2,1)S(1)} collective-permute-done((bf16[512,256]{1,0:T(8,128)(2,1)S(1)}, bf16[512,256]{1,0:T(8,128)(2,1)S(1)}, u32[]{:S(2)}, u32[]{:S(2)}) %collective-permute-start.4) | collective-permute-done | bytes 262176 | tf_op jit(solution)/shard_map/ppermute | solution.py:438
  24.4 1.7 %statistics_1.1 = (bf16[528,256]{1,0:T(8,128)(2,1)S(1)}, f32[512,1024]{1,0:T(8,128)S(1)}) custom-call(bf16[512,256]{1,0:T(8,128)(2,1)S(1)} %collective-permute-done.3.refs_0_, bf16[512,256]{1,0:T(8,128)(2,1)S(1)} %collective-permute-done.6.refs_1_, bf16[528,256]{1,0:T(8,128)(2,1)S(1)} %get-tuple-element.29.refs_2_.exp_ref.refs_6_, ...), custom_call_target="tpu_custom_call" | custom-call | flops 1024 | bytes 1024 | tf_op jit(solution)/shard_map/statistics_1/pallas_call | solution.py:294
  26.1 1.7 %statistics_3.1 = (bf16[528,256]{1,0:T(8,128)(2,1)S(1)}, f32[512,1024]{1,0:T(8,128)S(1)}) custom-call(bf16[512,256]{1,0:T(8,128)(2,1)S(1)} %collective-permute-done.4.refs_0_, bf16[512,256]{1,0:T(8,128)(2,1)S(1)} %collective-permute-done.5.refs_1_, bf16[528,256]{1,0:T(8,128)(2,1)S(1)} %get-tuple-element.29.refs_2_.exp_ref.refs_6_, ...), custom_call_target="tpu_custom_call" | custom-call | flops 1024 | bytes 1024 | tf_op jit(solution)/shard_map/statistics_3/pallas_call | solution.py:294
  27.8 0.4 collective-permute-start.11
  28.2 1.9 %collective-permute-done.7.refs_0_ = bf16[544,256]{1,0:T(8,128)(2,1)S(1)} collective-permute-done((bf16[544,256]{1,0:T(8,128)(2,1)S(1)}, bf16[544,256]{1,0:T(8,128)(2,1)S(1)}, u32[]{:S(2)}, u32[]{:S(2)}) %collective-permute-start.7) | collective-permute-done | bytes 278560 | tf_op jit(solution)/shard_map/ppermute | solution.py:438
  30.2 1.7 %statistics_0.1 = (f32[256,256]{1,0:T(8,128)S(1)}, f32[256,256]{1,0:T(8,128)S(1)}, f32[512,1024]{1,0:T(8,128)S(1)}) custom-call(bf16[512,256]{1,0:T(8,128)(2,1)S(1)} %get-tuple-element.26.refs_0_, bf16[784,256]{1,0:T(8,128)(2,1)S(1)} %collective-permute-done.refs_4_.refs_1_, bf16[528,256]{1,0:T(8,128)(2,1)S(1)} %get-tuple-element.29.refs_2_.exp_ref.refs_6_, ...), custom_call_target="tpu_custom_call" | custom-call | flops 1024 | bytes 1024 | tf_op jit(solution)/shard_map/statistics_0/pallas_call | solution.py:294
  31.9 1.7 %statistics_2.1 = (bf16[528,256]{1,0:T(8,128)(2,1)S(1)}, f32[256,1024]{1,0:T(8,128)S(1)}, bf16[256,512]{1,0:T(8,128)(2,1)S(1)}, bf16[256,512]{1,0:T(8,128)(2,1)S(1)}) custom-call(bf16[544,256]{1,0:T(8,128)(2,1)S(1)} %collective-permute-done.7.refs_0_, bf16[512,256]{1,0:T(8,128)(2,1)S(1)} %collective-permute-done.8.refs_1_, ...), custom_call_target="tpu_custom_call" | custom-call | flops 1024 | bytes 1024 | tf_op jit(solution)/shard_map/statistics_2/pallas_call | solution.py:294
  33.5 3.2 %collective-permute-done.11.came_ref = bf16[528,256]{1,0:T(8,128)(2,1)S(1)} collective-permute-done((bf16[528,256]{1,0:T(8,128)(2,1)S(1)}, bf16[528,256]{1,0:T(8,128)(2,1)S(1)}, u32[]{:S(2)}, u32[]{:S(2)}) %collective-permute-start.11) | collective-permute-done | bytes 270368 | tf_op jit(solution)/shard_map/ppermute | solution.py:438
  36.8 2.4 %collective-permute-start.12 = (bf16[528,256]{1,0:T(8,128)(2,1)S(1)}, bf16[528,256]{1,0:T(8,128)(2,1)S(1)}, u32[]{:S(2)}, u32[]{:S(2)}) collective-permute-start(bf16[528,256]{1,0:T(8,128)(2,1)S(1)} %add_came.1), channel_id=1, source_target_pairs={{0,12},{4,0},{8,4},{12,8},{1,13},{5,1},{9,5},{13,9},{2,14},{6,2},{... | collective-permute-start | bytes 811016 | tf_op jit(solution)/shard_map/ppermute | solution.py:438
  39.2 0.5 collective-permute-start.14
  39.7 1.0 %collective-permute-done.15.came_ref = bf16[256,512]{1,0:T(8,128)(2,1)S(1)} collective-permute-done((bf16[256,512]{1,0:T(8,128)(2,1)S(1)}, bf16[256,512]{1,0:T(8,128)(2,1)S(1)}, u32[]{:S(2)}, u32[]{:S(2)}) %collective-permute-start.15) | collective-permute-done | bytes 262176 | tf_op jit(solution)/shard_map/ppermute | solution.py:465
  40.8 1.4 %collective-permute-start.16 = (bf16[256,512]{1,0:T(8,128)(2,1)S(1)}, bf16[256,512]{1,0:T(8,128)(2,1)S(1)}, u32[]{:S(2)}, u32[]{:S(2)}) collective-permute-start(bf16[256,512]{1,0:T(8,128)(2,1)S(1)} %merge_items.1), channel_id=1, source_target_pairs={{0,2},{2,0},{1,3},{3,1},{4,6},{6,4},{5,7},{7,5},{8,10},{10,8},{9,1... | collective-permute-start | bytes 786440 | tf_op jit(solution)/shard_map/ppermute | solution.py:446
  42.2 3.9 %collective-permute-done.12.refs_4_ = bf16[528,256]{1,0:T(8,128)(2,1)S(1)} collective-permute-done((bf16[528,256]{1,0:T(8,128)(2,1)S(1)}, bf16[528,256]{1,0:T(8,128)(2,1)S(1)}, u32[]{:S(2)}, u32[]{:S(2)}) %collective-permute-start.12) | collective-permute-done | bytes 270368 | tf_op jit(solution)/shard_map/ppermute | solution.py:438
  46.1 5.4 %collective-permute-done.9.refs_3_ = bf16[528,256]{1,0:T(8,128)(2,1)S(1)} collective-permute-done((bf16[528,256]{1,0:T(8,128)(2,1)S(1)}, bf16[528,256]{1,0:T(8,128)(2,1)S(1)}, u32[]{:S(2)}, u32[]{:S(2)}) %collective-permute-start.9) | collective-permute-done | bytes 270368 | tf_op jit(solution)/shard_map/ppermute | solution.py:438
  51.6 1.0 %finish_items.1 = f32[512,256]{1,0:T(8,128)} custom-call(bf16[528,256]{1,0:T(8,128)(2,1)S(1)} %get-tuple-element.29.refs_2_.exp_ref.refs_6_, f32[256,1024]{1,0:T(8,128)S(1)} %get-tuple-element.41.mine_ref.own_ref, bf16[256,512]{1,0:T(8,128)(2,1)S(1)} %collective-permute-done.14.refs_0_, bf16[256,512]{1,0:T(8,128)(2,1)S(1)} %collective-permute-done.16.refs_1_), custom_call_target="tpu_custom_call" | custom-call | flops 1024 | bytes 1024 | tf_op jit(solution)/shard_map/finish_items/pallas_call | solution.py:425
  52.6 0.3 collective-permute-done.10.refs_2_
  52.9 1.4 %finish_users.1 = (f32[512,256]{1,0:T(8,128)}, f32[512,256]{1,0:T(8,128)}, f32[512,256]{1,0:T(8,128)}) custom-call(bf16[512,256]{1,0:T(8,128)(2,1)S(1)} %get-tuple-element.26.refs_0_, f32[256,256]{1,0:T(8,128)S(1)} %get-tuple-element.33.refs_1_, bf16[256,256]{1,0:T(8,128)(2,1)S(1)} %collective-permute-done.10.refs_2_, ...), custom_call_target="tpu_custom_call" | custom-call | flops 1024 | bytes 1024 | tf_op jit(solution)/shard_map/finish_users/pallas_call | solution.py:393
  (26 shorter events, 0.5 us)
Async XLA Ops:
  3.4 11.4 %collective-permute-start.3 = (bf16[512,256]{1,0:T(8,128)(2,1)S(1)}, bf16[512,256]{1,0:T(8,128)(2,1)S(1)}, u32[]{:S(2)}, u32[]{:S(2)}) collective-permute-start(bf16[512,256]{1,0:T(8,128)(2,1)S(1)} %get-tuple-element.26.refs_0_), channel_id=1, source_target_pairs={{0,4},{4,8},{8,12},{12,0},{1,5},{5,9},{9,13},{13,1},{2,6},{6,10},{... | collective-permute-start | bytes 786440 | tf_op jit(solution)/shard_map/ppermute | solution.py:438
  6.5 11.3 %collective-permute-start.1 = (bf16[528,256]{1,0:T(8,128)(2,1)S(1)}, bf16[528,256]{1,0:T(8,128)(2,1)S(1)}, u32[]{:S(2)}, u32[]{:S(2)}) collective-permute-start(bf16[528,256]{1,0:T(8,128)(2,1)S(1)} %get-tuple-element.29.refs_2_.exp_ref.refs_6_), channel_id=1, source_target_pairs={{0,2},{2,0},{1,3},{3,1},{4,6},{6,4},{5,7},{7,5},{8,10},{10,8},{9,1... | collective-permute-start | bytes 811016 | tf_op jit(solution)/shard_map/ppermute | solution.py:446
  14.8 9.6 %collective-permute-start.4 = (bf16[512,256]{1,0:T(8,128)(2,1)S(1)}, bf16[512,256]{1,0:T(8,128)(2,1)S(1)}, u32[]{:S(2)}, u32[]{:S(2)}) collective-permute-start(bf16[512,256]{1,0:T(8,128)(2,1)S(1)} %collective-permute-done.3.refs_0_), channel_id=1, source_target_pairs={{0,4},{4,8},{8,12},{12,0},{1,5},{5,9},{9,13},{13,1},{2,6},{6,10},{... | collective-permute-start | bytes 786440 | tf_op jit(solution)/shard_map/ppermute | solution.py:438
  17.7 6.7 %collective-permute-start = (bf16[784,256]{1,0:T(8,128)(2,1)S(1)}, bf16[784,256]{1,0:T(8,128)(2,1)S(1)}, u32[]{:S(2)}, u32[]{:S(2)}) collective-permute-start(bf16[784,256]{1,0:T(8,128)(2,1)S(1)} %get-tuple-element.28), channel_id=1, source_target_pairs={{0,1},{1,0},{2,3},{3,2},{4,5},{5,4},{6,7},{7,6},{8,9},{9,8},{10,11... | collective-permute-start | bytes 1204232 | tf_op jit(solution)/shard_map/ppermute | solution.py:465
  17.8 6.6 %collective-permute-start.2 = (bf16[528,256]{1,0:T(8,128)(2,1)S(1)}, bf16[528,256]{1,0:T(8,128)(2,1)S(1)}, u32[]{:S(2)}, u32[]{:S(2)}) collective-permute-start(bf16[528,256]{1,0:T(8,128)(2,1)S(1)} %collective-permute-done.1.refs_3_.refs_7_), channel_id=1, source_target_pairs={{0,1},{1,0},{2,3},{3,2},{4,5},{5,4},{6,7},{7,6},{8,9},{9,8},{10,11... | collective-permute-start | bytes 811016 | tf_op jit(solution)/shard_map/ppermute | solution.py:465
  18.3 11.8 %collective-permute-start.7 = (bf16[544,256]{1,0:T(8,128)(2,1)S(1)}, bf16[544,256]{1,0:T(8,128)(2,1)S(1)}, u32[]{:S(2)}, u32[]{:S(2)}) collective-permute-start(bf16[544,256]{1,0:T(8,128)(2,1)S(1)} %get-tuple-element.36), channel_id=1, source_target_pairs={{0,12},{4,0},{8,4},{12,8},{1,13},{5,1},{9,5},{13,9},{2,14},{6,2},{... | collective-permute-start | bytes 835592 | tf_op jit(solution)/shard_map/ppermute | solution.py:438
  22.8 1.6 %collective-permute-start.6 = (bf16[512,256]{1,0:T(8,128)(2,1)S(1)}, bf16[512,256]{1,0:T(8,128)(2,1)S(1)}, u32[]{:S(2)}, u32[]{:S(2)}) collective-permute-start(bf16[512,256]{1,0:T(8,128)(2,1)S(1)} %collective-permute-done.3.refs_0_), channel_id=1, source_target_pairs={{0,1},{1,0},{2,3},{3,2},{4,5},{5,4},{6,7},{7,6},{8,9},{9,8},{10,11... | collective-permute-start | bytes 786440 | tf_op jit(solution)/shard_map/ppermute | solution.py:465
  24.4 1.7 %collective-permute-start.5 = (bf16[512,256]{1,0:T(8,128)(2,1)S(1)}, bf16[512,256]{1,0:T(8,128)(2,1)S(1)}, u32[]{:S(2)}, u32[]{:S(2)}) collective-permute-start(bf16[512,256]{1,0:T(8,128)(2,1)S(1)} %collective-permute-done.4.refs_0_), channel_id=1, source_target_pairs={{0,1},{1,0},{2,3},{3,2},{4,5},{5,4},{6,7},{7,6},{8,9},{9,8},{10,11... | collective-permute-start | bytes 786440 | tf_op jit(solution)/shard_map/ppermute | solution.py:465
  27.8 8.9 %collective-permute-start.11 = (bf16[528,256]{1,0:T(8,128)(2,1)S(1)}, bf16[528,256]{1,0:T(8,128)(2,1)S(1)}, u32[]{:S(2)}, u32[]{:S(2)}) collective-permute-start(bf16[528,256]{1,0:T(8,128)(2,1)S(1)} %get-tuple-element.40), channel_id=1, source_target_pairs={{0,12},{4,0},{8,4},{12,8},{1,13},{5,1},{9,5},{13,9},{2,14},{6,2},{... | collective-permute-start | bytes 811016 | tf_op jit(solution)/shard_map/ppermute | solution.py:438
  30.1 1.8 %collective-permute-start.8 = (bf16[512,256]{1,0:T(8,128)(2,1)S(1)}, bf16[512,256]{1,0:T(8,128)(2,1)S(1)}, u32[]{:S(2)}, u32[]{:S(2)}) collective-permute-start(bf16[512,256]{1,0:T(8,128)(2,1)S(1)} %slice.8), channel_id=1, source_target_pairs={{0,1},{1,0},{2,3},{3,2},{4,5},{5,4},{6,7},{7,6},{8,9},{9,8},{10,11... | collective-permute-start | bytes 786440 | tf_op jit(solution)/shard_map/ppermute | solution.py:465
  36.8 9.3 %collective-permute-start.12 = (bf16[528,256]{1,0:T(8,128)(2,1)S(1)}, bf16[528,256]{1,0:T(8,128)(2,1)S(1)}, u32[]{:S(2)}, u32[]{:S(2)}) collective-permute-start(bf16[528,256]{1,0:T(8,128)(2,1)S(1)} %add_came.1), channel_id=1, source_target_pairs={{0,12},{4,0},{8,4},{12,8},{1,13},{5,1},{9,5},{13,9},{2,14},{6,2},{... | collective-permute-start | bytes 811016 | tf_op jit(solution)/shard_map/ppermute | solution.py:438
  39.2 12.3 %collective-permute-start.9 = (bf16[528,256]{1,0:T(8,128)(2,1)S(1)}, bf16[528,256]{1,0:T(8,128)(2,1)S(1)}, u32[]{:S(2)}, u32[]{:S(2)}) collective-permute-start(bf16[528,256]{1,0:T(8,128)(2,1)S(1)} %get-tuple-element.38), channel_id=1, source_target_pairs={{0,4},{4,8},{8,12},{12,0},{1,5},{5,9},{9,13},{13,1},{2,6},{6,10},{... | collective-permute-start | bytes 811016 | tf_op jit(solution)/shard_map/ppermute | solution.py:438
  39.2 1.5 %collective-permute-start.15 = (bf16[256,512]{1,0:T(8,128)(2,1)S(1)}, bf16[256,512]{1,0:T(8,128)(2,1)S(1)}, u32[]{:S(2)}, u32[]{:S(2)}) collective-permute-start(bf16[256,512]{1,0:T(8,128)(2,1)S(1)} %get-tuple-element.43), channel_id=1, source_target_pairs={{0,1},{1,0},{2,3},{3,2},{4,5},{5,4},{6,7},{7,6},{8,9},{9,8},{10,11... | collective-permute-start | bytes 786440 | tf_op jit(solution)/shard_map/ppermute | solution.py:465
  39.2 12.4 %collective-permute-start.14 = (bf16[256,512]{1,0:T(8,128)(2,1)S(1)}, bf16[256,512]{1,0:T(8,128)(2,1)S(1)}, u32[]{:S(2)}, u32[]{:S(2)}) collective-permute-start(bf16[256,512]{1,0:T(8,128)(2,1)S(1)} %get-tuple-element.42), channel_id=1, source_target_pairs={{0,1},{1,0},{2,3},{3,2},{4,5},{5,4},{6,7},{7,6},{8,9},{9,8},{10,11... | collective-permute-start | bytes 786440 | tf_op jit(solution)/shard_map/ppermute | solution.py:465
  40.7 12.2 %copy-start = (f32[1,512]{1,0:T(1,128)S(1)}, f32[1,512]{1,0:T(1,128)}, u32[]{:S(2)}) copy-start(f32[1,512]{1,0:T(1,128)} %refs_8_.1) | copy-start | bytes 6148
  40.7 12.2 %copy-start.1 = (f32[1,512]{1,0:T(1,128)S(1)}, f32[1,512]{1,0:T(1,128)}, u32[]{:S(2)}) copy-start(f32[1,512]{1,0:T(1,128)} %refs_9_.1) | copy-start | bytes 6148
  40.8 10.8 %collective-permute-start.16 = (bf16[256,512]{1,0:T(8,128)(2,1)S(1)}, bf16[256,512]{1,0:T(8,128)(2,1)S(1)}, u32[]{:S(2)}, u32[]{:S(2)}) collective-permute-start(bf16[256,512]{1,0:T(8,128)(2,1)S(1)} %merge_items.1), channel_id=1, source_target_pairs={{0,2},{2,0},{1,3},{3,1},{4,6},{6,4},{5,7},{7,5},{8,10},{10,8},{9,1... | collective-permute-start | bytes 786440 | tf_op jit(solution)/shard_map/ppermute | solution.py:446
  46.1 6.5 %collective-permute-start.13 = (bf16[528,256]{1,0:T(8,128)(2,1)S(1)}, bf16[528,256]{1,0:T(8,128)(2,1)S(1)}, u32[]{:S(2)}, u32[]{:S(2)}) collective-permute-start(bf16[528,256]{1,0:T(8,128)(2,1)S(1)} %collective-permute-done.12.refs_4_), channel_id=1, source_target_pairs={{0,1},{1,0},{2,3},{3,2},{4,5},{5,4},{6,7},{7,6},{8,9},{9,8},{10,11... | collective-permute-start | bytes 811016 | tf_op jit(solution)/shard_map/ppermute | solution.py:465
  51.5 1.4 %collective-permute-start.10 = (bf16[256,256]{1,0:T(8,128)(2,1)S(1)}, bf16[256,256]{1,0:T(8,128)(2,1)S(1)}, u32[]{:S(2)}, u32[]{:S(2)}) collective-permute-start(bf16[256,256]{1,0:T(8,128)(2,1)S(1)} %convert_add_fusion), channel_id=1, source_target_pairs={{0,1},{1,0},{2,3},{3,2},{4,5},{5,4},{6,7},{7,6},{8,9},{9,8},{10,11... | collective-permute-start | bytes 393224 | tf_op jit(solution)/shard_map/ppermute | solution.py:465

commit v9 on v8

--- a/solution.py
+++ b/solution.py
@@ -107,7 +107,7 @@
         item_ref[start : start + chunk_i, :] = value
         pack_ref[half + start : half + start + chunk_i, :] = value
         beta_total += jnp.sum(x * inv_rate, axis=0, keepdims=True)
-    wide_ref[2 * half :, :] = jnp.zeros((2 * EXTRA, wide_ref.shape[1]), BF16)
+    wide_ref[2 * half :, :] = jnp.zeros((3 * EXTRA, wide_ref.shape[1]), BF16)
     extra = encode([theta_total, beta_total])
     item_ref[rows:, :] = extra
     pack_ref[half + rows :, :] = extra
@@ -119,7 +119,7 @@
     half = rows // 2
     chunk_u = min(half, 128)
     chunk_i = min(item_rows, 128)
-    shapes = [rows, rows + 2 * EXTRA, item_rows + EXTRA, half + item_rows + EXTRA]
+    shapes = [rows, rows + 3 * EXTRA, item_rows + EXTRA, half + item_rows + EXTRA]
     return pl.pallas_call(
         functools.partial(expected_kernel, chunk_u, chunk_i),
         in_specs=[pl.BlockSpec(memory_space=HBM)] * 4,
@@ -217,7 +217,7 @@
     take = lambda n: [refs.pop(0) for _ in range(n)]
     mine_ref, other_ref = take(2)
     mine = mine_ref[:half, :]
-    other = other_ref[half : 2 * half, :] if at else other_ref[:half, :]
+    other = other_ref[half : 2 * half, :] if at and not last else other_ref[:half, :]
     item_mine = take(pieces)
     item_other = take(pieces)
     (counts_ref,) = take(1)
@@ -361,7 +361,7 @@
     copies.append(pltpu.make_async_copy(bufs[0].at[pl.ds(start, half)], outs[0].at[pl.ds(start, half)], sems.at[0]))
     copies[-1].start()
 
-    total = sum_ref[...].astype(F32) + last_ref[half : 2 * half, :].astype(F32)
+    total = sum_ref[:half, :].astype(F32) + last_ref[...].astype(F32)
     start = pl.multiple_of((1 - core) * half, half)
     bufs[0][pl.ds(start, half), :] = 0.3 + both_ref[half:, :].astype(F32) * total
     copies.append(pltpu.make_async_copy(bufs[0].at[pl.ds(start, half)], outs[0].at[pl.ds(start, half)], sems.at[1]))
@@ -478,7 +478,6 @@
         item_rows,
         n_user,
     )
-    pack, dense = lax.optimization_barrier((pack, dense))
     came_pack = sibling(pack)
 
     ahead = range(1, n_item // 2)
@@ -492,7 +491,7 @@
     item_mine = [item_exp]
     for p in range(1, n_user):
         low = p & -p
-        item_mine.append(along_user(item_mine[p ^ low], low, n_user))
+        item_mine.append(along_user(after(item_mine[p ^ low], dense), low, n_user))
     item_other = [came_pack] + [sibling(x) for x in item_mine[1:]]
 
     order = [2 * d - 1 for d in behind] + [2 * d for d in ahead]
@@ -501,7 +500,8 @@
     stats = {}
     latest = None
     for i in order:
-        other = sibling(shards[i][:rows]) if i else came_pack
+        passed = after(shards[i], stats[n_item - 1][0])[half_rows:rows] if i == order[-1] else shards[i]
+        other = sibling(passed) if i else came_pack
         stats[i], accs = statistics(
             i, [shards[i], other], item_mine, item_other, dense, acc, i == order[-1], half_rows
         )
@@ -528,8 +528,8 @@
     for x in joined[:-1]:
         other_sum = lax.optimization_barrier(other_sum + x[half_rows:rows].astype(F32))
     other_sum = other_sum.astype(BF16)
-    other_sum = sibling(other_sum)
-    other_last = sibling(joined[-1])
+    other_sum = sibling(jnp.concatenate([other_sum, other_sum[: half_rows // 2]]))
+    other_last = sibling(joined[-1][half_rows:rows])
     other_last = after(other_last, new_beta_shape)
     new_theta_shape, new_theta_rate, new_beta_rate = finish_users(
         both, own, other_sum, joined, other_last, item_mine, user_activity, item_popularity

time: 54.7 us -> 53.9 us (0.985)
  waiting for transfers between devices: 24.1 us -> 21.7 us
  starting transfers between devices: 14.6 us -> 16.3 us
    ppermute x6, starting transfers between devices: 10.4 us -> 12.1 us  [along_item(): return lax.ppermute(x, 'item', [(i, (i + shift) % n) for i in range(n)])]
    ppermute x6, waiting for transfers between devices: 22.7 us -> 21.3 us  [along_item(): return lax.ppermute(x, 'item', [(i, (i + shift) % n) for i in range(n)])]
    ppermute x9, waiting for transfers between devices: 1.38 us -> 0.37 us  [sibling(): return lax.ppermute(x, 'ka', [(h, n_ka - 1 - h) for h in range(n_ka)])]
  transfers between devices with their start and end apart: 17 -> 17, of which waited for: 8 -> 7; matrix products, arithmetic and copies ran while one was open for 0% -> 0% of each run, Pallas kernels for 18% -> 19%
where the time goes in v9:
time: 53.9 us; the launch traced here: 53.7 us
  waiting for transfers between devices  21.7 us (40%)
  starting transfers between devices  16.3 us (30%)
  Pallas kernels  14.2 us (26%)
  between operations  1.45 us (3%)
    ppermute x6, waiting for transfers between devices, along_item(): return lax.ppermute(x, 'item', [(i, (i + shift) % n) for i in range(n)])  21.3 us
    ppermute x6, starting transfers between devices, along_item(): return lax.ppermute(x, 'item', [(i, (i + shift) % n) for i in range(n)])  12.1 us
    pallas_call x4, Pallas kernels, statistics(): pl.pallas_call(functools.partial(stat_kernel, len(item_mine), half_rows,...  6.66 us
    ppermute x2, starting transfers between devices, along_user(): return lax.ppermute(x, 'user', [(i, i ^ distance) for i in range(n)])  2.87 us
    pallas_call x1, Pallas kernels, expected(): pl.pallas_call(functools.partial(expected_kernel, chunk_u, chunk_i), in_s...  2.76 us
    pallas_call x1, Pallas kernels, dense_counts(): pl.pallas_call(functools.partial(dense_kernel, n_item, item_rows // n_use...  2.24 us
    pallas_call x1, Pallas kernels, finish_users(): pl.pallas_call(functools.partial(finish_users_kernel, len(joined), len(it...  1.42 us
    ppermute x9, starting transfers between devices, sibling(): return lax.ppermute(x, 'ka', [(h, n_ka - 1 - h) for h in range(n_ka)])  1.32 us
  transfers between devices with their start and end apart: 17, of which 7 were waited for; matrix products, arithmetic and copies ran while one was open for 0% of the time, Pallas kernels for 19%

profile of v9, /device:TPU:0, one launch (start us, length us, event | category | flops | bytes accessed | tf_op | source)
XLA Modules:
  0.0 53.7 jit_solution(1341427893747548923)
XLA Ops:
  0.6 2.8 %expected.1 = (bf16[512,256]{1,0:T(8,128)(2,1)S(1)}, bf16[560,256]{1,0:T(8,128)(2,1)S(1)}, bf16[528,256]{1,0:T(8,128)(2,1)S(1)}, bf16[784,256]{1,0:T(8,128)(2,1)S(1)}) custom-call(f32[512,256]{1,0:T(8,128)} %bitcast.14, f32[512,256]{1,0:T(8,128)} %bitcast.15, f32[512,256]{1,0:T(8,128)} %bitcast.16, f32[512,256]{1,0:T(8,128)} %bitcast.17), custom_call_target="tpu_custom_call" | custom-call | flops 1024 | bytes 1024 | tf_op jit(solution)/shard_map/expected/pallas_call | solution.py:123
  3.4 3.1 %collective-permute-start.3 = (bf16[512,256]{1,0:T(8,128)(2,1)S(1)}, bf16[512,256]{1,0:T(8,128)(2,1)S(1)}, u32[]{:S(2)}, u32[]{:S(2)}) collective-permute-start(bf16[512,256]{1,0:T(8,128)(2,1)S(1)} %get-tuple-element.26.refs_0_), channel_id=1, source_target_pairs={{0,4},{4,8},{8,12},{12,0},{1,5},{5,9},{9,13},{13,1},{2,6},{6,10},{... | collective-permute-start | bytes 786440 | tf_op jit(solution)/shard_map/ppermute | solution.py:438
  7.1 2.2 %dense_counts.1.refs_6_ = bf16[1024,1024]{1,0:T(8,128)(2,1)S(1)} custom-call(s32[64]{0:T(128)} %bitcast.19, s32[64]{0:T(128)} %bitcast.20, s32[1]{0:T(128)} %bitcast.12.live_ref, s32[64,128,128]{2,1,0:T(8,128)} %bitcast.13), custom_call_target="tpu_custom_call" | custom-call | flops 1024 | bytes 1024 | tf_op jit(solution)/shard_map/dense_counts/pallas_call | solution.py:197
  9.4 1.6 %collective-permute-start.1 = (bf16[528,256]{1,0:T(8,128)(2,1)S(1)}, bf16[528,256]{1,0:T(8,128)(2,1)S(1)}, u32[]{:S(2)}, u32[]{:S(2)}) collective-permute-start(bf16[528,256]{1,0:T(8,128)(2,1)S(1)} %get-tuple-element.29.refs_2_.exp_ref.refs_6_), channel_id=1, source_target_pairs={{0,2},{2,0},{1,3},{3,1},{4,6},{6,4},{5,7},{7,5},{8,10},{10,8},{9,1... | collective-permute-start | bytes 811016 | tf_op jit(solution)/shard_map/ppermute | solution.py:446
  10.9 3.9 %collective-permute-done.3.refs_0_ = bf16[512,256]{1,0:T(8,128)(2,1)S(1)} collective-permute-done((bf16[512,256]{1,0:T(8,128)(2,1)S(1)}, bf16[512,256]{1,0:T(8,128)(2,1)S(1)}, u32[]{:S(2)}, u32[]{:S(2)}) %collective-permute-start.3) | collective-permute-done | bytes 262176 | tf_op jit(solution)/shard_map/ppermute | solution.py:438
  14.8 3.8 %collective-permute-start.7 = (bf16[560,256]{1,0:T(8,128)(2,1)S(1)}, bf16[560,256]{1,0:T(8,128)(2,1)S(1)}, u32[]{:S(2)}, u32[]{:S(2)}) collective-permute-start(bf16[560,256]{1,0:T(8,128)(2,1)S(1)} %get-tuple-element.35), channel_id=1, source_target_pairs={{0,12},{4,0},{8,4},{12,8},{1,13},{5,1},{9,5},{13,9},{2,14},{6,2},{... | collective-permute-start | bytes 860168 | tf_op jit(solution)/shard_map/ppermute | solution.py:438
  18.9 0.3 collective-permute-start.6
  19.1 6.7 %collective-permute-done.4.refs_0_ = bf16[512,256]{1,0:T(8,128)(2,1)S(1)} collective-permute-done((bf16[512,256]{1,0:T(8,128)(2,1)S(1)}, bf16[512,256]{1,0:T(8,128)(2,1)S(1)}, u32[]{:S(2)}, u32[]{:S(2)}) %collective-permute-start.4) | collective-permute-done | bytes 262176 | tf_op jit(solution)/shard_map/ppermute | solution.py:438
  25.9 1.7 %statistics_1.1 = (bf16[528,256]{1,0:T(8,128)(2,1)S(1)}, f32[512,1024]{1,0:T(8,128)S(1)}) custom-call(bf16[512,256]{1,0:T(8,128)(2,1)S(1)} %collective-permute-done.3.refs_0_, bf16[512,256]{1,0:T(8,128)(2,1)S(1)} %collective-permute-done.6.refs_1_, bf16[528,256]{1,0:T(8,128)(2,1)S(1)} %get-tuple-element.29.refs_2_.exp_ref.refs_6_, ...), custom_call_target="tpu_custom_call" | custom-call | flops 1024 | bytes 1024 | tf_op jit(solution)/shard_map/statistics_1/pallas_call | solution.py:294
  27.6 1.7 %statistics_3.1 = (bf16[528,256]{1,0:T(8,128)(2,1)S(1)}, f32[512,1024]{1,0:T(8,128)S(1)}) custom-call(bf16[512,256]{1,0:T(8,128)(2,1)S(1)} %collective-permute-done.4.refs_0_, bf16[512,256]{1,0:T(8,128)(2,1)S(1)} %collective-permute-done.5.refs_1_, bf16[528,256]{1,0:T(8,128)(2,1)S(1)} %get-tuple-element.29.refs_2_.exp_ref.refs_6_, ...), custom_call_target="tpu_custom_call" | custom-call | flops 1024 | bytes 1024 | tf_op jit(solution)/shard_map/statistics_3/pallas_call | solution.py:294
  29.3 0.4 collective-permute-done.7.refs_0_
  29.8 0.8 %collective-permute-start.11 = (bf16[528,256]{1,0:T(8,128)(2,1)S(1)}, bf16[528,256]{1,0:T(8,128)(2,1)S(1)}, u32[]{:S(2)}, u32[]{:S(2)}) collective-permute-start(bf16[528,256]{1,0:T(8,128)(2,1)S(1)} %get-tuple-element.36), channel_id=1, source_target_pairs={{0,12},{4,0},{8,4},{12,8},{1,13},{5,1},{9,5},{13,9},{2,14},{6,2},{... | collective-permute-start | bytes 811016 | tf_op jit(solution)/shard_map/ppermute | solution.py:438
  30.7 1.7 %statistics_0.1 = (f32[256,256]{1,0:T(8,128)S(1)}, f32[256,256]{1,0:T(8,128)S(1)}, f32[512,1024]{1,0:T(8,128)S(1)}) custom-call(bf16[512,256]{1,0:T(8,128)(2,1)S(1)} %get-tuple-element.26.refs_0_, bf16[784,256]{1,0:T(8,128)(2,1)S(1)} %collective-permute-done.refs_4_.refs_1_, bf16[528,256]{1,0:T(8,128)(2,1)S(1)} %get-tuple-element.29.refs_2_.exp_ref.refs_6_, ...), custom_call_target="tpu_custom_call" | custom-call | flops 1024 | bytes 1024 | tf_op jit(solution)/shard_map/statistics_0/pallas_call | solution.py:294
  32.4 1.7 %statistics_2.1 = (bf16[528,256]{1,0:T(8,128)(2,1)S(1)}, f32[256,1024]{1,0:T(8,128)S(1)}, bf16[256,512]{1,0:T(8,128)(2,1)S(1)}, bf16[256,512]{1,0:T(8,128)(2,1)S(1)}) custom-call(bf16[560,256]{1,0:T(8,128)(2,1)S(1)} %collective-permute-done.7.refs_0_, bf16[256,256]{1,0:T(8,128)(2,1)S(1)} %collective-permute-done.8.refs_1_, ...), custom_call_target="tpu_custom_call" | custom-call | flops 1024 | bytes 1024 | tf_op jit(solution)/shard_map/statistics_2/pallas_call | solution.py:294
  34.0 1.3 %collective-permute-start.9 = (bf16[528,256]{1,0:T(8,128)(2,1)S(1)}, bf16[528,256]{1,0:T(8,128)(2,1)S(1)}, u32[]{:S(2)}, u32[]{:S(2)}) collective-permute-start(bf16[528,256]{1,0:T(8,128)(2,1)S(1)} %get-tuple-element.39), channel_id=1, source_target_pairs={{0,4},{4,8},{8,12},{12,0},{1,5},{5,9},{9,13},{13,1},{2,6},{6,10},{... | collective-permute-start | bytes 811016 | tf_op jit(solution)/shard_map/ppermute | solution.py:438
  35.3 0.5 collective-permute-start.14
  35.8 2.9 %collective-permute-done.11.came_ref = bf16[528,256]{1,0:T(8,128)(2,1)S(1)} collective-permute-done((bf16[528,256]{1,0:T(8,128)(2,1)S(1)}, bf16[528,256]{1,0:T(8,128)(2,1)S(1)}, u32[]{:S(2)}, u32[]{:S(2)}) %collective-permute-start.11) | collective-permute-done | bytes 270368 | tf_op jit(solution)/shard_map/ppermute | solution.py:438
  38.7 3.1 %collective-permute-start.12 = (bf16[528,256]{1,0:T(8,128)(2,1)S(1)}, bf16[528,256]{1,0:T(8,128)(2,1)S(1)}, u32[]{:S(2)}, u32[]{:S(2)}) collective-permute-start(bf16[528,256]{1,0:T(8,128)(2,1)S(1)} %add_came.1), channel_id=1, source_target_pairs={{0,12},{4,0},{8,4},{12,8},{1,13},{5,1},{9,5},{13,9},{2,14},{6,2},{... | collective-permute-start | bytes 811016 | tf_op jit(solution)/shard_map/ppermute | solution.py:438
  42.0 1.3 %collective-permute-start.16 = (bf16[256,512]{1,0:T(8,128)(2,1)S(1)}, bf16[256,512]{1,0:T(8,128)(2,1)S(1)}, u32[]{:S(2)}, u32[]{:S(2)}) collective-permute-start(bf16[256,512]{1,0:T(8,128)(2,1)S(1)} %merge_items.1), channel_id=1, source_target_pairs={{0,2},{2,0},{1,3},{3,1},{4,6},{6,4},{5,7},{7,5},{8,10},{10,8},{9,1... | collective-permute-start | bytes 786440 | tf_op jit(solution)/shard_map/ppermute | solution.py:446
  43.3 2.3 %collective-permute-done.9.refs_3_ = bf16[528,256]{1,0:T(8,128)(2,1)S(1)} collective-permute-done((bf16[528,256]{1,0:T(8,128)(2,1)S(1)}, bf16[528,256]{1,0:T(8,128)(2,1)S(1)}, u32[]{:S(2)}, u32[]{:S(2)}) %collective-permute-start.9) | collective-permute-done | bytes 270368 | tf_op jit(solution)/shard_map/ppermute | solution.py:438
  45.7 5.2 %collective-permute-done.12.refs_4_ = bf16[528,256]{1,0:T(8,128)(2,1)S(1)} collective-permute-done((bf16[528,256]{1,0:T(8,128)(2,1)S(1)}, bf16[528,256]{1,0:T(8,128)(2,1)S(1)}, u32[]{:S(2)}, u32[]{:S(2)}) %collective-permute-start.12) | collective-permute-done | bytes 270368 | tf_op jit(solution)/shard_map/ppermute | solution.py:438
  51.0 1.0 %finish_items.1 = f32[512,256]{1,0:T(8,128)} custom-call(bf16[528,256]{1,0:T(8,128)(2,1)S(1)} %get-tuple-element.29.refs_2_.exp_ref.refs_6_, f32[256,1024]{1,0:T(8,128)S(1)} %get-tuple-element.41.mine_ref.own_ref, bf16[256,512]{1,0:T(8,128)(2,1)S(1)} %collective-permute-done.14.refs_0_, bf16[256,512]{1,0:T(8,128)(2,1)S(1)} %collective-permute-done.16.refs_1_), custom_call_target="tpu_custom_call" | custom-call | flops 1024 | bytes 1024 | tf_op jit(solution)/shard_map/finish_items/pallas_call | solution.py:425
  51.9 0.3 collective-permute-done.13.refs_5_
  52.3 1.4 %finish_users.1 = (f32[512,256]{1,0:T(8,128)}, f32[512,256]{1,0:T(8,128)}, f32[512,256]{1,0:T(8,128)}) custom-call(bf16[512,256]{1,0:T(8,128)(2,1)S(1)} %get-tuple-element.26.refs_0_, f32[256,256]{1,0:T(8,128)S(1)} %get-tuple-element.32.refs_1_, bf16[384,256]{1,0:T(8,128)(2,1)S(1)} %collective-permute-done.10.refs_2_, ...), custom_call_target="tpu_custom_call" | custom-call | flops 1024 | bytes 1024 | tf_op jit(solution)/shard_map/finish_users/pallas_call | solution.py:393
  (29 shorter events, 0.8 us)
Async XLA Ops:
  3.4 11.4 %collective-permute-start.3 = (bf16[512,256]{1,0:T(8,128)(2,1)S(1)}, bf16[512,256]{1,0:T(8,128)(2,1)S(1)}, u32[]{:S(2)}, u32[]{:S(2)}) collective-permute-start(bf16[512,256]{1,0:T(8,128)(2,1)S(1)} %get-tuple-element.26.refs_0_), channel_id=1, source_target_pairs={{0,4},{4,8},{8,12},{12,0},{1,5},{5,9},{9,13},{13,1},{2,6},{6,10},{... | collective-permute-start | bytes 786440 | tf_op jit(solution)/shard_map/ppermute | solution.py:438
  9.4 9.3 %collective-permute-start.1 = (bf16[528,256]{1,0:T(8,128)(2,1)S(1)}, bf16[528,256]{1,0:T(8,128)(2,1)S(1)}, u32[]{:S(2)}, u32[]{:S(2)}) collective-permute-start(bf16[528,256]{1,0:T(8,128)(2,1)S(1)} %get-tuple-element.29.refs_2_.exp_ref.refs_6_), channel_id=1, source_target_pairs={{0,2},{2,0},{1,3},{3,1},{4,6},{6,4},{5,7},{7,5},{8,10},{10,8},{9,1... | collective-permute-start | bytes 811016 | tf_op jit(solution)/shard_map/ppermute | solution.py:446
  14.8 11.1 %collective-permute-start.4 = (bf16[512,256]{1,0:T(8,128)(2,1)S(1)}, bf16[512,256]{1,0:T(8,128)(2,1)S(1)}, u32[]{:S(2)}, u32[]{:S(2)}) collective-permute-start(bf16[512,256]{1,0:T(8,128)(2,1)S(1)} %collective-permute-done.3.refs_0_), channel_id=1, source_target_pairs={{0,4},{4,8},{8,12},{12,0},{1,5},{5,9},{9,13},{13,1},{2,6},{6,10},{... | collective-permute-start | bytes 786440 | tf_op jit(solution)/shard_map/ppermute | solution.py:438
  14.8 11.1 %collective-permute-start = (bf16[784,256]{1,0:T(8,128)(2,1)S(1)}, bf16[784,256]{1,0:T(8,128)(2,1)S(1)}, u32[]{:S(2)}, u32[]{:S(2)}) collective-permute-start(bf16[784,256]{1,0:T(8,128)(2,1)S(1)} %get-tuple-element.27), channel_id=1, source_target_pairs={{0,1},{1,0},{2,3},{3,2},{4,5},{5,4},{6,7},{7,6},{8,9},{9,8},{10,11... | collective-permute-start | bytes 1204232 | tf_op jit(solution)/shard_map/ppermute | solution.py:465
  14.8 14.9 %collective-permute-start.7 = (bf16[560,256]{1,0:T(8,128)(2,1)S(1)}, bf16[560,256]{1,0:T(8,128)(2,1)S(1)}, u32[]{:S(2)}, u32[]{:S(2)}) collective-permute-start(bf16[560,256]{1,0:T(8,128)(2,1)S(1)} %get-tuple-element.35), channel_id=1, source_target_pairs={{0,12},{4,0},{8,4},{12,8},{1,13},{5,1},{9,5},{13,9},{2,14},{6,2},{... | collective-permute-start | bytes 860168 | tf_op jit(solution)/shard_map/ppermute | solution.py:438
  18.6 7.3 %collective-permute-start.2 = (bf16[528,256]{1,0:T(8,128)(2,1)S(1)}, bf16[528,256]{1,0:T(8,128)(2,1)S(1)}, u32[]{:S(2)}, u32[]{:S(2)}) collective-permute-start(bf16[528,256]{1,0:T(8,128)(2,1)S(1)} %collective-permute-done.1.refs_3_.refs_7_), channel_id=1, source_target_pairs={{0,1},{1,0},{2,3},{3,2},{4,5},{5,4},{6,7},{7,6},{8,9},{9,8},{10,11... | collective-permute-start | bytes 811016 | tf_op jit(solution)/shard_map/ppermute | solution.py:465
  18.9 7.0 %collective-permute-start.6 = (bf16[512,256]{1,0:T(8,128)(2,1)S(1)}, bf16[512,256]{1,0:T(8,128)(2,1)S(1)}, u32[]{:S(2)}, u32[]{:S(2)}) collective-permute-start(bf16[512,256]{1,0:T(8,128)(2,1)S(1)} %collective-permute-done.3.refs_0_), channel_id=1, source_target_pairs={{0,1},{1,0},{2,3},{3,2},{4,5},{5,4},{6,7},{7,6},{8,9},{9,8},{10,11... | collective-permute-start | bytes 786440 | tf_op jit(solution)/shard_map/ppermute | solution.py:465
  25.9 1.7 %collective-permute-start.5 = (bf16[512,256]{1,0:T(8,128)(2,1)S(1)}, bf16[512,256]{1,0:T(8,128)(2,1)S(1)}, u32[]{:S(2)}, u32[]{:S(2)}) collective-permute-start(bf16[512,256]{1,0:T(8,128)(2,1)S(1)} %collective-permute-done.4.refs_0_), channel_id=1, source_target_pairs={{0,1},{1,0},{2,3},{3,2},{4,5},{5,4},{6,7},{7,6},{8,9},{9,8},{10,11... | collective-permute-start | bytes 786440 | tf_op jit(solution)/shard_map/ppermute | solution.py:465
  29.7 2.7 %collective-permute-start.8 = (bf16[256,256]{1,0:T(8,128)(2,1)S(1)}, bf16[256,256]{1,0:T(8,128)(2,1)S(1)}, u32[]{:S(2)}, u32[]{:S(2)}) collective-permute-start(bf16[256,256]{1,0:T(8,128)(2,1)S(1)} %slice.12), channel_id=1, source_target_pairs={{0,1},{1,0},{2,3},{3,2},{4,5},{5,4},{6,7},{7,6},{8,9},{9,8},{10,11... | collective-permute-start | bytes 393224 | tf_op jit(solution)/shard_map/ppermute | solution.py:465
  29.8 8.8 %collective-permute-start.11 = (bf16[528,256]{1,0:T(8,128)(2,1)S(1)}, bf16[528,256]{1,0:T(8,128)(2,1)S(1)}, u32[]{:S(2)}, u32[]{:S(2)}) collective-permute-start(bf16[528,256]{1,0:T(8,128)(2,1)S(1)} %get-tuple-element.36), channel_id=1, source_target_pairs={{0,12},{4,0},{8,4},{12,8},{1,13},{5,1},{9,5},{13,9},{2,14},{6,2},{... | collective-permute-start | bytes 811016 | tf_op jit(solution)/shard_map/ppermute | solution.py:438
  34.0 11.5 %collective-permute-start.9 = (bf16[528,256]{1,0:T(8,128)(2,1)S(1)}, bf16[528,256]{1,0:T(8,128)(2,1)S(1)}, u32[]{:S(2)}, u32[]{:S(2)}) collective-permute-start(bf16[528,256]{1,0:T(8,128)(2,1)S(1)} %get-tuple-element.39), channel_id=1, source_target_pairs={{0,4},{4,8},{8,12},{12,0},{1,5},{5,9},{9,13},{13,1},{2,6},{6,10},{... | collective-permute-start | bytes 811016 | tf_op jit(solution)/shard_map/ppermute | solution.py:438
  35.3 6.6 %collective-permute-start.15 = (bf16[256,512]{1,0:T(8,128)(2,1)S(1)}, bf16[256,512]{1,0:T(8,128)(2,1)S(1)}, u32[]{:S(2)}, u32[]{:S(2)}) collective-permute-start(bf16[256,512]{1,0:T(8,128)(2,1)S(1)} %get-tuple-element.43), channel_id=1, source_target_pairs={{0,1},{1,0},{2,3},{3,2},{4,5},{5,4},{6,7},{7,6},{8,9},{9,8},{10,11... | collective-permute-start | bytes 786440 | tf_op jit(solution)/shard_map/ppermute | solution.py:465
  35.3 15.7 %collective-permute-start.14 = (bf16[256,512]{1,0:T(8,128)(2,1)S(1)}, bf16[256,512]{1,0:T(8,128)(2,1)S(1)}, u32[]{:S(2)}, u32[]{:S(2)}) collective-permute-start(bf16[256,512]{1,0:T(8,128)(2,1)S(1)} %get-tuple-element.42), channel_id=1, source_target_pairs={{0,1},{1,0},{2,3},{3,2},{4,5},{5,4},{6,7},{7,6},{8,9},{9,8},{10,11... | collective-permute-start | bytes 786440 | tf_op jit(solution)/shard_map/ppermute | solution.py:465
  38.7 12.1 %collective-permute-start.12 = (bf16[528,256]{1,0:T(8,128)(2,1)S(1)}, bf16[528,256]{1,0:T(8,128)(2,1)S(1)}, u32[]{:S(2)}, u32[]{:S(2)}) collective-permute-start(bf16[528,256]{1,0:T(8,128)(2,1)S(1)} %add_came.1), channel_id=1, source_target_pairs={{0,12},{4,0},{8,4},{12,8},{1,13},{5,1},{9,5},{13,9},{2,14},{6,2},{... | collective-permute-start | bytes 811016 | tf_op jit(solution)/shard_map/ppermute | solution.py:438
  41.9 10.3 %copy-start = (f32[1,512]{1,0:T(1,128)S(1)}, f32[1,512]{1,0:T(1,128)}, u32[]{:S(2)}) copy-start(f32[1,512]{1,0:T(1,128)} %refs_8_.1) | copy-start | bytes 6148
  42.0 10.3 %copy-start.1 = (f32[1,512]{1,0:T(1,128)S(1)}, f32[1,512]{1,0:T(1,128)}, u32[]{:S(2)}) copy-start(f32[1,512]{1,0:T(1,128)} %refs_9_.1) | copy-start | bytes 6148
  42.0 9.0 %collective-permute-start.16 = (bf16[256,512]{1,0:T(8,128)(2,1)S(1)}, bf16[256,512]{1,0:T(8,128)(2,1)S(1)}, u32[]{:S(2)}, u32[]{:S(2)}) collective-permute-start(bf16[256,512]{1,0:T(8,128)(2,1)S(1)} %merge_items.1), channel_id=1, source_target_pairs={{0,2},{2,0},{1,3},{3,1},{4,6},{6,4},{5,7},{7,5},{8,10},{10,8},{9,1... | collective-permute-start | bytes 786440 | tf_op jit(solution)/shard_map/ppermute | solution.py:446
  45.6 6.7 %collective-permute-start.10 = (bf16[384,256]{1,0:T(8,128)(2,1)S(1)}, bf16[384,256]{1,0:T(8,128)(2,1)S(1)}, u32[]{:S(2)}, u32[]{:S(2)}) collective-permute-start(bf16[384,256]{1,0:T(8,128)(2,1)S(1)} %pad_maximum_fusion), channel_id=1, source_target_pairs={{0,1},{1,0},{2,3},{3,2},{4,5},{5,4},{6,7},{7,6},{8,9},{9,8},{10,11... | collective-permute-start | bytes 589832 | tf_op jit(solution)/shard_map/ppermute | solution.py:465
  50.9 1.4 %collective-permute-start.13 = (bf16[256,256]{1,0:T(8,128)(2,1)S(1)}, bf16[256,256]{1,0:T(8,128)(2,1)S(1)}, u32[]{:S(2)}, u32[]{:S(2)}) collective-permute-start(bf16[256,256]{1,0:T(8,128)(2,1)S(1)} %slice.18), channel_id=1, source_target_pairs={{0,1},{1,0},{2,3},{3,2},{4,5},{5,4},{6,7},{7,6},{8,9},{9,8},{10,11... | collective-permute-start | bytes 393224 | tf_op jit(solution)/shard_map/ppermute | solution.py:465

commit v10 on v9

--- a/solution.py
+++ b/solution.py
@@ -69,74 +69,89 @@
     return copies
 
 
-def expected_kernel(chunk_u, chunk_i, theta_ref, trate_ref, beta_ref, brate_ref, *refs):
-    both_ref, wide_ref, item_ref, pack_ref, theta_buf, trate_buf, beta_buf, brate_buf, user_sems, item_sems = refs
+def users_kernel(chunk, shape_ref, rate_ref, both_ref, wide_ref, total_ref, shape_buf, rate_buf, sems):
     core = lax.axis_index("ka")
     half = both_ref.shape[0] // 2
-    rows = beta_ref.shape[0]
-    steps = half // chunk_u
+    steps = half // chunk
     starts = []
-    for side in (1 - core, core):
-        starts += [pl.multiple_of(side * half + j * chunk_u, chunk_u) for j in range(steps)]
-    item_starts = list(range(0, rows, chunk_i))
-    user_copies = chunk_copies(starts, chunk_u, (theta_ref, trate_ref), (theta_buf, trate_buf), user_sems)
-    item_copies = chunk_copies(item_starts, chunk_i, (beta_ref, brate_ref), (beta_buf, brate_buf), item_sems)
-    theta_total = jnp.zeros((1, both_ref.shape[1]), F32)
+    for side in (core, 1 - core):
+        starts += [pl.multiple_of(side * half + j * chunk, chunk) for j in range(steps)]
+    copies = chunk_copies(starts, chunk, (shape_ref, rate_ref), (shape_buf, rate_buf), sems)
+    total = jnp.zeros(total_ref.shape, F32)
     for j, start in enumerate(starts):
-        for copy in user_copies[j]:
+        for copy in copies[j]:
             copy.wait()
-        x = theta_buf[pl.ds(start, chunk_u), :]
-        inv_rate = reciprocal(trate_buf[pl.ds(start, chunk_u), :])
+        x = shape_buf[pl.ds(start, chunk), :]
+        inv_rate = reciprocal(rate_buf[pl.ds(start, chunk), :])
         value = exp_digamma(x, inv_rate).astype(BF16)
-        at = (j % steps) * chunk_u
-        if j < steps:
-            both_ref[half + at : half + at + chunk_u, :] = value
-            wide_ref[half + at : half + at + chunk_u, :] = value
-            pack_ref[at : at + chunk_u, :] = value
-        else:
-            both_ref[at : at + chunk_u, :] = value
-            wide_ref[at : at + chunk_u, :] = value
-        theta_total += jnp.sum(x * inv_rate, axis=0, keepdims=True)
-    beta_total = jnp.zeros((1, both_ref.shape[1]), F32)
-    for j, start in enumerate(item_starts):
-        for copy in item_copies[j]:
-            copy.wait()
-        x = beta_buf[start : start + chunk_i, :]
-        inv_rate = reciprocal(brate_buf[start : start + chunk_i, :])
-        value = exp_digamma(x, inv_rate).astype(BF16)
-        item_ref[start : start + chunk_i, :] = value
-        pack_ref[half + start : half + start + chunk_i, :] = value
-        beta_total += jnp.sum(x * inv_rate, axis=0, keepdims=True)
-    wide_ref[2 * half :, :] = jnp.zeros((3 * EXTRA, wide_ref.shape[1]), BF16)
-    extra = encode([theta_total, beta_total])
-    item_ref[rows:, :] = extra
-    pack_ref[half + rows :, :] = extra
-
-
-def expected(theta, trate, beta, brate):
-    rows, cols = theta.shape
-    item_rows = beta.shape[0]
-    half = rows // 2
-    chunk_u = min(half, 128)
-    chunk_i = min(item_rows, 128)
-    shapes = [rows, rows + 3 * EXTRA, item_rows + EXTRA, half + item_rows + EXTRA]
-    return pl.pallas_call(
-        functools.partial(expected_kernel, chunk_u, chunk_i),
-        in_specs=[pl.BlockSpec(memory_space=HBM)] * 4,
-        out_specs=[pl.BlockSpec(memory_space=VMEM)] * len(shapes),
-        out_shape=[jax.ShapeDtypeStruct((r, cols), BF16) for r in shapes],
+        both_ref[j * chunk : (j + 1) * chunk, :] = value
+        wide_ref[j * chunk : (j + 1) * chunk, :] = value
+        total += jnp.sum(x * inv_rate, axis=0, keepdims=True)
+    total_ref[...] = total
+    wide_ref[2 * half :, :] = jnp.zeros((wide_ref.shape[0] - 2 * half, wide_ref.shape[1]), BF16)
+
+
+def expected_users(shape_arg, rate_arg):
+    rows, cols = shape_arg.shape
+    chunk = min(rows // 2, 128)
+    return pl.pallas_call(
+        functools.partial(users_kernel, chunk),
+        in_specs=[pl.BlockSpec(memory_space=HBM)] * 2,
+        out_specs=[pl.BlockSpec(memory_space=VMEM)] * 3,
+        out_shape=[
+            jax.ShapeDtypeStruct((rows, cols), BF16),
+            jax.ShapeDtypeStruct((rows + 3 * EXTRA, cols), BF16),
+            jax.ShapeDtypeStruct((1, cols), F32),
+        ],
         scratch_shapes=[
             pltpu.VMEM((rows, cols), F32),
             pltpu.VMEM((rows, cols), F32),
-            pltpu.VMEM((item_rows, cols), F32),
-            pltpu.VMEM((item_rows, cols), F32),
-            pltpu.SemaphoreType.DMA((2, rows // chunk_u)),
-            pltpu.SemaphoreType.DMA((2, item_rows // chunk_i)),
+            pltpu.SemaphoreType.DMA((2, rows // chunk)),
         ],
-        compiler_params=pltpu.CompilerParams(vmem_limit_bytes=6 * MIB),
-        cost_estimate=CHEAP,
-        name="expected",
-    )(pinned(theta), pinned(trate), pinned(beta), pinned(brate))
+        compiler_params=pltpu.CompilerParams(vmem_limit_bytes=4 * MIB),
+        cost_estimate=CHEAP,
+        name="expected_users",
+    )(pinned(shape_arg), pinned(rate_arg))
+
+
+def items_kernel(chunk, shape_ref, rate_ref, both_ref, theta_ref, item_ref, pack_ref, shape_buf, rate_buf, sems):
+    rows = shape_ref.shape[0]
+    half = both_ref.shape[0] // 2
+    starts = list(range(0, rows, chunk))
+    copies = chunk_copies(starts, chunk, (shape_ref, rate_ref), (shape_buf, rate_buf), sems)
+    pack_ref[:half, :] = both_ref[half:, :]
+    total = jnp.zeros(theta_ref.shape, F32)
+    for j, start in enumerate(starts):
+        for copy in copies[j]:
+            copy.wait()
+        x = shape_buf[start : start + chunk, :]
+        inv_rate = reciprocal(rate_buf[start : start + chunk, :])
+        value = exp_digamma(x, inv_rate).astype(BF16)
+        item_ref[start : start + chunk, :] = value
+        pack_ref[half + start : half + start + chunk, :] = value
+        total += jnp.sum(x * inv_rate, axis=0, keepdims=True)
+    extra = encode([theta_ref[...], total])
+    item_ref[rows:, :] = extra
+    pack_ref[half + rows :, :] = extra
+
+
+def expected_items(shape_arg, rate_arg, both, theta_local):
+    rows, cols = shape_arg.shape
+    chunk = min(rows, 128)
+    return pl.pallas_call(
+        functools.partial(items_kernel, chunk),
+        in_specs=[pl.BlockSpec(memory_space=m) for m in (HBM, HBM, VMEM, VMEM)],
+        out_specs=[pl.BlockSpec(memory_space=VMEM)] * 2,
+        out_shape=[jax.ShapeDtypeStruct((r + EXTRA, cols), BF16) for r in (rows, both.shape[0] // 2 + rows)],
+        scratch_shapes=[
+            pltpu.VMEM((rows, cols), F32),
+            pltpu.VMEM((rows, cols), F32),
+            pltpu.SemaphoreType.DMA((2, rows // chunk)),
+        ],
+        compiler_params=pltpu.CompilerParams(vmem_limit_bytes=4 * MIB),
+        cost_estimate=CHEAP,
+        name="expected_items",
+    )(pinned(shape_arg), pinned(rate_arg), both, theta_local)
 
 
 def dense_kernel(n_item, shard_tiles, chunk, rows, users_in, items_in, live_ref, counts_ref, out_ref, *scratch):
@@ -464,7 +479,8 @@
     def sibling(x):
         return lax.ppermute(x, "ka", [(h, n_ka - 1 - h) for h in range(n_ka)])
 
-    both, wide, item_exp, pack = expected(theta_shape[0], theta_rate[0], beta_shape[0], beta_rate[0])
+    both, wide, theta_local = expected_users(theta_shape[0], theta_rate[0])
+    item_exp, pack = expected_items(beta_shape[0], beta_rate[0], both, theta_local)
     rows = both.shape[0]
     half_rows = rows // 2
     item_rows = beta_shape.shape[1] * n_user

time: 53.9 us -> 52.9 us (0.981)
  waiting for transfers between devices: 21.7 us -> 20.1 us
  Pallas kernels: 14.2 us -> 14.9 us
    ppermute x6, waiting for transfers between devices: 21.3 us -> 19.2 us  [along_item(): return lax.ppermute(x, 'item', [(i, (i + shift) % n) for i in range(n)])]
    pallas_call x1 -> x2, Pallas kernels: 2.76 us -> 3.53 us  [the longest x1 1.77 us: expected_users(): pl.pallas_call(functools.partial(users_kernel, chunk), in_specs=[pl.Block...]
  transfers between devices with their start and end apart: 17 -> 17, of which waited for: 7 -> 8; matrix products, arithmetic and copies ran while one was open for 0% -> 0% of each run, Pallas kernels for 19% -> 22%
where the time goes in v10:
time: 52.9 us; the launch traced here: 52.7 us
  waiting for transfers between devices  20.1 us (38%)
  starting transfers between devices  16.2 us (31%)
  Pallas kernels  14.9 us (28%)
  between operations  1.46 us (3%)
    ppermute x6, waiting for transfers between devices, along_item(): return lax.ppermute(x, 'item', [(i, (i + shift) % n) for i in range(n)])  19.2 us
    ppermute x6, starting transfers between devices, along_item(): return lax.ppermute(x, 'item', [(i, (i + shift) % n) for i in range(n)])  12.1 us
    pallas_call x4, Pallas kernels, statistics(): pl.pallas_call(functools.partial(stat_kernel, len(item_mine), half_rows,...  6.63 us
    ppermute x2, starting transfers between devices, along_user(): return lax.ppermute(x, 'user', [(i, i ^ distance) for i in range(n)])  2.87 us
    pallas_call x1, Pallas kernels, dense_counts(): pl.pallas_call(functools.partial(dense_kernel, n_item, item_rows // n_use...  2.24 us
    pallas_call x1, Pallas kernels, expected_users(): pl.pallas_call(functools.partial(users_kernel, chunk), in_specs=[pl.Block...  1.77 us
    pallas_call x1, Pallas kernels, expected_items(): pl.pallas_call(functools.partial(items_kernel, chunk), in_specs=[pl.Block...  1.76 us
    pallas_call x1, Pallas kernels, finish_users(): pl.pallas_call(functools.partial(finish_users_kernel, len(joined), len(it...  1.42 us
  transfers between devices with their start and end apart: 17, of which 8 were waited for; matrix products, arithmetic and copies ran while one was open for 0% of the time, Pallas kernels for 22%

profile of v10, /device:TPU:0, one launch (start us, length us, event | category | flops | bytes accessed | tf_op | source)
XLA Modules:
  0.0 52.7 jit_solution(18116786687843245101)
XLA Ops:
  0.6 1.8 %expected_users.1 = (bf16[512,256]{1,0:T(8,128)(2,1)S(1)}, bf16[560,256]{1,0:T(8,128)(2,1)S(1)}, f32[1,256]{1,0:T(1,128)S(1)}) custom-call(f32[512,256]{1,0:T(8,128)} %bitcast.14, f32[512,256]{1,0:T(8,128)} %bitcast.15), custom_call_target="tpu_custom_call" | custom-call | flops 1024 | bytes 1024 | tf_op jit(solution)/shard_map/expected_users/pallas_call | solution.py:97
  2.4 3.1 %collective-permute-start.3 = (bf16[512,256]{1,0:T(8,128)(2,1)S(1)}, bf16[512,256]{1,0:T(8,128)(2,1)S(1)}, u32[]{:S(2)}, u32[]{:S(2)}) collective-permute-start(bf16[512,256]{1,0:T(8,128)(2,1)S(1)} %get-tuple-element.27.both_ref.refs_0_), channel_id=1, source_target_pairs={{0,4},{4,8},{8,12},{12,0},{1,5},{5,9},{9,13},{13,1},{2,6},{6,10},{... | collective-permute-start | bytes 786440 | tf_op jit(solution)/shard_map/ppermute | solution.py:453
  5.5 1.8 %expected_items.1 = (bf16[528,256]{1,0:T(8,128)(2,1)S(1)}, bf16[784,256]{1,0:T(8,128)(2,1)S(1)}) custom-call(f32[512,256]{1,0:T(8,128)} %bitcast.16, f32[512,256]{1,0:T(8,128)} %bitcast.17, bf16[512,256]{1,0:T(8,128)(2,1)S(1)} %get-tuple-element.27.both_ref.refs_0_, f32[1,256]{1,0:T(1,128)S(1)} %get-tuple-element.28.theta_ref), custom_call_target="tpu_custom_call" | custom-call | flops 1024 | bytes 1024 | tf_op jit(solution)/shard_map/expected_items/pallas_call | solution.py:141
  7.9 2.2 %dense_counts.1.refs_6_ = bf16[1024,1024]{1,0:T(8,128)(2,1)S(1)} custom-call(s32[64]{0:T(128)} %bitcast.19, s32[64]{0:T(128)} %bitcast.20, s32[1]{0:T(128)} %bitcast.12.live_ref, s32[64,128,128]{2,1,0:T(8,128)} %bitcast.13), custom_call_target="tpu_custom_call" | custom-call | flops 1024 | bytes 1024 | tf_op jit(solution)/shard_map/dense_counts/pallas_call | solution.py:212
  10.1 1.6 %collective-permute-start.1 = (bf16[528,256]{1,0:T(8,128)(2,1)S(1)}, bf16[528,256]{1,0:T(8,128)(2,1)S(1)}, u32[]{:S(2)}, u32[]{:S(2)}) collective-permute-start(bf16[528,256]{1,0:T(8,128)(2,1)S(1)} %get-tuple-element.31.refs_2_.exp_ref.refs_6_), channel_id=1, source_target_pairs={{0,2},{2,0},{1,3},{3,1},{4,6},{6,4},{5,7},{7,5},{8,10},{10,8},{9,1... | collective-permute-start | bytes 811016 | tf_op jit(solution)/shard_map/ppermute | solution.py:461
  11.7 2.1 %collective-permute-done.3.refs_0_ = bf16[512,256]{1,0:T(8,128)(2,1)S(1)} collective-permute-done((bf16[512,256]{1,0:T(8,128)(2,1)S(1)}, bf16[512,256]{1,0:T(8,128)(2,1)S(1)}, u32[]{:S(2)}, u32[]{:S(2)}) %collective-permute-start.3) | collective-permute-done | bytes 262176 | tf_op jit(solution)/shard_map/ppermute | solution.py:453
  13.9 3.7 %collective-permute-start.7 = (bf16[560,256]{1,0:T(8,128)(2,1)S(1)}, bf16[560,256]{1,0:T(8,128)(2,1)S(1)}, u32[]{:S(2)}, u32[]{:S(2)}) collective-permute-start(bf16[560,256]{1,0:T(8,128)(2,1)S(1)} %get-tuple-element.37), channel_id=1, source_target_pairs={{0,12},{4,0},{8,4},{12,8},{1,13},{5,1},{9,5},{13,9},{2,14},{6,2},{... | collective-permute-start | bytes 860168 | tf_op jit(solution)/shard_map/ppermute | solution.py:453
  17.6 0.5 collective-permute-done.1.refs_3_.refs_7_
  18.2 0.5 collective-permute-start.6
  18.7 6.2 %collective-permute-done.4.refs_0_ = bf16[512,256]{1,0:T(8,128)(2,1)S(1)} collective-permute-done((bf16[512,256]{1,0:T(8,128)(2,1)S(1)}, bf16[512,256]{1,0:T(8,128)(2,1)S(1)}, u32[]{:S(2)}, u32[]{:S(2)}) %collective-permute-start.4) | collective-permute-done | bytes 262176 | tf_op jit(solution)/shard_map/ppermute | solution.py:453
  24.9 1.7 %statistics_1.1 = (bf16[528,256]{1,0:T(8,128)(2,1)S(1)}, f32[512,1024]{1,0:T(8,128)S(1)}) custom-call(bf16[512,256]{1,0:T(8,128)(2,1)S(1)} %collective-permute-done.3.refs_0_, bf16[512,256]{1,0:T(8,128)(2,1)S(1)} %collective-permute-done.6.refs_1_, bf16[528,256]{1,0:T(8,128)(2,1)S(1)} %get-tuple-element.31.refs_2_.exp_ref.refs_6_, ...), custom_call_target="tpu_custom_call" | custom-call | flops 1024 | bytes 1024 | tf_op jit(solution)/shard_map/statistics_1/pallas_call | solution.py:309
  26.6 1.7 %statistics_3.1 = (bf16[528,256]{1,0:T(8,128)(2,1)S(1)}, f32[512,1024]{1,0:T(8,128)S(1)}) custom-call(bf16[512,256]{1,0:T(8,128)(2,1)S(1)} %collective-permute-done.4.refs_0_, bf16[512,256]{1,0:T(8,128)(2,1)S(1)} %collective-permute-done.5.refs_1_, bf16[528,256]{1,0:T(8,128)(2,1)S(1)} %get-tuple-element.31.refs_2_.exp_ref.refs_6_, ...), custom_call_target="tpu_custom_call" | custom-call | flops 1024 | bytes 1024 | tf_op jit(solution)/shard_map/statistics_3/pallas_call | solution.py:309
  28.3 0.5 collective-permute-done.7.refs_0_
  28.9 0.8 %collective-permute-start.11 = (bf16[528,256]{1,0:T(8,128)(2,1)S(1)}, bf16[528,256]{1,0:T(8,128)(2,1)S(1)}, u32[]{:S(2)}, u32[]{:S(2)}) collective-permute-start(bf16[528,256]{1,0:T(8,128)(2,1)S(1)} %get-tuple-element.38), channel_id=1, source_target_pairs={{0,12},{4,0},{8,4},{12,8},{1,13},{5,1},{9,5},{13,9},{2,14},{6,2},{... | collective-permute-start | bytes 811016 | tf_op jit(solution)/shard_map/ppermute | solution.py:453
  29.7 1.7 %statistics_0.1 = (f32[256,256]{1,0:T(8,128)S(1)}, f32[256,256]{1,0:T(8,128)S(1)}, f32[512,1024]{1,0:T(8,128)S(1)}) custom-call(bf16[512,256]{1,0:T(8,128)(2,1)S(1)} %get-tuple-element.27.both_ref.refs_0_, bf16[784,256]{1,0:T(8,128)(2,1)S(1)} %collective-permute-done.refs_4_.refs_1_, bf16[528,256]{1,0:T(8,128)(2,1)S(1)} %get-tuple-element.31.refs_2_.exp_ref.refs_6_, ...), custom_call_target="tpu_custom_call" | custom-call | flops 1024 | bytes 1024 | tf_op jit(solution)/shard_map/statistics_0/pallas_call | solution.py:309
  31.4 1.7 %statistics_2.1 = (bf16[528,256]{1,0:T(8,128)(2,1)S(1)}, f32[256,1024]{1,0:T(8,128)S(1)}, bf16[256,512]{1,0:T(8,128)(2,1)S(1)}, bf16[256,512]{1,0:T(8,128)(2,1)S(1)}) custom-call(bf16[560,256]{1,0:T(8,128)(2,1)S(1)} %collective-permute-done.7.refs_0_, bf16[256,256]{1,0:T(8,128)(2,1)S(1)} %collective-permute-done.8.refs_1_, ...), custom_call_target="tpu_custom_call" | custom-call | flops 1024 | bytes 1024 | tf_op jit(solution)/shard_map/statistics_2/pallas_call | solution.py:309
  33.0 1.3 %collective-permute-start.9 = (bf16[528,256]{1,0:T(8,128)(2,1)S(1)}, bf16[528,256]{1,0:T(8,128)(2,1)S(1)}, u32[]{:S(2)}, u32[]{:S(2)}) collective-permute-start(bf16[528,256]{1,0:T(8,128)(2,1)S(1)} %get-tuple-element.41), channel_id=1, source_target_pairs={{0,4},{4,8},{8,12},{12,0},{1,5},{5,9},{9,13},{13,1},{2,6},{6,10},{... | collective-permute-start | bytes 811016 | tf_op jit(solution)/shard_map/ppermute | solution.py:453
  34.8 2.9 %collective-permute-done.11.came_ref = bf16[528,256]{1,0:T(8,128)(2,1)S(1)} collective-permute-done((bf16[528,256]{1,0:T(8,128)(2,1)S(1)}, bf16[528,256]{1,0:T(8,128)(2,1)S(1)}, u32[]{:S(2)}, u32[]{:S(2)}) %collective-permute-start.11) | collective-permute-done | bytes 270368 | tf_op jit(solution)/shard_map/ppermute | solution.py:453
  37.8 3.1 %collective-permute-start.12 = (bf16[528,256]{1,0:T(8,128)(2,1)S(1)}, bf16[528,256]{1,0:T(8,128)(2,1)S(1)}, u32[]{:S(2)}, u32[]{:S(2)}) collective-permute-start(bf16[528,256]{1,0:T(8,128)(2,1)S(1)} %add_came.1), channel_id=1, source_target_pairs={{0,12},{4,0},{8,4},{12,8},{1,13},{5,1},{9,5},{13,9},{2,14},{6,2},{... | collective-permute-start | bytes 811016 | tf_op jit(solution)/shard_map/ppermute | solution.py:453
  41.0 1.3 %collective-permute-start.16 = (bf16[256,512]{1,0:T(8,128)(2,1)S(1)}, bf16[256,512]{1,0:T(8,128)(2,1)S(1)}, u32[]{:S(2)}, u32[]{:S(2)}) collective-permute-start(bf16[256,512]{1,0:T(8,128)(2,1)S(1)} %merge_items.1), channel_id=1, source_target_pairs={{0,2},{2,0},{1,3},{3,1},{4,6},{6,4},{5,7},{7,5},{8,10},{10,8},{9,1... | collective-permute-start | bytes 786440 | tf_op jit(solution)/shard_map/ppermute | solution.py:461
  42.3 2.3 %collective-permute-done.9.refs_3_ = bf16[528,256]{1,0:T(8,128)(2,1)S(1)} collective-permute-done((bf16[528,256]{1,0:T(8,128)(2,1)S(1)}, bf16[528,256]{1,0:T(8,128)(2,1)S(1)}, u32[]{:S(2)}, u32[]{:S(2)}) %collective-permute-start.9) | collective-permute-done | bytes 270368 | tf_op jit(solution)/shard_map/ppermute | solution.py:453
  44.7 5.1 %collective-permute-done.12.refs_4_ = bf16[528,256]{1,0:T(8,128)(2,1)S(1)} collective-permute-done((bf16[528,256]{1,0:T(8,128)(2,1)S(1)}, bf16[528,256]{1,0:T(8,128)(2,1)S(1)}, u32[]{:S(2)}, u32[]{:S(2)}) %collective-permute-start.12) | collective-permute-done | bytes 270368 | tf_op jit(solution)/shard_map/ppermute | solution.py:453
  50.0 1.0 %finish_items.1 = f32[512,256]{1,0:T(8,128)} custom-call(bf16[528,256]{1,0:T(8,128)(2,1)S(1)} %get-tuple-element.31.refs_2_.exp_ref.refs_6_, f32[256,1024]{1,0:T(8,128)S(1)} %get-tuple-element.43.mine_ref.own_ref, bf16[256,512]{1,0:T(8,128)(2,1)S(1)} %collective-permute-done.14.refs_0_, bf16[256,512]{1,0:T(8,128)(2,1)S(1)} %collective-permute-done.16.refs_1_), custom_call_target="tpu_custom_call" | custom-call | flops 1024 | bytes 1024 | tf_op jit(solution)/shard_map/finish_items/pallas_call | solution.py:440
  51.3 1.4 %finish_users.1 = (f32[512,256]{1,0:T(8,128)}, f32[512,256]{1,0:T(8,128)}, f32[512,256]{1,0:T(8,128)}) custom-call(bf16[512,256]{1,0:T(8,128)(2,1)S(1)} %get-tuple-element.27.both_ref.refs_0_, f32[256,256]{1,0:T(8,128)S(1)} %get-tuple-element.34.refs_1_, bf16[384,256]{1,0:T(8,128)(2,1)S(1)} %collective-permute-done.10.refs_2_, ...), custom_call_target="tpu_custom_call" | custom-call | flops 1024 | bytes 1024 | tf_op jit(solution)/shard_map/finish_users/pallas_call | solution.py:408
  (30 shorter events, 1.4 us)
Async XLA Ops:
  2.4 11.4 %collective-permute-start.3 = (bf16[512,256]{1,0:T(8,128)(2,1)S(1)}, bf16[512,256]{1,0:T(8,128)(2,1)S(1)}, u32[]{:S(2)}, u32[]{:S(2)}) collective-permute-start(bf16[512,256]{1,0:T(8,128)(2,1)S(1)} %get-tuple-element.27.both_ref.refs_0_), channel_id=1, source_target_pairs={{0,4},{4,8},{8,12},{12,0},{1,5},{5,9},{9,13},{13,1},{2,6},{6,10},{... | collective-permute-start | bytes 786440 | tf_op jit(solution)/shard_map/ppermute | solution.py:453
  10.1 8.0 %collective-permute-start.1 = (bf16[528,256]{1,0:T(8,128)(2,1)S(1)}, bf16[528,256]{1,0:T(8,128)(2,1)S(1)}, u32[]{:S(2)}, u32[]{:S(2)}) collective-permute-start(bf16[528,256]{1,0:T(8,128)(2,1)S(1)} %get-tuple-element.31.refs_2_.exp_ref.refs_6_), channel_id=1, source_target_pairs={{0,2},{2,0},{1,3},{3,1},{4,6},{6,4},{5,7},{7,5},{8,10},{10,8},{9,1... | collective-permute-start | bytes 811016 | tf_op jit(solution)/shard_map/ppermute | solution.py:461
  13.8 11.1 %collective-permute-start.4 = (bf16[512,256]{1,0:T(8,128)(2,1)S(1)}, bf16[512,256]{1,0:T(8,128)(2,1)S(1)}, u32[]{:S(2)}, u32[]{:S(2)}) collective-permute-start(bf16[512,256]{1,0:T(8,128)(2,1)S(1)} %collective-permute-done.3.refs_0_), channel_id=1, source_target_pairs={{0,4},{4,8},{8,12},{12,0},{1,5},{5,9},{9,13},{13,1},{2,6},{6,10},{... | collective-permute-start | bytes 786440 | tf_op jit(solution)/shard_map/ppermute | solution.py:453
  13.9 11.0 %collective-permute-start = (bf16[784,256]{1,0:T(8,128)(2,1)S(1)}, bf16[784,256]{1,0:T(8,128)(2,1)S(1)}, u32[]{:S(2)}, u32[]{:S(2)}) collective-permute-start(bf16[784,256]{1,0:T(8,128)(2,1)S(1)} %get-tuple-element.29), channel_id=1, source_target_pairs={{0,1},{1,0},{2,3},{3,2},{4,5},{5,4},{6,7},{7,6},{8,9},{9,8},{10,11... | collective-permute-start | bytes 1204232 | tf_op jit(solution)/shard_map/ppermute | solution.py:480
  13.9 14.9 %collective-permute-start.7 = (bf16[560,256]{1,0:T(8,128)(2,1)S(1)}, bf16[560,256]{1,0:T(8,128)(2,1)S(1)}, u32[]{:S(2)}, u32[]{:S(2)}) collective-permute-start(bf16[560,256]{1,0:T(8,128)(2,1)S(1)} %get-tuple-element.37), channel_id=1, source_target_pairs={{0,12},{4,0},{8,4},{12,8},{1,13},{5,1},{9,5},{13,9},{2,14},{6,2},{... | collective-permute-start | bytes 860168 | tf_op jit(solution)/shard_map/ppermute | solution.py:453
  18.2 6.8 %collective-permute-start.2 = (bf16[528,256]{1,0:T(8,128)(2,1)S(1)}, bf16[528,256]{1,0:T(8,128)(2,1)S(1)}, u32[]{:S(2)}, u32[]{:S(2)}) collective-permute-start(bf16[528,256]{1,0:T(8,128)(2,1)S(1)} %collective-permute-done.1.refs_3_.refs_7_), channel_id=1, source_target_pairs={{0,1},{1,0},{2,3},{3,2},{4,5},{5,4},{6,7},{7,6},{8,9},{9,8},{10,11... | collective-permute-start | bytes 811016 | tf_op jit(solution)/shard_map/ppermute | solution.py:480
  18.2 6.8 %collective-permute-start.6 = (bf16[512,256]{1,0:T(8,128)(2,1)S(1)}, bf16[512,256]{1,0:T(8,128)(2,1)S(1)}, u32[]{:S(2)}, u32[]{:S(2)}) collective-permute-start(bf16[512,256]{1,0:T(8,128)(2,1)S(1)} %collective-permute-done.3.refs_0_), channel_id=1, source_target_pairs={{0,1},{1,0},{2,3},{3,2},{4,5},{5,4},{6,7},{7,6},{8,9},{9,8},{10,11... | collective-permute-start | bytes 786440 | tf_op jit(solution)/shard_map/ppermute | solution.py:480
  24.9 1.7 %collective-permute-start.5 = (bf16[512,256]{1,0:T(8,128)(2,1)S(1)}, bf16[512,256]{1,0:T(8,128)(2,1)S(1)}, u32[]{:S(2)}, u32[]{:S(2)}) collective-permute-start(bf16[512,256]{1,0:T(8,128)(2,1)S(1)} %collective-permute-done.4.refs_0_), channel_id=1, source_target_pairs={{0,1},{1,0},{2,3},{3,2},{4,5},{5,4},{6,7},{7,6},{8,9},{9,8},{10,11... | collective-permute-start | bytes 786440 | tf_op jit(solution)/shard_map/ppermute | solution.py:480
  28.8 2.6 %collective-permute-start.8 = (bf16[256,256]{1,0:T(8,128)(2,1)S(1)}, bf16[256,256]{1,0:T(8,128)(2,1)S(1)}, u32[]{:S(2)}, u32[]{:S(2)}) collective-permute-start(bf16[256,256]{1,0:T(8,128)(2,1)S(1)} %slice.12), channel_id=1, source_target_pairs={{0,1},{1,0},{2,3},{3,2},{4,5},{5,4},{6,7},{7,6},{8,9},{9,8},{10,11... | collective-permute-start | bytes 393224 | tf_op jit(solution)/shard_map/ppermute | solution.py:480
  28.9 8.9 %collective-permute-start.11 = (bf16[528,256]{1,0:T(8,128)(2,1)S(1)}, bf16[528,256]{1,0:T(8,128)(2,1)S(1)}, u32[]{:S(2)}, u32[]{:S(2)}) collective-permute-start(bf16[528,256]{1,0:T(8,128)(2,1)S(1)} %get-tuple-element.38), channel_id=1, source_target_pairs={{0,12},{4,0},{8,4},{12,8},{1,13},{5,1},{9,5},{13,9},{2,14},{6,2},{... | collective-permute-start | bytes 811016 | tf_op jit(solution)/shard_map/ppermute | solution.py:453
  33.0 11.5 %collective-permute-start.9 = (bf16[528,256]{1,0:T(8,128)(2,1)S(1)}, bf16[528,256]{1,0:T(8,128)(2,1)S(1)}, u32[]{:S(2)}, u32[]{:S(2)}) collective-permute-start(bf16[528,256]{1,0:T(8,128)(2,1)S(1)} %get-tuple-element.41), channel_id=1, source_target_pairs={{0,4},{4,8},{8,12},{12,0},{1,5},{5,9},{9,13},{13,1},{2,6},{6,10},{... | collective-permute-start | bytes 811016 | tf_op jit(solution)/shard_map/ppermute | solution.py:453
  34.3 6.6 %collective-permute-start.15 = (bf16[256,512]{1,0:T(8,128)(2,1)S(1)}, bf16[256,512]{1,0:T(8,128)(2,1)S(1)}, u32[]{:S(2)}, u32[]{:S(2)}) collective-permute-start(bf16[256,512]{1,0:T(8,128)(2,1)S(1)} %get-tuple-element.45), channel_id=1, source_target_pairs={{0,1},{1,0},{2,3},{3,2},{4,5},{5,4},{6,7},{7,6},{8,9},{9,8},{10,11... | collective-permute-start | bytes 786440 | tf_op jit(solution)/shard_map/ppermute | solution.py:480
  34.3 15.6 %collective-permute-start.14 = (bf16[256,512]{1,0:T(8,128)(2,1)S(1)}, bf16[256,512]{1,0:T(8,128)(2,1)S(1)}, u32[]{:S(2)}, u32[]{:S(2)}) collective-permute-start(bf16[256,512]{1,0:T(8,128)(2,1)S(1)} %get-tuple-element.44), channel_id=1, source_target_pairs={{0,1},{1,0},{2,3},{3,2},{4,5},{5,4},{6,7},{7,6},{8,9},{9,8},{10,11... | collective-permute-start | bytes 786440 | tf_op jit(solution)/shard_map/ppermute | solution.py:480
  37.8 12.0 %collective-permute-start.12 = (bf16[528,256]{1,0:T(8,128)(2,1)S(1)}, bf16[528,256]{1,0:T(8,128)(2,1)S(1)}, u32[]{:S(2)}, u32[]{:S(2)}) collective-permute-start(bf16[528,256]{1,0:T(8,128)(2,1)S(1)} %add_came.1), channel_id=1, source_target_pairs={{0,12},{4,0},{8,4},{12,8},{1,13},{5,1},{9,5},{13,9},{2,14},{6,2},{... | collective-permute-start | bytes 811016 | tf_op jit(solution)/shard_map/ppermute | solution.py:453
  40.9 10.3 %copy-start = (f32[1,512]{1,0:T(1,128)S(1)}, f32[1,512]{1,0:T(1,128)}, u32[]{:S(2)}) copy-start(f32[1,512]{1,0:T(1,128)} %refs_8_.1) | copy-start | bytes 6148
  41.0 10.3 %copy-start.1 = (f32[1,512]{1,0:T(1,128)S(1)}, f32[1,512]{1,0:T(1,128)}, u32[]{:S(2)}) copy-start(f32[1,512]{1,0:T(1,128)} %refs_9_.1) | copy-start | bytes 6148
  41.0 9.0 %collective-permute-start.16 = (bf16[256,512]{1,0:T(8,128)(2,1)S(1)}, bf16[256,512]{1,0:T(8,128)(2,1)S(1)}, u32[]{:S(2)}, u32[]{:S(2)}) collective-permute-start(bf16[256,512]{1,0:T(8,128)(2,1)S(1)} %merge_items.1), channel_id=1, source_target_pairs={{0,2},{2,0},{1,3},{3,1},{4,6},{6,4},{5,7},{7,5},{8,10},{10,8},{9,1... | collective-permute-start | bytes 786440 | tf_op jit(solution)/shard_map/ppermute | solution.py:461
  44.6 6.7 %collective-permute-start.10 = (bf16[384,256]{1,0:T(8,128)(2,1)S(1)}, bf16[384,256]{1,0:T(8,128)(2,1)S(1)}, u32[]{:S(2)}, u32[]{:S(2)}) collective-permute-start(bf16[384,256]{1,0:T(8,128)(2,1)S(1)} %pad_maximum_fusion), channel_id=1, source_target_pairs={{0,1},{1,0},{2,3},{3,2},{4,5},{5,4},{6,7},{7,6},{8,9},{9,8},{10,11... | collective-permute-start | bytes 589832 | tf_op jit(solution)/shard_map/ppermute | solution.py:480
  49.9 1.4 %collective-permute-start.13 = (bf16[256,256]{1,0:T(8,128)(2,1)S(1)}, bf16[256,256]{1,0:T(8,128)(2,1)S(1)}, u32[]{:S(2)}, u32[]{:S(2)}) collective-permute-start(bf16[256,256]{1,0:T(8,128)(2,1)S(1)} %slice.18), channel_id=1, source_target_pairs={{0,1},{1,0},{2,3},{3,2},{4,5},{5,4},{6,7},{7,6},{8,9},{9,8},{10,11... | collective-permute-start | bytes 393224 | tf_op jit(solution)/shard_map/ppermute | solution.py:480

commit v11 on v10

--- a/solution.py
+++ b/solution.py
@@ -324,16 +324,29 @@
     out_ref[rows:, :] = encode(sum_totals([stat_ref[rows:, :], came_ref[rows:, :]]))
 
 
-def add_came(stat, came):
-    return pl.pallas_call(
-        add_kernel,
+def split_kernel(stat_ref, came_ref, other_ref, mine_ref):
+    half = other_ref.shape[0] - EXTRA
+    total = stat_ref[: 2 * half, :].astype(F32) + came_ref[: 2 * half, :].astype(F32)
+    other_ref[:half, :] = total[half:, :].astype(BF16)
+    other_ref[half:, :] = encode(sum_totals([stat_ref[2 * half :, :], came_ref[2 * half :, :]]))
+    mine_ref[:half, :] = total[:half, :].astype(BF16)
+    mine_ref[half:, :] = jnp.zeros((2 * EXTRA, mine_ref.shape[1]), BF16)
+
+
+def add_came(stat, came, split):
+    rows, cols = stat.shape
+    half = (rows - EXTRA) // 2
+    shapes = [half + EXTRA, half + 2 * EXTRA] if split else [rows]
+    out = pl.pallas_call(
+        split_kernel if split else add_kernel,
         in_specs=[pl.BlockSpec(memory_space=VMEM)] * 2,
-        out_specs=pl.BlockSpec(memory_space=VMEM),
-        out_shape=jax.ShapeDtypeStruct(stat.shape, BF16),
+        out_specs=[pl.BlockSpec(memory_space=VMEM)] * len(shapes),
+        out_shape=[jax.ShapeDtypeStruct((r, cols), BF16) for r in shapes],
         compiler_params=pltpu.CompilerParams(vmem_limit_bytes=2 * MIB),
         cost_estimate=CHEAP,
         name="add_came",
     )(stat, came)
+    return list(out)
 
 
 def merge_items_kernel(p, mine_ref, came_ref, out_ref):
@@ -353,65 +366,77 @@
     )(mine, came)
 
 
-def finish_users_kernel(n_joined, pieces, *refs):
+def finish_rates_kernel(pieces, n_came, *refs):
     refs = list(refs)
     take = lambda n: [refs.pop(0) for _ in range(n)]
-    both_ref, own_ref, sum_ref = take(3)
-    joined = take(n_joined)
-    (last_ref,) = take(1)
     item_refs = take(pieces)
-    activity_ref, popularity_ref = take(2)
-    outs = take(3)
-    bufs = take(3)
+    came = take(n_came)
+    columns = take(2)
+    outs = take(2)
+    bufs = take(2)
     (sems,) = take(1)
-    core = lax.axis_index("ka")
-    half = own_ref.shape[0]
+    theta_total, beta_total = sum_totals([ref[-EXTRA:, :] for ref in item_refs + came])
     copies = []
-
-    total = own_ref[...]
-    for ref in joined:
-        total += ref[:half, :].astype(F32)
-    start = pl.multiple_of(core * half, half)
-    bufs[0][pl.ds(start, half), :] = 0.3 + both_ref[:half, :].astype(F32) * total
-    copies.append(pltpu.make_async_copy(bufs[0].at[pl.ds(start, half)], outs[0].at[pl.ds(start, half)], sems.at[0]))
-    copies[-1].start()
-
-    total = sum_ref[:half, :].astype(F32) + last_ref[...].astype(F32)
-    start = pl.multiple_of((1 - core) * half, half)
-    bufs[0][pl.ds(start, half), :] = 0.3 + both_ref[half:, :].astype(F32) * total
-    copies.append(pltpu.make_async_copy(bufs[0].at[pl.ds(start, half)], outs[0].at[pl.ds(start, half)], sems.at[1]))
-    copies[-1].start()
-
-    theta_total, beta_total = row_totals(item_refs)
-    for ref in joined:
-        came = decode(ref[-EXTRA:, :])
-        theta_total += came[0]
-        beta_total += came[1]
-    for i, (column_ref, total) in enumerate(((activity_ref, beta_total), (popularity_ref, theta_total))):
-        rows = column_ref.shape[1]
-        column = jnp.broadcast_to(column_ref[...], (total.shape[1], rows)).T
-        bufs[1 + i][...] = column + total
-        copies.append(pltpu.make_async_copy(bufs[1 + i], outs[1 + i], sems.at[2 + i]))
+    for i, total in enumerate((beta_total, theta_total)):
+        rows = columns[i].shape[1]
+        column = jnp.broadcast_to(columns[i][...], (total.shape[1], rows)).T
+        bufs[i][...] = column + total
+        copies.append(pltpu.make_async_copy(bufs[i], outs[i], sems.at[i]))
         copies[-1].start()
     for copy in copies:
         copy.wait()
 
 
-def finish_users(both, own, other_sum, joined, other_last, items, activity, popularity):
+def finish_rates(items, came, activity, popularity):
+    args = [*items, *came, activity, popularity]
+    out_shape = [jax.ShapeDtypeStruct((c.shape[1], items[0].shape[1]), F32) for c in (activity, popularity)]
+    return pl.pallas_call(
+        functools.partial(finish_rates_kernel, len(items), len(came)),
+        in_specs=[pl.BlockSpec(memory_space=VMEM)] * len(args),
+        out_specs=[pl.BlockSpec(memory_space=HBM)] * 2,
+        out_shape=out_shape,
+        scratch_shapes=[pltpu.VMEM(o.shape, F32) for o in out_shape] + [pltpu.SemaphoreType.DMA((2,))],
+        compiler_params=pltpu.CompilerParams(vmem_limit_bytes=6 * MIB),
+        cost_estimate=CHEAP,
+        name="finish_rates",
+    )(*args)
+
+
+def finish_users_kernel(n_ahead, *refs):
+    refs = list(refs)
+    take = lambda n: [refs.pop(0) for _ in range(n)]
+    both_ref, own_ref, other_ref, last_ref, mine_ref = take(5)
+    ahead = take(n_ahead)
+    out_ref, buf, sems = take(3)
+    core = lax.axis_index("ka")
+    half = own_ref.shape[0]
+
+    def send(i, side, rows, total):
+        here = pl.ds(pl.multiple_of(side * half, half), half)
+        buf[here, :] = 0.3 + both_ref[rows, :].astype(F32) * total
+        copy = pltpu.make_async_copy(buf.at[here], out_ref.at[here], sems.at[i])
+        copy.start()
+        return copy
+
+    total = own_ref[...] + mine_ref[:half, :].astype(F32)
+    for ref in ahead:
+        total += ref[:half, :].astype(F32)
+    other = other_ref[...].astype(F32) + last_ref[:half, :].astype(F32)
+    copies = [send(0, core, slice(0, half), total), send(1, 1 - core, slice(half, 2 * half), other)]
+    for copy in copies:
+        copy.wait()
+
+
+def finish_users(both, own, other_sum, other_last, mine, ahead):
     rows, half = both.shape
-    args = [both, own, other_sum, *joined, other_last, *items, activity, popularity]
-    out_shape = [
-        jax.ShapeDtypeStruct((rows, half), F32),
-        jax.ShapeDtypeStruct((activity.shape[1], half), F32),
-        jax.ShapeDtypeStruct((popularity.shape[1], half), F32),
-    ]
+    args = [both, own, other_sum, other_last, mine, *ahead]
     return pl.pallas_call(
-        functools.partial(finish_users_kernel, len(joined), len(items)),
+        functools.partial(finish_users_kernel, len(ahead)),
         in_specs=[pl.BlockSpec(memory_space=VMEM)] * len(args),
-        out_specs=[pl.BlockSpec(memory_space=HBM)] * 3,
-        out_shape=out_shape,
-        scratch_shapes=[pltpu.VMEM(o.shape, F32) for o in out_shape] + [pltpu.SemaphoreType.DMA((4,))],
-        compiler_params=pltpu.CompilerParams(vmem_limit_bytes=8 * MIB),
+        out_specs=pl.BlockSpec(memory_space=HBM),
+        out_shape=jax.ShapeDtypeStruct((rows, half), F32),
+        scratch_shapes=[pltpu.VMEM((rows, half), F32), pltpu.SemaphoreType.DMA((2,))],
+        compiler_params=pltpu.CompilerParams(vmem_limit_bytes=4 * MIB),
         cost_estimate=CHEAP,
         name="finish_users",
     )(*args)
@@ -525,31 +550,38 @@
         latest = stats[i][0]
     own, own_other = stats[0]
 
-    joined = []
-    for distances, step in ((ahead, 1), (behind, -1)):
-        moving = None
-        for d in reversed(distances):
-            stat = stats[2 * d - (step < 0)][0]
-            moving = along_item(stat if moving is None else add_came(stat, moving), step, n_item)
-        if moving is not None:
-            joined.append(moving)
-
     came = [sibling(accs[1])]
     for p in range(1, n_user):
         sent = merge_items(p, acc, sibling(accs[1 + p]))
         came.append(along_user(sent, p, n_user))
     new_beta_shape = finish_items(item_exp, acc, came)
 
+    moving = []
+    for d in reversed(ahead):
+        stat = stats[2 * d][0]
+        parts = add_came(stat, moving[0], False) if moving else [stat]
+        moving = [along_item(x, 1, n_item) for x in parts]
+    came_ahead = moving
+    moving = []
+    for d in reversed(behind):
+        stat = stats[2 * d - 1][0]
+        if d == 1 and n_user > 1:
+            stat = after(stat, sent)
+        parts = add_came(stat, moving[0], d == 1) if moving else [stat]
+        moving = [along_item(x, -1, n_item) for x in parts]
+    other_behind, mine_behind = moving
+
     other_sum = own_other
-    for x in joined[:-1]:
+    for x in came_ahead:
         other_sum = lax.optimization_barrier(other_sum + x[half_rows:rows].astype(F32))
     other_sum = other_sum.astype(BF16)
-    other_sum = sibling(jnp.concatenate([other_sum, other_sum[: half_rows // 2]]))
-    other_last = sibling(joined[-1][half_rows:rows])
-    other_last = after(other_last, new_beta_shape)
-    new_theta_shape, new_theta_rate, new_beta_rate = finish_users(
-        both, own, other_sum, joined, other_last, item_mine, user_activity, item_popularity
+    other_sum = sibling(other_sum)
+    other_last = after(sibling(other_behind), new_beta_shape)
+    new_theta_rate, new_beta_rate = finish_rates(
+        item_mine, [*came_ahead, other_behind], user_activity, item_popularity
     )
+    mine_behind = after(mine_behind, new_theta_rate)
+    new_theta_shape = finish_users(both, own, other_sum, other_last, mine_behind, came_ahead)
     return (new_theta_shape[None], new_theta_rate[None], new_beta_shape[None], new_beta_rate[None])
 
 

time: 52.9 us -> 52.3 us (0.989)
  waiting for transfers between devices: 20.1 us -> 18 us
  starting transfers between devices: 16.2 us -> 17.1 us
  Pallas kernels: 14.9 us -> 15.5 us
    ppermute x6 -> x7, waiting for transfers between devices: 19.2 us -> 16.8 us  [along_item(): return lax.ppermute(x, 'item', [(i, (i + shift) % n) for i in range(n)])]
    ppermute x2, starting transfers between devices: 2.87 us -> 3.43 us  [along_user(): return lax.ppermute(x, 'user', [(i, i ^ distance) for i in range(n)])]
    pallas_call x2 -> x3, Pallas kernels: 1.5 us -> 2.06 us  [the longest x1 1.12 us: finish_rates(): pl.pallas_call(functools.partial(finish_rates_kernel, len(items), len(cam...]
    ppermute x6 -> x7, starting transfers between devices: 12.1 us -> 12.2 us  [along_item(): return lax.ppermute(x, 'item', [(i, (i + shift) % n) for i in range(n)])]
  transfers between devices with their start and end apart: 17 -> 18, of which waited for: 8 -> 8; matrix products, arithmetic and copies ran while one was open for 0% -> 0% of each run, Pallas kernels for 22% -> 25%
where the time goes in v11:
time: 52.3 us; the launch traced here: 52.1 us
  waiting for transfers between devices  18 us (34%)
  starting transfers between devices  17.1 us (33%)
  Pallas kernels  15.5 us (30%)
  between operations  1.43 us (3%)
    ppermute x7, waiting for transfers between devices, along_item(): return lax.ppermute(x, 'item', [(i, (i + shift) % n) for i in range(n)])  16.8 us
    ppermute x7, starting transfers between devices, along_item(): return lax.ppermute(x, 'item', [(i, (i + shift) % n) for i in range(n)])  12.2 us
    pallas_call x4, Pallas kernels, statistics(): pl.pallas_call(functools.partial(stat_kernel, len(item_mine), half_rows,...  6.64 us
    ppermute x2, starting transfers between devices, along_user(): return lax.ppermute(x, 'user', [(i, i ^ distance) for i in range(n)])  3.43 us
    pallas_call x1, Pallas kernels, dense_counts(): pl.pallas_call(functools.partial(dense_kernel, n_item, item_rows // n_use...  2.24 us
    pallas_call x1, Pallas kernels, expected_users(): pl.pallas_call(functools.partial(users_kernel, chunk), in_specs=[pl.Block...  1.77 us
    pallas_call x1, Pallas kernels, expected_items(): pl.pallas_call(functools.partial(items_kernel, chunk), in_specs=[pl.Block...  1.76 us
    ppermute x9, starting transfers between devices, sibling(): return lax.ppermute(x, 'ka', [(h, n_ka - 1 - h) for h in range(n_ka)])  1.47 us
  transfers between devices with their start and end apart: 18, of which 8 were waited for; matrix products, arithmetic and copies ran while one was open for 0% of the time, Pallas kernels for 25%

profile of v11, /device:TPU:0, one launch (start us, length us, event | category | flops | bytes accessed | tf_op | source)
XLA Modules:
  0.0 52.1 jit_solution(14397134625927103700)
XLA Ops:
  0.6 1.8 %expected_users.1 = (bf16[512,256]{1,0:T(8,128)(2,1)S(1)}, bf16[560,256]{1,0:T(8,128)(2,1)S(1)}, f32[1,256]{1,0:T(1,128)S(1)}) custom-call(f32[512,256]{1,0:T(8,128)} %bitcast.14, f32[512,256]{1,0:T(8,128)} %bitcast.15), custom_call_target="tpu_custom_call" | custom-call | flops 1024 | bytes 1024 | tf_op jit(solution)/shard_map/expected_users/pallas_call | solution.py:97
  2.4 3.1 %collective-permute-start.3 = (bf16[512,256]{1,0:T(8,128)(2,1)S(1)}, bf16[512,256]{1,0:T(8,128)(2,1)S(1)}, u32[]{:S(2)}, u32[]{:S(2)}) collective-permute-start(bf16[512,256]{1,0:T(8,128)(2,1)S(1)} %get-tuple-element.30.both_ref.refs_0_), channel_id=1, source_target_pairs={{0,4},{4,8},{8,12},{12,0},{1,5},{5,9},{9,13},{13,1},{2,6},{6,10},{... | collective-permute-start | bytes 786440 | tf_op jit(solution)/shard_map/ppermute | solution.py:478
  5.5 1.8 %expected_items.1 = (bf16[528,256]{1,0:T(8,128)(2,1)S(1)}, bf16[784,256]{1,0:T(8,128)(2,1)S(1)}) custom-call(f32[512,256]{1,0:T(8,128)} %bitcast.16, f32[512,256]{1,0:T(8,128)} %bitcast.17, bf16[512,256]{1,0:T(8,128)(2,1)S(1)} %get-tuple-element.30.both_ref.refs_0_, f32[1,256]{1,0:T(1,128)S(1)} %get-tuple-element.31.theta_ref), custom_call_target="tpu_custom_call" | custom-call | flops 1024 | bytes 1024 | tf_op jit(solution)/shard_map/expected_items/pallas_call | solution.py:141
  7.9 2.2 %dense_counts.1.refs_6_ = bf16[1024,1024]{1,0:T(8,128)(2,1)S(1)} custom-call(s32[64]{0:T(128)} %bitcast.20, s32[64]{0:T(128)} %bitcast.21, s32[1]{0:T(128)} %bitcast.12.live_ref, s32[64,128,128]{2,1,0:T(8,128)} %bitcast.13), custom_call_target="tpu_custom_call" | custom-call | flops 1024 | bytes 1024 | tf_op jit(solution)/shard_map/dense_counts/pallas_call | solution.py:212
  10.1 2.2 %collective-permute-start.1 = (bf16[528,256]{1,0:T(8,128)(2,1)S(1)}, bf16[528,256]{1,0:T(8,128)(2,1)S(1)}, u32[]{:S(2)}, u32[]{:S(2)}) collective-permute-start(bf16[528,256]{1,0:T(8,128)(2,1)S(1)} %get-tuple-element.34.refs_2_.exp_ref.refs_0_), channel_id=1, source_target_pairs={{0,2},{2,0},{1,3},{3,1},{4,6},{6,4},{5,7},{7,5},{8,10},{10,8},{9,1... | collective-permute-start | bytes 811016 | tf_op jit(solution)/shard_map/ppermute | solution.py:486
  12.3 1.5 %collective-permute-done.3.refs_0_ = bf16[512,256]{1,0:T(8,128)(2,1)S(1)} collective-permute-done((bf16[512,256]{1,0:T(8,128)(2,1)S(1)}, bf16[512,256]{1,0:T(8,128)(2,1)S(1)}, u32[]{:S(2)}, u32[]{:S(2)}) %collective-permute-start.3) | collective-permute-done | bytes 262176 | tf_op jit(solution)/shard_map/ppermute | solution.py:478
  13.8 3.8 %collective-permute-start.7 = (bf16[560,256]{1,0:T(8,128)(2,1)S(1)}, bf16[560,256]{1,0:T(8,128)(2,1)S(1)}, u32[]{:S(2)}, u32[]{:S(2)}) collective-permute-start(bf16[560,256]{1,0:T(8,128)(2,1)S(1)} %get-tuple-element.40), channel_id=1, source_target_pairs={{0,12},{4,0},{8,4},{12,8},{1,13},{5,1},{9,5},{13,9},{2,14},{6,2},{... | collective-permute-start | bytes 860168 | tf_op jit(solution)/shard_map/ppermute | solution.py:478
  17.6 1.0 %collective-permute-done.1.refs_3_.refs_1_ = bf16[528,256]{1,0:T(8,128)(2,1)S(1)} collective-permute-done((bf16[528,256]{1,0:T(8,128)(2,1)S(1)}, bf16[528,256]{1,0:T(8,128)(2,1)S(1)}, u32[]{:S(2)}, u32[]{:S(2)}) %collective-permute-start.1) | collective-permute-done | bytes 270368 | tf_op jit(solution)/shard_map/ppermute | solution.py:486
  19.2 5.7 %collective-permute-done.4.refs_0_ = bf16[512,256]{1,0:T(8,128)(2,1)S(1)} collective-permute-done((bf16[512,256]{1,0:T(8,128)(2,1)S(1)}, bf16[512,256]{1,0:T(8,128)(2,1)S(1)}, u32[]{:S(2)}, u32[]{:S(2)}) %collective-permute-start.4) | collective-permute-done | bytes 262176 | tf_op jit(solution)/shard_map/ppermute | solution.py:478
  24.9 1.7 %statistics_1.1 = (bf16[528,256]{1,0:T(8,128)(2,1)S(1)}, f32[512,1024]{1,0:T(8,128)S(1)}) custom-call(bf16[512,256]{1,0:T(8,128)(2,1)S(1)} %collective-permute-done.3.refs_0_, bf16[512,256]{1,0:T(8,128)(2,1)S(1)} %collective-permute-done.6.refs_1_, bf16[528,256]{1,0:T(8,128)(2,1)S(1)} %get-tuple-element.34.refs_2_.exp_ref.refs_0_, ...), custom_call_target="tpu_custom_call" | custom-call | flops 1024 | bytes 1024 | tf_op jit(solution)/shard_map/statistics_1/pallas_call | solution.py:309
  26.6 1.7 %statistics_3.1 = (bf16[528,256]{1,0:T(8,128)(2,1)S(1)}, f32[512,1024]{1,0:T(8,128)S(1)}) custom-call(bf16[512,256]{1,0:T(8,128)(2,1)S(1)} %collective-permute-done.4.refs_0_, bf16[512,256]{1,0:T(8,128)(2,1)S(1)} %collective-permute-done.5.refs_1_, bf16[528,256]{1,0:T(8,128)(2,1)S(1)} %get-tuple-element.34.refs_2_.exp_ref.refs_0_, ...), custom_call_target="tpu_custom_call" | custom-call | flops 1024 | bytes 1024 | tf_op jit(solution)/shard_map/statistics_3/pallas_call | solution.py:309
  28.9 0.8 %collective-permute-start.12 = (bf16[528,256]{1,0:T(8,128)(2,1)S(1)}, bf16[528,256]{1,0:T(8,128)(2,1)S(1)}, u32[]{:S(2)}, u32[]{:S(2)}) collective-permute-start(bf16[528,256]{1,0:T(8,128)(2,1)S(1)} %get-tuple-element.41), channel_id=1, source_target_pairs={{0,12},{4,0},{8,4},{12,8},{1,13},{5,1},{9,5},{13,9},{2,14},{6,2},{... | collective-permute-start | bytes 811016 | tf_op jit(solution)/shard_map/ppermute | solution.py:478
  29.7 1.7 %statistics_0.1 = (f32[256,256]{1,0:T(8,128)S(1)}, f32[256,256]{1,0:T(8,128)S(1)}, f32[512,1024]{1,0:T(8,128)S(1)}) custom-call(bf16[512,256]{1,0:T(8,128)(2,1)S(1)} %get-tuple-element.30.both_ref.refs_0_, bf16[784,256]{1,0:T(8,128)(2,1)S(1)} %collective-permute-done.refs_4_.refs_1_, bf16[528,256]{1,0:T(8,128)(2,1)S(1)} %get-tuple-element.34.refs_2_.exp_ref.refs_0_, ...), custom_call_target="tpu_custom_call" | custom-call | flops 1024 | bytes 1024 | tf_op jit(solution)/shard_map/statistics_0/pallas_call | solution.py:309
  31.4 1.7 %statistics_2.1 = (bf16[528,256]{1,0:T(8,128)(2,1)S(1)}, f32[256,1024]{1,0:T(8,128)S(1)}, bf16[256,512]{1,0:T(8,128)(2,1)S(1)}, bf16[256,512]{1,0:T(8,128)(2,1)S(1)}) custom-call(bf16[560,256]{1,0:T(8,128)(2,1)S(1)} %collective-permute-done.7.refs_0_, bf16[256,256]{1,0:T(8,128)(2,1)S(1)} %collective-permute-done.8.refs_1_, ...), custom_call_target="tpu_custom_call" | custom-call | flops 1024 | bytes 1024 | tf_op jit(solution)/shard_map/statistics_2/pallas_call | solution.py:309
  33.3 1.2 %collective-permute-start.9 = (bf16[528,256]{1,0:T(8,128)(2,1)S(1)}, bf16[528,256]{1,0:T(8,128)(2,1)S(1)}, u32[]{:S(2)}, u32[]{:S(2)}) collective-permute-start(bf16[528,256]{1,0:T(8,128)(2,1)S(1)} %get-tuple-element.44), channel_id=1, source_target_pairs={{0,4},{4,8},{8,12},{12,0},{1,5},{5,9},{9,13},{13,1},{2,6},{6,10},{... | collective-permute-start | bytes 811016 | tf_op jit(solution)/shard_map/ppermute | solution.py:478
  34.7 3.0 %collective-permute-done.12.came_ref = bf16[528,256]{1,0:T(8,128)(2,1)S(1)} collective-permute-done((bf16[528,256]{1,0:T(8,128)(2,1)S(1)}, bf16[528,256]{1,0:T(8,128)(2,1)S(1)}, u32[]{:S(2)}, u32[]{:S(2)}) %collective-permute-start.12) | collective-permute-done | bytes 270368 | tf_op jit(solution)/shard_map/ppermute | solution.py:478
  37.8 3.1 %collective-permute-start.13 = (bf16[272,256]{1,0:T(8,128)(2,1)S(1)}, bf16[272,256]{1,0:T(8,128)(2,1)S(1)}, u32[]{:S(2)}, u32[]{:S(2)}) collective-permute-start(bf16[272,256]{1,0:T(8,128)(2,1)S(1)} %get-tuple-element.49), channel_id=1, source_target_pairs={{0,12},{4,0},{8,4},{12,8},{1,13},{5,1},{9,5},{13,9},{2,14},{6,2},{... | collective-permute-start | bytes 417800 | tf_op jit(solution)/shard_map/ppermute | solution.py:478
  40.9 1.2 %collective-permute-start.16 = (bf16[256,512]{1,0:T(8,128)(2,1)S(1)}, bf16[256,512]{1,0:T(8,128)(2,1)S(1)}, u32[]{:S(2)}, u32[]{:S(2)}) collective-permute-start(bf16[256,512]{1,0:T(8,128)(2,1)S(1)} %merge_items.1), channel_id=1, source_target_pairs={{0,2},{2,0},{1,3},{3,1},{4,6},{6,4},{5,7},{7,5},{8,10},{10,8},{9,1... | collective-permute-start | bytes 786440 | tf_op jit(solution)/shard_map/ppermute | solution.py:486
  42.3 4.9 %collective-permute-done.13.refs_3_ = bf16[272,256]{1,0:T(8,128)(2,1)S(1)} collective-permute-done((bf16[272,256]{1,0:T(8,128)(2,1)S(1)}, bf16[272,256]{1,0:T(8,128)(2,1)S(1)}, u32[]{:S(2)}, u32[]{:S(2)}) %collective-permute-start.13) | collective-permute-done | bytes 139296 | tf_op jit(solution)/shard_map/ppermute | solution.py:478
  47.2 0.6 %collective-permute-start.10 = (bf16[256,256]{1,0:T(8,128)(2,1)S(1)}, bf16[256,256]{1,0:T(8,128)(2,1)S(1)}, u32[]{:S(2)}, u32[]{:S(2)}) collective-permute-start(bf16[256,256]{1,0:T(8,128)(2,1)S(1)} %convert_add_fusion), channel_id=1, source_target_pairs={{0,1},{1,0},{2,3},{3,2},{4,5},{5,4},{6,7},{7,6},{8,9},{9,8},{10,11... | collective-permute-start | bytes 393224 | tf_op jit(solution)/shard_map/ppermute | solution.py:505
  47.8 1.1 %finish_rates.1 = (f32[512,256]{1,0:T(8,128)}, f32[512,256]{1,0:T(8,128)}) custom-call(bf16[528,256]{1,0:T(8,128)(2,1)S(1)} %get-tuple-element.34.refs_2_.exp_ref.refs_0_, bf16[528,256]{1,0:T(8,128)(2,1)S(1)} %collective-permute-done.1.refs_3_.refs_1_, bf16[528,256]{1,0:T(8,128)(2,1)S(1)} %collective-permute-done.9.refs_2_.refs_5_, ...), custom_call_target="tpu_custom_call" | custom-call | flops 1024 | bytes 1024 | tf_op jit(solution)/shard_map/finish_rates/pallas_call | solution.py:393
  48.9 1.3 %collective-permute-done.17.refs_4_ = bf16[288,256]{1,0:T(8,128)(2,1)S(1)} collective-permute-done((bf16[288,256]{1,0:T(8,128)(2,1)S(1)}, bf16[288,256]{1,0:T(8,128)(2,1)S(1)}, u32[]{:S(2)}, u32[]{:S(2)}) %collective-permute-start.17) | collective-permute-done | bytes 147488 | tf_op jit(solution)/shard_map/ppermute | solution.py:478
  50.2 1.0 %finish_items.1 = f32[512,256]{1,0:T(8,128)} custom-call(bf16[528,256]{1,0:T(8,128)(2,1)S(1)} %get-tuple-element.34.refs_2_.exp_ref.refs_0_, f32[256,1024]{1,0:T(8,128)S(1)} %get-tuple-element.46.mine_ref.own_ref, bf16[256,512]{1,0:T(8,128)(2,1)S(1)} %collective-permute-done.15.refs_0_, bf16[256,512]{1,0:T(8,128)(2,1)S(1)} %collective-permute-done.16.refs_1_), custom_call_target="tpu_custom_call" | custom-call | flops 1024 | bytes 1024 | tf_op jit(solution)/shard_map/finish_items/pallas_call | solution.py:465
  51.2 0.9 %finish_users.1 = f32[512,256]{1,0:T(8,128)} custom-call(bf16[512,256]{1,0:T(8,128)(2,1)S(1)} %get-tuple-element.30.both_ref.refs_0_, f32[256,256]{1,0:T(8,128)S(1)} %get-tuple-element.37.refs_1_, bf16[256,256]{1,0:T(8,128)(2,1)S(1)} %collective-permute-done.10.refs_2_, bf16[272,256]{1,0:T(8,128)(2,1)S(1)} %collective-permute-done.14.refs_3_, ...), custom_call_target="tpu_custom_call" | custom-call | flops 1024 | bytes 1024 | tf_op jit(solution)/shard_map/finish_users/pallas_call | solution.py:433
  (30 shorter events, 1.9 us)
Async XLA Ops:
  2.4 11.4 %collective-permute-start.3 = (bf16[512,256]{1,0:T(8,128)(2,1)S(1)}, bf16[512,256]{1,0:T(8,128)(2,1)S(1)}, u32[]{:S(2)}, u32[]{:S(2)}) collective-permute-start(bf16[512,256]{1,0:T(8,128)(2,1)S(1)} %get-tuple-element.30.both_ref.refs_0_), channel_id=1, source_target_pairs={{0,4},{4,8},{8,12},{12,0},{1,5},{5,9},{9,13},{13,1},{2,6},{6,10},{... | collective-permute-start | bytes 786440 | tf_op jit(solution)/shard_map/ppermute | solution.py:478
  10.1 8.5 %collective-permute-start.1 = (bf16[528,256]{1,0:T(8,128)(2,1)S(1)}, bf16[528,256]{1,0:T(8,128)(2,1)S(1)}, u32[]{:S(2)}, u32[]{:S(2)}) collective-permute-start(bf16[528,256]{1,0:T(8,128)(2,1)S(1)} %get-tuple-element.34.refs_2_.exp_ref.refs_0_), channel_id=1, source_target_pairs={{0,2},{2,0},{1,3},{3,1},{4,6},{6,4},{5,7},{7,5},{8,10},{10,8},{9,1... | collective-permute-start | bytes 811016 | tf_op jit(solution)/shard_map/ppermute | solution.py:486
  13.8 11.1 %collective-permute-start.4 = (bf16[512,256]{1,0:T(8,128)(2,1)S(1)}, bf16[512,256]{1,0:T(8,128)(2,1)S(1)}, u32[]{:S(2)}, u32[]{:S(2)}) collective-permute-start(bf16[512,256]{1,0:T(8,128)(2,1)S(1)} %collective-permute-done.3.refs_0_), channel_id=1, source_target_pairs={{0,4},{4,8},{8,12},{12,0},{1,5},{5,9},{9,13},{13,1},{2,6},{6,10},{... | collective-permute-start | bytes 786440 | tf_op jit(solution)/shard_map/ppermute | solution.py:478
  13.8 11.1 %collective-permute-start = (bf16[784,256]{1,0:T(8,128)(2,1)S(1)}, bf16[784,256]{1,0:T(8,128)(2,1)S(1)}, u32[]{:S(2)}, u32[]{:S(2)}) collective-permute-start(bf16[784,256]{1,0:T(8,128)(2,1)S(1)} %get-tuple-element.32), channel_id=1, source_target_pairs={{0,1},{1,0},{2,3},{3,2},{4,5},{5,4},{6,7},{7,6},{8,9},{9,8},{10,11... | collective-permute-start | bytes 1204232 | tf_op jit(solution)/shard_map/ppermute | solution.py:505
  13.8 14.9 %collective-permute-start.7 = (bf16[560,256]{1,0:T(8,128)(2,1)S(1)}, bf16[560,256]{1,0:T(8,128)(2,1)S(1)}, u32[]{:S(2)}, u32[]{:S(2)}) collective-permute-start(bf16[560,256]{1,0:T(8,128)(2,1)S(1)} %get-tuple-element.40), channel_id=1, source_target_pairs={{0,12},{4,0},{8,4},{12,8},{1,13},{5,1},{9,5},{13,9},{2,14},{6,2},{... | collective-permute-start | bytes 860168 | tf_op jit(solution)/shard_map/ppermute | solution.py:478
  18.7 6.2 %collective-permute-start.2 = (bf16[528,256]{1,0:T(8,128)(2,1)S(1)}, bf16[528,256]{1,0:T(8,128)(2,1)S(1)}, u32[]{:S(2)}, u32[]{:S(2)}) collective-permute-start(bf16[528,256]{1,0:T(8,128)(2,1)S(1)} %collective-permute-done.1.refs_3_.refs_1_), channel_id=1, source_target_pairs={{0,1},{1,0},{2,3},{3,2},{4,5},{5,4},{6,7},{7,6},{8,9},{9,8},{10,11... | collective-permute-start | bytes 811016 | tf_op jit(solution)/shard_map/ppermute | solution.py:505
  18.7 6.2 %collective-permute-start.6 = (bf16[512,256]{1,0:T(8,128)(2,1)S(1)}, bf16[512,256]{1,0:T(8,128)(2,1)S(1)}, u32[]{:S(2)}, u32[]{:S(2)}) collective-permute-start(bf16[512,256]{1,0:T(8,128)(2,1)S(1)} %collective-permute-done.3.refs_0_), channel_id=1, source_target_pairs={{0,1},{1,0},{2,3},{3,2},{4,5},{5,4},{6,7},{7,6},{8,9},{9,8},{10,11... | collective-permute-start | bytes 786440 | tf_op jit(solution)/shard_map/ppermute | solution.py:505
  24.9 1.7 %collective-permute-start.5 = (bf16[512,256]{1,0:T(8,128)(2,1)S(1)}, bf16[512,256]{1,0:T(8,128)(2,1)S(1)}, u32[]{:S(2)}, u32[]{:S(2)}) collective-permute-start(bf16[512,256]{1,0:T(8,128)(2,1)S(1)} %collective-permute-done.4.refs_0_), channel_id=1, source_target_pairs={{0,1},{1,0},{2,3},{3,2},{4,5},{5,4},{6,7},{7,6},{8,9},{9,8},{10,11... | collective-permute-start | bytes 786440 | tf_op jit(solution)/shard_map/ppermute | solution.py:505
  28.7 2.6 %collective-permute-start.8 = (bf16[256,256]{1,0:T(8,128)(2,1)S(1)}, bf16[256,256]{1,0:T(8,128)(2,1)S(1)}, u32[]{:S(2)}, u32[]{:S(2)}) collective-permute-start(bf16[256,256]{1,0:T(8,128)(2,1)S(1)} %slice.6), channel_id=1, source_target_pairs={{0,1},{1,0},{2,3},{3,2},{4,5},{5,4},{6,7},{7,6},{8,9},{9,8},{10,11... | collective-permute-start | bytes 393224 | tf_op jit(solution)/shard_map/ppermute | solution.py:505
  28.9 8.8 %collective-permute-start.12 = (bf16[528,256]{1,0:T(8,128)(2,1)S(1)}, bf16[528,256]{1,0:T(8,128)(2,1)S(1)}, u32[]{:S(2)}, u32[]{:S(2)}) collective-permute-start(bf16[528,256]{1,0:T(8,128)(2,1)S(1)} %get-tuple-element.41), channel_id=1, source_target_pairs={{0,12},{4,0},{8,4},{12,8},{1,13},{5,1},{9,5},{13,9},{2,14},{6,2},{... | collective-permute-start | bytes 811016 | tf_op jit(solution)/shard_map/ppermute | solution.py:478
  33.0 14.8 %copy-start = (f32[1,512]{1,0:T(1,128)S(1)}, f32[1,512]{1,0:T(1,128)}, u32[]{:S(2)}) copy-start(f32[1,512]{1,0:T(1,128)} %refs_4_.1) | copy-start | bytes 6148
  33.0 14.8 %copy-start.1 = (f32[1,512]{1,0:T(1,128)S(1)}, f32[1,512]{1,0:T(1,128)}, u32[]{:S(2)}) copy-start(f32[1,512]{1,0:T(1,128)} %refs_5_.1) | copy-start | bytes 6148
  33.0 1.6 %collective-permute-start.11 = (bf16[256,512]{1,0:T(8,128)(2,1)S(1)}, bf16[256,512]{1,0:T(8,128)(2,1)S(1)}, u32[]{:S(2)}, u32[]{:S(2)}) collective-permute-start(bf16[256,512]{1,0:T(8,128)(2,1)S(1)} %get-tuple-element.47), channel_id=1, source_target_pairs={{0,1},{1,0},{2,3},{3,2},{4,5},{5,4},{6,7},{7,6},{8,9},{9,8},{10,11... | collective-permute-start | bytes 786440 | tf_op jit(solution)/shard_map/ppermute | solution.py:505
  33.3 13.9 %collective-permute-start.9 = (bf16[528,256]{1,0:T(8,128)(2,1)S(1)}, bf16[528,256]{1,0:T(8,128)(2,1)S(1)}, u32[]{:S(2)}, u32[]{:S(2)}) collective-permute-start(bf16[528,256]{1,0:T(8,128)(2,1)S(1)} %get-tuple-element.44), channel_id=1, source_target_pairs={{0,4},{4,8},{8,12},{12,0},{1,5},{5,9},{9,13},{13,1},{2,6},{6,10},{... | collective-permute-start | bytes 811016 | tf_op jit(solution)/shard_map/ppermute | solution.py:478
  37.8 9.4 %collective-permute-start.13 = (bf16[272,256]{1,0:T(8,128)(2,1)S(1)}, bf16[272,256]{1,0:T(8,128)(2,1)S(1)}, u32[]{:S(2)}, u32[]{:S(2)}) collective-permute-start(bf16[272,256]{1,0:T(8,128)(2,1)S(1)} %get-tuple-element.49), channel_id=1, source_target_pairs={{0,12},{4,0},{8,4},{12,8},{1,13},{5,1},{9,5},{13,9},{2,14},{6,2},{... | collective-permute-start | bytes 417800 | tf_op jit(solution)/shard_map/ppermute | solution.py:478
  40.9 9.3 %collective-permute-start.15 = (bf16[256,512]{1,0:T(8,128)(2,1)S(1)}, bf16[256,512]{1,0:T(8,128)(2,1)S(1)}, u32[]{:S(2)}, u32[]{:S(2)}) collective-permute-start(bf16[256,512]{1,0:T(8,128)(2,1)S(1)} %get-tuple-element.50), channel_id=1, source_target_pairs={{0,1},{1,0},{2,3},{3,2},{4,5},{5,4},{6,7},{7,6},{8,9},{9,8},{10,11... | collective-permute-start | bytes 786440 | tf_op jit(solution)/shard_map/ppermute | solution.py:505
  40.9 9.3 %collective-permute-start.16 = (bf16[256,512]{1,0:T(8,128)(2,1)S(1)}, bf16[256,512]{1,0:T(8,128)(2,1)S(1)}, u32[]{:S(2)}, u32[]{:S(2)}) collective-permute-start(bf16[256,512]{1,0:T(8,128)(2,1)S(1)} %merge_items.1), channel_id=1, source_target_pairs={{0,2},{2,0},{1,3},{3,1},{4,6},{6,4},{5,7},{7,5},{8,10},{10,8},{9,1... | collective-permute-start | bytes 786440 | tf_op jit(solution)/shard_map/ppermute | solution.py:486
  42.1 8.1 %collective-permute-start.17 = (bf16[288,256]{1,0:T(8,128)(2,1)S(1)}, bf16[288,256]{1,0:T(8,128)(2,1)S(1)}, u32[]{:S(2)}, u32[]{:S(2)}) collective-permute-start(bf16[288,256]{1,0:T(8,128)(2,1)S(1)} %get-tuple-element.52), channel_id=1, source_target_pairs={{0,12},{4,0},{8,4},{12,8},{1,13},{5,1},{9,5},{13,9},{2,14},{6,2},{... | collective-permute-start | bytes 442376 | tf_op jit(solution)/shard_map/ppermute | solution.py:478
  47.2 4.0 %collective-permute-start.14 = (bf16[272,256]{1,0:T(8,128)(2,1)S(1)}, bf16[272,256]{1,0:T(8,128)(2,1)S(1)}, u32[]{:S(2)}, u32[]{:S(2)}) collective-permute-start(bf16[272,256]{1,0:T(8,128)(2,1)S(1)} %collective-permute-done.13.refs_3_), channel_id=1, source_target_pairs={{0,1},{1,0},{2,3},{3,2},{4,5},{5,4},{6,7},{7,6},{8,9},{9,8},{10,11... | collective-permute-start | bytes 417800 | tf_op jit(solution)/shard_map/ppermute | solution.py:505
  47.2 4.0 %collective-permute-start.10 = (bf16[256,256]{1,0:T(8,128)(2,1)S(1)}, bf16[256,256]{1,0:T(8,128)(2,1)S(1)}, u32[]{:S(2)}, u32[]{:S(2)}) collective-permute-start(bf16[256,256]{1,0:T(8,128)(2,1)S(1)} %convert_add_fusion), channel_id=1, source_target_pairs={{0,1},{1,0},{2,3},{3,2},{4,5},{5,4},{6,7},{7,6},{8,9},{9,8},{10,11... | collective-permute-start | bytes 393224 | tf_op jit(solution)/shard_map/ppermute | solution.py:505

commit v12 on v11

--- a/solution.py
+++ b/solution.py
@@ -580,7 +580,7 @@
     new_theta_rate, new_beta_rate = finish_rates(
         item_mine, [*came_ahead, other_behind], user_activity, item_popularity
     )
-    mine_behind = after(mine_behind, new_theta_rate)
+    other_last = after(other_last, new_theta_rate)
     new_theta_shape = finish_users(both, own, other_sum, other_last, mine_behind, came_ahead)
     return (new_theta_shape[None], new_theta_rate[None], new_beta_shape[None], new_beta_rate[None])
 

time: 52.3 us -> 51.7 us (0.989)
  starting transfers between devices: 17.1 us -> 16.5 us
    ppermute x2, starting transfers between devices: 3.43 us -> 2.77 us  [along_user(): return lax.ppermute(x, 'user', [(i, i ^ distance) for i in range(n)])]
where the time goes in v12:
time: 51.7 us; the launch traced here: 51.5 us
  waiting for transfers between devices  18.1 us (35%)
  starting transfers between devices  16.5 us (32%)
  Pallas kernels  15.5 us (30%)
  between operations  1.45 us (3%)
    ppermute x7, waiting for transfers between devices, along_item(): return lax.ppermute(x, 'item', [(i, (i + shift) % n) for i in range(n)])  16.6 us
    ppermute x7, starting transfers between devices, along_item(): return lax.ppermute(x, 'item', [(i, (i + shift) % n) for i in range(n)])  12.2 us
    pallas_call x4, Pallas kernels, statistics(): pl.pallas_call(functools.partial(stat_kernel, len(item_mine), half_rows,...  6.64 us
    ppermute x2, starting transfers between devices, along_user(): return lax.ppermute(x, 'user', [(i, i ^ distance) for i in range(n)])  2.77 us
    pallas_call x1, Pallas kernels, dense_counts(): pl.pallas_call(functools.partial(dense_kernel, n_item, item_rows // n_use...  2.24 us
    pallas_call x1, Pallas kernels, expected_users(): pl.pallas_call(functools.partial(users_kernel, chunk), in_specs=[pl.Block...  1.77 us
    pallas_call x1, Pallas kernels, expected_items(): pl.pallas_call(functools.partial(items_kernel, chunk), in_specs=[pl.Block...  1.76 us
    ppermute x9, starting transfers between devices, sibling(): return lax.ppermute(x, 'ka', [(h, n_ka - 1 - h) for h in range(n_ka)])  1.47 us
  transfers between devices with their start and end apart: 18, of which 8 were waited for; matrix products, arithmetic and copies ran while one was open for 0% of the time, Pallas kernels for 25%

profile of v12, /device:TPU:0, one launch (start us, length us, event | category | flops | bytes accessed | tf_op | source)
XLA Modules:
  0.0 51.5 jit_solution(9453610192820662592)
XLA Ops:
  0.6 1.8 %expected_users.1 = (bf16[512,256]{1,0:T(8,128)(2,1)S(1)}, bf16[560,256]{1,0:T(8,128)(2,1)S(1)}, f32[1,256]{1,0:T(1,128)S(1)}) custom-call(f32[512,256]{1,0:T(8,128)} %bitcast.14, f32[512,256]{1,0:T(8,128)} %bitcast.15), custom_call_target="tpu_custom_call" | custom-call | flops 1024 | bytes 1024 | tf_op jit(solution)/shard_map/expected_users/pallas_call | solution.py:97
  2.4 3.1 %collective-permute-start.3 = (bf16[512,256]{1,0:T(8,128)(2,1)S(1)}, bf16[512,256]{1,0:T(8,128)(2,1)S(1)}, u32[]{:S(2)}, u32[]{:S(2)}) collective-permute-start(bf16[512,256]{1,0:T(8,128)(2,1)S(1)} %get-tuple-element.30.both_ref.refs_0_), channel_id=1, source_target_pairs={{0,4},{4,8},{8,12},{12,0},{1,5},{5,9},{9,13},{13,1},{2,6},{6,10},{... | collective-permute-start | bytes 786440 | tf_op jit(solution)/shard_map/ppermute | solution.py:478
  5.5 1.8 %expected_items.1 = (bf16[528,256]{1,0:T(8,128)(2,1)S(1)}, bf16[784,256]{1,0:T(8,128)(2,1)S(1)}) custom-call(f32[512,256]{1,0:T(8,128)} %bitcast.16, f32[512,256]{1,0:T(8,128)} %bitcast.17, bf16[512,256]{1,0:T(8,128)(2,1)S(1)} %get-tuple-element.30.both_ref.refs_0_, f32[1,256]{1,0:T(1,128)S(1)} %get-tuple-element.31.theta_ref), custom_call_target="tpu_custom_call" | custom-call | flops 1024 | bytes 1024 | tf_op jit(solution)/shard_map/expected_items/pallas_call | solution.py:141
  7.9 2.2 %dense_counts.1.refs_6_ = bf16[1024,1024]{1,0:T(8,128)(2,1)S(1)} custom-call(s32[64]{0:T(128)} %bitcast.20, s32[64]{0:T(128)} %bitcast.21, s32[1]{0:T(128)} %bitcast.12.live_ref, s32[64,128,128]{2,1,0:T(8,128)} %bitcast.13), custom_call_target="tpu_custom_call" | custom-call | flops 1024 | bytes 1024 | tf_op jit(solution)/shard_map/dense_counts/pallas_call | solution.py:212
  10.1 1.6 %collective-permute-start.1 = (bf16[528,256]{1,0:T(8,128)(2,1)S(1)}, bf16[528,256]{1,0:T(8,128)(2,1)S(1)}, u32[]{:S(2)}, u32[]{:S(2)}) collective-permute-start(bf16[528,256]{1,0:T(8,128)(2,1)S(1)} %get-tuple-element.34.refs_2_.exp_ref.refs_0_), channel_id=1, source_target_pairs={{0,2},{2,0},{1,3},{3,1},{4,6},{6,4},{5,7},{7,5},{8,10},{10,8},{9,1... | collective-permute-start | bytes 811016 | tf_op jit(solution)/shard_map/ppermute | solution.py:486
  11.7 2.1 %collective-permute-done.3.refs_0_ = bf16[512,256]{1,0:T(8,128)(2,1)S(1)} collective-permute-done((bf16[512,256]{1,0:T(8,128)(2,1)S(1)}, bf16[512,256]{1,0:T(8,128)(2,1)S(1)}, u32[]{:S(2)}, u32[]{:S(2)}) %collective-permute-start.3) | collective-permute-done | bytes 262176 | tf_op jit(solution)/shard_map/ppermute | solution.py:478
  13.8 3.8 %collective-permute-start.7 = (bf16[560,256]{1,0:T(8,128)(2,1)S(1)}, bf16[560,256]{1,0:T(8,128)(2,1)S(1)}, u32[]{:S(2)}, u32[]{:S(2)}) collective-permute-start(bf16[560,256]{1,0:T(8,128)(2,1)S(1)} %get-tuple-element.40), channel_id=1, source_target_pairs={{0,12},{4,0},{8,4},{12,8},{1,13},{5,1},{9,5},{13,9},{2,14},{6,2},{... | collective-permute-start | bytes 860168 | tf_op jit(solution)/shard_map/ppermute | solution.py:478
  17.6 0.5 collective-permute-done.1.refs_3_.refs_1_
  18.7 6.2 %collective-permute-done.4.refs_0_ = bf16[512,256]{1,0:T(8,128)(2,1)S(1)} collective-permute-done((bf16[512,256]{1,0:T(8,128)(2,1)S(1)}, bf16[512,256]{1,0:T(8,128)(2,1)S(1)}, u32[]{:S(2)}, u32[]{:S(2)}) %collective-permute-start.4) | collective-permute-done | bytes 262176 | tf_op jit(solution)/shard_map/ppermute | solution.py:478
  24.9 1.7 %statistics_1.1 = (bf16[528,256]{1,0:T(8,128)(2,1)S(1)}, f32[512,1024]{1,0:T(8,128)S(1)}) custom-call(bf16[512,256]{1,0:T(8,128)(2,1)S(1)} %collective-permute-done.3.refs_0_, bf16[512,256]{1,0:T(8,128)(2,1)S(1)} %collective-permute-done.6.refs_1_, bf16[528,256]{1,0:T(8,128)(2,1)S(1)} %get-tuple-element.34.refs_2_.exp_ref.refs_0_, ...), custom_call_target="tpu_custom_call" | custom-call | flops 1024 | bytes 1024 | tf_op jit(solution)/shard_map/statistics_1/pallas_call | solution.py:309
  26.6 1.7 %statistics_3.1 = (bf16[528,256]{1,0:T(8,128)(2,1)S(1)}, f32[512,1024]{1,0:T(8,128)S(1)}) custom-call(bf16[512,256]{1,0:T(8,128)(2,1)S(1)} %collective-permute-done.4.refs_0_, bf16[512,256]{1,0:T(8,128)(2,1)S(1)} %collective-permute-done.5.refs_1_, bf16[528,256]{1,0:T(8,128)(2,1)S(1)} %get-tuple-element.34.refs_2_.exp_ref.refs_0_, ...), custom_call_target="tpu_custom_call" | custom-call | flops 1024 | bytes 1024 | tf_op jit(solution)/shard_map/statistics_3/pallas_call | solution.py:309
  28.8 0.9 %collective-permute-start.12 = (bf16[528,256]{1,0:T(8,128)(2,1)S(1)}, bf16[528,256]{1,0:T(8,128)(2,1)S(1)}, u32[]{:S(2)}, u32[]{:S(2)}) collective-permute-start(bf16[528,256]{1,0:T(8,128)(2,1)S(1)} %get-tuple-element.41), channel_id=1, source_target_pairs={{0,12},{4,0},{8,4},{12,8},{1,13},{5,1},{9,5},{13,9},{2,14},{6,2},{... | collective-permute-start | bytes 811016 | tf_op jit(solution)/shard_map/ppermute | solution.py:478
  29.7 1.7 %statistics_0.1 = (f32[256,256]{1,0:T(8,128)S(1)}, f32[256,256]{1,0:T(8,128)S(1)}, f32[512,1024]{1,0:T(8,128)S(1)}) custom-call(bf16[512,256]{1,0:T(8,128)(2,1)S(1)} %get-tuple-element.30.both_ref.refs_0_, bf16[784,256]{1,0:T(8,128)(2,1)S(1)} %collective-permute-done.refs_4_.refs_1_, bf16[528,256]{1,0:T(8,128)(2,1)S(1)} %get-tuple-element.34.refs_2_.exp_ref.refs_0_, ...), custom_call_target="tpu_custom_call" | custom-call | flops 1024 | bytes 1024 | tf_op jit(solution)/shard_map/statistics_0/pallas_call | solution.py:309
  31.4 1.7 %statistics_2.1 = (bf16[528,256]{1,0:T(8,128)(2,1)S(1)}, f32[256,1024]{1,0:T(8,128)S(1)}, bf16[256,512]{1,0:T(8,128)(2,1)S(1)}, bf16[256,512]{1,0:T(8,128)(2,1)S(1)}) custom-call(bf16[560,256]{1,0:T(8,128)(2,1)S(1)} %collective-permute-done.7.refs_0_, bf16[256,256]{1,0:T(8,128)(2,1)S(1)} %collective-permute-done.8.refs_1_, ...), custom_call_target="tpu_custom_call" | custom-call | flops 1024 | bytes 1024 | tf_op jit(solution)/shard_map/statistics_2/pallas_call | solution.py:309
  33.3 1.2 %collective-permute-start.9 = (bf16[528,256]{1,0:T(8,128)(2,1)S(1)}, bf16[528,256]{1,0:T(8,128)(2,1)S(1)}, u32[]{:S(2)}, u32[]{:S(2)}) collective-permute-start(bf16[528,256]{1,0:T(8,128)(2,1)S(1)} %get-tuple-element.44), channel_id=1, source_target_pairs={{0,4},{4,8},{8,12},{12,0},{1,5},{5,9},{9,13},{13,1},{2,6},{6,10},{... | collective-permute-start | bytes 811016 | tf_op jit(solution)/shard_map/ppermute | solution.py:478
  34.7 2.9 %collective-permute-done.12.came_ref = bf16[528,256]{1,0:T(8,128)(2,1)S(1)} collective-permute-done((bf16[528,256]{1,0:T(8,128)(2,1)S(1)}, bf16[528,256]{1,0:T(8,128)(2,1)S(1)}, u32[]{:S(2)}, u32[]{:S(2)}) %collective-permute-start.12) | collective-permute-done | bytes 270368 | tf_op jit(solution)/shard_map/ppermute | solution.py:478
  37.8 3.2 %collective-permute-start.13 = (bf16[272,256]{1,0:T(8,128)(2,1)S(1)}, bf16[272,256]{1,0:T(8,128)(2,1)S(1)}, u32[]{:S(2)}, u32[]{:S(2)}) collective-permute-start(bf16[272,256]{1,0:T(8,128)(2,1)S(1)} %get-tuple-element.49), channel_id=1, source_target_pairs={{0,12},{4,0},{8,4},{12,8},{1,13},{5,1},{9,5},{13,9},{2,14},{6,2},{... | collective-permute-start | bytes 417800 | tf_op jit(solution)/shard_map/ppermute | solution.py:478
  40.9 1.2 %collective-permute-start.16 = (bf16[256,512]{1,0:T(8,128)(2,1)S(1)}, bf16[256,512]{1,0:T(8,128)(2,1)S(1)}, u32[]{:S(2)}, u32[]{:S(2)}) collective-permute-start(bf16[256,512]{1,0:T(8,128)(2,1)S(1)} %merge_items.1), channel_id=1, source_target_pairs={{0,2},{2,0},{1,3},{3,1},{4,6},{6,4},{5,7},{7,5},{8,10},{10,8},{9,1... | collective-permute-start | bytes 786440 | tf_op jit(solution)/shard_map/ppermute | solution.py:486
  42.3 4.9 %collective-permute-done.13.refs_3_ = bf16[272,256]{1,0:T(8,128)(2,1)S(1)} collective-permute-done((bf16[272,256]{1,0:T(8,128)(2,1)S(1)}, bf16[272,256]{1,0:T(8,128)(2,1)S(1)}, u32[]{:S(2)}, u32[]{:S(2)}) %collective-permute-start.13) | collective-permute-done | bytes 139296 | tf_op jit(solution)/shard_map/ppermute | solution.py:478
  47.2 0.6 %collective-permute-start.10 = (bf16[256,256]{1,0:T(8,128)(2,1)S(1)}, bf16[256,256]{1,0:T(8,128)(2,1)S(1)}, u32[]{:S(2)}, u32[]{:S(2)}) collective-permute-start(bf16[256,256]{1,0:T(8,128)(2,1)S(1)} %convert_add_fusion), channel_id=1, source_target_pairs={{0,1},{1,0},{2,3},{3,2},{4,5},{5,4},{6,7},{7,6},{8,9},{9,8},{10,11... | collective-permute-start | bytes 393224 | tf_op jit(solution)/shard_map/ppermute | solution.py:505
  47.8 1.1 %finish_rates.1 = (f32[512,256]{1,0:T(8,128)}, f32[512,256]{1,0:T(8,128)}) custom-call(bf16[528,256]{1,0:T(8,128)(2,1)S(1)} %get-tuple-element.34.refs_2_.exp_ref.refs_0_, bf16[528,256]{1,0:T(8,128)(2,1)S(1)} %collective-permute-done.1.refs_3_.refs_1_, bf16[528,256]{1,0:T(8,128)(2,1)S(1)} %collective-permute-done.9.refs_2_.refs_5_, ...), custom_call_target="tpu_custom_call" | custom-call | flops 1024 | bytes 1024 | tf_op jit(solution)/shard_map/finish_rates/pallas_call | solution.py:393
  48.9 0.7 %collective-permute-done.16.refs_1_ = bf16[256,512]{1,0:T(8,128)(2,1)S(1)} collective-permute-done((bf16[256,512]{1,0:T(8,128)(2,1)S(1)}, bf16[256,512]{1,0:T(8,128)(2,1)S(1)}, u32[]{:S(2)}, u32[]{:S(2)}) %collective-permute-start.16) | collective-permute-done | bytes 262176 | tf_op jit(solution)/shard_map/ppermute | solution.py:486
  49.6 1.0 %finish_items.1 = f32[512,256]{1,0:T(8,128)} custom-call(bf16[528,256]{1,0:T(8,128)(2,1)S(1)} %get-tuple-element.34.refs_2_.exp_ref.refs_0_, f32[256,1024]{1,0:T(8,128)S(1)} %get-tuple-element.46.mine_ref.own_ref, bf16[256,512]{1,0:T(8,128)(2,1)S(1)} %collective-permute-done.15.refs_0_, bf16[256,512]{1,0:T(8,128)(2,1)S(1)} %collective-permute-done.16.refs_1_), custom_call_target="tpu_custom_call" | custom-call | flops 1024 | bytes 1024 | tf_op jit(solution)/shard_map/finish_items/pallas_call | solution.py:465
  50.6 0.9 %finish_users.1 = f32[512,256]{1,0:T(8,128)} custom-call(bf16[512,256]{1,0:T(8,128)(2,1)S(1)} %get-tuple-element.30.both_ref.refs_0_, f32[256,256]{1,0:T(8,128)S(1)} %get-tuple-element.37.refs_1_, bf16[256,256]{1,0:T(8,128)(2,1)S(1)} %collective-permute-done.10.refs_2_, bf16[272,256]{1,0:T(8,128)(2,1)S(1)} %collective-permute-done.14.refs_3_, ...), custom_call_target="tpu_custom_call" | custom-call | flops 1024 | bytes 1024 | tf_op jit(solution)/shard_map/finish_users/pallas_call | solution.py:433
  (30 shorter events, 1.9 us)
Async XLA Ops:
  2.4 11.4 %collective-permute-start.3 = (bf16[512,256]{1,0:T(8,128)(2,1)S(1)}, bf16[512,256]{1,0:T(8,128)(2,1)S(1)}, u32[]{:S(2)}, u32[]{:S(2)}) collective-permute-start(bf16[512,256]{1,0:T(8,128)(2,1)S(1)} %get-tuple-element.30.both_ref.refs_0_), channel_id=1, source_target_pairs={{0,4},{4,8},{8,12},{12,0},{1,5},{5,9},{9,13},{13,1},{2,6},{6,10},{... | collective-permute-start | bytes 786440 | tf_op jit(solution)/shard_map/ppermute | solution.py:478
  10.1 8.0 %collective-permute-start.1 = (bf16[528,256]{1,0:T(8,128)(2,1)S(1)}, bf16[528,256]{1,0:T(8,128)(2,1)S(1)}, u32[]{:S(2)}, u32[]{:S(2)}) collective-permute-start(bf16[528,256]{1,0:T(8,128)(2,1)S(1)} %get-tuple-element.34.refs_2_.exp_ref.refs_0_), channel_id=1, source_target_pairs={{0,2},{2,0},{1,3},{3,1},{4,6},{6,4},{5,7},{7,5},{8,10},{10,8},{9,1... | collective-permute-start | bytes 811016 | tf_op jit(solution)/shard_map/ppermute | solution.py:486
  13.8 11.1 %collective-permute-start.4 = (bf16[512,256]{1,0:T(8,128)(2,1)S(1)}, bf16[512,256]{1,0:T(8,128)(2,1)S(1)}, u32[]{:S(2)}, u32[]{:S(2)}) collective-permute-start(bf16[512,256]{1,0:T(8,128)(2,1)S(1)} %collective-permute-done.3.refs_0_), channel_id=1, source_target_pairs={{0,4},{4,8},{8,12},{12,0},{1,5},{5,9},{9,13},{13,1},{2,6},{6,10},{... | collective-permute-start | bytes 786440 | tf_op jit(solution)/shard_map/ppermute | solution.py:478
  13.8 11.1 %collective-permute-start = (bf16[784,256]{1,0:T(8,128)(2,1)S(1)}, bf16[784,256]{1,0:T(8,128)(2,1)S(1)}, u32[]{:S(2)}, u32[]{:S(2)}) collective-permute-start(bf16[784,256]{1,0:T(8,128)(2,1)S(1)} %get-tuple-element.32), channel_id=1, source_target_pairs={{0,1},{1,0},{2,3},{3,2},{4,5},{5,4},{6,7},{7,6},{8,9},{9,8},{10,11... | collective-permute-start | bytes 1204232 | tf_op jit(solution)/shard_map/ppermute | solution.py:505
  13.8 14.9 %collective-permute-start.7 = (bf16[560,256]{1,0:T(8,128)(2,1)S(1)}, bf16[560,256]{1,0:T(8,128)(2,1)S(1)}, u32[]{:S(2)}, u32[]{:S(2)}) collective-permute-start(bf16[560,256]{1,0:T(8,128)(2,1)S(1)} %get-tuple-element.40), channel_id=1, source_target_pairs={{0,12},{4,0},{8,4},{12,8},{1,13},{5,1},{9,5},{13,9},{2,14},{6,2},{... | collective-permute-start | bytes 860168 | tf_op jit(solution)/shard_map/ppermute | solution.py:478
  18.2 6.8 %collective-permute-start.2 = (bf16[528,256]{1,0:T(8,128)(2,1)S(1)}, bf16[528,256]{1,0:T(8,128)(2,1)S(1)}, u32[]{:S(2)}, u32[]{:S(2)}) collective-permute-start(bf16[528,256]{1,0:T(8,128)(2,1)S(1)} %collective-permute-done.1.refs_3_.refs_1_), channel_id=1, source_target_pairs={{0,1},{1,0},{2,3},{3,2},{4,5},{5,4},{6,7},{7,6},{8,9},{9,8},{10,11... | collective-permute-start | bytes 811016 | tf_op jit(solution)/shard_map/ppermute | solution.py:505
  18.2 6.8 %collective-permute-start.6 = (bf16[512,256]{1,0:T(8,128)(2,1)S(1)}, bf16[512,256]{1,0:T(8,128)(2,1)S(1)}, u32[]{:S(2)}, u32[]{:S(2)}) collective-permute-start(bf16[512,256]{1,0:T(8,128)(2,1)S(1)} %collective-permute-done.3.refs_0_), channel_id=1, source_target_pairs={{0,1},{1,0},{2,3},{3,2},{4,5},{5,4},{6,7},{7,6},{8,9},{9,8},{10,11... | collective-permute-start | bytes 786440 | tf_op jit(solution)/shard_map/ppermute | solution.py:505
  24.9 1.7 %collective-permute-start.5 = (bf16[512,256]{1,0:T(8,128)(2,1)S(1)}, bf16[512,256]{1,0:T(8,128)(2,1)S(1)}, u32[]{:S(2)}, u32[]{:S(2)}) collective-permute-start(bf16[512,256]{1,0:T(8,128)(2,1)S(1)} %collective-permute-done.4.refs_0_), channel_id=1, source_target_pairs={{0,1},{1,0},{2,3},{3,2},{4,5},{5,4},{6,7},{7,6},{8,9},{9,8},{10,11... | collective-permute-start | bytes 786440 | tf_op jit(solution)/shard_map/ppermute | solution.py:505
  28.7 2.7 %collective-permute-start.8 = (bf16[256,256]{1,0:T(8,128)(2,1)S(1)}, bf16[256,256]{1,0:T(8,128)(2,1)S(1)}, u32[]{:S(2)}, u32[]{:S(2)}) collective-permute-start(bf16[256,256]{1,0:T(8,128)(2,1)S(1)} %slice.6), channel_id=1, source_target_pairs={{0,1},{1,0},{2,3},{3,2},{4,5},{5,4},{6,7},{7,6},{8,9},{9,8},{10,11... | collective-permute-start | bytes 393224 | tf_op jit(solution)/shard_map/ppermute | solution.py:505
  28.8 8.8 %collective-permute-start.12 = (bf16[528,256]{1,0:T(8,128)(2,1)S(1)}, bf16[528,256]{1,0:T(8,128)(2,1)S(1)}, u32[]{:S(2)}, u32[]{:S(2)}) collective-permute-start(bf16[528,256]{1,0:T(8,128)(2,1)S(1)} %get-tuple-element.41), channel_id=1, source_target_pairs={{0,12},{4,0},{8,4},{12,8},{1,13},{5,1},{9,5},{13,9},{2,14},{6,2},{... | collective-permute-start | bytes 811016 | tf_op jit(solution)/shard_map/ppermute | solution.py:478
  33.1 14.7 %copy-start = (f32[1,512]{1,0:T(1,128)S(1)}, f32[1,512]{1,0:T(1,128)}, u32[]{:S(2)}) copy-start(f32[1,512]{1,0:T(1,128)} %refs_4_.1) | copy-start | bytes 6148
  33.1 14.7 %copy-start.1 = (f32[1,512]{1,0:T(1,128)S(1)}, f32[1,512]{1,0:T(1,128)}, u32[]{:S(2)}) copy-start(f32[1,512]{1,0:T(1,128)} %refs_5_.1) | copy-start | bytes 6148
  33.1 1.6 %collective-permute-start.11 = (bf16[256,512]{1,0:T(8,128)(2,1)S(1)}, bf16[256,512]{1,0:T(8,128)(2,1)S(1)}, u32[]{:S(2)}, u32[]{:S(2)}) collective-permute-start(bf16[256,512]{1,0:T(8,128)(2,1)S(1)} %get-tuple-element.47), channel_id=1, source_target_pairs={{0,1},{1,0},{2,3},{3,2},{4,5},{5,4},{6,7},{7,6},{8,9},{9,8},{10,11... | collective-permute-start | bytes 786440 | tf_op jit(solution)/shard_map/ppermute | solution.py:505
  33.3 13.9 %collective-permute-start.9 = (bf16[528,256]{1,0:T(8,128)(2,1)S(1)}, bf16[528,256]{1,0:T(8,128)(2,1)S(1)}, u32[]{:S(2)}, u32[]{:S(2)}) collective-permute-start(bf16[528,256]{1,0:T(8,128)(2,1)S(1)} %get-tuple-element.44), channel_id=1, source_target_pairs={{0,4},{4,8},{8,12},{12,0},{1,5},{5,9},{9,13},{13,1},{2,6},{6,10},{... | collective-permute-start | bytes 811016 | tf_op jit(solution)/shard_map/ppermute | solution.py:478
  37.8 9.4 %collective-permute-start.13 = (bf16[272,256]{1,0:T(8,128)(2,1)S(1)}, bf16[272,256]{1,0:T(8,128)(2,1)S(1)}, u32[]{:S(2)}, u32[]{:S(2)}) collective-permute-start(bf16[272,256]{1,0:T(8,128)(2,1)S(1)} %get-tuple-element.49), channel_id=1, source_target_pairs={{0,12},{4,0},{8,4},{12,8},{1,13},{5,1},{9,5},{13,9},{2,14},{6,2},{... | collective-permute-start | bytes 417800 | tf_op jit(solution)/shard_map/ppermute | solution.py:478
  40.9 8.0 %collective-permute-start.15 = (bf16[256,512]{1,0:T(8,128)(2,1)S(1)}, bf16[256,512]{1,0:T(8,128)(2,1)S(1)}, u32[]{:S(2)}, u32[]{:S(2)}) collective-permute-start(bf16[256,512]{1,0:T(8,128)(2,1)S(1)} %get-tuple-element.50), channel_id=1, source_target_pairs={{0,1},{1,0},{2,3},{3,2},{4,5},{5,4},{6,7},{7,6},{8,9},{9,8},{10,11... | collective-permute-start | bytes 786440 | tf_op jit(solution)/shard_map/ppermute | solution.py:505
  40.9 8.7 %collective-permute-start.16 = (bf16[256,512]{1,0:T(8,128)(2,1)S(1)}, bf16[256,512]{1,0:T(8,128)(2,1)S(1)}, u32[]{:S(2)}, u32[]{:S(2)}) collective-permute-start(bf16[256,512]{1,0:T(8,128)(2,1)S(1)} %merge_items.1), channel_id=1, source_target_pairs={{0,2},{2,0},{1,3},{3,1},{4,6},{6,4},{5,7},{7,5},{8,10},{10,8},{9,1... | collective-permute-start | bytes 786440 | tf_op jit(solution)/shard_map/ppermute | solution.py:486
  42.1 8.5 %collective-permute-start.17 = (bf16[288,256]{1,0:T(8,128)(2,1)S(1)}, bf16[288,256]{1,0:T(8,128)(2,1)S(1)}, u32[]{:S(2)}, u32[]{:S(2)}) collective-permute-start(bf16[288,256]{1,0:T(8,128)(2,1)S(1)} %get-tuple-element.54), channel_id=1, source_target_pairs={{0,12},{4,0},{8,4},{12,8},{1,13},{5,1},{9,5},{13,9},{2,14},{6,2},{... | collective-permute-start | bytes 442376 | tf_op jit(solution)/shard_map/ppermute | solution.py:478
  47.2 3.4 %collective-permute-start.14 = (bf16[272,256]{1,0:T(8,128)(2,1)S(1)}, bf16[272,256]{1,0:T(8,128)(2,1)S(1)}, u32[]{:S(2)}, u32[]{:S(2)}) collective-permute-start(bf16[272,256]{1,0:T(8,128)(2,1)S(1)} %collective-permute-done.13.refs_3_), channel_id=1, source_target_pairs={{0,1},{1,0},{2,3},{3,2},{4,5},{5,4},{6,7},{7,6},{8,9},{9,8},{10,11... | collective-permute-start | bytes 417800 | tf_op jit(solution)/shard_map/ppermute | solution.py:505
  47.2 3.4 %collective-permute-start.10 = (bf16[256,256]{1,0:T(8,128)(2,1)S(1)}, bf16[256,256]{1,0:T(8,128)(2,1)S(1)}, u32[]{:S(2)}, u32[]{:S(2)}) collective-permute-start(bf16[256,256]{1,0:T(8,128)(2,1)S(1)} %convert_add_fusion), channel_id=1, source_target_pairs={{0,1},{1,0},{2,3},{3,2},{4,5},{5,4},{6,7},{7,6},{8,9},{9,8},{10,11... | collective-permute-start | bytes 393224 | tf_op jit(solution)/shard_map/ppermute | solution.py:505

commit v13 on v12

--- a/solution.py
+++ b/solution.py
@@ -100,7 +100,7 @@
         out_specs=[pl.BlockSpec(memory_space=VMEM)] * 3,
         out_shape=[
             jax.ShapeDtypeStruct((rows, cols), BF16),
-            jax.ShapeDtypeStruct((rows + 3 * EXTRA, cols), BF16),
+            jax.ShapeDtypeStruct((rows + 1 * EXTRA, cols), BF16),
             jax.ShapeDtypeStruct((1, cols), F32),
         ],
         scratch_shapes=[

time: 51.7 us -> 53.5 us (1.035)
  waiting for transfers between devices: 18.1 us -> 19.3 us
  starting transfers between devices: 16.5 us -> 17.3 us
    ppermute x2, waiting for transfers between devices: 1.22 us -> 5.28 us  [along_user(): return lax.ppermute(x, 'user', [(i, i ^ distance) for i in range(n)])]
    ppermute x7, waiting for transfers between devices: 16.6 us -> 12.6 us  [along_item(): return lax.ppermute(x, 'item', [(i, (i + shift) % n) for i in range(n)])]
    ppermute x9, waiting for transfers between devices: 0.23 us -> 1.39 us  [sibling(): return lax.ppermute(x, 'ka', [(h, n_ka - 1 - h) for h in range(n_ka)])]
    ppermute x7, starting transfers between devices: 12.2 us -> 12.8 us  [along_item(): return lax.ppermute(x, 'item', [(i, (i + shift) % n) for i in range(n)])]
  transfers between devices with their start and end apart: 18 -> 18, of which waited for: 8 -> 8; matrix products, arithmetic and copies ran while one was open for 0% -> 0% of each run, Pallas kernels for 25% -> 24%
where the time goes in v13:
time: 53.5 us
  waiting for transfers between devices  19.3 us (36%)
  starting transfers between devices  17.3 us (32%)
  Pallas kernels  15.5 us (29%)
  between operations  1.44 us (3%)
    ppermute x7, starting transfers between devices, along_item(): return lax.ppermute(x, 'item', [(i, (i + shift) % n) for i in range(n)])  12.8 us
    ppermute x7, waiting for transfers between devices, along_item(): return lax.ppermute(x, 'item', [(i, (i + shift) % n) for i in range(n)])  12.6 us
    pallas_call x4, Pallas kernels, statistics(): pl.pallas_call(functools.partial(stat_kernel, len(item_mine), half_rows,...  6.63 us
    ppermute x2, waiting for transfers between devices, along_user(): return lax.ppermute(x, 'user', [(i, i ^ distance) for i in range(n)])  5.28 us
    ppermute x2, starting transfers between devices, along_user(): return lax.ppermute(x, 'user', [(i, i ^ distance) for i in range(n)])  3.3 us
    pallas_call x1, Pallas kernels, dense_counts(): pl.pallas_call(functools.partial(dense_kernel, n_item, item_rows // n_use...  2.24 us
    pallas_call x1, Pallas kernels, expected_users(): pl.pallas_call(functools.partial(users_kernel, chunk), in_specs=[pl.Block...  1.77 us
    pallas_call x1, Pallas kernels, expected_items(): pl.pallas_call(functools.partial(items_kernel, chunk), in_specs=[pl.Block...  1.76 us
  transfers between devices with their start and end apart: 18, of which 8 were waited for; matrix products, arithmetic and copies ran while one was open for 0% of the time, Pallas kernels for 24%

profile of v13, /device:TPU:0, one launch (start us, length us, event | category | flops | bytes accessed | tf_op | source)
XLA Modules:
  0.0 53.5 jit_solution(3537821895820356723)
XLA Ops:
  0.6 1.8 %expected_users.1 = (bf16[512,256]{1,0:T(8,128)(2,1)S(1)}, bf16[528,256]{1,0:T(8,128)(2,1)S(1)}, f32[1,256]{1,0:T(1,128)S(1)}) custom-call(f32[512,256]{1,0:T(8,128)} %bitcast.14, f32[512,256]{1,0:T(8,128)} %bitcast.15), custom_call_target="tpu_custom_call" | custom-call | flops 1024 | bytes 1024 | tf_op jit(solution)/shard_map/expected_users/pallas_call | solution.py:97
  2.4 3.1 %collective-permute-start.3 = (bf16[512,256]{1,0:T(8,128)(2,1)S(1)}, bf16[512,256]{1,0:T(8,128)(2,1)S(1)}, u32[]{:S(2)}, u32[]{:S(2)}) collective-permute-start(bf16[512,256]{1,0:T(8,128)(2,1)S(1)} %get-tuple-element.30.both_ref.refs_0_), channel_id=1, source_target_pairs={{0,4},{4,8},{8,12},{12,0},{1,5},{5,9},{9,13},{13,1},{2,6},{6,10},{... | collective-permute-start | bytes 786440 | tf_op jit(solution)/shard_map/ppermute | solution.py:478
  5.5 1.8 %expected_items.1 = (bf16[528,256]{1,0:T(8,128)(2,1)S(1)}, bf16[784,256]{1,0:T(8,128)(2,1)S(1)}) custom-call(f32[512,256]{1,0:T(8,128)} %bitcast.16, f32[512,256]{1,0:T(8,128)} %bitcast.17, bf16[512,256]{1,0:T(8,128)(2,1)S(1)} %get-tuple-element.30.both_ref.refs_0_, f32[1,256]{1,0:T(1,128)S(1)} %get-tuple-element.31.theta_ref), custom_call_target="tpu_custom_call" | custom-call | flops 1024 | bytes 1024 | tf_op jit(solution)/shard_map/expected_items/pallas_call | solution.py:141
  7.9 2.2 %dense_counts.1.refs_6_ = bf16[1024,1024]{1,0:T(8,128)(2,1)S(1)} custom-call(s32[64]{0:T(128)} %bitcast.20, s32[64]{0:T(128)} %bitcast.21, s32[1]{0:T(128)} %bitcast.12.live_ref, s32[64,128,128]{2,1,0:T(8,128)} %bitcast.13), custom_call_target="tpu_custom_call" | custom-call | flops 1024 | bytes 1024 | tf_op jit(solution)/shard_map/dense_counts/pallas_call | solution.py:212
  10.1 1.6 %collective-permute-start.1 = (bf16[528,256]{1,0:T(8,128)(2,1)S(1)}, bf16[528,256]{1,0:T(8,128)(2,1)S(1)}, u32[]{:S(2)}, u32[]{:S(2)}) collective-permute-start(bf16[528,256]{1,0:T(8,128)(2,1)S(1)} %get-tuple-element.34.refs_2_.exp_ref.refs_0_), channel_id=1, source_target_pairs={{0,2},{2,0},{1,3},{3,1},{4,6},{6,4},{5,7},{7,5},{8,10},{10,8},{9,1... | collective-permute-start | bytes 811016 | tf_op jit(solution)/shard_map/ppermute | solution.py:486
  11.7 2.1 %collective-permute-done.3.refs_0_ = bf16[512,256]{1,0:T(8,128)(2,1)S(1)} collective-permute-done((bf16[512,256]{1,0:T(8,128)(2,1)S(1)}, bf16[512,256]{1,0:T(8,128)(2,1)S(1)}, u32[]{:S(2)}, u32[]{:S(2)}) %collective-permute-start.3) | collective-permute-done | bytes 262176 | tf_op jit(solution)/shard_map/ppermute | solution.py:478
  13.8 4.3 %collective-permute-done.1.refs_3_.refs_1_ = bf16[528,256]{1,0:T(8,128)(2,1)S(1)} collective-permute-done((bf16[528,256]{1,0:T(8,128)(2,1)S(1)}, bf16[528,256]{1,0:T(8,128)(2,1)S(1)}, u32[]{:S(2)}, u32[]{:S(2)}) %collective-permute-start.1) | collective-permute-done | bytes 270368 | tf_op jit(solution)/shard_map/ppermute | solution.py:486
  18.2 2.6 %collective-permute-start.7 = (bf16[528,256]{1,0:T(8,128)(2,1)S(1)}, bf16[528,256]{1,0:T(8,128)(2,1)S(1)}, u32[]{:S(2)}, u32[]{:S(2)}) collective-permute-start(bf16[528,256]{1,0:T(8,128)(2,1)S(1)} %get-tuple-element.40), channel_id=1, source_target_pairs={{0,12},{4,0},{8,4},{12,8},{1,13},{5,1},{9,5},{13,9},{2,14},{6,2},{... | collective-permute-start | bytes 811016 | tf_op jit(solution)/shard_map/ppermute | solution.py:478
  21.0 2.2 %collective-permute-done.4.refs_0_ = bf16[512,256]{1,0:T(8,128)(2,1)S(1)} collective-permute-done((bf16[512,256]{1,0:T(8,128)(2,1)S(1)}, bf16[512,256]{1,0:T(8,128)(2,1)S(1)}, u32[]{:S(2)}, u32[]{:S(2)}) %collective-permute-start.4) | collective-permute-done | bytes 262176 | tf_op jit(solution)/shard_map/ppermute | solution.py:478
  23.2 1.7 %statistics_1.1 = (bf16[528,256]{1,0:T(8,128)(2,1)S(1)}, f32[512,1024]{1,0:T(8,128)S(1)}) custom-call(bf16[512,256]{1,0:T(8,128)(2,1)S(1)} %collective-permute-done.3.refs_0_, bf16[512,256]{1,0:T(8,128)(2,1)S(1)} %collective-permute-done.6.refs_1_, bf16[528,256]{1,0:T(8,128)(2,1)S(1)} %get-tuple-element.34.refs_2_.exp_ref.refs_0_, ...), custom_call_target="tpu_custom_call" | custom-call | flops 1024 | bytes 1024 | tf_op jit(solution)/shard_map/statistics_1/pallas_call | solution.py:309
  24.9 1.7 %statistics_3.1 = (bf16[528,256]{1,0:T(8,128)(2,1)S(1)}, f32[512,1024]{1,0:T(8,128)S(1)}) custom-call(bf16[512,256]{1,0:T(8,128)(2,1)S(1)} %collective-permute-done.4.refs_0_, bf16[512,256]{1,0:T(8,128)(2,1)S(1)} %collective-permute-done.5.refs_1_, bf16[528,256]{1,0:T(8,128)(2,1)S(1)} %get-tuple-element.34.refs_2_.exp_ref.refs_0_, ...), custom_call_target="tpu_custom_call" | custom-call | flops 1024 | bytes 1024 | tf_op jit(solution)/shard_map/statistics_3/pallas_call | solution.py:309
  26.6 2.3 %collective-permute-done.7.refs_0_ = bf16[528,256]{1,0:T(8,128)(2,1)S(1)} collective-permute-done((bf16[528,256]{1,0:T(8,128)(2,1)S(1)}, bf16[528,256]{1,0:T(8,128)(2,1)S(1)}, u32[]{:S(2)}, u32[]{:S(2)}) %collective-permute-start.7) | collective-permute-done | bytes 270368 | tf_op jit(solution)/shard_map/ppermute | solution.py:478
  29.1 2.6 %collective-permute-start.12 = (bf16[528,256]{1,0:T(8,128)(2,1)S(1)}, bf16[528,256]{1,0:T(8,128)(2,1)S(1)}, u32[]{:S(2)}, u32[]{:S(2)}) collective-permute-start(bf16[528,256]{1,0:T(8,128)(2,1)S(1)} %get-tuple-element.41), channel_id=1, source_target_pairs={{0,12},{4,0},{8,4},{12,8},{1,13},{5,1},{9,5},{13,9},{2,14},{6,2},{... | collective-permute-start | bytes 811016 | tf_op jit(solution)/shard_map/ppermute | solution.py:478
  31.6 1.7 %statistics_0.1 = (f32[256,256]{1,0:T(8,128)S(1)}, f32[256,256]{1,0:T(8,128)S(1)}, f32[512,1024]{1,0:T(8,128)S(1)}) custom-call(bf16[512,256]{1,0:T(8,128)(2,1)S(1)} %get-tuple-element.30.both_ref.refs_0_, bf16[784,256]{1,0:T(8,128)(2,1)S(1)} %collective-permute-done.refs_4_.refs_1_, bf16[528,256]{1,0:T(8,128)(2,1)S(1)} %get-tuple-element.34.refs_2_.exp_ref.refs_0_, ...), custom_call_target="tpu_custom_call" | custom-call | flops 1024 | bytes 1024 | tf_op jit(solution)/shard_map/statistics_0/pallas_call | solution.py:309
  33.3 1.7 %statistics_2.1 = (bf16[528,256]{1,0:T(8,128)(2,1)S(1)}, f32[256,1024]{1,0:T(8,128)S(1)}, bf16[256,512]{1,0:T(8,128)(2,1)S(1)}, bf16[256,512]{1,0:T(8,128)(2,1)S(1)}) custom-call(bf16[528,256]{1,0:T(8,128)(2,1)S(1)} %collective-permute-done.7.refs_0_, bf16[256,256]{1,0:T(8,128)(2,1)S(1)} %collective-permute-done.8.refs_1_, ...), custom_call_target="tpu_custom_call" | custom-call | flops 1024 | bytes 1024 | tf_op jit(solution)/shard_map/statistics_2/pallas_call | solution.py:309
  35.2 1.4 %collective-permute-done.11.came_ref = bf16[256,512]{1,0:T(8,128)(2,1)S(1)} collective-permute-done((bf16[256,512]{1,0:T(8,128)(2,1)S(1)}, bf16[256,512]{1,0:T(8,128)(2,1)S(1)}, u32[]{:S(2)}, u32[]{:S(2)}) %collective-permute-start.11) | collective-permute-done | bytes 262176 | tf_op jit(solution)/shard_map/ppermute | solution.py:505
  36.6 1.8 %collective-permute-done.12.came_ref = bf16[528,256]{1,0:T(8,128)(2,1)S(1)} collective-permute-done((bf16[528,256]{1,0:T(8,128)(2,1)S(1)}, bf16[528,256]{1,0:T(8,128)(2,1)S(1)}, u32[]{:S(2)}, u32[]{:S(2)}) %collective-permute-start.12) | collective-permute-done | bytes 270368 | tf_op jit(solution)/shard_map/ppermute | solution.py:478
  38.5 4.3 %collective-permute-start.13 = (bf16[272,256]{1,0:T(8,128)(2,1)S(1)}, bf16[272,256]{1,0:T(8,128)(2,1)S(1)}, u32[]{:S(2)}, u32[]{:S(2)}) collective-permute-start(bf16[272,256]{1,0:T(8,128)(2,1)S(1)} %get-tuple-element.49), channel_id=1, source_target_pairs={{0,12},{4,0},{8,4},{12,8},{1,13},{5,1},{9,5},{13,9},{2,14},{6,2},{... | collective-permute-start | bytes 417800 | tf_op jit(solution)/shard_map/ppermute | solution.py:478
  42.9 1.7 %collective-permute-start.16 = (bf16[256,512]{1,0:T(8,128)(2,1)S(1)}, bf16[256,512]{1,0:T(8,128)(2,1)S(1)}, u32[]{:S(2)}, u32[]{:S(2)}) collective-permute-start(bf16[256,512]{1,0:T(8,128)(2,1)S(1)} %merge_items.1), channel_id=1, source_target_pairs={{0,2},{2,0},{1,3},{3,1},{4,6},{6,4},{5,7},{7,5},{8,10},{10,8},{9,1... | collective-permute-start | bytes 786440 | tf_op jit(solution)/shard_map/ppermute | solution.py:486
  44.8 4.1 %collective-permute-done.13.refs_3_ = bf16[272,256]{1,0:T(8,128)(2,1)S(1)} collective-permute-done((bf16[272,256]{1,0:T(8,128)(2,1)S(1)}, bf16[272,256]{1,0:T(8,128)(2,1)S(1)}, u32[]{:S(2)}, u32[]{:S(2)}) %collective-permute-start.13) | collective-permute-done | bytes 139296 | tf_op jit(solution)/shard_map/ppermute | solution.py:478
  49.5 1.1 %finish_rates.1 = (f32[512,256]{1,0:T(8,128)}, f32[512,256]{1,0:T(8,128)}) custom-call(bf16[528,256]{1,0:T(8,128)(2,1)S(1)} %get-tuple-element.34.refs_2_.exp_ref.refs_0_, bf16[528,256]{1,0:T(8,128)(2,1)S(1)} %collective-permute-done.1.refs_3_.refs_1_, bf16[528,256]{1,0:T(8,128)(2,1)S(1)} %collective-permute-done.9.refs_2_.refs_5_, ...), custom_call_target="tpu_custom_call" | custom-call | flops 1024 | bytes 1024 | tf_op jit(solution)/shard_map/finish_rates/pallas_call | solution.py:393
  50.6 1.0 %collective-permute-done.16.refs_1_ = bf16[256,512]{1,0:T(8,128)(2,1)S(1)} collective-permute-done((bf16[256,512]{1,0:T(8,128)(2,1)S(1)}, bf16[256,512]{1,0:T(8,128)(2,1)S(1)}, u32[]{:S(2)}, u32[]{:S(2)}) %collective-permute-start.16) | collective-permute-done | bytes 262176 | tf_op jit(solution)/shard_map/ppermute | solution.py:486
  51.6 1.0 %finish_items.1 = f32[512,256]{1,0:T(8,128)} custom-call(bf16[528,256]{1,0:T(8,128)(2,1)S(1)} %get-tuple-element.34.refs_2_.exp_ref.refs_0_, f32[256,1024]{1,0:T(8,128)S(1)} %get-tuple-element.46.mine_ref.own_ref, bf16[256,512]{1,0:T(8,128)(2,1)S(1)} %collective-permute-done.15.refs_0_, bf16[256,512]{1,0:T(8,128)(2,1)S(1)} %collective-permute-done.16.refs_1_), custom_call_target="tpu_custom_call" | custom-call | flops 1024 | bytes 1024 | tf_op jit(solution)/shard_map/finish_items/pallas_call | solution.py:465
  52.6 0.9 %finish_users.1 = f32[512,256]{1,0:T(8,128)} custom-call(bf16[512,256]{1,0:T(8,128)(2,1)S(1)} %get-tuple-element.30.both_ref.refs_0_, f32[256,256]{1,0:T(8,128)S(1)} %get-tuple-element.37.refs_1_, bf16[256,256]{1,0:T(8,128)(2,1)S(1)} %collective-permute-done.10.refs_2_, bf16[272,256]{1,0:T(8,128)(2,1)S(1)} %collective-permute-done.14.refs_3_, ...), custom_call_target="tpu_custom_call" | custom-call | flops 1024 | bytes 1024 | tf_op jit(solution)/shard_map/finish_users/pallas_call | solution.py:433
  (30 shorter events, 1.5 us)
Async XLA Ops:
  2.4 11.4 %collective-permute-start.3 = (bf16[512,256]{1,0:T(8,128)(2,1)S(1)}, bf16[512,256]{1,0:T(8,128)(2,1)S(1)}, u32[]{:S(2)}, u32[]{:S(2)}) collective-permute-start(bf16[512,256]{1,0:T(8,128)(2,1)S(1)} %get-tuple-element.30.both_ref.refs_0_), channel_id=1, source_target_pairs={{0,4},{4,8},{8,12},{12,0},{1,5},{5,9},{9,13},{13,1},{2,6},{6,10},{... | collective-permute-start | bytes 786440 | tf_op jit(solution)/shard_map/ppermute | solution.py:478
  10.1 8.0 %collective-permute-start.1 = (bf16[528,256]{1,0:T(8,128)(2,1)S(1)}, bf16[528,256]{1,0:T(8,128)(2,1)S(1)}, u32[]{:S(2)}, u32[]{:S(2)}) collective-permute-start(bf16[528,256]{1,0:T(8,128)(2,1)S(1)} %get-tuple-element.34.refs_2_.exp_ref.refs_0_), channel_id=1, source_target_pairs={{0,2},{2,0},{1,3},{3,1},{4,6},{6,4},{5,7},{7,5},{8,10},{10,8},{9,1... | collective-permute-start | bytes 811016 | tf_op jit(solution)/shard_map/ppermute | solution.py:486
  13.8 9.4 %collective-permute-start.4 = (bf16[512,256]{1,0:T(8,128)(2,1)S(1)}, bf16[512,256]{1,0:T(8,128)(2,1)S(1)}, u32[]{:S(2)}, u32[]{:S(2)}) collective-permute-start(bf16[512,256]{1,0:T(8,128)(2,1)S(1)} %collective-permute-done.3.refs_0_), channel_id=1, source_target_pairs={{0,4},{4,8},{8,12},{12,0},{1,5},{5,9},{9,13},{13,1},{2,6},{6,10},{... | collective-permute-start | bytes 786440 | tf_op jit(solution)/shard_map/ppermute | solution.py:478
  13.8 9.4 %collective-permute-start = (bf16[784,256]{1,0:T(8,128)(2,1)S(1)}, bf16[784,256]{1,0:T(8,128)(2,1)S(1)}, u32[]{:S(2)}, u32[]{:S(2)}) collective-permute-start(bf16[784,256]{1,0:T(8,128)(2,1)S(1)} %get-tuple-element.32), channel_id=1, source_target_pairs={{0,1},{1,0},{2,3},{3,2},{4,5},{5,4},{6,7},{7,6},{8,9},{9,8},{10,11... | collective-permute-start | bytes 1204232 | tf_op jit(solution)/shard_map/ppermute | solution.py:505
  18.2 5.1 %collective-permute-start.2 = (bf16[528,256]{1,0:T(8,128)(2,1)S(1)}, bf16[528,256]{1,0:T(8,128)(2,1)S(1)}, u32[]{:S(2)}, u32[]{:S(2)}) collective-permute-start(bf16[528,256]{1,0:T(8,128)(2,1)S(1)} %collective-permute-done.1.refs_3_.refs_1_), channel_id=1, source_target_pairs={{0,1},{1,0},{2,3},{3,2},{4,5},{5,4},{6,7},{7,6},{8,9},{9,8},{10,11... | collective-permute-start | bytes 811016 | tf_op jit(solution)/shard_map/ppermute | solution.py:505
  18.2 10.7 %collective-permute-start.7 = (bf16[528,256]{1,0:T(8,128)(2,1)S(1)}, bf16[528,256]{1,0:T(8,128)(2,1)S(1)}, u32[]{:S(2)}, u32[]{:S(2)}) collective-permute-start(bf16[528,256]{1,0:T(8,128)(2,1)S(1)} %get-tuple-element.40), channel_id=1, source_target_pairs={{0,12},{4,0},{8,4},{12,8},{1,13},{5,1},{9,5},{13,9},{2,14},{6,2},{... | collective-permute-start | bytes 811016 | tf_op jit(solution)/shard_map/ppermute | solution.py:478
  20.8 2.4 %collective-permute-start.6 = (bf16[512,256]{1,0:T(8,128)(2,1)S(1)}, bf16[512,256]{1,0:T(8,128)(2,1)S(1)}, u32[]{:S(2)}, u32[]{:S(2)}) collective-permute-start(bf16[512,256]{1,0:T(8,128)(2,1)S(1)} %collective-permute-done.3.refs_0_), channel_id=1, source_target_pairs={{0,1},{1,0},{2,3},{3,2},{4,5},{5,4},{6,7},{7,6},{8,9},{9,8},{10,11... | collective-permute-start | bytes 786440 | tf_op jit(solution)/shard_map/ppermute | solution.py:505
  23.2 1.7 %collective-permute-start.5 = (bf16[512,256]{1,0:T(8,128)(2,1)S(1)}, bf16[512,256]{1,0:T(8,128)(2,1)S(1)}, u32[]{:S(2)}, u32[]{:S(2)}) collective-permute-start(bf16[512,256]{1,0:T(8,128)(2,1)S(1)} %collective-permute-done.4.refs_0_), channel_id=1, source_target_pairs={{0,1},{1,0},{2,3},{3,2},{4,5},{5,4},{6,7},{7,6},{8,9},{9,8},{10,11... | collective-permute-start | bytes 786440 | tf_op jit(solution)/shard_map/ppermute | solution.py:505
  28.9 4.4 %collective-permute-start.8 = (bf16[256,256]{1,0:T(8,128)(2,1)S(1)}, bf16[256,256]{1,0:T(8,128)(2,1)S(1)}, u32[]{:S(2)}, u32[]{:S(2)}) collective-permute-start(bf16[256,256]{1,0:T(8,128)(2,1)S(1)} %slice.6), channel_id=1, source_target_pairs={{0,1},{1,0},{2,3},{3,2},{4,5},{5,4},{6,7},{7,6},{8,9},{9,8},{10,11... | collective-permute-start | bytes 393224 | tf_op jit(solution)/shard_map/ppermute | solution.py:505
  29.1 9.4 %collective-permute-start.12 = (bf16[528,256]{1,0:T(8,128)(2,1)S(1)}, bf16[528,256]{1,0:T(8,128)(2,1)S(1)}, u32[]{:S(2)}, u32[]{:S(2)}) collective-permute-start(bf16[528,256]{1,0:T(8,128)(2,1)S(1)} %get-tuple-element.41), channel_id=1, source_target_pairs={{0,12},{4,0},{8,4},{12,8},{1,13},{5,1},{9,5},{13,9},{2,14},{6,2},{... | collective-permute-start | bytes 811016 | tf_op jit(solution)/shard_map/ppermute | solution.py:478
  35.0 14.5 %copy-start = (f32[1,512]{1,0:T(1,128)S(1)}, f32[1,512]{1,0:T(1,128)}, u32[]{:S(2)}) copy-start(f32[1,512]{1,0:T(1,128)} %refs_4_.1) | copy-start | bytes 6148
  35.0 14.5 %copy-start.1 = (f32[1,512]{1,0:T(1,128)S(1)}, f32[1,512]{1,0:T(1,128)}, u32[]{:S(2)}) copy-start(f32[1,512]{1,0:T(1,128)} %refs_5_.1) | copy-start | bytes 6148
  35.0 1.6 %collective-permute-start.11 = (bf16[256,512]{1,0:T(8,128)(2,1)S(1)}, bf16[256,512]{1,0:T(8,128)(2,1)S(1)}, u32[]{:S(2)}, u32[]{:S(2)}) collective-permute-start(bf16[256,512]{1,0:T(8,128)(2,1)S(1)} %get-tuple-element.47), channel_id=1, source_target_pairs={{0,1},{1,0},{2,3},{3,2},{4,5},{5,4},{6,7},{7,6},{8,9},{9,8},{10,11... | collective-permute-start | bytes 786440 | tf_op jit(solution)/shard_map/ppermute | solution.py:505
  35.2 13.7 %collective-permute-start.9 = (bf16[528,256]{1,0:T(8,128)(2,1)S(1)}, bf16[528,256]{1,0:T(8,128)(2,1)S(1)}, u32[]{:S(2)}, u32[]{:S(2)}) collective-permute-start(bf16[528,256]{1,0:T(8,128)(2,1)S(1)} %get-tuple-element.44), channel_id=1, source_target_pairs={{0,4},{4,8},{8,12},{12,0},{1,5},{5,9},{9,13},{13,1},{2,6},{6,10},{... | collective-permute-start | bytes 811016 | tf_op jit(solution)/shard_map/ppermute | solution.py:478
  38.5 10.3 %collective-permute-start.13 = (bf16[272,256]{1,0:T(8,128)(2,1)S(1)}, bf16[272,256]{1,0:T(8,128)(2,1)S(1)}, u32[]{:S(2)}, u32[]{:S(2)}) collective-permute-start(bf16[272,256]{1,0:T(8,128)(2,1)S(1)} %get-tuple-element.49), channel_id=1, source_target_pairs={{0,12},{4,0},{8,4},{12,8},{1,13},{5,1},{9,5},{13,9},{2,14},{6,2},{... | collective-permute-start | bytes 417800 | tf_op jit(solution)/shard_map/ppermute | solution.py:478
  42.9 7.8 %collective-permute-start.15 = (bf16[256,512]{1,0:T(8,128)(2,1)S(1)}, bf16[256,512]{1,0:T(8,128)(2,1)S(1)}, u32[]{:S(2)}, u32[]{:S(2)}) collective-permute-start(bf16[256,512]{1,0:T(8,128)(2,1)S(1)} %get-tuple-element.50), channel_id=1, source_target_pairs={{0,1},{1,0},{2,3},{3,2},{4,5},{5,4},{6,7},{7,6},{8,9},{9,8},{10,11... | collective-permute-start | bytes 786440 | tf_op jit(solution)/shard_map/ppermute | solution.py:505
  42.9 8.7 %collective-permute-start.16 = (bf16[256,512]{1,0:T(8,128)(2,1)S(1)}, bf16[256,512]{1,0:T(8,128)(2,1)S(1)}, u32[]{:S(2)}, u32[]{:S(2)}) collective-permute-start(bf16[256,512]{1,0:T(8,128)(2,1)S(1)} %merge_items.1), channel_id=1, source_target_pairs={{0,2},{2,0},{1,3},{3,1},{4,6},{6,4},{5,7},{7,5},{8,10},{10,8},{9,1... | collective-permute-start | bytes 786440 | tf_op jit(solution)/shard_map/ppermute | solution.py:486
  44.6 8.0 %collective-permute-start.17 = (bf16[288,256]{1,0:T(8,128)(2,1)S(1)}, bf16[288,256]{1,0:T(8,128)(2,1)S(1)}, u32[]{:S(2)}, u32[]{:S(2)}) collective-permute-start(bf16[288,256]{1,0:T(8,128)(2,1)S(1)} %get-tuple-element.54), channel_id=1, source_target_pairs={{0,12},{4,0},{8,4},{12,8},{1,13},{5,1},{9,5},{13,9},{2,14},{6,2},{... | collective-permute-start | bytes 442376 | tf_op jit(solution)/shard_map/ppermute | solution.py:478
  48.9 3.7 %collective-permute-start.14 = (bf16[272,256]{1,0:T(8,128)(2,1)S(1)}, bf16[272,256]{1,0:T(8,128)(2,1)S(1)}, u32[]{:S(2)}, u32[]{:S(2)}) collective-permute-start(bf16[272,256]{1,0:T(8,128)(2,1)S(1)} %collective-permute-done.13.refs_3_), channel_id=1, source_target_pairs={{0,1},{1,0},{2,3},{3,2},{4,5},{5,4},{6,7},{7,6},{8,9},{9,8},{10,11... | collective-permute-start | bytes 417800 | tf_op jit(solution)/shard_map/ppermute | solution.py:505
  48.9 3.6 %collective-permute-start.10 = (bf16[256,256]{1,0:T(8,128)(2,1)S(1)}, bf16[256,256]{1,0:T(8,128)(2,1)S(1)}, u32[]{:S(2)}, u32[]{:S(2)}) collective-permute-start(bf16[256,256]{1,0:T(8,128)(2,1)S(1)} %convert_add_fusion), channel_id=1, source_target_pairs={{0,1},{1,0},{2,3},{3,2},{4,5},{5,4},{6,7},{7,6},{8,9},{9,8},{10,11... | collective-permute-start | bytes 393224 | tf_op jit(solution)/shard_map/ppermute | solution.py:505

commit v14 on v13

--- a/solution.py
+++ b/solution.py
@@ -69,7 +69,7 @@
     return copies
 
 
-def users_kernel(chunk, shape_ref, rate_ref, both_ref, wide_ref, total_ref, shape_buf, rate_buf, sems):
+def users_kernel(chunk, shape_ref, rate_ref, both_ref, keep_ref, give_ref, total_ref, shape_buf, rate_buf, sems):
     core = lax.axis_index("ka")
     half = both_ref.shape[0] // 2
     steps = half // chunk
@@ -85,10 +85,12 @@
         inv_rate = reciprocal(rate_buf[pl.ds(start, chunk), :])
         value = exp_digamma(x, inv_rate).astype(BF16)
         both_ref[j * chunk : (j + 1) * chunk, :] = value
-        wide_ref[j * chunk : (j + 1) * chunk, :] = value
+        target = keep_ref if j < steps else give_ref
+        target[(j % steps) * chunk : (j % steps + 1) * chunk, :] = value
         total += jnp.sum(x * inv_rate, axis=0, keepdims=True)
     total_ref[...] = total
-    wide_ref[2 * half :, :] = jnp.zeros((wide_ref.shape[0] - 2 * half, wide_ref.shape[1]), BF16)
+    for target in (keep_ref, give_ref):
+        target[half:, :] = jnp.zeros((32, target.shape[1]), BF16)
 
 
 def expected_users(shape_arg, rate_arg):
@@ -97,10 +99,11 @@
     return pl.pallas_call(
         functools.partial(users_kernel, chunk),
         in_specs=[pl.BlockSpec(memory_space=HBM)] * 2,
-        out_specs=[pl.BlockSpec(memory_space=VMEM)] * 3,
+        out_specs=[pl.BlockSpec(memory_space=VMEM)] * 4,
         out_shape=[
             jax.ShapeDtypeStruct((rows, cols), BF16),
-            jax.ShapeDtypeStruct((rows + 1 * EXTRA, cols), BF16),
+            jax.ShapeDtypeStruct((rows // 2 + 32, cols), BF16),
+            jax.ShapeDtypeStruct((rows // 2 + 32, cols), BF16),
             jax.ShapeDtypeStruct((1, cols), F32),
         ],
         scratch_shapes=[
@@ -232,7 +235,7 @@
     take = lambda n: [refs.pop(0) for _ in range(n)]
     mine_ref, other_ref = take(2)
     mine = mine_ref[:half, :]
-    other = other_ref[half : 2 * half, :] if at and not last else other_ref[:half, :]
+    other = other_ref[:half, :]
     item_mine = take(pieces)
     item_other = take(pieces)
     (counts_ref,) = take(1)
@@ -478,6 +481,11 @@
     return lax.ppermute(x, "item", [(i, (i + shift) % n) for i in range(n)])
 
 
+def across_item(x, shift, n, n_ka):
+    pairs = [(i * n_ka + h, (i + shift) % n * n_ka + n_ka - 1 - h) for i in range(n) for h in range(n_ka)]
+    return lax.ppermute(x, ("item", "ka"), pairs)
+
+
 def after(x, y):
     return lax.optimization_barrier((x, y))[0]
 
@@ -504,7 +512,7 @@
     def sibling(x):
         return lax.ppermute(x, "ka", [(h, n_ka - 1 - h) for h in range(n_ka)])
 
-    both, wide, theta_local = expected_users(theta_shape[0], theta_rate[0])
+    both, keep, give, theta_local = expected_users(theta_shape[0], theta_rate[0])
     item_exp, pack = expected_items(beta_shape[0], beta_rate[0], both, theta_local)
     rows = both.shape[0]
     half_rows = rows // 2
@@ -526,8 +534,14 @@
     shards = {0: both}
     for d in behind:
         shards[2 * d - 1] = along_item(shards[max(2 * d - 3, 0)], 1, n_item)
+    crossed = {}
     for d in ahead:
-        shards[2 * d] = along_item(after(wide, shards[1]) if d == 1 else shards[2 * d - 2], -1, n_item)
+        if d == 1:
+            shards[2] = along_item(after(keep, shards[1]), -1, n_item)
+            crossed[2] = across_item(after(give, shards[1]), -1, n_item, n_ka)
+        else:
+            shards[2 * d] = along_item(shards[2 * d - 2], -1, n_item)
+            crossed[2 * d] = along_item(crossed[2 * d - 2], -1, n_item)
 
     item_mine = [item_exp]
     for p in range(1, n_user):
@@ -541,8 +555,10 @@
     stats = {}
     latest = None
     for i in order:
-        passed = after(shards[i], stats[n_item - 1][0])[half_rows:rows] if i == order[-1] else shards[i]
-        other = sibling(passed) if i else came_pack
+        if i == 0:
+            other = came_pack
+        else:
+            other = sibling(shards[i][half_rows:]) if i % 2 else crossed[i]
         stats[i], accs = statistics(
             i, [shards[i], other], item_mine, item_other, dense, acc, i == order[-1], half_rows
         )

time: 53.5 us -> 51.8 us (0.968)
  waiting for transfers between devices: 19.3 us -> 15.7 us
  starting transfers between devices: 17.3 us -> 18.7 us
    ppermute x7, waiting for transfers between devices: 12.6 us -> 10.8 us  [along_item(): return lax.ppermute(x, 'item', [(i, (i + shift) % n) for i in range(n)])]
    ppermute x7, starting transfers between devices: 12.8 us -> 14.2 us  [along_item(): return lax.ppermute(x, 'item', [(i, (i + shift) % n) for i in range(n)])]
    ppermute x9 -> x8, waiting for transfers between devices: 1.39 us -> 0.3 us  [sibling(): return lax.ppermute(x, 'ka', [(h, n_ka - 1 - h) for h in range(n_ka)])]
    ppermute x2, waiting for transfers between devices: 5.28 us -> 4.33 us  [along_user(): return lax.ppermute(x, 'user', [(i, i ^ distance) for i in range(n)])]
    ppermute x9 -> x8, starting transfers between devices: 1.18 us -> 1.51 us  [sibling(): return lax.ppermute(x, 'ka', [(h, n_ka - 1 - h) for h in range(n_ka)])]
  transfers between devices with their start and end apart: 18 -> 18, of which waited for: 8 -> 7; matrix products, arithmetic and copies ran while one was open for 0% -> 0% of each run, Pallas kernels for 24% -> 25%
where the time goes in v14:
time: 51.8 us; the launch traced here: 51.4 us
  starting transfers between devices  18.7 us (36%)
  waiting for transfers between devices  15.7 us (30%)
  Pallas kernels  15.5 us (30%)
  between operations  1.45 us (3%)
    ppermute x7, starting transfers between devices, along_item(): return lax.ppermute(x, 'item', [(i, (i + shift) % n) for i in range(n)])  14.2 us
    ppermute x7, waiting for transfers between devices, along_item(): return lax.ppermute(x, 'item', [(i, (i + shift) % n) for i in range(n)])  10.8 us
    pallas_call x4, Pallas kernels, statistics(): pl.pallas_call(functools.partial(stat_kernel, len(item_mine), half_rows,...  6.63 us
    ppermute x2, waiting for transfers between devices, along_user(): return lax.ppermute(x, 'user', [(i, i ^ distance) for i in range(n)])  4.33 us
    ppermute x2, starting transfers between devices, along_user(): return lax.ppermute(x, 'user', [(i, i ^ distance) for i in range(n)])  3.08 us
    pallas_call x1, Pallas kernels, dense_counts(): pl.pallas_call(functools.partial(dense_kernel, n_item, item_rows // n_use...  2.24 us
    pallas_call x1, Pallas kernels, expected_users(): pl.pallas_call(functools.partial(users_kernel, chunk), in_specs=[pl.Block...  1.77 us
    pallas_call x1, Pallas kernels, expected_items(): pl.pallas_call(functools.partial(items_kernel, chunk), in_specs=[pl.Block...  1.76 us
  transfers between devices with their start and end apart: 18, of which 7 were waited for; matrix products, arithmetic and copies ran while one was open for 0% of the time, Pallas kernels for 25%

profile of v14, /device:TPU:0, one launch (start us, length us, event | category | flops | bytes accessed | tf_op | source)
XLA Modules:
  0.0 51.4 jit_solution(960221690432057310)
XLA Ops:
  0.6 1.8 %expected_users.1 = (bf16[512,256]{1,0:T(8,128)(2,1)S(1)}, bf16[288,256]{1,0:T(8,128)(2,1)S(1)}, bf16[288,256]{1,0:T(8,128)(2,1)S(1)}, f32[1,256]{1,0:T(1,128)S(1)}) custom-call(f32[512,256]{1,0:T(8,128)} %bitcast.14, f32[512,256]{1,0:T(8,128)} %bitcast.15), custom_call_target="tpu_custom_call" | custom-call | flops 1024 | bytes 1024 | tf_op jit(solution)/shard_map/expected_users/pallas_call | solution.py:99
  2.4 3.1 %collective-permute-start.3 = (bf16[512,256]{1,0:T(8,128)(2,1)S(1)}, bf16[512,256]{1,0:T(8,128)(2,1)S(1)}, u32[]{:S(2)}, u32[]{:S(2)}) collective-permute-start(bf16[512,256]{1,0:T(8,128)(2,1)S(1)} %get-tuple-element.31.both_ref.refs_0_), channel_id=1, source_target_pairs={{0,4},{4,8},{8,12},{12,0},{1,5},{5,9},{9,13},{13,1},{2,6},{6,10},{... | collective-permute-start | bytes 786440 | tf_op jit(solution)/shard_map/ppermute | solution.py:481
  5.5 1.8 %expected_items.1 = (bf16[528,256]{1,0:T(8,128)(2,1)S(1)}, bf16[784,256]{1,0:T(8,128)(2,1)S(1)}) custom-call(f32[512,256]{1,0:T(8,128)} %bitcast.16, f32[512,256]{1,0:T(8,128)} %bitcast.17, bf16[512,256]{1,0:T(8,128)(2,1)S(1)} %get-tuple-element.31.both_ref.refs_0_, f32[1,256]{1,0:T(1,128)S(1)} %get-tuple-element.32.theta_ref), custom_call_target="tpu_custom_call" | custom-call | flops 1024 | bytes 1024 | tf_op jit(solution)/shard_map/expected_items/pallas_call | solution.py:144
  7.9 2.2 %dense_counts.1.refs_6_ = bf16[1024,1024]{1,0:T(8,128)(2,1)S(1)} custom-call(s32[64]{0:T(128)} %bitcast.20, s32[64]{0:T(128)} %bitcast.21, s32[1]{0:T(128)} %bitcast.12.live_ref, s32[64,128,128]{2,1,0:T(8,128)} %bitcast.13), custom_call_target="tpu_custom_call" | custom-call | flops 1024 | bytes 1024 | tf_op jit(solution)/shard_map/dense_counts/pallas_call | solution.py:215
  10.1 1.6 %collective-permute-start.1 = (bf16[528,256]{1,0:T(8,128)(2,1)S(1)}, bf16[528,256]{1,0:T(8,128)(2,1)S(1)}, u32[]{:S(2)}, u32[]{:S(2)}) collective-permute-start(bf16[528,256]{1,0:T(8,128)(2,1)S(1)} %get-tuple-element.35.refs_2_.exp_ref.refs_0_), channel_id=1, source_target_pairs={{0,2},{2,0},{1,3},{3,1},{4,6},{6,4},{5,7},{7,5},{8,10},{10,8},{9,1... | collective-permute-start | bytes 811016 | tf_op jit(solution)/shard_map/ppermute | solution.py:494
  11.7 2.1 %collective-permute-done.3.refs_0_ = bf16[512,256]{1,0:T(8,128)(2,1)S(1)} collective-permute-done((bf16[512,256]{1,0:T(8,128)(2,1)S(1)}, bf16[512,256]{1,0:T(8,128)(2,1)S(1)}, u32[]{:S(2)}, u32[]{:S(2)}) %collective-permute-start.3) | collective-permute-done | bytes 262176 | tf_op jit(solution)/shard_map/ppermute | solution.py:481
  13.8 4.3 %collective-permute-done.1.refs_3_.refs_1_ = bf16[528,256]{1,0:T(8,128)(2,1)S(1)} collective-permute-done((bf16[528,256]{1,0:T(8,128)(2,1)S(1)}, bf16[528,256]{1,0:T(8,128)(2,1)S(1)}, u32[]{:S(2)}, u32[]{:S(2)}) %collective-permute-start.1) | collective-permute-done | bytes 270368 | tf_op jit(solution)/shard_map/ppermute | solution.py:494
  18.2 0.6 %collective-permute-start.6 = (bf16[256,256]{1,0:T(8,128)(2,1)S(1)}, bf16[256,256]{1,0:T(8,128)(2,1)S(1)}, u32[]{:S(2)}, u32[]{:S(2)}) collective-permute-start(bf16[256,256]{1,0:T(8,128)(2,1)S(1)} %slice.13), channel_id=1, source_target_pairs={{0,1},{1,0},{2,3},{3,2},{4,5},{5,4},{6,7},{7,6},{8,9},{9,8},{10,11... | collective-permute-start | bytes 393224 | tf_op jit(solution)/shard_map/ppermute | solution.py:513
  18.7 2.5 %collective-permute-start.7 = (bf16[288,256]{1,0:T(8,128)(2,1)S(1)}, bf16[288,256]{1,0:T(8,128)(2,1)S(1)}, u32[]{:S(2)}, u32[]{:S(2)}) collective-permute-start(bf16[288,256]{1,0:T(8,128)(2,1)S(1)} %get-tuple-element.41), channel_id=1, source_target_pairs={{0,12},{4,0},{8,4},{12,8},{1,13},{5,1},{9,5},{13,9},{2,14},{6,2},{... | collective-permute-start | bytes 442376 | tf_op jit(solution)/shard_map/ppermute | solution.py:481
  21.3 2.0 %collective-permute-done.4.refs_0_ = bf16[512,256]{1,0:T(8,128)(2,1)S(1)} collective-permute-done((bf16[512,256]{1,0:T(8,128)(2,1)S(1)}, bf16[512,256]{1,0:T(8,128)(2,1)S(1)}, u32[]{:S(2)}, u32[]{:S(2)}) %collective-permute-start.4) | collective-permute-done | bytes 262176 | tf_op jit(solution)/shard_map/ppermute | solution.py:481
  23.4 1.7 %statistics_1.1 = (bf16[528,256]{1,0:T(8,128)(2,1)S(1)}, f32[512,1024]{1,0:T(8,128)S(1)}) custom-call(bf16[512,256]{1,0:T(8,128)(2,1)S(1)} %collective-permute-done.3.refs_0_, bf16[256,256]{1,0:T(8,128)(2,1)S(1)} %collective-permute-done.6.refs_1_, bf16[528,256]{1,0:T(8,128)(2,1)S(1)} %get-tuple-element.35.refs_2_.exp_ref.refs_0_, ...), custom_call_target="tpu_custom_call" | custom-call | flops 1024 | bytes 1024 | tf_op jit(solution)/shard_map/statistics_1/pallas_call | solution.py:312
  25.1 1.7 %statistics_3.1 = (bf16[528,256]{1,0:T(8,128)(2,1)S(1)}, f32[512,1024]{1,0:T(8,128)S(1)}) custom-call(bf16[512,256]{1,0:T(8,128)(2,1)S(1)} %collective-permute-done.4.refs_0_, bf16[256,256]{1,0:T(8,128)(2,1)S(1)} %collective-permute-done.5.refs_1_, bf16[528,256]{1,0:T(8,128)(2,1)S(1)} %get-tuple-element.35.refs_2_.exp_ref.refs_0_, ...), custom_call_target="tpu_custom_call" | custom-call | flops 1024 | bytes 1024 | tf_op jit(solution)/shard_map/statistics_3/pallas_call | solution.py:312
  26.8 0.7 %collective-permute-start.12 = (bf16[528,256]{1,0:T(8,128)(2,1)S(1)}, bf16[528,256]{1,0:T(8,128)(2,1)S(1)}, u32[]{:S(2)}, u32[]{:S(2)}) collective-permute-start(bf16[528,256]{1,0:T(8,128)(2,1)S(1)} %get-tuple-element.50), channel_id=1, source_target_pairs={{0,12},{4,0},{8,4},{12,8},{1,13},{5,1},{9,5},{13,9},{2,14},{6,2},{... | collective-permute-start | bytes 811016 | tf_op jit(solution)/shard_map/ppermute | solution.py:481
  27.5 1.7 %statistics_0.1 = (f32[256,256]{1,0:T(8,128)S(1)}, f32[256,256]{1,0:T(8,128)S(1)}, f32[512,1024]{1,0:T(8,128)S(1)}) custom-call(bf16[512,256]{1,0:T(8,128)(2,1)S(1)} %get-tuple-element.31.both_ref.refs_0_, bf16[784,256]{1,0:T(8,128)(2,1)S(1)} %collective-permute-done.refs_4_.refs_1_, bf16[528,256]{1,0:T(8,128)(2,1)S(1)} %get-tuple-element.35.refs_2_.exp_ref.refs_0_, ...), custom_call_target="tpu_custom_call" | custom-call | flops 1024 | bytes 1024 | tf_op jit(solution)/shard_map/statistics_0/pallas_call | solution.py:312
  29.4 1.7 %statistics_2.1 = (bf16[528,256]{1,0:T(8,128)(2,1)S(1)}, f32[256,1024]{1,0:T(8,128)S(1)}, bf16[256,512]{1,0:T(8,128)(2,1)S(1)}, bf16[256,512]{1,0:T(8,128)(2,1)S(1)}) custom-call(bf16[288,256]{1,0:T(8,128)(2,1)S(1)} %collective-permute-done.7.refs_0_, bf16[288,256]{1,0:T(8,128)(2,1)S(1)} %collective-permute-done.8.refs_1_, ...), custom_call_target="tpu_custom_call" | custom-call | flops 1024 | bytes 1024 | tf_op jit(solution)/shard_map/statistics_2/pallas_call | solution.py:312
  31.3 1.1 %collective-permute-start.9 = (bf16[528,256]{1,0:T(8,128)(2,1)S(1)}, bf16[528,256]{1,0:T(8,128)(2,1)S(1)}, u32[]{:S(2)}, u32[]{:S(2)}) collective-permute-start(bf16[528,256]{1,0:T(8,128)(2,1)S(1)} %get-tuple-element.45), channel_id=1, source_target_pairs={{0,4},{4,8},{8,12},{12,0},{1,5},{5,9},{9,13},{13,1},{2,6},{6,10},{... | collective-permute-start | bytes 811016 | tf_op jit(solution)/shard_map/ppermute | solution.py:481
  32.8 2.9 %collective-permute-done.12.came_ref = bf16[528,256]{1,0:T(8,128)(2,1)S(1)} collective-permute-done((bf16[528,256]{1,0:T(8,128)(2,1)S(1)}, bf16[528,256]{1,0:T(8,128)(2,1)S(1)}, u32[]{:S(2)}, u32[]{:S(2)}) %collective-permute-start.12) | collective-permute-done | bytes 270368 | tf_op jit(solution)/shard_map/ppermute | solution.py:481
  35.7 2.8 %collective-permute-start.13 = (bf16[272,256]{1,0:T(8,128)(2,1)S(1)}, bf16[272,256]{1,0:T(8,128)(2,1)S(1)}, u32[]{:S(2)}, u32[]{:S(2)}) collective-permute-start(bf16[272,256]{1,0:T(8,128)(2,1)S(1)} %get-tuple-element.51), channel_id=1, source_target_pairs={{0,12},{4,0},{8,4},{12,8},{1,13},{5,1},{9,5},{13,9},{2,14},{6,2},{... | collective-permute-start | bytes 417800 | tf_op jit(solution)/shard_map/ppermute | solution.py:481
  38.5 1.5 %collective-permute-start.16 = (bf16[256,512]{1,0:T(8,128)(2,1)S(1)}, bf16[256,512]{1,0:T(8,128)(2,1)S(1)}, u32[]{:S(2)}, u32[]{:S(2)}) collective-permute-start(bf16[256,512]{1,0:T(8,128)(2,1)S(1)} %merge_items.1), channel_id=1, source_target_pairs={{0,2},{2,0},{1,3},{3,1},{4,6},{6,4},{5,7},{7,5},{8,10},{10,8},{9,1... | collective-permute-start | bytes 786440 | tf_op jit(solution)/shard_map/ppermute | solution.py:494
  40.1 3.8 %collective-permute-start.17 = (bf16[288,256]{1,0:T(8,128)(2,1)S(1)}, bf16[288,256]{1,0:T(8,128)(2,1)S(1)}, u32[]{:S(2)}, u32[]{:S(2)}) collective-permute-start(bf16[288,256]{1,0:T(8,128)(2,1)S(1)} %get-tuple-element.56), channel_id=1, source_target_pairs={{0,12},{4,0},{8,4},{12,8},{1,13},{5,1},{9,5},{13,9},{2,14},{6,2},{... | collective-permute-start | bytes 442376 | tf_op jit(solution)/shard_map/ppermute | solution.py:481
  43.9 3.9 %collective-permute-done.13.refs_3_ = bf16[272,256]{1,0:T(8,128)(2,1)S(1)} collective-permute-done((bf16[272,256]{1,0:T(8,128)(2,1)S(1)}, bf16[272,256]{1,0:T(8,128)(2,1)S(1)}, u32[]{:S(2)}, u32[]{:S(2)}) %collective-permute-start.13) | collective-permute-done | bytes 139296 | tf_op jit(solution)/shard_map/ppermute | solution.py:481
  48.4 1.1 %finish_rates.1 = (f32[512,256]{1,0:T(8,128)}, f32[512,256]{1,0:T(8,128)}) custom-call(bf16[528,256]{1,0:T(8,128)(2,1)S(1)} %get-tuple-element.35.refs_2_.exp_ref.refs_0_, bf16[528,256]{1,0:T(8,128)(2,1)S(1)} %collective-permute-done.1.refs_3_.refs_1_, bf16[528,256]{1,0:T(8,128)(2,1)S(1)} %collective-permute-done.9.refs_2_.refs_5_, ...), custom_call_target="tpu_custom_call" | custom-call | flops 1024 | bytes 1024 | tf_op jit(solution)/shard_map/finish_rates/pallas_call | solution.py:396
  49.5 1.0 %finish_items.1 = f32[512,256]{1,0:T(8,128)} custom-call(bf16[528,256]{1,0:T(8,128)(2,1)S(1)} %get-tuple-element.35.refs_2_.exp_ref.refs_0_, f32[256,1024]{1,0:T(8,128)S(1)} %get-tuple-element.47.mine_ref.own_ref, bf16[256,512]{1,0:T(8,128)(2,1)S(1)} %collective-permute-done.15.refs_0_, bf16[256,512]{1,0:T(8,128)(2,1)S(1)} %collective-permute-done.16.refs_1_), custom_call_target="tpu_custom_call" | custom-call | flops 1024 | bytes 1024 | tf_op jit(solution)/shard_map/finish_items/pallas_call | solution.py:468
  50.5 0.9 %finish_users.1 = f32[512,256]{1,0:T(8,128)} custom-call(bf16[512,256]{1,0:T(8,128)(2,1)S(1)} %get-tuple-element.31.both_ref.refs_0_, f32[256,256]{1,0:T(8,128)S(1)} %get-tuple-element.38.refs_1_, bf16[256,256]{1,0:T(8,128)(2,1)S(1)} %collective-permute-done.10.refs_2_, bf16[272,256]{1,0:T(8,128)(2,1)S(1)} %collective-permute-done.14.refs_3_, ...), custom_call_target="tpu_custom_call" | custom-call | flops 1024 | bytes 1024 | tf_op jit(solution)/shard_map/finish_users/pallas_call | solution.py:436
  (31 shorter events, 1.7 us)
Async XLA Ops:
  2.4 11.4 %collective-permute-start.3 = (bf16[512,256]{1,0:T(8,128)(2,1)S(1)}, bf16[512,256]{1,0:T(8,128)(2,1)S(1)}, u32[]{:S(2)}, u32[]{:S(2)}) collective-permute-start(bf16[512,256]{1,0:T(8,128)(2,1)S(1)} %get-tuple-element.31.both_ref.refs_0_), channel_id=1, source_target_pairs={{0,4},{4,8},{8,12},{12,0},{1,5},{5,9},{9,13},{13,1},{2,6},{6,10},{... | collective-permute-start | bytes 786440 | tf_op jit(solution)/shard_map/ppermute | solution.py:481
  10.1 8.0 %collective-permute-start.1 = (bf16[528,256]{1,0:T(8,128)(2,1)S(1)}, bf16[528,256]{1,0:T(8,128)(2,1)S(1)}, u32[]{:S(2)}, u32[]{:S(2)}) collective-permute-start(bf16[528,256]{1,0:T(8,128)(2,1)S(1)} %get-tuple-element.35.refs_2_.exp_ref.refs_0_), channel_id=1, source_target_pairs={{0,2},{2,0},{1,3},{3,1},{4,6},{6,4},{5,7},{7,5},{8,10},{10,8},{9,1... | collective-permute-start | bytes 811016 | tf_op jit(solution)/shard_map/ppermute | solution.py:494
  13.8 9.4 %collective-permute-start.4 = (bf16[512,256]{1,0:T(8,128)(2,1)S(1)}, bf16[512,256]{1,0:T(8,128)(2,1)S(1)}, u32[]{:S(2)}, u32[]{:S(2)}) collective-permute-start(bf16[512,256]{1,0:T(8,128)(2,1)S(1)} %collective-permute-done.3.refs_0_), channel_id=1, source_target_pairs={{0,4},{4,8},{8,12},{12,0},{1,5},{5,9},{9,13},{13,1},{2,6},{6,10},{... | collective-permute-start | bytes 786440 | tf_op jit(solution)/shard_map/ppermute | solution.py:481
  13.8 9.6 %collective-permute-start = (bf16[784,256]{1,0:T(8,128)(2,1)S(1)}, bf16[784,256]{1,0:T(8,128)(2,1)S(1)}, u32[]{:S(2)}, u32[]{:S(2)}) collective-permute-start(bf16[784,256]{1,0:T(8,128)(2,1)S(1)} %get-tuple-element.33), channel_id=1, source_target_pairs={{0,1},{1,0},{2,3},{3,2},{4,5},{5,4},{6,7},{7,6},{8,9},{9,8},{10,11... | collective-permute-start | bytes 1204232 | tf_op jit(solution)/shard_map/ppermute | solution.py:513
  18.2 5.3 %collective-permute-start.2 = (bf16[528,256]{1,0:T(8,128)(2,1)S(1)}, bf16[528,256]{1,0:T(8,128)(2,1)S(1)}, u32[]{:S(2)}, u32[]{:S(2)}) collective-permute-start(bf16[528,256]{1,0:T(8,128)(2,1)S(1)} %collective-permute-done.1.refs_3_.refs_1_), channel_id=1, source_target_pairs={{0,1},{1,0},{2,3},{3,2},{4,5},{5,4},{6,7},{7,6},{8,9},{9,8},{10,11... | collective-permute-start | bytes 811016 | tf_op jit(solution)/shard_map/ppermute | solution.py:513
  18.2 5.1 %collective-permute-start.6 = (bf16[256,256]{1,0:T(8,128)(2,1)S(1)}, bf16[256,256]{1,0:T(8,128)(2,1)S(1)}, u32[]{:S(2)}, u32[]{:S(2)}) collective-permute-start(bf16[256,256]{1,0:T(8,128)(2,1)S(1)} %slice.13), channel_id=1, source_target_pairs={{0,1},{1,0},{2,3},{3,2},{4,5},{5,4},{6,7},{7,6},{8,9},{9,8},{10,11... | collective-permute-start | bytes 393224 | tf_op jit(solution)/shard_map/ppermute | solution.py:513
  18.7 10.4 %collective-permute-start.7 = (bf16[288,256]{1,0:T(8,128)(2,1)S(1)}, bf16[288,256]{1,0:T(8,128)(2,1)S(1)}, u32[]{:S(2)}, u32[]{:S(2)}) collective-permute-start(bf16[288,256]{1,0:T(8,128)(2,1)S(1)} %get-tuple-element.41), channel_id=1, source_target_pairs={{0,12},{4,0},{8,4},{12,8},{1,13},{5,1},{9,5},{13,9},{2,14},{6,2},{... | collective-permute-start | bytes 442376 | tf_op jit(solution)/shard_map/ppermute | solution.py:481
  23.2 6.2 %collective-permute-start.8 = (bf16[288,256]{1,0:T(8,128)(2,1)S(1)}, bf16[288,256]{1,0:T(8,128)(2,1)S(1)}, u32[]{:S(2)}, u32[]{:S(2)}) collective-permute-start(bf16[288,256]{1,0:T(8,128)(2,1)S(1)} %get-tuple-element.43), channel_id=1, source_target_pairs={{0,13},{1,12},{4,1},{5,0},{8,5},{9,4},{12,9},{13,8},{2,15},{3,14},... | collective-permute-start | bytes 442376 | tf_op jit(solution)/shard_map/ppermute | solution.py:486
  23.2 1.8 %collective-permute-start.5 = (bf16[256,256]{1,0:T(8,128)(2,1)S(1)}, bf16[256,256]{1,0:T(8,128)(2,1)S(1)}, u32[]{:S(2)}, u32[]{:S(2)}) collective-permute-start(bf16[256,256]{1,0:T(8,128)(2,1)S(1)} %slice.12), channel_id=1, source_target_pairs={{0,1},{1,0},{2,3},{3,2},{4,5},{5,4},{6,7},{7,6},{8,9},{9,8},{10,11... | collective-permute-start | bytes 393224 | tf_op jit(solution)/shard_map/ppermute | solution.py:513
  26.8 8.9 %collective-permute-start.12 = (bf16[528,256]{1,0:T(8,128)(2,1)S(1)}, bf16[528,256]{1,0:T(8,128)(2,1)S(1)}, u32[]{:S(2)}, u32[]{:S(2)}) collective-permute-start(bf16[528,256]{1,0:T(8,128)(2,1)S(1)} %get-tuple-element.50), channel_id=1, source_target_pairs={{0,12},{4,0},{8,4},{12,8},{1,13},{5,1},{9,5},{13,9},{2,14},{6,2},{... | collective-permute-start | bytes 811016 | tf_op jit(solution)/shard_map/ppermute | solution.py:481
  31.1 17.3 %copy-start = (f32[1,512]{1,0:T(1,128)S(1)}, f32[1,512]{1,0:T(1,128)}, u32[]{:S(2)}) copy-start(f32[1,512]{1,0:T(1,128)} %refs_4_.1) | copy-start | bytes 6148
  31.1 17.3 %copy-start.1 = (f32[1,512]{1,0:T(1,128)S(1)}, f32[1,512]{1,0:T(1,128)}, u32[]{:S(2)}) copy-start(f32[1,512]{1,0:T(1,128)} %refs_5_.1) | copy-start | bytes 6148
  31.1 1.6 %collective-permute-start.11 = (bf16[256,512]{1,0:T(8,128)(2,1)S(1)}, bf16[256,512]{1,0:T(8,128)(2,1)S(1)}, u32[]{:S(2)}, u32[]{:S(2)}) collective-permute-start(bf16[256,512]{1,0:T(8,128)(2,1)S(1)} %get-tuple-element.48), channel_id=1, source_target_pairs={{0,1},{1,0},{2,3},{3,2},{4,5},{5,4},{6,7},{7,6},{8,9},{9,8},{10,11... | collective-permute-start | bytes 786440 | tf_op jit(solution)/shard_map/ppermute | solution.py:513
  31.3 16.5 %collective-permute-start.9 = (bf16[528,256]{1,0:T(8,128)(2,1)S(1)}, bf16[528,256]{1,0:T(8,128)(2,1)S(1)}, u32[]{:S(2)}, u32[]{:S(2)}) collective-permute-start(bf16[528,256]{1,0:T(8,128)(2,1)S(1)} %get-tuple-element.45), channel_id=1, source_target_pairs={{0,4},{4,8},{8,12},{12,0},{1,5},{5,9},{9,13},{13,1},{2,6},{6,10},{... | collective-permute-start | bytes 811016 | tf_op jit(solution)/shard_map/ppermute | solution.py:481
  35.7 12.1 %collective-permute-start.13 = (bf16[272,256]{1,0:T(8,128)(2,1)S(1)}, bf16[272,256]{1,0:T(8,128)(2,1)S(1)}, u32[]{:S(2)}, u32[]{:S(2)}) collective-permute-start(bf16[272,256]{1,0:T(8,128)(2,1)S(1)} %get-tuple-element.51), channel_id=1, source_target_pairs={{0,12},{4,0},{8,4},{12,8},{1,13},{5,1},{9,5},{13,9},{2,14},{6,2},{... | collective-permute-start | bytes 417800 | tf_op jit(solution)/shard_map/ppermute | solution.py:481
  38.5 11.0 %collective-permute-start.15 = (bf16[256,512]{1,0:T(8,128)(2,1)S(1)}, bf16[256,512]{1,0:T(8,128)(2,1)S(1)}, u32[]{:S(2)}, u32[]{:S(2)}) collective-permute-start(bf16[256,512]{1,0:T(8,128)(2,1)S(1)} %get-tuple-element.52), channel_id=1, source_target_pairs={{0,1},{1,0},{2,3},{3,2},{4,5},{5,4},{6,7},{7,6},{8,9},{9,8},{10,11... | collective-permute-start | bytes 786440 | tf_op jit(solution)/shard_map/ppermute | solution.py:513
  38.5 11.0 %collective-permute-start.16 = (bf16[256,512]{1,0:T(8,128)(2,1)S(1)}, bf16[256,512]{1,0:T(8,128)(2,1)S(1)}, u32[]{:S(2)}, u32[]{:S(2)}) collective-permute-start(bf16[256,512]{1,0:T(8,128)(2,1)S(1)} %merge_items.1), channel_id=1, source_target_pairs={{0,2},{2,0},{1,3},{3,1},{4,6},{6,4},{5,7},{7,5},{8,10},{10,8},{9,1... | collective-permute-start | bytes 786440 | tf_op jit(solution)/shard_map/ppermute | solution.py:494
  40.1 10.5 %collective-permute-start.17 = (bf16[288,256]{1,0:T(8,128)(2,1)S(1)}, bf16[288,256]{1,0:T(8,128)(2,1)S(1)}, u32[]{:S(2)}, u32[]{:S(2)}) collective-permute-start(bf16[288,256]{1,0:T(8,128)(2,1)S(1)} %get-tuple-element.56), channel_id=1, source_target_pairs={{0,12},{4,0},{8,4},{12,8},{1,13},{5,1},{9,5},{13,9},{2,14},{6,2},{... | collective-permute-start | bytes 442376 | tf_op jit(solution)/shard_map/ppermute | solution.py:481
  47.8 2.7 %collective-permute-start.14 = (bf16[272,256]{1,0:T(8,128)(2,1)S(1)}, bf16[272,256]{1,0:T(8,128)(2,1)S(1)}, u32[]{:S(2)}, u32[]{:S(2)}) collective-permute-start(bf16[272,256]{1,0:T(8,128)(2,1)S(1)} %collective-permute-done.13.refs_3_), channel_id=1, source_target_pairs={{0,1},{1,0},{2,3},{3,2},{4,5},{5,4},{6,7},{7,6},{8,9},{9,8},{10,11... | collective-permute-start | bytes 417800 | tf_op jit(solution)/shard_map/ppermute | solution.py:513
  47.8 2.7 %collective-permute-start.10 = (bf16[256,256]{1,0:T(8,128)(2,1)S(1)}, bf16[256,256]{1,0:T(8,128)(2,1)S(1)}, u32[]{:S(2)}, u32[]{:S(2)}) collective-permute-start(bf16[256,256]{1,0:T(8,128)(2,1)S(1)} %convert_add_fusion), channel_id=1, source_target_pairs={{0,1},{1,0},{2,3},{3,2},{4,5},{5,4},{6,7},{7,6},{8,9},{9,8},{10,11... | collective-permute-start | bytes 393224 | tf_op jit(solution)/shard_map/ppermute | solution.py:513

commit v15 on v12

--- a/solution.py
+++ b/solution.py
@@ -556,19 +556,20 @@
         came.append(along_user(sent, p, n_user))
     new_beta_shape = finish_items(item_exp, acc, came)
 
+    back = []
+    for d in reversed(behind):
+        if d > 1:
+            stat = stats[2 * d - 1][0]
+            back = [along_item(add_came(stat, back[0], False)[0] if back else stat, -1, n_item)]
     moving = []
     for d in reversed(ahead):
         stat = stats[2 * d][0]
+        stat = after(stat, back[0]) if d == 1 else stat
         parts = add_came(stat, moving[0], False) if moving else [stat]
         moving = [along_item(x, 1, n_item) for x in parts]
     came_ahead = moving
-    moving = []
-    for d in reversed(behind):
-        stat = stats[2 * d - 1][0]
-        if d == 1 and n_user > 1:
-            stat = after(stat, sent)
-        parts = add_came(stat, moving[0], d == 1) if moving else [stat]
-        moving = [along_item(x, -1, n_item) for x in parts]
+    stat = after(stats[1][0], sent) if n_user > 1 else stats[1][0]
+    moving = [along_item(x, -1, n_item) for x in add_came(stat, back[0], True)]
     other_behind, mine_behind = moving
 
     other_sum = own_other

time: 51.7 us -> 53.5 us (1.035)
  waiting for transfers between devices: 18.1 us -> 20.5 us
  starting transfers between devices: 16.5 us -> 15.9 us
    ppermute x7, waiting for transfers between devices: 16.6 us -> 19.9 us  [along_item(): return lax.ppermute(x, 'item', [(i, (i + shift) % n) for i in range(n)])]
    ppermute x7, starting transfers between devices: 12.2 us -> 11.1 us  [along_item(): return lax.ppermute(x, 'item', [(i, (i + shift) % n) for i in range(n)])]
    ppermute x2, waiting for transfers between devices: 1.22 us -> 0.51 us  [along_user(): return lax.ppermute(x, 'user', [(i, i ^ distance) for i in range(n)])]
  transfers between devices with their start and end apart: 18 -> 18, of which waited for: 8 -> 6; matrix products, arithmetic and copies ran while one was open for 0% -> 0% of each run, Pallas kernels for 25% -> 24%
where the time goes in v15:
time: 53.5 us; the launch traced here: 53.3 us
  waiting for transfers between devices  20.5 us (38%)
  starting transfers between devices  15.9 us (30%)
  Pallas kernels  15.5 us (29%)
  between operations  1.47 us (3%)
    ppermute x7, waiting for transfers between devices, along_item(): return lax.ppermute(x, 'item', [(i, (i + shift) % n) for i in range(n)])  19.9 us
    ppermute x7, starting transfers between devices, along_item(): return lax.ppermute(x, 'item', [(i, (i + shift) % n) for i in range(n)])  11.1 us
    pallas_call x4, Pallas kernels, statistics(): pl.pallas_call(functools.partial(stat_kernel, len(item_mine), half_rows,...  6.64 us
    ppermute x2, starting transfers between devices, along_user(): return lax.ppermute(x, 'user', [(i, i ^ distance) for i in range(n)])  3.05 us
    pallas_call x1, Pallas kernels, dense_counts(): pl.pallas_call(functools.partial(dense_kernel, n_item, item_rows // n_use...  2.24 us
    pallas_call x1, Pallas kernels, expected_users(): pl.pallas_call(functools.partial(users_kernel, chunk), in_specs=[pl.Block...  1.77 us
    pallas_call x1, Pallas kernels, expected_items(): pl.pallas_call(functools.partial(items_kernel, chunk), in_specs=[pl.Block...  1.76 us
    ppermute x9, starting transfers between devices, sibling(): return lax.ppermute(x, 'ka', [(h, n_ka - 1 - h) for h in range(n_ka)])  1.73 us
  transfers between devices with their start and end apart: 18, of which 6 were waited for; matrix products, arithmetic and copies ran while one was open for 0% of the time, Pallas kernels for 24%

profile of v15, /device:TPU:0, one launch (start us, length us, event | category | flops | bytes accessed | tf_op | source)
XLA Modules:
  0.0 53.3 jit_solution(15233420349213752768)
XLA Ops:
  0.6 1.8 %expected_users.1 = (bf16[512,256]{1,0:T(8,128)(2,1)S(1)}, bf16[560,256]{1,0:T(8,128)(2,1)S(1)}, f32[1,256]{1,0:T(1,128)S(1)}) custom-call(f32[512,256]{1,0:T(8,128)} %bitcast.14, f32[512,256]{1,0:T(8,128)} %bitcast.15), custom_call_target="tpu_custom_call" | custom-call | flops 1024 | bytes 1024 | tf_op jit(solution)/shard_map/expected_users/pallas_call | solution.py:97
  2.4 3.1 %collective-permute-start.3 = (bf16[512,256]{1,0:T(8,128)(2,1)S(1)}, bf16[512,256]{1,0:T(8,128)(2,1)S(1)}, u32[]{:S(2)}, u32[]{:S(2)}) collective-permute-start(bf16[512,256]{1,0:T(8,128)(2,1)S(1)} %get-tuple-element.31.both_ref.refs_0_), channel_id=1, source_target_pairs={{0,4},{4,8},{8,12},{12,0},{1,5},{5,9},{9,13},{13,1},{2,6},{6,10},{... | collective-permute-start | bytes 786440 | tf_op jit(solution)/shard_map/ppermute | solution.py:478
  5.5 1.8 %expected_items.1 = (bf16[528,256]{1,0:T(8,128)(2,1)S(1)}, bf16[784,256]{1,0:T(8,128)(2,1)S(1)}) custom-call(f32[512,256]{1,0:T(8,128)} %bitcast.16, f32[512,256]{1,0:T(8,128)} %bitcast.17, bf16[512,256]{1,0:T(8,128)(2,1)S(1)} %get-tuple-element.31.both_ref.refs_0_, f32[1,256]{1,0:T(1,128)S(1)} %get-tuple-element.32.theta_ref), custom_call_target="tpu_custom_call" | custom-call | flops 1024 | bytes 1024 | tf_op jit(solution)/shard_map/expected_items/pallas_call | solution.py:141
  7.9 2.2 %dense_counts.1.refs_6_ = bf16[1024,1024]{1,0:T(8,128)(2,1)S(1)} custom-call(s32[64]{0:T(128)} %bitcast.20, s32[64]{0:T(128)} %bitcast.21, s32[1]{0:T(128)} %bitcast.12.live_ref, s32[64,128,128]{2,1,0:T(8,128)} %bitcast.13), custom_call_target="tpu_custom_call" | custom-call | flops 1024 | bytes 1024 | tf_op jit(solution)/shard_map/dense_counts/pallas_call | solution.py:212
  10.1 1.6 %collective-permute-start.1 = (bf16[528,256]{1,0:T(8,128)(2,1)S(1)}, bf16[528,256]{1,0:T(8,128)(2,1)S(1)}, u32[]{:S(2)}, u32[]{:S(2)}) collective-permute-start(bf16[528,256]{1,0:T(8,128)(2,1)S(1)} %get-tuple-element.35.refs_2_.exp_ref.refs_0_), channel_id=1, source_target_pairs={{0,2},{2,0},{1,3},{3,1},{4,6},{6,4},{5,7},{7,5},{8,10},{10,8},{9,1... | collective-permute-start | bytes 811016 | tf_op jit(solution)/shard_map/ppermute | solution.py:486
  11.7 2.1 %collective-permute-done.3.refs_0_ = bf16[512,256]{1,0:T(8,128)(2,1)S(1)} collective-permute-done((bf16[512,256]{1,0:T(8,128)(2,1)S(1)}, bf16[512,256]{1,0:T(8,128)(2,1)S(1)}, u32[]{:S(2)}, u32[]{:S(2)}) %collective-permute-start.3) | collective-permute-done | bytes 262176 | tf_op jit(solution)/shard_map/ppermute | solution.py:478
  13.8 3.8 %collective-permute-start.7 = (bf16[560,256]{1,0:T(8,128)(2,1)S(1)}, bf16[560,256]{1,0:T(8,128)(2,1)S(1)}, u32[]{:S(2)}, u32[]{:S(2)}) collective-permute-start(bf16[560,256]{1,0:T(8,128)(2,1)S(1)} %get-tuple-element.41), channel_id=1, source_target_pairs={{0,12},{4,0},{8,4},{12,8},{1,13},{5,1},{9,5},{13,9},{2,14},{6,2},{... | collective-permute-start | bytes 860168 | tf_op jit(solution)/shard_map/ppermute | solution.py:478
  17.6 0.5 collective-permute-done.1.refs_3_.refs_1_
  18.2 0.5 collective-permute-start.6
  18.7 6.2 %collective-permute-done.4.refs_0_ = bf16[512,256]{1,0:T(8,128)(2,1)S(1)} collective-permute-done((bf16[512,256]{1,0:T(8,128)(2,1)S(1)}, bf16[512,256]{1,0:T(8,128)(2,1)S(1)}, u32[]{:S(2)}, u32[]{:S(2)}) %collective-permute-start.4) | collective-permute-done | bytes 262176 | tf_op jit(solution)/shard_map/ppermute | solution.py:478
  24.9 1.7 %statistics_1.1 = (bf16[528,256]{1,0:T(8,128)(2,1)S(1)}, f32[512,1024]{1,0:T(8,128)S(1)}) custom-call(bf16[512,256]{1,0:T(8,128)(2,1)S(1)} %collective-permute-done.3.refs_0_, bf16[512,256]{1,0:T(8,128)(2,1)S(1)} %collective-permute-done.6.refs_1_, bf16[528,256]{1,0:T(8,128)(2,1)S(1)} %get-tuple-element.35.refs_2_.exp_ref.refs_0_, ...), custom_call_target="tpu_custom_call" | custom-call | flops 1024 | bytes 1024 | tf_op jit(solution)/shard_map/statistics_1/pallas_call | solution.py:309
  26.6 1.7 %statistics_3.1 = (bf16[528,256]{1,0:T(8,128)(2,1)S(1)}, f32[512,1024]{1,0:T(8,128)S(1)}) custom-call(bf16[512,256]{1,0:T(8,128)(2,1)S(1)} %collective-permute-done.4.refs_0_, bf16[512,256]{1,0:T(8,128)(2,1)S(1)} %collective-permute-done.5.refs_1_, bf16[528,256]{1,0:T(8,128)(2,1)S(1)} %get-tuple-element.35.refs_2_.exp_ref.refs_0_, ...), custom_call_target="tpu_custom_call" | custom-call | flops 1024 | bytes 1024 | tf_op jit(solution)/shard_map/statistics_3/pallas_call | solution.py:309
  28.3 0.4 collective-permute-done.7.refs_0_
  28.9 1.7 %statistics_0.1 = (f32[256,256]{1,0:T(8,128)S(1)}, f32[256,256]{1,0:T(8,128)S(1)}, f32[512,1024]{1,0:T(8,128)S(1)}) custom-call(bf16[512,256]{1,0:T(8,128)(2,1)S(1)} %get-tuple-element.31.both_ref.refs_0_, bf16[784,256]{1,0:T(8,128)(2,1)S(1)} %collective-permute-done.refs_4_.refs_1_, bf16[528,256]{1,0:T(8,128)(2,1)S(1)} %get-tuple-element.35.refs_2_.exp_ref.refs_0_, ...), custom_call_target="tpu_custom_call" | custom-call | flops 1024 | bytes 1024 | tf_op jit(solution)/shard_map/statistics_0/pallas_call | solution.py:309
  30.6 1.7 %statistics_2.1 = (bf16[528,256]{1,0:T(8,128)(2,1)S(1)}, f32[256,1024]{1,0:T(8,128)S(1)}, bf16[256,512]{1,0:T(8,128)(2,1)S(1)}, bf16[256,512]{1,0:T(8,128)(2,1)S(1)}) custom-call(bf16[560,256]{1,0:T(8,128)(2,1)S(1)} %collective-permute-done.7.refs_0_, bf16[256,256]{1,0:T(8,128)(2,1)S(1)} %collective-permute-done.8.refs_1_, ...), custom_call_target="tpu_custom_call" | custom-call | flops 1024 | bytes 1024 | tf_op jit(solution)/shard_map/statistics_2/pallas_call | solution.py:309
  32.3 0.4 collective-permute-start.12
  32.7 4.5 %collective-permute-done.9.came_ref = bf16[528,256]{1,0:T(8,128)(2,1)S(1)} collective-permute-done((bf16[528,256]{1,0:T(8,128)(2,1)S(1)}, bf16[528,256]{1,0:T(8,128)(2,1)S(1)}, u32[]{:S(2)}, u32[]{:S(2)}) %collective-permute-start.9) | collective-permute-done | bytes 270368 | tf_op jit(solution)/shard_map/ppermute | solution.py:478
  37.3 3.9 %collective-permute-start.13 = (bf16[272,256]{1,0:T(8,128)(2,1)S(1)}, bf16[272,256]{1,0:T(8,128)(2,1)S(1)}, u32[]{:S(2)}, u32[]{:S(2)}) collective-permute-start(bf16[272,256]{1,0:T(8,128)(2,1)S(1)} %get-tuple-element.51), channel_id=1, source_target_pairs={{0,12},{4,0},{8,4},{12,8},{1,13},{5,1},{9,5},{13,9},{2,14},{6,2},{... | collective-permute-start | bytes 417800 | tf_op jit(solution)/shard_map/ppermute | solution.py:478
  41.2 1.5 %collective-permute-start.16 = (bf16[256,512]{1,0:T(8,128)(2,1)S(1)}, bf16[256,512]{1,0:T(8,128)(2,1)S(1)}, u32[]{:S(2)}, u32[]{:S(2)}) collective-permute-start(bf16[256,512]{1,0:T(8,128)(2,1)S(1)} %merge_items.1), channel_id=1, source_target_pairs={{0,2},{2,0},{1,3},{3,1},{4,6},{6,4},{5,7},{7,5},{8,10},{10,8},{9,1... | collective-permute-start | bytes 786440 | tf_op jit(solution)/shard_map/ppermute | solution.py:486
  43.0 6.7 %collective-permute-done.13.refs_3_ = bf16[272,256]{1,0:T(8,128)(2,1)S(1)} collective-permute-done((bf16[272,256]{1,0:T(8,128)(2,1)S(1)}, bf16[272,256]{1,0:T(8,128)(2,1)S(1)}, u32[]{:S(2)}, u32[]{:S(2)}) %collective-permute-start.13) | collective-permute-done | bytes 139296 | tf_op jit(solution)/shard_map/ppermute | solution.py:478
  49.8 0.6 %collective-permute-start.11 = (bf16[256,256]{1,0:T(8,128)(2,1)S(1)}, bf16[256,256]{1,0:T(8,128)(2,1)S(1)}, u32[]{:S(2)}, u32[]{:S(2)}) collective-permute-start(bf16[256,256]{1,0:T(8,128)(2,1)S(1)} %convert_add_fusion), channel_id=1, source_target_pairs={{0,1},{1,0},{2,3},{3,2},{4,5},{5,4},{6,7},{7,6},{8,9},{9,8},{10,11... | collective-permute-start | bytes 393224 | tf_op jit(solution)/shard_map/ppermute | solution.py:505
  50.3 1.1 %finish_rates.1 = (f32[512,256]{1,0:T(8,128)}, f32[512,256]{1,0:T(8,128)}) custom-call(bf16[528,256]{1,0:T(8,128)(2,1)S(1)} %get-tuple-element.35.refs_2_.exp_ref.refs_0_, bf16[528,256]{1,0:T(8,128)(2,1)S(1)} %collective-permute-done.1.refs_3_.refs_1_, bf16[528,256]{1,0:T(8,128)(2,1)S(1)} %collective-permute-done.10.refs_2_.refs_5_, ...), custom_call_target="tpu_custom_call" | custom-call | flops 1024 | bytes 1024 | tf_op jit(solution)/shard_map/finish_rates/pallas_call | solution.py:393
  51.5 1.0 %finish_items.1 = f32[512,256]{1,0:T(8,128)} custom-call(bf16[528,256]{1,0:T(8,128)(2,1)S(1)} %get-tuple-element.35.refs_2_.exp_ref.refs_0_, f32[256,1024]{1,0:T(8,128)S(1)} %get-tuple-element.48.mine_ref.own_ref, bf16[256,512]{1,0:T(8,128)(2,1)S(1)} %collective-permute-done.15.refs_0_, bf16[256,512]{1,0:T(8,128)(2,1)S(1)} %collective-permute-done.16.refs_1_), custom_call_target="tpu_custom_call" | custom-call | flops 1024 | bytes 1024 | tf_op jit(solution)/shard_map/finish_items/pallas_call | solution.py:465
  52.5 0.9 %finish_users.1 = f32[512,256]{1,0:T(8,128)} custom-call(bf16[512,256]{1,0:T(8,128)(2,1)S(1)} %get-tuple-element.31.both_ref.refs_0_, f32[256,256]{1,0:T(8,128)S(1)} %get-tuple-element.38.refs_1_, bf16[256,256]{1,0:T(8,128)(2,1)S(1)} %collective-permute-done.11.refs_2_, bf16[272,256]{1,0:T(8,128)(2,1)S(1)} %collective-permute-done.14.refs_3_, ...), custom_call_target="tpu_custom_call" | custom-call | flops 1024 | bytes 1024 | tf_op jit(solution)/shard_map/finish_users/pallas_call | solution.py:433
  (30 shorter events, 0.8 us)
Async XLA Ops:
  2.4 11.4 %collective-permute-start.3 = (bf16[512,256]{1,0:T(8,128)(2,1)S(1)}, bf16[512,256]{1,0:T(8,128)(2,1)S(1)}, u32[]{:S(2)}, u32[]{:S(2)}) collective-permute-start(bf16[512,256]{1,0:T(8,128)(2,1)S(1)} %get-tuple-element.31.both_ref.refs_0_), channel_id=1, source_target_pairs={{0,4},{4,8},{8,12},{12,0},{1,5},{5,9},{9,13},{13,1},{2,6},{6,10},{... | collective-permute-start | bytes 786440 | tf_op jit(solution)/shard_map/ppermute | solution.py:478
  10.1 8.0 %collective-permute-start.1 = (bf16[528,256]{1,0:T(8,128)(2,1)S(1)}, bf16[528,256]{1,0:T(8,128)(2,1)S(1)}, u32[]{:S(2)}, u32[]{:S(2)}) collective-permute-start(bf16[528,256]{1,0:T(8,128)(2,1)S(1)} %get-tuple-element.35.refs_2_.exp_ref.refs_0_), channel_id=1, source_target_pairs={{0,2},{2,0},{1,3},{3,1},{4,6},{6,4},{5,7},{7,5},{8,10},{10,8},{9,1... | collective-permute-start | bytes 811016 | tf_op jit(solution)/shard_map/ppermute | solution.py:486
  13.8 11.1 %collective-permute-start.4 = (bf16[512,256]{1,0:T(8,128)(2,1)S(1)}, bf16[512,256]{1,0:T(8,128)(2,1)S(1)}, u32[]{:S(2)}, u32[]{:S(2)}) collective-permute-start(bf16[512,256]{1,0:T(8,128)(2,1)S(1)} %collective-permute-done.3.refs_0_), channel_id=1, source_target_pairs={{0,4},{4,8},{8,12},{12,0},{1,5},{5,9},{9,13},{13,1},{2,6},{6,10},{... | collective-permute-start | bytes 786440 | tf_op jit(solution)/shard_map/ppermute | solution.py:478
  13.8 11.1 %collective-permute-start = (bf16[784,256]{1,0:T(8,128)(2,1)S(1)}, bf16[784,256]{1,0:T(8,128)(2,1)S(1)}, u32[]{:S(2)}, u32[]{:S(2)}) collective-permute-start(bf16[784,256]{1,0:T(8,128)(2,1)S(1)} %get-tuple-element.33), channel_id=1, source_target_pairs={{0,1},{1,0},{2,3},{3,2},{4,5},{5,4},{6,7},{7,6},{8,9},{9,8},{10,11... | collective-permute-start | bytes 1204232 | tf_op jit(solution)/shard_map/ppermute | solution.py:505
  13.8 14.9 %collective-permute-start.7 = (bf16[560,256]{1,0:T(8,128)(2,1)S(1)}, bf16[560,256]{1,0:T(8,128)(2,1)S(1)}, u32[]{:S(2)}, u32[]{:S(2)}) collective-permute-start(bf16[560,256]{1,0:T(8,128)(2,1)S(1)} %get-tuple-element.41), channel_id=1, source_target_pairs={{0,12},{4,0},{8,4},{12,8},{1,13},{5,1},{9,5},{13,9},{2,14},{6,2},{... | collective-permute-start | bytes 860168 | tf_op jit(solution)/shard_map/ppermute | solution.py:478
  18.2 6.8 %collective-permute-start.2 = (bf16[528,256]{1,0:T(8,128)(2,1)S(1)}, bf16[528,256]{1,0:T(8,128)(2,1)S(1)}, u32[]{:S(2)}, u32[]{:S(2)}) collective-permute-start(bf16[528,256]{1,0:T(8,128)(2,1)S(1)} %collective-permute-done.1.refs_3_.refs_1_), channel_id=1, source_target_pairs={{0,1},{1,0},{2,3},{3,2},{4,5},{5,4},{6,7},{7,6},{8,9},{9,8},{10,11... | collective-permute-start | bytes 811016 | tf_op jit(solution)/shard_map/ppermute | solution.py:505
  18.2 6.8 %collective-permute-start.6 = (bf16[512,256]{1,0:T(8,128)(2,1)S(1)}, bf16[512,256]{1,0:T(8,128)(2,1)S(1)}, u32[]{:S(2)}, u32[]{:S(2)}) collective-permute-start(bf16[512,256]{1,0:T(8,128)(2,1)S(1)} %collective-permute-done.3.refs_0_), channel_id=1, source_target_pairs={{0,1},{1,0},{2,3},{3,2},{4,5},{5,4},{6,7},{7,6},{8,9},{9,8},{10,11... | collective-permute-start | bytes 786440 | tf_op jit(solution)/shard_map/ppermute | solution.py:505
  24.9 1.7 %collective-permute-start.5 = (bf16[512,256]{1,0:T(8,128)(2,1)S(1)}, bf16[512,256]{1,0:T(8,128)(2,1)S(1)}, u32[]{:S(2)}, u32[]{:S(2)}) collective-permute-start(bf16[512,256]{1,0:T(8,128)(2,1)S(1)} %collective-permute-done.4.refs_0_), channel_id=1, source_target_pairs={{0,1},{1,0},{2,3},{3,2},{4,5},{5,4},{6,7},{7,6},{8,9},{9,8},{10,11... | collective-permute-start | bytes 786440 | tf_op jit(solution)/shard_map/ppermute | solution.py:505
  28.3 8.9 %collective-permute-start.9 = (bf16[528,256]{1,0:T(8,128)(2,1)S(1)}, bf16[528,256]{1,0:T(8,128)(2,1)S(1)}, u32[]{:S(2)}, u32[]{:S(2)}) collective-permute-start(bf16[528,256]{1,0:T(8,128)(2,1)S(1)} %get-tuple-element.42), channel_id=1, source_target_pairs={{0,12},{4,0},{8,4},{12,8},{1,13},{5,1},{9,5},{13,9},{2,14},{6,2},{... | collective-permute-start | bytes 811016 | tf_op jit(solution)/shard_map/ppermute | solution.py:478
  28.7 1.9 %collective-permute-start.8 = (bf16[256,256]{1,0:T(8,128)(2,1)S(1)}, bf16[256,256]{1,0:T(8,128)(2,1)S(1)}, u32[]{:S(2)}, u32[]{:S(2)}) collective-permute-start(bf16[256,256]{1,0:T(8,128)(2,1)S(1)} %slice.6), channel_id=1, source_target_pairs={{0,1},{1,0},{2,3},{3,2},{4,5},{5,4},{6,7},{7,6},{8,9},{9,8},{10,11... | collective-permute-start | bytes 393224 | tf_op jit(solution)/shard_map/ppermute | solution.py:505
  32.3 18.1 %copy-start = (f32[1,512]{1,0:T(1,128)S(1)}, f32[1,512]{1,0:T(1,128)}, u32[]{:S(2)}) copy-start(f32[1,512]{1,0:T(1,128)} %refs_4_.1) | copy-start | bytes 6148
  32.3 18.1 %copy-start.1 = (f32[1,512]{1,0:T(1,128)S(1)}, f32[1,512]{1,0:T(1,128)}, u32[]{:S(2)}) copy-start(f32[1,512]{1,0:T(1,128)} %refs_5_.1) | copy-start | bytes 6148
  32.3 4.9 %collective-permute-start.12 = (bf16[256,512]{1,0:T(8,128)(2,1)S(1)}, bf16[256,512]{1,0:T(8,128)(2,1)S(1)}, u32[]{:S(2)}, u32[]{:S(2)}) collective-permute-start(bf16[256,512]{1,0:T(8,128)(2,1)S(1)} %get-tuple-element.49), channel_id=1, source_target_pairs={{0,1},{1,0},{2,3},{3,2},{4,5},{5,4},{6,7},{7,6},{8,9},{9,8},{10,11... | collective-permute-start | bytes 786440 | tf_op jit(solution)/shard_map/ppermute | solution.py:505
  37.2 12.5 %collective-permute-start.10 = (bf16[528,256]{1,0:T(8,128)(2,1)S(1)}, bf16[528,256]{1,0:T(8,128)(2,1)S(1)}, u32[]{:S(2)}, u32[]{:S(2)}) collective-permute-start(bf16[528,256]{1,0:T(8,128)(2,1)S(1)} %get-tuple-element.46), channel_id=1, source_target_pairs={{0,4},{4,8},{8,12},{12,0},{1,5},{5,9},{9,13},{13,1},{2,6},{6,10},{... | collective-permute-start | bytes 811016 | tf_op jit(solution)/shard_map/ppermute | solution.py:478
  37.3 12.4 %collective-permute-start.13 = (bf16[272,256]{1,0:T(8,128)(2,1)S(1)}, bf16[272,256]{1,0:T(8,128)(2,1)S(1)}, u32[]{:S(2)}, u32[]{:S(2)}) collective-permute-start(bf16[272,256]{1,0:T(8,128)(2,1)S(1)} %get-tuple-element.51), channel_id=1, source_target_pairs={{0,12},{4,0},{8,4},{12,8},{1,13},{5,1},{9,5},{13,9},{2,14},{6,2},{... | collective-permute-start | bytes 417800 | tf_op jit(solution)/shard_map/ppermute | solution.py:478
  41.2 10.2 %collective-permute-start.15 = (bf16[256,512]{1,0:T(8,128)(2,1)S(1)}, bf16[256,512]{1,0:T(8,128)(2,1)S(1)}, u32[]{:S(2)}, u32[]{:S(2)}) collective-permute-start(bf16[256,512]{1,0:T(8,128)(2,1)S(1)} %get-tuple-element.52), channel_id=1, source_target_pairs={{0,1},{1,0},{2,3},{3,2},{4,5},{5,4},{6,7},{7,6},{8,9},{9,8},{10,11... | collective-permute-start | bytes 786440 | tf_op jit(solution)/shard_map/ppermute | solution.py:505
  41.2 10.3 %collective-permute-start.16 = (bf16[256,512]{1,0:T(8,128)(2,1)S(1)}, bf16[256,512]{1,0:T(8,128)(2,1)S(1)}, u32[]{:S(2)}, u32[]{:S(2)}) collective-permute-start(bf16[256,512]{1,0:T(8,128)(2,1)S(1)} %merge_items.1), channel_id=1, source_target_pairs={{0,2},{2,0},{1,3},{3,1},{4,6},{6,4},{5,7},{7,5},{8,10},{10,8},{9,1... | collective-permute-start | bytes 786440 | tf_op jit(solution)/shard_map/ppermute | solution.py:486
  42.7 9.7 %collective-permute-start.17 = (bf16[288,256]{1,0:T(8,128)(2,1)S(1)}, bf16[288,256]{1,0:T(8,128)(2,1)S(1)}, u32[]{:S(2)}, u32[]{:S(2)}) collective-permute-start(bf16[288,256]{1,0:T(8,128)(2,1)S(1)} %get-tuple-element.56), channel_id=1, source_target_pairs={{0,12},{4,0},{8,4},{12,8},{1,13},{5,1},{9,5},{13,9},{2,14},{6,2},{... | collective-permute-start | bytes 442376 | tf_op jit(solution)/shard_map/ppermute | solution.py:478
  49.7 2.7 %collective-permute-start.14 = (bf16[272,256]{1,0:T(8,128)(2,1)S(1)}, bf16[272,256]{1,0:T(8,128)(2,1)S(1)}, u32[]{:S(2)}, u32[]{:S(2)}) collective-permute-start(bf16[272,256]{1,0:T(8,128)(2,1)S(1)} %collective-permute-done.13.refs_3_), channel_id=1, source_target_pairs={{0,1},{1,0},{2,3},{3,2},{4,5},{5,4},{6,7},{7,6},{8,9},{9,8},{10,11... | collective-permute-start | bytes 417800 | tf_op jit(solution)/shard_map/ppermute | solution.py:505
  49.8 2.7 %collective-permute-start.11 = (bf16[256,256]{1,0:T(8,128)(2,1)S(1)}, bf16[256,256]{1,0:T(8,128)(2,1)S(1)}, u32[]{:S(2)}, u32[]{:S(2)}) collective-permute-start(bf16[256,256]{1,0:T(8,128)(2,1)S(1)} %convert_add_fusion), channel_id=1, source_target_pairs={{0,1},{1,0},{2,3},{3,2},{4,5},{5,4},{6,7},{7,6},{8,9},{9,8},{10,11... | collective-permute-start | bytes 393224 | tf_op jit(solution)/shard_map/ppermute | solution.py:505

commit v16 on v13

--- a/solution.py
+++ b/solution.py
@@ -100,7 +100,7 @@
         out_specs=[pl.BlockSpec(memory_space=VMEM)] * 3,
         out_shape=[
             jax.ShapeDtypeStruct((rows, cols), BF16),
-            jax.ShapeDtypeStruct((rows + 1 * EXTRA, cols), BF16),
+            jax.ShapeDtypeStruct((rows + 2 * EXTRA, cols), BF16),
             jax.ShapeDtypeStruct((1, cols), F32),
         ],
         scratch_shapes=[

time: 53.5 us -> 51.8 us (0.968)
  waiting for transfers between devices: 19.3 us -> 17 us
    ppermute x2, waiting for transfers between devices: 5.28 us -> 1.64 us  [along_user(): return lax.ppermute(x, 'user', [(i, i ^ distance) for i in range(n)])]
    ppermute x7, waiting for transfers between devices: 12.6 us -> 15.3 us  [along_item(): return lax.ppermute(x, 'item', [(i, (i + shift) % n) for i in range(n)])]
    ppermute x9, waiting for transfers between devices: 1.39 us -> 0.11 us  [sibling(): return lax.ppermute(x, 'ka', [(h, n_ka - 1 - h) for h in range(n_ka)])]
    ppermute x7, starting transfers between devices: 12.8 us -> 12.1 us  [along_item(): return lax.ppermute(x, 'item', [(i, (i + shift) % n) for i in range(n)])]
  transfers between devices with their start and end apart: 18 -> 18, of which waited for: 8 -> 8; matrix products, arithmetic and copies ran while one was open for 0% -> 0% of each run, Pallas kernels for 24% -> 25%
where the time goes in v16:
time: 51.8 us; the launch traced here: 51.3 us
  starting transfers between devices  17.3 us (33%)
  waiting for transfers between devices  17 us (33%)
  Pallas kernels  15.5 us (30%)
  between operations  1.45 us (3%)
    ppermute x7, waiting for transfers between devices, along_item(): return lax.ppermute(x, 'item', [(i, (i + shift) % n) for i in range(n)])  15.3 us
    ppermute x7, starting transfers between devices, along_item(): return lax.ppermute(x, 'item', [(i, (i + shift) % n) for i in range(n)])  12.1 us
    pallas_call x4, Pallas kernels, statistics(): pl.pallas_call(functools.partial(stat_kernel, len(item_mine), half_rows,...  6.64 us
    ppermute x2, starting transfers between devices, along_user(): return lax.ppermute(x, 'user', [(i, i ^ distance) for i in range(n)])  3.5 us
    pallas_call x1, Pallas kernels, dense_counts(): pl.pallas_call(functools.partial(dense_kernel, n_item, item_rows // n_use...  2.24 us
    pallas_call x1, Pallas kernels, expected_users(): pl.pallas_call(functools.partial(users_kernel, chunk), in_specs=[pl.Block...  1.77 us
    pallas_call x1, Pallas kernels, expected_items(): pl.pallas_call(functools.partial(items_kernel, chunk), in_specs=[pl.Block...  1.76 us
    ppermute x9, starting transfers between devices, sibling(): return lax.ppermute(x, 'ka', [(h, n_ka - 1 - h) for h in range(n_ka)])  1.65 us
  transfers between devices with their start and end apart: 18, of which 8 were waited for; matrix products, arithmetic and copies ran while one was open for 0% of the time, Pallas kernels for 25%

profile of v16, /device:TPU:0, one launch (start us, length us, event | category | flops | bytes accessed | tf_op | source)
XLA Modules:
  0.0 51.3 jit_solution(4251162516297843027)
XLA Ops:
  0.6 1.8 %expected_users.1 = (bf16[512,256]{1,0:T(8,128)(2,1)S(1)}, bf16[544,256]{1,0:T(8,128)(2,1)S(1)}, f32[1,256]{1,0:T(1,128)S(1)}) custom-call(f32[512,256]{1,0:T(8,128)} %bitcast.14, f32[512,256]{1,0:T(8,128)} %bitcast.15), custom_call_target="tpu_custom_call" | custom-call | flops 1024 | bytes 1024 | tf_op jit(solution)/shard_map/expected_users/pallas_call | solution.py:97
  2.4 3.1 %collective-permute-start.3 = (bf16[512,256]{1,0:T(8,128)(2,1)S(1)}, bf16[512,256]{1,0:T(8,128)(2,1)S(1)}, u32[]{:S(2)}, u32[]{:S(2)}) collective-permute-start(bf16[512,256]{1,0:T(8,128)(2,1)S(1)} %get-tuple-element.30.both_ref.refs_0_), channel_id=1, source_target_pairs={{0,4},{4,8},{8,12},{12,0},{1,5},{5,9},{9,13},{13,1},{2,6},{6,10},{... | collective-permute-start | bytes 786440 | tf_op jit(solution)/shard_map/ppermute | solution.py:478
  5.5 1.8 %expected_items.1 = (bf16[528,256]{1,0:T(8,128)(2,1)S(1)}, bf16[784,256]{1,0:T(8,128)(2,1)S(1)}) custom-call(f32[512,256]{1,0:T(8,128)} %bitcast.16, f32[512,256]{1,0:T(8,128)} %bitcast.17, bf16[512,256]{1,0:T(8,128)(2,1)S(1)} %get-tuple-element.30.both_ref.refs_0_, f32[1,256]{1,0:T(1,128)S(1)} %get-tuple-element.31.theta_ref), custom_call_target="tpu_custom_call" | custom-call | flops 1024 | bytes 1024 | tf_op jit(solution)/shard_map/expected_items/pallas_call | solution.py:141
  7.9 2.2 %dense_counts.1.refs_6_ = bf16[1024,1024]{1,0:T(8,128)(2,1)S(1)} custom-call(s32[64]{0:T(128)} %bitcast.20, s32[64]{0:T(128)} %bitcast.21, s32[1]{0:T(128)} %bitcast.12.live_ref, s32[64,128,128]{2,1,0:T(8,128)} %bitcast.13), custom_call_target="tpu_custom_call" | custom-call | flops 1024 | bytes 1024 | tf_op jit(solution)/shard_map/dense_counts/pallas_call | solution.py:212
  10.1 2.3 %collective-permute-start.1 = (bf16[528,256]{1,0:T(8,128)(2,1)S(1)}, bf16[528,256]{1,0:T(8,128)(2,1)S(1)}, u32[]{:S(2)}, u32[]{:S(2)}) collective-permute-start(bf16[528,256]{1,0:T(8,128)(2,1)S(1)} %get-tuple-element.34.refs_2_.exp_ref.refs_0_), channel_id=1, source_target_pairs={{0,2},{2,0},{1,3},{3,1},{4,6},{6,4},{5,7},{7,5},{8,10},{10,8},{9,1... | collective-permute-start | bytes 811016 | tf_op jit(solution)/shard_map/ppermute | solution.py:486
  12.4 1.4 %collective-permute-done.3.refs_0_ = bf16[512,256]{1,0:T(8,128)(2,1)S(1)} collective-permute-done((bf16[512,256]{1,0:T(8,128)(2,1)S(1)}, bf16[512,256]{1,0:T(8,128)(2,1)S(1)}, u32[]{:S(2)}, u32[]{:S(2)}) %collective-permute-start.3) | collective-permute-done | bytes 262176 | tf_op jit(solution)/shard_map/ppermute | solution.py:478
  13.8 3.8 %collective-permute-start.7 = (bf16[544,256]{1,0:T(8,128)(2,1)S(1)}, bf16[544,256]{1,0:T(8,128)(2,1)S(1)}, u32[]{:S(2)}, u32[]{:S(2)}) collective-permute-start(bf16[544,256]{1,0:T(8,128)(2,1)S(1)} %get-tuple-element.40), channel_id=1, source_target_pairs={{0,12},{4,0},{8,4},{12,8},{1,13},{5,1},{9,5},{13,9},{2,14},{6,2},{... | collective-permute-start | bytes 835592 | tf_op jit(solution)/shard_map/ppermute | solution.py:478
  17.6 1.0 %collective-permute-done.1.refs_3_.refs_1_ = bf16[528,256]{1,0:T(8,128)(2,1)S(1)} collective-permute-done((bf16[528,256]{1,0:T(8,128)(2,1)S(1)}, bf16[528,256]{1,0:T(8,128)(2,1)S(1)}, u32[]{:S(2)}, u32[]{:S(2)}) %collective-permute-start.1) | collective-permute-done | bytes 270368 | tf_op jit(solution)/shard_map/ppermute | solution.py:486
  19.1 5.8 %collective-permute-done.4.refs_0_ = bf16[512,256]{1,0:T(8,128)(2,1)S(1)} collective-permute-done((bf16[512,256]{1,0:T(8,128)(2,1)S(1)}, bf16[512,256]{1,0:T(8,128)(2,1)S(1)}, u32[]{:S(2)}, u32[]{:S(2)}) %collective-permute-start.4) | collective-permute-done | bytes 262176 | tf_op jit(solution)/shard_map/ppermute | solution.py:478
  24.9 1.7 %statistics_1.1 = (bf16[528,256]{1,0:T(8,128)(2,1)S(1)}, f32[512,1024]{1,0:T(8,128)S(1)}) custom-call(bf16[512,256]{1,0:T(8,128)(2,1)S(1)} %collective-permute-done.3.refs_0_, bf16[512,256]{1,0:T(8,128)(2,1)S(1)} %collective-permute-done.6.refs_1_, bf16[528,256]{1,0:T(8,128)(2,1)S(1)} %get-tuple-element.34.refs_2_.exp_ref.refs_0_, ...), custom_call_target="tpu_custom_call" | custom-call | flops 1024 | bytes 1024 | tf_op jit(solution)/shard_map/statistics_1/pallas_call | solution.py:309
  26.6 1.7 %statistics_3.1 = (bf16[528,256]{1,0:T(8,128)(2,1)S(1)}, f32[512,1024]{1,0:T(8,128)S(1)}) custom-call(bf16[512,256]{1,0:T(8,128)(2,1)S(1)} %collective-permute-done.4.refs_0_, bf16[512,256]{1,0:T(8,128)(2,1)S(1)} %collective-permute-done.5.refs_1_, bf16[528,256]{1,0:T(8,128)(2,1)S(1)} %get-tuple-element.34.refs_2_.exp_ref.refs_0_, ...), custom_call_target="tpu_custom_call" | custom-call | flops 1024 | bytes 1024 | tf_op jit(solution)/shard_map/statistics_3/pallas_call | solution.py:309
  28.9 0.7 %collective-permute-start.12 = (bf16[528,256]{1,0:T(8,128)(2,1)S(1)}, bf16[528,256]{1,0:T(8,128)(2,1)S(1)}, u32[]{:S(2)}, u32[]{:S(2)}) collective-permute-start(bf16[528,256]{1,0:T(8,128)(2,1)S(1)} %get-tuple-element.41), channel_id=1, source_target_pairs={{0,12},{4,0},{8,4},{12,8},{1,13},{5,1},{9,5},{13,9},{2,14},{6,2},{... | collective-permute-start | bytes 811016 | tf_op jit(solution)/shard_map/ppermute | solution.py:478
  29.5 1.7 %statistics_0.1 = (f32[256,256]{1,0:T(8,128)S(1)}, f32[256,256]{1,0:T(8,128)S(1)}, f32[512,1024]{1,0:T(8,128)S(1)}) custom-call(bf16[512,256]{1,0:T(8,128)(2,1)S(1)} %get-tuple-element.30.both_ref.refs_0_, bf16[784,256]{1,0:T(8,128)(2,1)S(1)} %collective-permute-done.refs_4_.refs_1_, bf16[528,256]{1,0:T(8,128)(2,1)S(1)} %get-tuple-element.34.refs_2_.exp_ref.refs_0_, ...), custom_call_target="tpu_custom_call" | custom-call | flops 1024 | bytes 1024 | tf_op jit(solution)/shard_map/statistics_0/pallas_call | solution.py:309
  31.2 1.7 %statistics_2.1 = (bf16[528,256]{1,0:T(8,128)(2,1)S(1)}, f32[256,1024]{1,0:T(8,128)S(1)}, bf16[256,512]{1,0:T(8,128)(2,1)S(1)}, bf16[256,512]{1,0:T(8,128)(2,1)S(1)}) custom-call(bf16[544,256]{1,0:T(8,128)(2,1)S(1)} %collective-permute-done.7.refs_0_, bf16[256,256]{1,0:T(8,128)(2,1)S(1)} %collective-permute-done.8.refs_1_, ...), custom_call_target="tpu_custom_call" | custom-call | flops 1024 | bytes 1024 | tf_op jit(solution)/shard_map/statistics_2/pallas_call | solution.py:309
  33.1 1.3 %collective-permute-start.9 = (bf16[528,256]{1,0:T(8,128)(2,1)S(1)}, bf16[528,256]{1,0:T(8,128)(2,1)S(1)}, u32[]{:S(2)}, u32[]{:S(2)}) collective-permute-start(bf16[528,256]{1,0:T(8,128)(2,1)S(1)} %get-tuple-element.44), channel_id=1, source_target_pairs={{0,4},{4,8},{8,12},{12,0},{1,5},{5,9},{9,13},{13,1},{2,6},{6,10},{... | collective-permute-start | bytes 811016 | tf_op jit(solution)/shard_map/ppermute | solution.py:478
  34.5 2.9 %collective-permute-done.12.came_ref = bf16[528,256]{1,0:T(8,128)(2,1)S(1)} collective-permute-done((bf16[528,256]{1,0:T(8,128)(2,1)S(1)}, bf16[528,256]{1,0:T(8,128)(2,1)S(1)}, u32[]{:S(2)}, u32[]{:S(2)}) %collective-permute-start.12) | collective-permute-done | bytes 270368 | tf_op jit(solution)/shard_map/ppermute | solution.py:478
  37.6 3.1 %collective-permute-start.13 = (bf16[272,256]{1,0:T(8,128)(2,1)S(1)}, bf16[272,256]{1,0:T(8,128)(2,1)S(1)}, u32[]{:S(2)}, u32[]{:S(2)}) collective-permute-start(bf16[272,256]{1,0:T(8,128)(2,1)S(1)} %get-tuple-element.49), channel_id=1, source_target_pairs={{0,12},{4,0},{8,4},{12,8},{1,13},{5,1},{9,5},{13,9},{2,14},{6,2},{... | collective-permute-start | bytes 417800 | tf_op jit(solution)/shard_map/ppermute | solution.py:478
  40.7 1.2 %collective-permute-start.16 = (bf16[256,512]{1,0:T(8,128)(2,1)S(1)}, bf16[256,512]{1,0:T(8,128)(2,1)S(1)}, u32[]{:S(2)}, u32[]{:S(2)}) collective-permute-start(bf16[256,512]{1,0:T(8,128)(2,1)S(1)} %merge_items.1), channel_id=1, source_target_pairs={{0,2},{2,0},{1,3},{3,1},{4,6},{6,4},{5,7},{7,5},{8,10},{10,8},{9,1... | collective-permute-start | bytes 786440 | tf_op jit(solution)/shard_map/ppermute | solution.py:486
  42.1 4.9 %collective-permute-done.13.refs_3_ = bf16[272,256]{1,0:T(8,128)(2,1)S(1)} collective-permute-done((bf16[272,256]{1,0:T(8,128)(2,1)S(1)}, bf16[272,256]{1,0:T(8,128)(2,1)S(1)}, u32[]{:S(2)}, u32[]{:S(2)}) %collective-permute-start.13) | collective-permute-done | bytes 139296 | tf_op jit(solution)/shard_map/ppermute | solution.py:478
  47.0 0.6 %collective-permute-start.10 = (bf16[256,256]{1,0:T(8,128)(2,1)S(1)}, bf16[256,256]{1,0:T(8,128)(2,1)S(1)}, u32[]{:S(2)}, u32[]{:S(2)}) collective-permute-start(bf16[256,256]{1,0:T(8,128)(2,1)S(1)} %convert_add_fusion), channel_id=1, source_target_pairs={{0,1},{1,0},{2,3},{3,2},{4,5},{5,4},{6,7},{7,6},{8,9},{9,8},{10,11... | collective-permute-start | bytes 393224 | tf_op jit(solution)/shard_map/ppermute | solution.py:505
  47.6 1.1 %finish_rates.1 = (f32[512,256]{1,0:T(8,128)}, f32[512,256]{1,0:T(8,128)}) custom-call(bf16[528,256]{1,0:T(8,128)(2,1)S(1)} %get-tuple-element.34.refs_2_.exp_ref.refs_0_, bf16[528,256]{1,0:T(8,128)(2,1)S(1)} %collective-permute-done.1.refs_3_.refs_1_, bf16[528,256]{1,0:T(8,128)(2,1)S(1)} %collective-permute-done.9.refs_2_.refs_5_, ...), custom_call_target="tpu_custom_call" | custom-call | flops 1024 | bytes 1024 | tf_op jit(solution)/shard_map/finish_rates/pallas_call | solution.py:393
  48.7 0.7 %collective-permute-done.16.refs_1_ = bf16[256,512]{1,0:T(8,128)(2,1)S(1)} collective-permute-done((bf16[256,512]{1,0:T(8,128)(2,1)S(1)}, bf16[256,512]{1,0:T(8,128)(2,1)S(1)}, u32[]{:S(2)}, u32[]{:S(2)}) %collective-permute-start.16) | collective-permute-done | bytes 262176 | tf_op jit(solution)/shard_map/ppermute | solution.py:486
  49.4 0.9 %finish_items.1 = f32[512,256]{1,0:T(8,128)} custom-call(bf16[528,256]{1,0:T(8,128)(2,1)S(1)} %get-tuple-element.34.refs_2_.exp_ref.refs_0_, f32[256,1024]{1,0:T(8,128)S(1)} %get-tuple-element.46.mine_ref.own_ref, bf16[256,512]{1,0:T(8,128)(2,1)S(1)} %collective-permute-done.15.refs_0_, bf16[256,512]{1,0:T(8,128)(2,1)S(1)} %collective-permute-done.16.refs_1_), custom_call_target="tpu_custom_call" | custom-call | flops 1024 | bytes 1024 | tf_op jit(solution)/shard_map/finish_items/pallas_call | solution.py:465
  50.4 0.9 %finish_users.1 = f32[512,256]{1,0:T(8,128)} custom-call(bf16[512,256]{1,0:T(8,128)(2,1)S(1)} %get-tuple-element.30.both_ref.refs_0_, f32[256,256]{1,0:T(8,128)S(1)} %get-tuple-element.37.refs_1_, bf16[256,256]{1,0:T(8,128)(2,1)S(1)} %collective-permute-done.10.refs_2_, bf16[272,256]{1,0:T(8,128)(2,1)S(1)} %collective-permute-done.14.refs_3_, ...), custom_call_target="tpu_custom_call" | custom-call | flops 1024 | bytes 1024 | tf_op jit(solution)/shard_map/finish_users/pallas_call | solution.py:433
  (30 shorter events, 1.8 us)
Async XLA Ops:
  2.4 11.4 %collective-permute-start.3 = (bf16[512,256]{1,0:T(8,128)(2,1)S(1)}, bf16[512,256]{1,0:T(8,128)(2,1)S(1)}, u32[]{:S(2)}, u32[]{:S(2)}) collective-permute-start(bf16[512,256]{1,0:T(8,128)(2,1)S(1)} %get-tuple-element.30.both_ref.refs_0_), channel_id=1, source_target_pairs={{0,4},{4,8},{8,12},{12,0},{1,5},{5,9},{9,13},{13,1},{2,6},{6,10},{... | collective-permute-start | bytes 786440 | tf_op jit(solution)/shard_map/ppermute | solution.py:478
  10.1 8.5 %collective-permute-start.1 = (bf16[528,256]{1,0:T(8,128)(2,1)S(1)}, bf16[528,256]{1,0:T(8,128)(2,1)S(1)}, u32[]{:S(2)}, u32[]{:S(2)}) collective-permute-start(bf16[528,256]{1,0:T(8,128)(2,1)S(1)} %get-tuple-element.34.refs_2_.exp_ref.refs_0_), channel_id=1, source_target_pairs={{0,2},{2,0},{1,3},{3,1},{4,6},{6,4},{5,7},{7,5},{8,10},{10,8},{9,1... | collective-permute-start | bytes 811016 | tf_op jit(solution)/shard_map/ppermute | solution.py:486
  13.8 11.1 %collective-permute-start.4 = (bf16[512,256]{1,0:T(8,128)(2,1)S(1)}, bf16[512,256]{1,0:T(8,128)(2,1)S(1)}, u32[]{:S(2)}, u32[]{:S(2)}) collective-permute-start(bf16[512,256]{1,0:T(8,128)(2,1)S(1)} %collective-permute-done.3.refs_0_), channel_id=1, source_target_pairs={{0,4},{4,8},{8,12},{12,0},{1,5},{5,9},{9,13},{13,1},{2,6},{6,10},{... | collective-permute-start | bytes 786440 | tf_op jit(solution)/shard_map/ppermute | solution.py:478
  13.8 11.1 %collective-permute-start = (bf16[784,256]{1,0:T(8,128)(2,1)S(1)}, bf16[784,256]{1,0:T(8,128)(2,1)S(1)}, u32[]{:S(2)}, u32[]{:S(2)}) collective-permute-start(bf16[784,256]{1,0:T(8,128)(2,1)S(1)} %get-tuple-element.32), channel_id=1, source_target_pairs={{0,1},{1,0},{2,3},{3,2},{4,5},{5,4},{6,7},{7,6},{8,9},{9,8},{10,11... | collective-permute-start | bytes 1204232 | tf_op jit(solution)/shard_map/ppermute | solution.py:505
  13.8 14.7 %collective-permute-start.7 = (bf16[544,256]{1,0:T(8,128)(2,1)S(1)}, bf16[544,256]{1,0:T(8,128)(2,1)S(1)}, u32[]{:S(2)}, u32[]{:S(2)}) collective-permute-start(bf16[544,256]{1,0:T(8,128)(2,1)S(1)} %get-tuple-element.40), channel_id=1, source_target_pairs={{0,12},{4,0},{8,4},{12,8},{1,13},{5,1},{9,5},{13,9},{2,14},{6,2},{... | collective-permute-start | bytes 835592 | tf_op jit(solution)/shard_map/ppermute | solution.py:478
  18.6 6.3 %collective-permute-start.2 = (bf16[528,256]{1,0:T(8,128)(2,1)S(1)}, bf16[528,256]{1,0:T(8,128)(2,1)S(1)}, u32[]{:S(2)}, u32[]{:S(2)}) collective-permute-start(bf16[528,256]{1,0:T(8,128)(2,1)S(1)} %collective-permute-done.1.refs_3_.refs_1_), channel_id=1, source_target_pairs={{0,1},{1,0},{2,3},{3,2},{4,5},{5,4},{6,7},{7,6},{8,9},{9,8},{10,11... | collective-permute-start | bytes 811016 | tf_op jit(solution)/shard_map/ppermute | solution.py:505
  18.6 6.3 %collective-permute-start.6 = (bf16[512,256]{1,0:T(8,128)(2,1)S(1)}, bf16[512,256]{1,0:T(8,128)(2,1)S(1)}, u32[]{:S(2)}, u32[]{:S(2)}) collective-permute-start(bf16[512,256]{1,0:T(8,128)(2,1)S(1)} %collective-permute-done.3.refs_0_), channel_id=1, source_target_pairs={{0,1},{1,0},{2,3},{3,2},{4,5},{5,4},{6,7},{7,6},{8,9},{9,8},{10,11... | collective-permute-start | bytes 786440 | tf_op jit(solution)/shard_map/ppermute | solution.py:505
  24.9 1.7 %collective-permute-start.5 = (bf16[512,256]{1,0:T(8,128)(2,1)S(1)}, bf16[512,256]{1,0:T(8,128)(2,1)S(1)}, u32[]{:S(2)}, u32[]{:S(2)}) collective-permute-start(bf16[512,256]{1,0:T(8,128)(2,1)S(1)} %collective-permute-done.4.refs_0_), channel_id=1, source_target_pairs={{0,1},{1,0},{2,3},{3,2},{4,5},{5,4},{6,7},{7,6},{8,9},{9,8},{10,11... | collective-permute-start | bytes 786440 | tf_op jit(solution)/shard_map/ppermute | solution.py:505
  28.5 2.7 %collective-permute-start.8 = (bf16[256,256]{1,0:T(8,128)(2,1)S(1)}, bf16[256,256]{1,0:T(8,128)(2,1)S(1)}, u32[]{:S(2)}, u32[]{:S(2)}) collective-permute-start(bf16[256,256]{1,0:T(8,128)(2,1)S(1)} %slice.6), channel_id=1, source_target_pairs={{0,1},{1,0},{2,3},{3,2},{4,5},{5,4},{6,7},{7,6},{8,9},{9,8},{10,11... | collective-permute-start | bytes 393224 | tf_op jit(solution)/shard_map/ppermute | solution.py:505
  28.9 8.6 %collective-permute-start.12 = (bf16[528,256]{1,0:T(8,128)(2,1)S(1)}, bf16[528,256]{1,0:T(8,128)(2,1)S(1)}, u32[]{:S(2)}, u32[]{:S(2)}) collective-permute-start(bf16[528,256]{1,0:T(8,128)(2,1)S(1)} %get-tuple-element.41), channel_id=1, source_target_pairs={{0,12},{4,0},{8,4},{12,8},{1,13},{5,1},{9,5},{13,9},{2,14},{6,2},{... | collective-permute-start | bytes 811016 | tf_op jit(solution)/shard_map/ppermute | solution.py:478
  32.9 14.8 %copy-start = (f32[1,512]{1,0:T(1,128)S(1)}, f32[1,512]{1,0:T(1,128)}, u32[]{:S(2)}) copy-start(f32[1,512]{1,0:T(1,128)} %refs_4_.1) | copy-start | bytes 6148
  32.9 14.7 %copy-start.1 = (f32[1,512]{1,0:T(1,128)S(1)}, f32[1,512]{1,0:T(1,128)}, u32[]{:S(2)}) copy-start(f32[1,512]{1,0:T(1,128)} %refs_5_.1) | copy-start | bytes 6148
  32.9 1.6 %collective-permute-start.11 = (bf16[256,512]{1,0:T(8,128)(2,1)S(1)}, bf16[256,512]{1,0:T(8,128)(2,1)S(1)}, u32[]{:S(2)}, u32[]{:S(2)}) collective-permute-start(bf16[256,512]{1,0:T(8,128)(2,1)S(1)} %get-tuple-element.47), channel_id=1, source_target_pairs={{0,1},{1,0},{2,3},{3,2},{4,5},{5,4},{6,7},{7,6},{8,9},{9,8},{10,11... | collective-permute-start | bytes 786440 | tf_op jit(solution)/shard_map/ppermute | solution.py:505
  33.1 13.9 %collective-permute-start.9 = (bf16[528,256]{1,0:T(8,128)(2,1)S(1)}, bf16[528,256]{1,0:T(8,128)(2,1)S(1)}, u32[]{:S(2)}, u32[]{:S(2)}) collective-permute-start(bf16[528,256]{1,0:T(8,128)(2,1)S(1)} %get-tuple-element.44), channel_id=1, source_target_pairs={{0,4},{4,8},{8,12},{12,0},{1,5},{5,9},{9,13},{13,1},{2,6},{6,10},{... | collective-permute-start | bytes 811016 | tf_op jit(solution)/shard_map/ppermute | solution.py:478
  37.6 9.4 %collective-permute-start.13 = (bf16[272,256]{1,0:T(8,128)(2,1)S(1)}, bf16[272,256]{1,0:T(8,128)(2,1)S(1)}, u32[]{:S(2)}, u32[]{:S(2)}) collective-permute-start(bf16[272,256]{1,0:T(8,128)(2,1)S(1)} %get-tuple-element.49), channel_id=1, source_target_pairs={{0,12},{4,0},{8,4},{12,8},{1,13},{5,1},{9,5},{13,9},{2,14},{6,2},{... | collective-permute-start | bytes 417800 | tf_op jit(solution)/shard_map/ppermute | solution.py:478
  40.7 8.0 %collective-permute-start.15 = (bf16[256,512]{1,0:T(8,128)(2,1)S(1)}, bf16[256,512]{1,0:T(8,128)(2,1)S(1)}, u32[]{:S(2)}, u32[]{:S(2)}) collective-permute-start(bf16[256,512]{1,0:T(8,128)(2,1)S(1)} %get-tuple-element.50), channel_id=1, source_target_pairs={{0,1},{1,0},{2,3},{3,2},{4,5},{5,4},{6,7},{7,6},{8,9},{9,8},{10,11... | collective-permute-start | bytes 786440 | tf_op jit(solution)/shard_map/ppermute | solution.py:505
  40.7 8.7 %collective-permute-start.16 = (bf16[256,512]{1,0:T(8,128)(2,1)S(1)}, bf16[256,512]{1,0:T(8,128)(2,1)S(1)}, u32[]{:S(2)}, u32[]{:S(2)}) collective-permute-start(bf16[256,512]{1,0:T(8,128)(2,1)S(1)} %merge_items.1), channel_id=1, source_target_pairs={{0,2},{2,0},{1,3},{3,1},{4,6},{6,4},{5,7},{7,5},{8,10},{10,8},{9,1... | collective-permute-start | bytes 786440 | tf_op jit(solution)/shard_map/ppermute | solution.py:486
  42.0 8.5 %collective-permute-start.17 = (bf16[288,256]{1,0:T(8,128)(2,1)S(1)}, bf16[288,256]{1,0:T(8,128)(2,1)S(1)}, u32[]{:S(2)}, u32[]{:S(2)}) collective-permute-start(bf16[288,256]{1,0:T(8,128)(2,1)S(1)} %get-tuple-element.54), channel_id=1, source_target_pairs={{0,12},{4,0},{8,4},{12,8},{1,13},{5,1},{9,5},{13,9},{2,14},{6,2},{... | collective-permute-start | bytes 442376 | tf_op jit(solution)/shard_map/ppermute | solution.py:478
  47.0 3.4 %collective-permute-start.14 = (bf16[272,256]{1,0:T(8,128)(2,1)S(1)}, bf16[272,256]{1,0:T(8,128)(2,1)S(1)}, u32[]{:S(2)}, u32[]{:S(2)}) collective-permute-start(bf16[272,256]{1,0:T(8,128)(2,1)S(1)} %collective-permute-done.13.refs_3_), channel_id=1, source_target_pairs={{0,1},{1,0},{2,3},{3,2},{4,5},{5,4},{6,7},{7,6},{8,9},{9,8},{10,11... | collective-permute-start | bytes 417800 | tf_op jit(solution)/shard_map/ppermute | solution.py:505
  47.0 3.4 %collective-permute-start.10 = (bf16[256,256]{1,0:T(8,128)(2,1)S(1)}, bf16[256,256]{1,0:T(8,128)(2,1)S(1)}, u32[]{:S(2)}, u32[]{:S(2)}) collective-permute-start(bf16[256,256]{1,0:T(8,128)(2,1)S(1)} %convert_add_fusion), channel_id=1, source_target_pairs={{0,1},{1,0},{2,3},{3,2},{4,5},{5,4},{6,7},{7,6},{8,9},{9,8},{10,11... | collective-permute-start | bytes 393224 | tf_op jit(solution)/shard_map/ppermute | solution.py:505
